TPU v7x, 256 devices: a whole 4x4x8 slice. The times are simulated.
256 devices in a mesh: frame: 16 (over y_lo, x, core), tok: 16 (over y_hi, z).
Axes of the slice: x: 4, y: 4 (y_hi: 2, y_lo: 2; y = y_hi * 2 + y_lo), z: 8, core: 2. Of those that a mesh axis runs over, the one named last changes fastest.
Arguments:
- inputs: bfloat16 [16, 2048, 4096], P('frame', 'tok'), may hold values from -40 to 40
- grad_attn: bfloat16 [16, 2048, 2048], P('frame', None, 'tok'), may hold values from -6 to 6
- w_qkv: bfloat16 [4096, 3, 2048], P(None, None, 'tok'), may hold values from -0.09375 to 0.09375
Outputs:
- grad_qkv: bfloat16 [4096, 3, 2048], P('frame', None, 'tok')
All inputs are finite; a program needn't handle non-finite values.
Results may differ from a plain program's by a relative error of at most 0.009.
The roundings to bfloat16 on the way count: a program that leaves them out, or rounds other values in their place, can miss the bound.
Values may be sent and summed in bfloat16 or wider, within the bound.
No kernel may reach another device: no remote copies, remote signals or barrier semaphores. Data moves between devices by JAX's collectives and lax.ppermute only.
A program may use at most 128 MiB of HBM per device.

v0:
```python
import math

import jax
import jax.numpy as jnp
from jax import lax
from jax.sharding import PartitionSpec as P

HEAD_DIM = 128


def attend_probs(query_t, key_t):
    factor = 1.0 / math.sqrt(query_t.shape[-1])
    scores = (
        jnp.einsum("tphd,sphd->phts", query_t, key_t, preferred_element_type=jnp.float32) * factor
    )
    frame_count = scores.shape[-1]
    steps_idx = jnp.arange(frame_count)
    causal = steps_idx[None, :] <= steps_idx[:, None]
    scores = jnp.where(causal, scores, -1e30)
    maxima = jnp.max(scores, axis=-1, keepdims=True)
    exponent = jnp.exp(scores - maxima)
    return exponent / jnp.sum(exponent, axis=-1, keepdims=True)


def attend_backward(query_t, key_t, value_t, attention, grad_t):
    factor = 1.0 / math.sqrt(query_t.shape[-1])
    grad_probs = jnp.einsum("tphd,sphd->phts", grad_t, value_t, preferred_element_type=jnp.float32)
    row_dot = jnp.sum(grad_probs * attention, axis=-1, keepdims=True)
    grad_scores = (attention * (grad_probs - row_dot)).astype(jnp.bfloat16)
    weights_b = attention.astype(jnp.bfloat16)
    grad_query = (
        jnp.einsum("phts,sphd->tphd", grad_scores, key_t, preferred_element_type=jnp.float32)
        * factor
    )
    grad_keys = (
        jnp.einsum("phts,tphd->sphd", grad_scores, query_t, preferred_element_type=jnp.float32)
        * factor
    )
    grad_values = jnp.einsum(
        "phts,tphd->sphd", weights_b, grad_t, preferred_element_type=jnp.float32
    )
    return (
        grad_query.astype(jnp.bfloat16),
        grad_keys.astype(jnp.bfloat16),
        grad_values.astype(jnp.bfloat16),
    )


def time_grads(projected, grad_heads):
    query_t = projected[:, :, 0]
    key_t = projected[:, :, 1]
    value_t = projected[:, :, 2]
    attention = attend_probs(query_t, key_t)
    grad_query, grad_keys, grad_values = attend_backward(
        query_t, key_t, value_t, attention, grad_heads
    )
    return jnp.stack((grad_query, grad_keys, grad_values), axis=2)


def local(inputs, grad_attn, w_qkv):
    width = inputs.shape[2]
    head_cols = w_qkv.shape[2]
    local_heads = head_cols // HEAD_DIM
    whole = lax.all_gather(inputs, "tok", axis=1, tiled=True)
    frames_here = whole.shape[0]
    rows_here = whole.shape[1]
    projected = jnp.einsum(
        "fpd,djc->fpjc", whole, w_qkv, preferred_element_type=jnp.float32
    ).astype(jnp.bfloat16)
    projected = projected.reshape(frames_here, rows_here, 3, local_heads, HEAD_DIM)
    grad_heads = grad_attn.reshape(1, rows_here, local_heads, HEAD_DIM)
    proj_time = lax.all_to_all(projected, "frame", split_axis=1, concat_axis=0, tiled=True)
    grad_time = lax.all_to_all(grad_heads, "frame", split_axis=1, concat_axis=0, tiled=True)
    stacked = time_grads(proj_time, grad_time)
    grads_back = lax.all_to_all(stacked, "frame", split_axis=0, concat_axis=1, tiled=True)
    grad_proj = grads_back[0].reshape(rows_here, 3, head_cols)
    rows_mat = whole.reshape(frames_here * rows_here, width)
    share = lax.psum_scatter(
        jnp.einsum("pr,pjc->rjc", rows_mat, grad_proj, preferred_element_type=jnp.float32),
        "frame",
        scatter_dimension=0,
        tiled=True,
    )
    return share.astype(jnp.bfloat16)


def solution(mesh):
    in_specs = (P("frame", "tok", None), P("frame", None, "tok"), P(None, None, "tok"))
    out_specs = P("frame", None, "tok")
    return jax.shard_map(local, mesh=mesh, in_specs=in_specs, out_specs=out_specs, check_vma=False)
```

profile of v0, /device:TPU:3, one launch (start us, length us, event | category | flops | bytes accessed | tf_op | source)
XLA Modules:
  0.0 419.2 jit_solution(7724349660740309038)
XLA Ops:
  6.5 0.0 copy-start
  6.5 0.0 all-gather.2.cloned.1.call-start
  6.5 0.7 all-gather.2.cloned.1.call-update
  7.3 2.8 copy.66
  10.1 0.5 broadcast.25
  10.6 13.4 %reduce.6 = bf16[2048,128]{1,0:T(8,128)(2,1)} reduce(bf16[2048,1,1,128]{3,2,1,0:T(2,128)(2,1)} %bitcast.70, bf16[]{:T(256)} %broadcast.25), dimensions={1,2}, to_apply=%bitcast.66.reduce_sub_computation | reduce | bytes 1048578
  23.9 2.0 reshape.96
  25.9 6.6 %all-to-all-start.1 = ((bf16[16,2,8192]{2,1,0:T(2,128)(2,1)}), bf16[16,2,8192]{2,1,0:T(2,128)(2,1)}, u32[]{:S(2)}, u32[]{:S(2)}) async-start(bf16[16,2,8192]{2,1,0:T(2,128)(2,1)} %reshape.96), calls=%async_computation.1 | async-start | bytes 1048576 | tf_op jit(solution)/shard_map/all_to_all | solution.py:73
  32.5 210.6 %all-gather.2.cloned.1.call-done = bf16[1,2048,4096]{2,1,0:T(8,128)(2,1)} async-done(((bf16[1,128,4096]{2,1,0:T(8,128)(2,1)}), bf16[1,2048,4096]{2,1,0:T(8,128)(2,1)}) %all-gather.2.cloned.1.call-update) | async-done | bytes 16777232 | tf_op jit(solution)/shard_map/all_gather | solution.py:64
  243.2 0.0 copy-done
  243.2 12.4 %fusion.11 = bf16[1,2048,3,1,128]{4,1,2,3,0:T(8,128)(2,1)S(1)} fusion(bf16[4096,3,128]{2,0,1:T(8,128)(2,1)S(1)} %copy-done, bf16[1,2048,4096]{2,1,0:T(8,128)(2,1)} %all-gather.2.cloned.1.call-done), kind=kOutput, calls=%fused_computation.7 | convolution fusion | flops 6443237376 | bytes 21495808 | tf_op jit(solution)/shard_map/fpd,djc->fpjc/dot_general | solution.py:67
  255.6 10.8 %copy.26 = bf16[1,2048,3,1,128]{4,2,3,0,1:T(4,128)(2,1)} copy(bf16[1,2048,3,1,128]{4,1,2,3,0:T(8,128)(2,1)S(1)} %fusion.11) | data formatting | bytes 3145728 | tf_op jit(solution)/shard_map/reshape | solution.py:70
  266.3 0.0 all-to-all-done.1
  266.3 5.6 %all-to-all-start = ((bf16[1,2048,3,1,128]{4,2,3,0,1:T(4,128)(2,1)}), bf16[1,2048,3,1,128]{4,2,3,0,1:T(4,128)(2,1)}, u32[]{:S(2)}, u32[]{:S(2)}) async-start(bf16[1,2048,3,1,128]{4,2,3,0,1:T(4,128)(2,1)} %copy.26), calls=%async_computation | async-start | bytes 4194304 | tf_op jit(solution)/shard_map/all_to_all | solution.py:72
  271.9 0.3 reduce-scatter.2.cloned.1.call-start
  272.2 3.5 reshape.97
  275.7 2.1 copy.41
  277.8 22.6 %all-to-all-done = bf16[1,2048,3,1,128]{4,2,3,0,1:T(4,128)(2,1)} async-done(((bf16[1,2048,3,1,128]{4,2,3,0,1:T(4,128)(2,1)}), bf16[1,2048,3,1,128]{4,2,3,0,1:T(4,128)(2,1)}, u32[]{:S(2)}, u32[]{:S(2)}) %all-to-all-start) | async-done | bytes 1572896 | tf_op jit(solution)/shard_map/all_to_all | solution.py:72
  300.4 1.8 copy.27
  302.3 1.2 fusion.25
  303.5 3.2 fusion.26
  306.7 0.0 copy-start.3
  306.7 0.0 copy-start.4
  306.7 0.0 copy-start.5
  306.7 2.0 fusion.21
  308.7 0.0 copy-done.3
  308.7 0.0 copy-done.4
  308.7 0.0 copy-done.5
  308.7 0.8 multiply_reduce_fusion
  309.5 0.0 copy-start.2
  309.5 0.0 copy-start.1
  309.6 0.2 multiply_convert_fusion
  309.8 0.8 copy-done.2
  310.6 0.5 fusion.19
  311.1 0.0 copy-done.1
  311.1 0.5 fusion.20
  311.6 0.2 pad_maximum_fusion
  311.8 0.4 copy.35
  312.2 23.5 %all_to_all.30 = bf16[16,128,3,1,128]{4,1,3,2,0:T(8,128)(2,1)S(1)} all-to-all(bf16[16,128,3,1,128]{4,1,3,2,0:T(8,128)(2,1)S(1)} %copy.35), channel_id=1, replica_groups=mesh['frame'=16,'tok'=16] {'frame'}, dimensions={0} | all-to-all | bytes 3145728 | tf_op jit(solution)/shard_map/all_to_all | solution.py:75
  335.6 0.1 copy.36
  335.7 12.2 %fusion.5 = f32[4096,3,128]{0,2,1:T(8,128)} fusion(bf16[2048,3,128]{2,0,1:T(8,128)(2,1)S(1)} %bitcast.67, bf16[1,2048,4096]{2,1,0:T(8,128)(2,1)} %all-gather.2.cloned.1.call-done), kind=kOutput, calls=%fused_computation.5 | convolution fusion | flops 6442450944 | bytes 24641536 | tf_op jit(solution)/shard_map/pr,pjc->rjc/dot_general | solution.py:79
  347.9 0.0 reduce-scatter.2.cloned.1.call-update
  347.9 62.6 %reduce-scatter.2.cloned.1.call-done = f32[256,3,128]{0,2,1:T(8,128)} async-done(((f32[4096,3,128]{0,2,1:T(8,128)}), f32[256,3,128]{0,2,1:T(8,128)}) %reduce-scatter.2.cloned.1.call-update) | async-done | bytes 393232 | tf_op jit(solution)/shard_map/reduce_scatter | solution.py:78
  410.5 1.0 convert_element_type.58
  411.6 0.8 copy.38
  (1 shorter events, 0.0 us)
Async XLA Ops:
  6.5 236.6 %copy-start = (bf16[4096,3,128]{2,0,1:T(8,128)(2,1)S(1)}, bf16[4096,3,128]{2,0,1:T(8,128)(2,1)}, u32[]{:S(2)}) copy-start(bf16[4096,3,128]{2,0,1:T(8,128)(2,1)} %param.5) | copy-start | bytes 9437188
  6.5 236.6 %all-gather.2.cloned.1.call-start = ((), (), s32[]{:S(2)}) async-start(), calls=%async_computation.4 | async-start | bytes 17825792 | tf_op jit(solution)/shard_map/all_gather | solution.py:64
  25.9 240.4 %all-to-all-start.1 = ((bf16[16,2,8192]{2,1,0:T(2,128)(2,1)}), bf16[16,2,8192]{2,1,0:T(2,128)(2,1)}, u32[]{:S(2)}, u32[]{:S(2)}) async-start(bf16[16,2,8192]{2,1,0:T(2,128)(2,1)} %reshape.96), calls=%async_computation.1 | async-start | bytes 1048576 | tf_op jit(solution)/shard_map/all_to_all | solution.py:73
  266.3 34.1 %all-to-all-start = ((bf16[1,2048,3,1,128]{4,2,3,0,1:T(4,128)(2,1)}), bf16[1,2048,3,1,128]{4,2,3,0,1:T(4,128)(2,1)}, u32[]{:S(2)}, u32[]{:S(2)}) async-start(bf16[1,2048,3,1,128]{4,2,3,0,1:T(4,128)(2,1)} %copy.26), calls=%async_computation | async-start | bytes 4194304 | tf_op jit(solution)/shard_map/all_to_all | solution.py:72
  271.9 138.6 %reduce-scatter.2.cloned.1.call-start = ((), (), s32[]{:S(2)}) async-start(), calls=%async_computation.5 | async-start | bytes 6684672 | tf_op jit(solution)/shard_map/reduce_scatter | solution.py:78
  306.7 2.0 copy-start.3
  306.7 2.0 copy-start.4
  306.7 2.0 copy-start.5
  309.5 1.0 copy-start.2
  309.5 1.5 copy-start.1
Sparse Core Ops, SparseCore 0:
  9.9 233.1 all-gather.1
  348.1 62.4 reduce-scatter.1
where the time goes:
time: 427 us; the launch traced here: 419 us
  waiting for transfers between devices  297 us (70%)
  matrix products  31.5 us (7%)
  local copies, waits for them, and re-layouts  26.8 us (6%)
  blocking collectives  23.5 us (6%)
  other arithmetic  14.8 us (3%)
  between operations  13.5 us (3%)
  starting transfers between devices  12.5 us (3%)
    all_gather x1, waiting for transfers between devices, local(): whole = lax.all_gather(inputs, 'tok', axis=1, tiled=True)  211 us
    reduce_scatter x1, waiting for transfers between devices, local(): lax.psum_scatter(jnp.einsum('pr,pjc->rjc', rows_mat, grad_proj, preferred...  62.6 us
    all_to_all x1, blocking collectives, local(): lax.all_to_all(stacked, 'frame', split_axis=0, concat_axis=1, tiled=True)  23.5 us
    all_to_all x1, waiting for transfers between devices, local(): lax.all_to_all(projected, 'frame', split_axis=1, concat_axis=0, tiled=True)  22.6 us
    unnamed x1, other arithmetic  13.4 us
    dot_general x1, matrix products, local(): jnp.einsum('fpd,djc->fpjc', whole, w_qkv, preferred_element_type=jnp.floa...  12.4 us
    dot_general x1, matrix products, local(): jnp.einsum('pr,pjc->rjc', rows_mat, grad_proj, preferred_element_type=jnp...  12.2 us
    reshape x1, local copies, waits for them, and re-layouts, local(): projected.reshape(frames_here, rows_here, 3, local_heads, HEAD_DIM)  10.8 us
  transfers between devices with their start and end apart: 4, of which 3 were waited for; matrix products, arithmetic and copies ran while one was open for 11% of the time, Pallas kernels for 0%

commit v1 on v0

v1 whole, which is shorter than its diff:
```python
import functools
import math

import jax
import jax.numpy as jnp
from jax import lax
from jax.experimental import pallas as pl
from jax.experimental.pallas import tpu as pltpu
from jax.sharding import Mesh, PartitionSpec as P

HEAD_DIM = 128
AXES = ("yl", "x", "core", "yh", "z")
SIZES = (2, 4, 2, 2, 8)
FRAME = AXES[:3]
TOK = AXES[3:]
FRAMES = 16
PATCHES = 128
WIDTH = 4096
COLS = 3 * HEAD_DIM
ROWS = FRAMES * PATCHES
GROUP = 16
STEP = 512

SAME_CORE = ((0, 0), (0, 1), (0, -1), (1, 0), (0, 2), (1, 1), (1, -1), (1, 2))
SLOTS = [(dy, dx, dc) for dy, dx in SAME_CORE for dc in (0, 1)]


def shift(value, axis, by):
    count = SIZES[AXES.index(axis)]
    return lax.ppermute(value, axis, [(i, (i + by) % count) for i in range(count)])


def transpose_mesh(value, place=lambda row, col: (col, row)):
    pairs = []
    for row in range(16):
        for col in range(16):
            to_row, to_col = place(row, col)
            pairs.append((row * 16 + col, to_row * 16 + to_col))
    return lax.ppermute(value, AXES, pairs)


def gather_frames(own):
    half = PATCHES // 2
    quarter = PATCHES // 4
    low, high = slice(0, half), slice(half, PATCHES)
    left = shift(own, "x", 1)
    right = shift(own, "x", -1)
    other = shift(own, "yl", 1)
    far_low = shift(left[low], "x", 1)
    far_high = shift(right[high], "x", -1)
    other_left_low = shift(left[low], "yl", 1)
    other_right_low = shift(right[low], "yl", 1)
    other_left_high = shift(other[high], "x", 1)
    other_right_high = shift(other[high], "x", -1)
    other_far_low = shift(far_low, "yl", 1)
    other_far_a = shift(other_left_high[:quarter], "x", 1)
    other_far_b = shift(other_right_high[quarter:], "x", -1)
    pieces = [
        (0, 0, own),
        (1, 0, right),
        (2, 0, left),
        (3, 0, other),
        (4, 0, far_low),
        (4, half, far_high),
        (5, 0, other_right_low),
        (5, half, other_right_high),
        (6, 0, other_left_low),
        (6, half, other_left_high),
        (7, 0, other_far_low),
        (7, half, other_far_a),
        (7, half + quarter, other_far_b),
    ]
    out = []
    for place, first, piece in pieces:
        out.append((2 * place, first, piece))
        out.append((2 * place + 1, first, shift(piece, "core", 1)))
    return out


def frame_ids():
    yl, x, core = (lax.axis_index(name) for name in FRAME)
    ids = []
    for dy, dx, dc in SLOTS:
        ids.append((((yl + dy) % 2) * 4 + (x + dx) % 4) * 2 + (core + dc) % 2)
    return jnp.stack(ids).astype(jnp.int32)


def visible(ids):
    frame = jnp.repeat(ids, GROUP)
    patch = jnp.tile(jnp.arange(GROUP, dtype=jnp.int32), FRAMES)
    allowed = (frame[None, :] <= frame[:, None]) & (patch[None, :] == patch[:, None])
    return allowed.astype(jnp.float32)


def attend(proj, grads, mask, out):
    factor = 1.0 / math.sqrt(HEAD_DIM)
    size = FRAMES * GROUP

    def body(step, carry):
        rows = pl.ds(pl.multiple_of(step * GROUP, GROUP), GROUP)
        part = proj[:, rows, :].reshape(size, COLS)
        query, key, value = (part[:, j * HEAD_DIM : (j + 1) * HEAD_DIM] for j in range(3))
        grad = grads[:, rows, :].reshape(size, HEAD_DIM)
        across = (((1,), (1,)), ((), ()))
        down = (((0,), (0,)), ((), ()))
        dot = functools.partial(lax.dot_general, preferred_element_type=jnp.float32)
        scores = dot(query, key, across) * factor
        scores = jnp.where(mask[...] > 0.5, scores, -1e30)
        exponent = jnp.exp(scores - jnp.max(scores, axis=-1, keepdims=True))
        probs = exponent / jnp.sum(exponent, axis=-1, keepdims=True)
        grad_probs = dot(grad, value, across)
        row_dot = jnp.sum(grad_probs * probs, axis=-1, keepdims=True)
        grad_scores = (probs * (grad_probs - row_dot)).astype(jnp.bfloat16)
        probs_b = probs.astype(jnp.bfloat16)
        grad_query = jnp.dot(grad_scores, key, preferred_element_type=jnp.float32) * factor
        grad_key = dot(grad_scores, query, down) * factor
        grad_value = dot(probs_b, grad, down)
        for j, result in enumerate((grad_query, grad_key, grad_value)):
            out[:, rows, j * HEAD_DIM : (j + 1) * HEAD_DIM] = result.astype(jnp.bfloat16).reshape(
                FRAMES, GROUP, HEAD_DIM
            )
        return carry

    lax.fori_loop(0, PATCHES // GROUP, body, 0)


def kernel(places, ids, mask, w_ref, g_ref, *refs):
    count = len(places)
    pieces, out = refs[:count], refs[count]
    tokens, proj, grads, grad_proj, turned, sems = refs[count + 1 :]
    copies = []
    for index, (slot, first, ref) in enumerate(zip(*zip(*places), pieces)):
        rows = ref.shape[0]
        copies.append(
            pltpu.make_async_copy(
                ref, tokens.at[slot, pl.ds(first, rows)], sems.at[index]
            )
        )
    for copy in copies:
        copy.start()
    for slot in range(FRAMES):
        grads[slot] = g_ref[ids[slot]]
    for copy in copies:
        copy.wait()

    def project(step, carry):
        two = pl.ds(step * 2, 2)
        rows = tokens[two].reshape(2 * PATCHES, WIDTH)
        value = jnp.dot(rows, w_ref[...], preferred_element_type=jnp.float32)
        proj[two] = value.astype(jnp.bfloat16).reshape(2, PATCHES, COLS)
        return carry

    lax.fori_loop(0, FRAMES // 2, project, 0)
    attend(proj, grads, mask, grad_proj)
    for slot in range(FRAMES):
        part = grad_proj[slot].astype(jnp.float32)
        turned[:, slot * PATCHES : (slot + 1) * PATCHES] = part.T.astype(jnp.bfloat16)

    def weigh(step, carry):
        columns = pl.ds(pl.multiple_of(step * STEP, STEP), STEP)
        rows = tokens[:, :, columns].reshape(ROWS, STEP)
        value = jnp.dot(turned[...], rows, preferred_element_type=jnp.float32)
        out[columns, :] = value.T.astype(jnp.bfloat16)
        return carry

    lax.fori_loop(0, WIDTH // STEP, weigh, 0)


def weight_share(pieces, ids, mask, w, g):
    places = [(slot, first) for slot, first, _ in pieces]
    vmem = pl.BlockSpec(memory_space=pltpu.VMEM)
    return pl.pallas_call(
        functools.partial(kernel, places),
        out_shape=jax.ShapeDtypeStruct((WIDTH, COLS), jnp.bfloat16),
        in_specs=[pl.BlockSpec(memory_space=pltpu.SMEM), vmem, vmem, vmem]
        + [pl.BlockSpec(memory_space=pl.ANY)] * len(pieces),
        out_specs=vmem,
        scratch_shapes=[
            pltpu.VMEM((FRAMES, PATCHES, WIDTH), jnp.bfloat16),
            pltpu.VMEM((FRAMES, PATCHES, COLS), jnp.bfloat16),
            pltpu.VMEM((FRAMES, PATCHES, HEAD_DIM), jnp.bfloat16),
            pltpu.VMEM((FRAMES, PATCHES, COLS), jnp.bfloat16),
            pltpu.VMEM((COLS, ROWS), jnp.bfloat16),
            pltpu.SemaphoreType.DMA((len(pieces),)),
        ],
        compiler_params=pltpu.CompilerParams(vmem_limit_bytes=56 * 2**20),
    )(ids, mask, w, g, *[piece for _, _, piece in pieces])


def local(inputs, grad_attn, w_qkv):
    frame = lax.axis_index(FRAME)
    yh = lax.axis_index("yh")
    start = (2 * (frame % 8) + frame // 8) * 256
    slice_w = lax.dynamic_slice_in_dim(w_qkv.reshape(WIDTH, COLS), start, 256, 0)
    slice_w = transpose_mesh(slice_w)
    swapped = shift(slice_w, "yh", 1)
    pair = jnp.where(
        yh == 0, jnp.concatenate((slice_w, swapped)), jnp.concatenate((swapped, slice_w))
    )
    w = lax.all_gather(pair, "z", axis=0, tiled=True)
    g = transpose_mesh(grad_attn[0]).reshape(FRAMES, PATCHES, HEAD_DIM)
    g = lax.all_to_all(g, TOK, split_axis=0, concat_axis=0, tiled=True)
    ids = frame_ids()
    mask = visible(ids)
    pieces = gather_frames(inputs[0])
    share = weight_share(pieces, ids, mask, w, g)
    mine = lax.psum_scatter(share, "z", scatter_dimension=0, tiled=True).reshape(2, 256, COLS)
    total = None
    for other in range(2):
        part = lax.dynamic_index_in_dim(mine, (yh + other) % 2, 0, keepdims=False)
        part = transpose_mesh(
            part, lambda row, col: (2 * (col % 8) + (col // 8 + other) % 2, row)
        ).astype(jnp.float32)
        total = part if total is None else total + part
    return total.astype(jnp.bfloat16).reshape(256, 3, HEAD_DIM)


def solution(mesh):
    fine = Mesh(mesh.devices.reshape(SIZES), AXES)
    in_specs = (P(FRAME, TOK, None), P(FRAME, None, TOK), P(None, None, TOK))
    out_specs = P(FRAME, None, TOK)
    return jax.shard_map(local, mesh=fine, in_specs=in_specs, out_specs=out_specs, check_vma=False)
```

time: 427 us -> 284 us (0.67)
  the two profiles are of different devices: /device:TPU:3 before, /device:TPU:31 now
where the time goes in v1:
time: 284 us; the launch traced here: 283 us
  waiting for transfers between devices  175 us (62%)
  starting transfers between devices  51.6 us (18%)
  Pallas kernels  34.6 us (12%)
  between operations  13.8 us (5%)
  local copies, waits for them, and re-layouts  6.66 us (2%)
    ppermute x4, waiting for transfers between devices, transpose_mesh(): return lax.ppermute(value, AXES, pairs)  75.8 us
    reduce_scatter x1, waiting for transfers between devices, local(): lax.psum_scatter(share, 'z', scatter_dimension=0, tiled=True)  44 us
    ppermute x26, waiting for transfers between devices, shift(): lax.ppermute(value, axis, [(i, (i + by) % count) for i in range(count)])  43.3 us
    pallas_call x1, Pallas kernels, weight_share(): pl.pallas_call(functools.partial(kernel, places), out_shape=jax.ShapeDtyp...  34.6 us
    ppermute x4, starting transfers between devices, transpose_mesh(): return lax.ppermute(value, AXES, pairs)  25.1 us
    ppermute x26, starting transfers between devices, shift(): lax.ppermute(value, axis, [(i, (i + by) % count) for i in range(count)])  20.5 us
    all_to_all x1, waiting for transfers between devices, local(): g = lax.all_to_all(g, TOK, split_axis=0, concat_axis=0, tiled=True)  11.7 us
    all_to_all x1, starting transfers between devices, local(): g = lax.all_to_all(g, TOK, split_axis=0, concat_axis=0, tiled=True)  5.95 us
  transfers between devices with their start and end apart: 33, of which 14 were waited for; matrix products, arithmetic and copies ran while one was open for 1% of the time, Pallas kernels for 0%

profile of v1, /device:TPU:31, one launch (start us, length us, event | category | flops | bytes accessed | tf_op | source)
XLA Modules:
  0.0 283.3 jit_solution(8460374544356543840)
XLA Ops:
  6.5 3.2 %copy.5 = bf16[4096,3,128]{0,2,1:T(8,128)(2,1)S(1)} copy(bf16[4096,3,128]{2,0,1:T(8,128)(2,1)} %param.5) | data formatting | bytes 6291456 | tf_op args[2]
  9.8 0.2 copy.10
  10.0 8.0 %collective-permute-start = (bf16[256,384]{1,0:T(8,128)(2,1)S(1)}, bf16[256,384]{1,0:T(8,128)(2,1)S(1)}, u32[]{:S(2)}, u32[]{:S(2)}) collective-permute-start(bf16[256,384]{1,0:T(8,128)(2,1)S(1)} %copy.10), channel_id=1, source_target_pairs={{0,0},{1,16},{2,32},{3,48},{4,64},{5,80},{6,96},{7,112},{8,128},{9... | collective-permute-start | bytes 589832 | tf_op jit(solution)/shard_map/ppermute | solution.py:39
  17.9 13.7 %collective-permute-done = bf16[256,384]{1,0:T(8,128)(2,1)S(1)} collective-permute-done((bf16[256,384]{1,0:T(8,128)(2,1)S(1)}, bf16[256,384]{1,0:T(8,128)(2,1)S(1)}, u32[]{:S(2)}, u32[]{:S(2)}) %collective-permute-start) | collective-permute-done | bytes 196640 | tf_op jit(solution)/shard_map/ppermute | solution.py:39
  31.6 1.9 collective-permute-start.1
  33.4 6.2 %collective-permute-done.1 = bf16[256,384]{1,0:T(8,128)(2,1)S(1)} collective-permute-done((bf16[256,384]{1,0:T(8,128)(2,1)S(1)}, bf16[256,384]{1,0:T(8,128)(2,1)S(1)}, u32[]{:S(2)}, u32[]{:S(2)}) %collective-permute-start.1) | collective-permute-done | bytes 196640 | tf_op jit(solution)/shard_map/ppermute | solution.py:30
  39.7 0.9 maximum_select_fusion
  40.6 0.1 collective-permute-start.8
  40.7 0.1 collective-permute-start.6
  40.8 1.5 collective-permute-start.4
  42.2 1.3 collective-permute-start.3
  43.5 9.7 %collective-permute-start.2 = (bf16[2048,128]{1,0:T(8,128)(2,1)}, bf16[2048,128]{1,0:T(8,128)(2,1)S(1)}, u32[]{:S(2)}, u32[]{:S(2)}) collective-permute-start(bf16[2048,128]{1,0:T(8,128)(2,1)} %bitcast.35), channel_id=1, source_target_pairs={{0,0},{1,16},{2,32},{3,48},{4,64},{5,80},{6,96},{7,112},{8,128},{9... | collective-permute-start | bytes 1572872 | tf_op jit(solution)/shard_map/ppermute | solution.py:39
  53.3 11.7 %collective-permute-done.8.refs_6_ = bf16[128,4096]{1,0:T(8,128)(2,1)S(1)} collective-permute-done((bf16[128,4096]{1,0:T(8,128)(2,1)}, bf16[128,4096]{1,0:T(8,128)(2,1)S(1)}, u32[]{:S(2)}, u32[]{:S(2)}) %collective-permute-start.8) | collective-permute-done | bytes 1048608 | tf_op jit(solution)/shard_map/ppermute | solution.py:30
  65.0 0.1 collective-permute-start.20
  65.1 1.4 collective-permute-start.16
  66.6 1.3 collective-permute-done.4.refs_2_
  67.9 0.1 collective-permute-start.10
  68.0 0.1 fusion
  68.1 30.8 %collective-permute-done.2 = bf16[2048,128]{1,0:T(8,128)(2,1)S(1)} collective-permute-done((bf16[2048,128]{1,0:T(8,128)(2,1)}, bf16[2048,128]{1,0:T(8,128)(2,1)S(1)}, u32[]{:S(2)}, u32[]{:S(2)}) %collective-permute-start.2) | collective-permute-done | bytes 524320 | tf_op jit(solution)/shard_map/ppermute | solution.py:39
  98.9 0.1 collective-permute-start.14
  99.0 1.4 collective-permute-start.18
  100.5 2.7 collective-permute-start.24
  103.2 0.1 collective-permute-start.26
  103.2 4.2 %collective-permute-done.24.refs_22_ = bf16[32,4096]{1,0:T(8,128)(2,1)S(1)} collective-permute-done((bf16[32,4096]{1,0:T(8,128)(2,1)S(1)}, bf16[32,4096]{1,0:T(8,128)(2,1)S(1)}, u32[]{:S(2)}, u32[]{:S(2)}) %collective-permute-start.24) | collective-permute-done | bytes 262176 | tf_op jit(solution)/shard_map/ppermute | solution.py:30
  107.5 2.2 collective-permute-start.25
  109.6 3.6 %collective-permute-done.12.refs_10_ = bf16[64,4096]{1,0:T(8,128)(2,1)} collective-permute-done((bf16[64,4096]{1,0:T(8,128)(2,1)S(1)}, bf16[64,4096]{1,0:T(8,128)(2,1)}, u32[]{:S(2)}, u32[]{:S(2)}) %collective-permute-start.12) | collective-permute-done | bytes 524320 | tf_op jit(solution)/shard_map/ppermute | solution.py:30
  113.2 0.1 collective-permute-start.22
  113.4 2.0 collective-permute-start.11
  115.4 7.9 %collective-permute-done.18.refs_16_ = bf16[64,4096]{1,0:T(8,128)(2,1)S(1)} collective-permute-done((bf16[64,4096]{1,0:T(8,128)(2,1)S(1)}, bf16[64,4096]{1,0:T(8,128)(2,1)S(1)}, u32[]{:S(2)}, u32[]{:S(2)}) %collective-permute-start.18) | collective-permute-done | bytes 524320 | tf_op jit(solution)/shard_map/ppermute | solution.py:30
  123.3 2.1 collective-permute-start.17
  125.4 0.1 collective-permute-start.21
  125.5 0.4 collective-permute-start.27
  125.9 2.1 collective-permute-done.27.refs_25_
  128.0 0.4 collective-permute-start.5
  128.4 6.1 %collective-permute-done.22.refs_20_ = bf16[64,4096]{1,0:T(8,128)(2,1)S(1)} collective-permute-done((bf16[64,4096]{1,0:T(8,128)(2,1)S(1)}, bf16[64,4096]{1,0:T(8,128)(2,1)S(1)}, u32[]{:S(2)}, u32[]{:S(2)}) %collective-permute-start.22) | collective-permute-done | bytes 524320 | tf_op jit(solution)/shard_map/ppermute | solution.py:30
  134.5 1.3 collective-permute-start.13
  135.8 0.1 collective-permute-start.7
  135.9 0.4 collective-permute-start.15
  136.3 0.2 collective-permute-start.9
  136.5 0.0 copy-done.9
  136.6 0.2 copy-done.10
  136.7 0.3 copy-done.11
  137.1 6.0 %all-to-all-start = ((bf16[16,128,128]{2,1,0:T(8,128)(2,1)}), bf16[16,128,128]{2,1,0:T(8,128)(2,1)}, u32[]{:S(2)}, u32[]{:S(2)}) async-start(bf16[16,128,128]{2,1,0:T(8,128)(2,1)} %bitcast.31), calls=%async_computation | async-start | bytes 1048576 | tf_op jit(solution)/shard_map/all_to_all | solution.py:202
  143.0 0.0 reduce-scatter.2.cloned.1.call-start
  143.1 0.5 collective-permute-start.19
  143.6 0.1 collective-permute-start.23
  143.7 0.1 stack.67.ids
  143.8 0.1 broadcast_in_dim.3
  143.9 0.1 le.15
  144.0 0.1 eq.70
  144.1 0.9 and_convert_fusion.mask
  144.9 11.7 %all-to-all-done.g_ref = bf16[16,128,128]{2,1,0:T(8,128)(2,1)} async-done(((bf16[16,128,128]{2,1,0:T(8,128)(2,1)}), bf16[16,128,128]{2,1,0:T(8,128)(2,1)}, u32[]{:S(2)}, u32[]{:S(2)}) %all-to-all-start) | async-done | bytes 524320 | tf_op jit(solution)/shard_map/all_to_all | solution.py:202
  156.7 0.0 all-gather.2.cloned.1.call-done.w_ref
  156.8 34.6 %shard_map.37 = bf16[4096,384]{1,0:T(8,128)(2,1)} custom-call(s32[16]{0:T(128)} %copy-done.17, f32[256,256]{1,0:T(8,128)} %and_convert_fusion.mask, bf16[4096,384]{1,0:T(8,128)(2,1)} %all-gather.2.cloned.1.call-done.w_ref, bf16[16,128,128]{2,1,0:T(8,128)(2,1)} %all-to-all-done.g_ref, bf16[128,4096]{1,0:T(8,128)(2,1)} %bitcast.29, ...), custom_call_target="tpu_custom_call" | custom-call | tf_op jit(solution)/shard_map/pallas_call | solution.py:172
  191.4 0.0 reduce-scatter.2.cloned.1.call-update
  191.4 44.0 %reduce-scatter.2.cloned.1.call-done = bf16[512,384]{1,0:T(8,128)(2,1)} async-done(((bf16[4096,384]{1,0:T(8,128)(2,1)}), bf16[512,384]{1,0:T(8,128)(2,1)}) %reduce-scatter.2.cloned.1.call-update) | async-done | bytes 393232 | tf_op jit(solution)/shard_map/reduce_scatter | solution.py:207
  235.4 1.1 constant_dynamic-slice_fusion.1
  236.5 0.1 copy.7
  236.6 3.4 %collective-permute-start.28 = (bf16[256,384]{0,1:T(8,128)(2,1)S(1)}, bf16[256,384]{0,1:T(8,128)(2,1)S(1)}, u32[]{:S(2)}, u32[]{:S(2)}) collective-permute-start(bf16[256,384]{0,1:T(8,128)(2,1)S(1)} %bitcast.33), channel_id=1, source_target_pairs={{0,0},{1,32},{2,64},{3,96},{4,128},{5,160},{6,192},{7,224},{8,16},... | collective-permute-start | bytes 589832 | tf_op jit(solution)/shard_map/ppermute | solution.py:39
  240.1 0.1 copy.8
  240.2 4.0 %collective-permute-start.29 = (bf16[256,384]{0,1:T(8,128)(2,1)S(1)}, bf16[256,384]{0,1:T(8,128)(2,1)S(1)}, u32[]{:S(2)}, u32[]{:S(2)}) collective-permute-start(bf16[256,384]{0,1:T(8,128)(2,1)S(1)} %bitcast.34), channel_id=1, source_target_pairs={{0,16},{1,48},{2,80},{3,112},{4,144},{5,176},{6,208},{7,240},{8,0}... | collective-permute-start | bytes 589832 | tf_op jit(solution)/shard_map/ppermute | solution.py:39
  244.2 22.0 %collective-permute-done.28 = bf16[256,384]{0,1:T(8,128)(2,1)S(1)} collective-permute-done((bf16[256,384]{0,1:T(8,128)(2,1)S(1)}, bf16[256,384]{0,1:T(8,128)(2,1)S(1)}, u32[]{:S(2)}, u32[]{:S(2)}) %collective-permute-start.28) | collective-permute-done | bytes 196640 | tf_op jit(solution)/shard_map/ppermute | solution.py:39
  266.2 9.4 %collective-permute-done.29 = bf16[256,384]{0,1:T(8,128)(2,1)S(1)} collective-permute-done((bf16[256,384]{0,1:T(8,128)(2,1)S(1)}, bf16[256,384]{0,1:T(8,128)(2,1)S(1)}, u32[]{:S(2)}, u32[]{:S(2)}) %collective-permute-start.29) | collective-permute-done | bytes 196640 | tf_op jit(solution)/shard_map/ppermute | solution.py:39
  275.6 0.8 copy.9
  (61 shorter events, 0.3 us)
Async XLA Ops:
  6.5 150.2 %all-gather.2.cloned.1.call-start = ((), (), s32[]{:S(2)}) async-start(), calls=%async_computation.2 | async-start | bytes 3538944 | tf_op jit(solution)/shard_map/all_gather | solution.py:200
  10.0 21.6 %collective-permute-start = (bf16[256,384]{1,0:T(8,128)(2,1)S(1)}, bf16[256,384]{1,0:T(8,128)(2,1)S(1)}, u32[]{:S(2)}, u32[]{:S(2)}) collective-permute-start(bf16[256,384]{1,0:T(8,128)(2,1)S(1)} %copy.10), channel_id=1, source_target_pairs={{0,0},{1,16},{2,32},{3,48},{4,64},{5,80},{6,96},{7,112},{8,128},{9... | collective-permute-start | bytes 589832 | tf_op jit(solution)/shard_map/ppermute | solution.py:39
  31.6 8.1 %collective-permute-start.1 = (bf16[256,384]{1,0:T(8,128)(2,1)S(1)}, bf16[256,384]{1,0:T(8,128)(2,1)S(1)}, u32[]{:S(2)}, u32[]{:S(2)}) collective-permute-start(bf16[256,384]{1,0:T(8,128)(2,1)S(1)} %collective-permute-done), channel_id=1, source_target_pairs={{0,8},{8,0},{1,9},{9,1},{2,10},{10,2},{3,11},{11,3},{4,12},{12,4},... | collective-permute-start | bytes 589832 | tf_op jit(solution)/shard_map/ppermute | solution.py:30
  40.6 24.4 %collective-permute-start.8 = (bf16[128,4096]{1,0:T(8,128)(2,1)}, bf16[128,4096]{1,0:T(8,128)(2,1)S(1)}, u32[]{:S(2)}, u32[]{:S(2)}) collective-permute-start(bf16[128,4096]{1,0:T(8,128)(2,1)} %bitcast.25), channel_id=1, source_target_pairs={{0,128},{128,0},{1,129},{129,1},{2,130},{130,2},{3,131},{131,3},{4... | collective-permute-start | bytes 3145736 | tf_op jit(solution)/shard_map/ppermute | solution.py:30
  40.7 24.4 %collective-permute-start.6 = (bf16[128,4096]{1,0:T(8,128)(2,1)}, bf16[128,4096]{1,0:T(8,128)(2,1)S(1)}, u32[]{:S(2)}, u32[]{:S(2)}) collective-permute-start(bf16[128,4096]{1,0:T(8,128)(2,1)} %bitcast.26), channel_id=1, source_target_pairs={{0,32},{32,64},{64,96},{96,0},{1,33},{33,65},{65,97},{97,1},{2,34}... | collective-permute-start | bytes 3145736 | tf_op jit(solution)/shard_map/ppermute | solution.py:30
  40.8 27.2 %collective-permute-start.4 = (bf16[128,4096]{1,0:T(8,128)(2,1)}, bf16[128,4096]{1,0:T(8,128)(2,1)S(1)}, u32[]{:S(2)}, u32[]{:S(2)}) collective-permute-start(bf16[128,4096]{1,0:T(8,128)(2,1)} %bitcast.27), channel_id=1, source_target_pairs={{0,96},{32,0},{64,32},{96,64},{1,97},{33,1},{65,33},{97,65},{2,98}... | collective-permute-start | bytes 3145736 | tf_op jit(solution)/shard_map/ppermute | solution.py:30
  42.2 56.6 %collective-permute-start.3 = (bf16[128,4096]{1,0:T(8,128)(2,1)}, bf16[128,4096]{1,0:T(8,128)(2,1)S(1)}, u32[]{:S(2)}, u32[]{:S(2)}) collective-permute-start(bf16[128,4096]{1,0:T(8,128)(2,1)} %bitcast.28), channel_id=1, source_target_pairs={{0,16},{16,0},{1,17},{17,1},{2,18},{18,2},{3,19},{19,3},{4,20},{20... | collective-permute-start | bytes 3145736 | tf_op jit(solution)/shard_map/ppermute | solution.py:30
  43.5 55.3 %collective-permute-start.2 = (bf16[2048,128]{1,0:T(8,128)(2,1)}, bf16[2048,128]{1,0:T(8,128)(2,1)S(1)}, u32[]{:S(2)}, u32[]{:S(2)}) collective-permute-start(bf16[2048,128]{1,0:T(8,128)(2,1)} %bitcast.35), channel_id=1, source_target_pairs={{0,0},{1,16},{2,32},{3,48},{4,64},{5,80},{6,96},{7,112},{8,128},{9... | collective-permute-start | bytes 1572872 | tf_op jit(solution)/shard_map/ppermute | solution.py:39
  65.0 72.1 %copy-start.1 = (bf16[128,4096]{1,0:T(8,128)(2,1)}, bf16[128,4096]{1,0:T(8,128)(2,1)S(1)}, u32[]{:S(2)}) copy-start(bf16[128,4096]{1,0:T(8,128)(2,1)S(1)} %collective-permute-done.8.refs_6_) | copy-start | bytes 3145732
  65.0 34.0 %collective-permute-start.20 = (bf16[64,4096]{1,0:T(8,128)(2,1)S(1)}, bf16[64,4096]{1,0:T(8,128)(2,1)S(1)}, u32[]{:S(2)}, u32[]{:S(2)}) collective-permute-start(bf16[64,4096]{1,0:T(8,128)(2,1)S(1)} %slice.29), channel_id=1, source_target_pairs={{0,32},{32,64},{64,96},{96,0},{1,33},{33,65},{65,97},{97,1},{2,34}... | collective-permute-start | bytes 1572872 | tf_op jit(solution)/shard_map/ppermute | solution.py:30
  65.1 91.6 %copy-start.2 = (bf16[128,4096]{1,0:T(8,128)(2,1)}, bf16[128,4096]{1,0:T(8,128)(2,1)S(1)}, u32[]{:S(2)}) copy-start(bf16[128,4096]{1,0:T(8,128)(2,1)S(1)} %collective-permute-done.6.refs_4_) | copy-start | bytes 3145732
  65.1 35.3 %collective-permute-start.16 = (bf16[64,4096]{1,0:T(8,128)(2,1)S(1)}, bf16[64,4096]{1,0:T(8,128)(2,1)S(1)}, u32[]{:S(2)}, u32[]{:S(2)}) collective-permute-start(bf16[64,4096]{1,0:T(8,128)(2,1)S(1)} %slice.29), channel_id=1, source_target_pairs={{0,96},{32,0},{64,32},{96,64},{1,97},{33,1},{65,33},{97,65},{2,98}... | collective-permute-start | bytes 1572872 | tf_op jit(solution)/shard_map/ppermute | solution.py:30
  67.9 88.8 %copy-start = (bf16[128,4096]{1,0:T(8,128)(2,1)}, bf16[128,4096]{1,0:T(8,128)(2,1)S(1)}, u32[]{:S(2)}) copy-start(bf16[128,4096]{1,0:T(8,128)(2,1)S(1)} %collective-permute-done.4.refs_2_) | copy-start | bytes 3145732
  67.9 35.2 %collective-permute-start.10 = (bf16[64,4096]{1,0:T(8,128)(2,1)S(1)}, bf16[64,4096]{1,0:T(8,128)(2,1)S(1)}, u32[]{:S(2)}, u32[]{:S(2)}) collective-permute-start(bf16[64,4096]{1,0:T(8,128)(2,1)S(1)} %slice.26), channel_id=1, source_target_pairs={{0,32},{32,64},{64,96},{96,0},{1,33},{33,65},{65,97},{97,1},{2,34}... | collective-permute-start | bytes 1572872 | tf_op jit(solution)/shard_map/ppermute | solution.py:30
  98.8 37.7 %copy-start.12 = (bf16[2048,128]{1,0:T(8,128)(2,1)}, bf16[2048,128]{1,0:T(8,128)(2,1)S(1)}, u32[]{:S(2)}) copy-start(bf16[2048,128]{1,0:T(8,128)(2,1)S(1)} %collective-permute-done.2) | copy-start | bytes 1572868
  98.8 14.4 %collective-permute-start.12 = (bf16[64,4096]{1,0:T(8,128)(2,1)S(1)}, bf16[64,4096]{1,0:T(8,128)(2,1)}, u32[]{:S(2)}, u32[]{:S(2)}) collective-permute-start(bf16[64,4096]{1,0:T(8,128)(2,1)S(1)} %get-tuple-element.6), channel_id=1, source_target_pairs={{0,96},{32,0},{64,32},{96,64},{1,97},{33,1},{65,33},{97,65},{2,98}... | collective-permute-start | bytes 1572872 | tf_op jit(solution)/shard_map/ppermute | solution.py:30
  98.8 37.7 %copy-start.5 = (bf16[128,4096]{1,0:T(8,128)(2,1)}, bf16[128,4096]{1,0:T(8,128)(2,1)S(1)}, u32[]{:S(2)}) copy-start(bf16[128,4096]{1,0:T(8,128)(2,1)S(1)} %collective-permute-done.3.refs_1_) | copy-start | bytes 3145732
  98.9 14.5 %collective-permute-start.14 = (bf16[64,4096]{1,0:T(8,128)(2,1)S(1)}, bf16[64,4096]{1,0:T(8,128)(2,1)}, u32[]{:S(2)}, u32[]{:S(2)}) collective-permute-start(bf16[64,4096]{1,0:T(8,128)(2,1)S(1)} %get-tuple-element.5), channel_id=1, source_target_pairs={{0,128},{128,0},{1,129},{129,1},{2,130},{130,2},{3,131},{131,3},{4... | collective-permute-start | bytes 1572872 | tf_op jit(solution)/shard_map/ppermute | solution.py:30
  99.0 37.3 %copy-start.3 = (bf16[64,4096]{1,0:T(8,128)(2,1)}, bf16[64,4096]{1,0:T(8,128)(2,1)S(1)}, u32[]{:S(2)}) copy-start(bf16[64,4096]{1,0:T(8,128)(2,1)S(1)} %collective-permute-done.20.refs_18_) | copy-start | bytes 1572868
  99.0 24.3 %collective-permute-start.18 = (bf16[64,4096]{1,0:T(8,128)(2,1)S(1)}, bf16[64,4096]{1,0:T(8,128)(2,1)S(1)}, u32[]{:S(2)}, u32[]{:S(2)}) collective-permute-start(bf16[64,4096]{1,0:T(8,128)(2,1)S(1)} %slice.26), channel_id=1, source_target_pairs={{0,128},{128,0},{1,129},{129,1},{2,130},{130,2},{3,131},{131,3},{4... | collective-permute-start | bytes 1572872 | tf_op jit(solution)/shard_map/ppermute | solution.py:30
  100.4 35.8 %copy-start.4 = (bf16[64,4096]{1,0:T(8,128)(2,1)}, bf16[64,4096]{1,0:T(8,128)(2,1)S(1)}, u32[]{:S(2)}) copy-start(bf16[64,4096]{1,0:T(8,128)(2,1)S(1)} %collective-permute-done.16.refs_14_) | copy-start | bytes 1572868
  100.5 7.0 %collective-permute-start.24 = (bf16[32,4096]{1,0:T(8,128)(2,1)S(1)}, bf16[32,4096]{1,0:T(8,128)(2,1)S(1)}, u32[]{:S(2)}, u32[]{:S(2)}) collective-permute-start(bf16[32,4096]{1,0:T(8,128)(2,1)S(1)} %slice.30), channel_id=1, source_target_pairs={{0,32},{32,64},{64,96},{96,0},{1,33},{33,65},{65,97},{97,1},{2,34}... | collective-permute-start | bytes 786440 | tf_op jit(solution)/shard_map/ppermute | solution.py:30
  103.1 33.4 %copy-start.6 = (bf16[64,4096]{1,0:T(8,128)(2,1)}, bf16[64,4096]{1,0:T(8,128)(2,1)S(1)}, u32[]{:S(2)}) copy-start(bf16[64,4096]{1,0:T(8,128)(2,1)S(1)} %collective-permute-done.10.refs_8_) | copy-start | bytes 1572868
  103.2 22.2 %collective-permute-start.26 = (bf16[32,4096]{1,0:T(8,128)(2,1)S(1)}, bf16[32,4096]{1,0:T(8,128)(2,1)S(1)}, u32[]{:S(2)}, u32[]{:S(2)}) collective-permute-start(bf16[32,4096]{1,0:T(8,128)(2,1)S(1)} %slice.31), channel_id=1, source_target_pairs={{0,96},{32,0},{64,32},{96,64},{1,97},{33,1},{65,33},{97,65},{2,98}... | collective-permute-start | bytes 786440 | tf_op jit(solution)/shard_map/ppermute | solution.py:30
  107.5 49.3 %copy-start.13 = (bf16[32,4096]{1,0:T(8,128)(2,1)}, bf16[32,4096]{1,0:T(8,128)(2,1)S(1)}, u32[]{:S(2)}) copy-start(bf16[32,4096]{1,0:T(8,128)(2,1)S(1)} %collective-permute-done.24.refs_22_) | copy-start | bytes 786436
  107.5 18.0 %collective-permute-start.25 = (bf16[32,4096]{1,0:T(8,128)(2,1)S(1)}, bf16[32,4096]{1,0:T(8,128)(2,1)S(1)}, u32[]{:S(2)}, u32[]{:S(2)}) collective-permute-start(bf16[32,4096]{1,0:T(8,128)(2,1)S(1)} %collective-permute-done.24.refs_22_), channel_id=1, source_target_pairs={{0,16},{16,0},{1,17},{17,1},{2,18},{18,2},{3,19},{19,3},{4,20},{20... | collective-permute-start | bytes 786440 | tf_op jit(solution)/shard_map/ppermute | solution.py:30
  113.2 21.3 %collective-permute-start.22 = (bf16[64,4096]{1,0:T(8,128)(2,1)S(1)}, bf16[64,4096]{1,0:T(8,128)(2,1)S(1)}, u32[]{:S(2)}, u32[]{:S(2)}) collective-permute-start(bf16[64,4096]{1,0:T(8,128)(2,1)S(1)} %collective-permute-done.10.refs_8_), channel_id=1, source_target_pairs={{0,128},{128,0},{1,129},{129,1},{2,130},{130,2},{3,131},{131,3},{4... | collective-permute-start | bytes 1572872 | tf_op jit(solution)/shard_map/ppermute | solution.py:30
  113.4 22.4 %collective-permute-start.11 = (bf16[64,4096]{1,0:T(8,128)(2,1)S(1)}, bf16[64,4096]{1,0:T(8,128)(2,1)S(1)}, u32[]{:S(2)}, u32[]{:S(2)}) collective-permute-start(bf16[64,4096]{1,0:T(8,128)(2,1)S(1)} %collective-permute-done.10.refs_8_), channel_id=1, source_target_pairs={{0,16},{16,0},{1,17},{17,1},{2,18},{18,2},{3,19},{19,3},{4,20},{20... | collective-permute-start | bytes 1572872 | tf_op jit(solution)/shard_map/ppermute | solution.py:30
  123.3 13.2 %copy-start.7 = (bf16[64,4096]{1,0:T(8,128)(2,1)}, bf16[64,4096]{1,0:T(8,128)(2,1)S(1)}, u32[]{:S(2)}) copy-start(bf16[64,4096]{1,0:T(8,128)(2,1)S(1)} %collective-permute-done.18.refs_16_) | copy-start | bytes 1572868
  123.3 12.6 %collective-permute-start.17 = (bf16[64,4096]{1,0:T(8,128)(2,1)S(1)}, bf16[64,4096]{1,0:T(8,128)(2,1)S(1)}, u32[]{:S(2)}, u32[]{:S(2)}) collective-permute-start(bf16[64,4096]{1,0:T(8,128)(2,1)S(1)} %collective-permute-done.16.refs_14_), channel_id=1, source_target_pairs={{0,16},{16,0},{1,17},{17,1},{2,18},{18,2},{3,19},{19,3},{4,20},{20... | collective-permute-start | bytes 1572872 | tf_op jit(solution)/shard_map/ppermute | solution.py:30
  125.4 11.1 %copy-start.14 = (bf16[32,4096]{1,0:T(8,128)(2,1)}, bf16[32,4096]{1,0:T(8,128)(2,1)S(1)}, u32[]{:S(2)}) copy-start(bf16[32,4096]{1,0:T(8,128)(2,1)S(1)} %collective-permute-done.26.refs_24_) | copy-start | bytes 786436
  125.4 10.9 %collective-permute-start.21 = (bf16[64,4096]{1,0:T(8,128)(2,1)S(1)}, bf16[64,4096]{1,0:T(8,128)(2,1)S(1)}, u32[]{:S(2)}, u32[]{:S(2)}) collective-permute-start(bf16[64,4096]{1,0:T(8,128)(2,1)S(1)} %collective-permute-done.20.refs_18_), channel_id=1, source_target_pairs={{0,16},{16,0},{1,17},{17,1},{2,18},{18,2},{3,19},{19,3},{4,20},{20... | collective-permute-start | bytes 1572872 | tf_op jit(solution)/shard_map/ppermute | solution.py:30
  125.5 11.0 %copy-start.15 = (bf16[32,4096]{1,0:T(8,128)(2,1)}, bf16[32,4096]{1,0:T(8,128)(2,1)S(1)}, u32[]{:S(2)}) copy-start(bf16[32,4096]{1,0:T(8,128)(2,1)S(1)} %collective-permute-done.25.refs_23_) | copy-start | bytes 786436
  125.5 2.5 collective-permute-start.27
  128.0 8.5 %copy-start.16 = (bf16[32,4096]{1,0:T(8,128)(2,1)}, bf16[32,4096]{1,0:T(8,128)(2,1)S(1)}, u32[]{:S(2)}) copy-start(bf16[32,4096]{1,0:T(8,128)(2,1)S(1)} %collective-permute-done.27.refs_25_) | copy-start | bytes 786436
  128.0 28.6 %collective-permute-start.5 = (bf16[128,4096]{1,0:T(8,128)(2,1)S(1)}, bf16[128,4096]{1,0:T(8,128)(2,1)}, u32[]{:S(2)}, u32[]{:S(2)}) collective-permute-start(bf16[128,4096]{1,0:T(8,128)(2,1)S(1)} %collective-permute-done.4.refs_2_), channel_id=1, source_target_pairs={{0,16},{16,0},{1,17},{17,1},{2,18},{18,2},{3,19},{19,3},{4,20},{20... | collective-permute-start | bytes 3145736 | tf_op jit(solution)/shard_map/ppermute | solution.py:30
  134.5 2.0 copy-start.8
  134.5 8.6 %collective-permute-start.13 = (bf16[64,4096]{1,0:T(8,128)(2,1)}, bf16[64,4096]{1,0:T(8,128)(2,1)}, u32[]{:S(2)}, u32[]{:S(2)}) collective-permute-start(bf16[64,4096]{1,0:T(8,128)(2,1)} %collective-permute-done.12.refs_10_), channel_id=1, source_target_pairs={{0,16},{16,0},{1,17},{17,1},{2,18},{18,2},{3,19},{19,3},{4,20},{20... | collective-permute-start | bytes 1572872 | tf_op jit(solution)/shard_map/ppermute | solution.py:30
  135.8 0.8 copy-start.9
  135.8 20.9 %collective-permute-start.7 = (bf16[128,4096]{1,0:T(8,128)(2,1)S(1)}, bf16[128,4096]{1,0:T(8,128)(2,1)}, u32[]{:S(2)}, u32[]{:S(2)}) collective-permute-start(bf16[128,4096]{1,0:T(8,128)(2,1)S(1)} %collective-permute-done.6.refs_4_), channel_id=1, source_target_pairs={{0,16},{16,0},{1,17},{17,1},{2,18},{18,2},{3,19},{19,3},{4,20},{20... | collective-permute-start | bytes 3145736 | tf_op jit(solution)/shard_map/ppermute | solution.py:30
  135.9 0.9 copy-start.10
  135.9 7.8 %collective-permute-start.15 = (bf16[64,4096]{1,0:T(8,128)(2,1)}, bf16[64,4096]{1,0:T(8,128)(2,1)}, u32[]{:S(2)}, u32[]{:S(2)}) collective-permute-start(bf16[64,4096]{1,0:T(8,128)(2,1)} %collective-permute-done.14.refs_12_), channel_id=1, source_target_pairs={{0,16},{16,0},{1,17},{17,1},{2,18},{18,2},{3,19},{19,3},{4,20},{20... | collective-permute-start | bytes 1572872 | tf_op jit(solution)/shard_map/ppermute | solution.py:30
  136.3 0.8 copy-start.11
  136.3 20.4 %collective-permute-start.9 = (bf16[128,4096]{1,0:T(8,128)(2,1)S(1)}, bf16[128,4096]{1,0:T(8,128)(2,1)}, u32[]{:S(2)}, u32[]{:S(2)}) collective-permute-start(bf16[128,4096]{1,0:T(8,128)(2,1)S(1)} %collective-permute-done.8.refs_6_), channel_id=1, source_target_pairs={{0,16},{16,0},{1,17},{17,1},{2,18},{18,2},{3,19},{19,3},{4,20},{20... | collective-permute-start | bytes 3145736 | tf_op jit(solution)/shard_map/ppermute | solution.py:30
  137.1 19.6 %all-to-all-start = ((bf16[16,128,128]{2,1,0:T(8,128)(2,1)}), bf16[16,128,128]{2,1,0:T(8,128)(2,1)}, u32[]{:S(2)}, u32[]{:S(2)}) async-start(bf16[16,128,128]{2,1,0:T(8,128)(2,1)} %bitcast.31), calls=%async_computation | async-start | bytes 1048576 | tf_op jit(solution)/shard_map/all_to_all | solution.py:202
  143.0 92.4 %reduce-scatter.2.cloned.1.call-start = ((), (), s32[]{:S(2)}) async-start(), calls=%async_computation.3 | async-start | bytes 3538944 | tf_op jit(solution)/shard_map/reduce_scatter | solution.py:207
  143.1 13.6 %collective-permute-start.19 = (bf16[64,4096]{1,0:T(8,128)(2,1)}, bf16[64,4096]{1,0:T(8,128)(2,1)}, u32[]{:S(2)}, u32[]{:S(2)}) collective-permute-start(bf16[64,4096]{1,0:T(8,128)(2,1)} %copy-done.7), channel_id=1, source_target_pairs={{0,16},{16,0},{1,17},{17,1},{2,18},{18,2},{3,19},{19,3},{4,20},{20... | collective-permute-start | bytes 1572872 | tf_op jit(solution)/shard_map/ppermute | solution.py:30
  143.6 13.1 %collective-permute-start.23 = (bf16[64,4096]{1,0:T(8,128)(2,1)}, bf16[64,4096]{1,0:T(8,128)(2,1)}, u32[]{:S(2)}, u32[]{:S(2)}) collective-permute-start(bf16[64,4096]{1,0:T(8,128)(2,1)} %copy-done.8), channel_id=1, source_target_pairs={{0,16},{16,0},{1,17},{17,1},{2,18},{18,2},{3,19},{19,3},{4,20},{20... | collective-permute-start | bytes 1572872 | tf_op jit(solution)/shard_map/ppermute | solution.py:30
  143.8 12.9 %copy-start.17 = (s32[16]{0:T(128)}, s32[16]{0:T(128)S(1)}, u32[]{:S(2)}) copy-start(s32[16]{0:T(128)S(1)} %stack.67.ids) | copy-start | bytes 196
  236.6 29.5 %collective-permute-start.28 = (bf16[256,384]{0,1:T(8,128)(2,1)S(1)}, bf16[256,384]{0,1:T(8,128)(2,1)S(1)}, u32[]{:S(2)}, u32[]{:S(2)}) collective-permute-start(bf16[256,384]{0,1:T(8,128)(2,1)S(1)} %bitcast.33), channel_id=1, source_target_pairs={{0,0},{1,32},{2,64},{3,96},{4,128},{5,160},{6,192},{7,224},{8,16},... | collective-permute-start | bytes 589832 | tf_op jit(solution)/shard_map/ppermute | solution.py:39
  240.2 35.3 %collective-permute-start.29 = (bf16[256,384]{0,1:T(8,128)(2,1)S(1)}, bf16[256,384]{0,1:T(8,128)(2,1)S(1)}, u32[]{:S(2)}, u32[]{:S(2)}) collective-permute-start(bf16[256,384]{0,1:T(8,128)(2,1)S(1)} %bitcast.34), channel_id=1, source_target_pairs={{0,16},{1,48},{2,80},{3,112},{4,144},{5,176},{6,208},{7,240},{8,0}... | collective-permute-start | bytes 589832 | tf_op jit(solution)/shard_map/ppermute | solution.py:39
Sparse Core Ops, SparseCore 0:
  40.7 76.7 all-gather.1
  191.5 43.8 reduce-scatter.1

commit v2 on v1

v2 whole, which is shorter than its diff:
```python
import functools
import math

import jax
import jax.numpy as jnp
import numpy as np
from jax import lax
from jax.experimental import pallas as pl
from jax.experimental.pallas import tpu as pltpu
from jax.sharding import Mesh, PartitionSpec as P

HEAD_DIM = 128
AXES = ("yl", "x", "core", "yh", "z")
SIZES = (2, 4, 2, 2, 8)
FRAME = AXES[:3]
TOK = AXES[3:]
FRAMES = 16
PATCHES = 128
HALF = PATCHES // 2
QUARTER = PATCHES // 4
WIDTH = 4096
COLS = 3 * HEAD_DIM
ROWS = FRAMES * PATCHES
GROUP = 16
CHUNK = WIDTH // 8

SAME_CORE = ((0, 0), (0, 1), (0, -1), (1, 0), (0, 2), (1, 1), (1, -1), (1, 2))
SLOTS = [(dy, dx, dc) for dy, dx in SAME_CORE for dc in (0, 1)]


def device(yl, x, core, yh, z):
    place = 0
    for value, size in zip((yl, x, core, yh, z), SIZES):
        place = place * size + value % size
    return place


def owner_moves(flip):
    pairs = []
    for yl in range(2):
        for x in range(4):
            for core in range(2):
                for yh in range(2):
                    for z in range(8):
                        source = device(yl, x, core, yh, z)
                        target = device(yl ^ (z // 4), x + z % 4, yh ^ flip, core, 4 * yl + x)
                        pairs.append((source, target))
    return pairs


def shift(value, axis, by):
    count = SIZES[AXES.index(axis)]
    return lax.ppermute(value, axis, [(i, (i + by) % count) for i in range(count)])


def gather_frames(own):
    join = lambda *parts: jnp.concatenate(parts, axis=0)
    left = shift(own, "x", 1)
    right = shift(own, "x", -1)
    other = shift(own, "yl", 1)
    twin = shift(own, "core", 1)
    from_left = shift(join(left[:HALF], other[HALF:]), "x", 1)
    from_right = shift(join(right[HALF:], other[HALF:]), "x", -1)
    from_other = shift(join(right[:HALF], left[:HALF]), "yl", 1)
    twin_a = shift(join(right, left, other), "core", 1)
    last_left = shift(from_left[HALF : HALF + QUARTER], "x", 1)
    last_right = shift(from_right[HALF + QUARTER :], "x", -1)
    last_other = shift(from_left[:HALF], "yl", 1)
    twin_b = shift(join(from_left, from_right, from_other), "core", 1)
    last = join(last_other, last_left, last_right)
    twin_c = shift(last, "core", 1)
    return (
        [own, twin, right, left, other, twin_a],
        [from_left, from_right, from_other, twin_b],
        [last, twin_c],
    )


FIRST = [
    [(0, 0, PATCHES)],
    [(1, 0, PATCHES)],
    [(2, 0, PATCHES)],
    [(4, 0, PATCHES)],
    [(6, 0, PATCHES)],
    [(3, 0, PATCHES), (5, 0, PATCHES), (7, 0, PATCHES)],
]


def second(core):
    return [
        [(8 + core, 0, HALF), (12 + core, HALF, HALF)],
        [(8 + core, HALF, HALF), (10 + core, HALF, HALF)],
        [(10 + core, 0, HALF), (12 + core, 0, HALF)],
    ]


SECOND = second(0) + [[part for buffer in second(1) for part in buffer]]
THIRD = [[(14, 0, PATCHES)], [(15, 0, PATCHES)]]


def parts_of(places):
    out = []
    for buffer, parts in enumerate(places):
        row = 0
        for slot, first, rows in parts:
            out.append((buffer, row // GROUP, slot, first // GROUP, rows // GROUP))
            row += rows
    return out


def tables():
    out = np.zeros((256, 48), np.int32)
    for yl, x, core, yh, z in np.ndindex(*SIZES):
        row = out[device(yl, x, core, yh, z)]
        for slot, (dy, dx, dc) in enumerate(SLOTS):
            row[slot] = (core ^ dc) * 8 + dy * 4 + dx % 4
            row[24 + slot] = ((yl ^ dy) * 4 + (x + dx) % 4) * 2 + (core ^ dc)
        for k in range(8):
            row[16 + k] = (yl ^ (k // 4)) * 4 + (x + k % 4) % 4
        row[40] = (yl ^ (z // 4)) * 4 + (x - z % 4) % 4
    return out


def visible(ids):
    frame = jnp.repeat(ids, GROUP)
    patch = jnp.tile(jnp.arange(GROUP, dtype=jnp.int32), FRAMES)
    allowed = (frame[None, :] <= frame[:, None]) & (patch[None, :] == patch[:, None])
    return allowed.astype(jnp.float32)


VMEM = pl.BlockSpec(memory_space=pltpu.VMEM)
SMEM = pl.BlockSpec(memory_space=pltpu.SMEM)
ANY = pl.BlockSpec(memory_space=pl.ANY)


def load_weights(w_ref, w, sem):
    copies = []
    for chunk in range(8):
        for j in range(3):
            copies.append(
                pltpu.make_async_copy(
                    w_ref.at[chunk, j],
                    w.at[pl.ds(chunk * CHUNK, CHUNK), pl.ds(j * HEAD_DIM, HEAD_DIM)],
                    sem.at[chunk * 3 + j],
                )
            )
    for copy in copies:
        copy.start()
    return copies


def project_rows(rows, w):
    return jnp.dot(rows, w[...], preferred_element_type=jnp.float32).astype(jnp.bfloat16)


def project_kernel(count, w_ref, *refs):
    buffers, out = refs[:count], refs[count]
    tokens, w, w_sem, sems = refs[count + 1 :]
    copies, at = [], 0
    for index, ref in enumerate(buffers):
        rows = ref.shape[0]
        copies.append(pltpu.make_async_copy(ref, tokens.at[pl.ds(at, rows)], sems.at[index]))
        at += rows
    loads = load_weights(w_ref, w, w_sem)
    for copy in copies:
        copy.start()
    for copy in loads + copies:
        copy.wait()
    block = 2 * PATCHES

    def body(step, carry):
        rows = pl.ds(pl.multiple_of(step * block, block), block)
        groups = pl.ds(step * (block // GROUP), block // GROUP)
        out[rows] = project_rows(tokens[groups].reshape(block, WIDTH), w)
        return carry

    lax.fori_loop(0, at * GROUP // block, body, 0)


def project(w, buffers):
    groups = sum(buffer.shape[0] for buffer in buffers)
    rows = groups * GROUP
    return pl.pallas_call(
        functools.partial(project_kernel, len(buffers)),
        out_shape=jax.ShapeDtypeStruct((rows, COLS), jnp.bfloat16),
        in_specs=[ANY] * (1 + len(buffers)),
        out_specs=VMEM,
        scratch_shapes=[
            pltpu.VMEM((groups, GROUP, WIDTH), jnp.bfloat16),
            pltpu.VMEM((WIDTH, COLS), jnp.bfloat16),
            pltpu.SemaphoreType.DMA((24,)),
            pltpu.SemaphoreType.DMA((len(buffers),)),
        ],
        compiler_params=pltpu.CompilerParams(vmem_limit_bytes=32 * 2**20),
        cost_estimate=pl.CostEstimate(
            flops=2 * rows * WIDTH * COLS, bytes_accessed=2 * (rows + COLS) * WIDTH, transcendentals=0
        ),
    )(w, *buffers)


def attend(proj, grads, mask, turned):
    factor = 1.0 / math.sqrt(HEAD_DIM)
    size = FRAMES * GROUP

    def body(step, carry):
        part = proj[step].reshape(size, COLS)
        query, key, value = (part[:, j * HEAD_DIM : (j + 1) * HEAD_DIM] for j in range(3))
        grad = grads[step].reshape(size, HEAD_DIM)
        across = (((1,), (1,)), ((), ()))
        down = (((0,), (0,)), ((), ()))
        dot = functools.partial(lax.dot_general, preferred_element_type=jnp.float32)
        scores = dot(query, key, across) * factor
        scores = jnp.where(mask[...] > 0.5, scores, -1e30)
        exponent = jnp.exp(scores - jnp.max(scores, axis=-1, keepdims=True))
        probs = exponent / jnp.sum(exponent, axis=-1, keepdims=True)
        grad_probs = dot(grad, value, across)
        row_dot = jnp.sum(grad_probs * probs, axis=-1, keepdims=True)
        grad_scores = (probs * (grad_probs - row_dot)).astype(jnp.bfloat16)
        probs_b = probs.astype(jnp.bfloat16)
        grad_query = jnp.dot(grad_scores, key, preferred_element_type=jnp.float32) * factor
        grad_key = dot(grad_scores, query, down) * factor
        grad_value = dot(probs_b, grad, down)
        columns = pl.ds(pl.multiple_of(step * size, size), size)
        for j, result in enumerate((grad_query, grad_key, grad_value)):
            turned[j * HEAD_DIM : (j + 1) * HEAD_DIM, columns] = result.T.astype(jnp.bfloat16)
        return carry

    lax.fori_loop(0, PATCHES // GROUP, body, 0)


def share_kernel(count, order, mask, w_ref, g_ref, proj_a, proj_b, *refs):
    buffers, out = refs[:count], refs[count]
    tokens, proj, grads, turned, w, shares, w_sem, x_sem, g_sem, p_sem, o_sem = refs[count + 1 :]
    token_copies = []
    for index, (buffer, at, slot, first, groups) in enumerate(parts_of(FIRST + SECOND + THIRD)):
        token_copies.append(
            pltpu.make_async_copy(
                buffers[buffer].at[pl.ds(at, groups)],
                tokens.at[pl.ds(first, groups), slot],
                x_sem.at[index],
            )
        )
    for copy in token_copies[-2:]:
        copy.start()
    loads = load_weights(w_ref, w, w_sem)
    small = []
    for slot in range(FRAMES):
        small.append(pltpu.make_async_copy(g_ref.at[order[slot]], grads.at[:, slot], g_sem.at[slot]))
    index = 0
    for source, places in ((proj_a, FIRST), (proj_b, SECOND)):
        at = 0
        for _, _, slot, first, groups in parts_of(places):
            small.append(
                pltpu.make_async_copy(
                    source.at[pl.ds(at, groups)],
                    proj.at[pl.ds(first, groups), slot],
                    p_sem.at[index],
                )
            )
            at += groups
            index += 1
    for copy in small + token_copies[:-2]:
        copy.start()
    for copy in token_copies[-2:] + loads:
        copy.wait()
    for slot in (14, 15):
        rows = project_rows(tokens[:, slot].reshape(PATCHES, WIDTH), w)
        proj[:, slot] = rows.reshape(PATCHES // GROUP, GROUP, COLS)
    for copy in small:
        copy.wait()
    attend(proj, grads, mask, turned)
    for copy in token_copies[:-2]:
        copy.wait()

    def weigh(step, carry):
        columns = pl.ds(pl.multiple_of(order[16 + step] * CHUNK, CHUNK), CHUNK)
        rows = tokens[:, :, :, columns].reshape(ROWS, CHUNK)
        value = jnp.dot(turned[...], rows, preferred_element_type=jnp.float32)
        for j in range(3):
            shares[step, j] = value[j * HEAD_DIM : (j + 1) * HEAD_DIM].T.astype(jnp.bfloat16)
        pltpu.make_async_copy(shares.at[step], out.at[step], o_sem.at[step]).start()
        return carry

    lax.fori_loop(0, 8, weigh, 0)
    for step in range(8):
        pltpu.make_async_copy(shares.at[step], out.at[step], o_sem.at[step]).wait()


def weight_share(order, mask, w, g, proj_a, proj_b, buffers):
    count = len(buffers)
    groups = PATCHES // GROUP
    token_parts = len(parts_of(FIRST + SECOND + THIRD))
    grouped = lambda value: value.reshape(-1, GROUP, COLS)
    return pl.pallas_call(
        functools.partial(share_kernel, count),
        out_shape=jax.ShapeDtypeStruct((8, 3, CHUNK, HEAD_DIM), jnp.bfloat16),
        in_specs=[SMEM, VMEM] + [ANY] * (4 + count),
        out_specs=ANY,
        scratch_shapes=[
            pltpu.VMEM((groups, FRAMES, GROUP, WIDTH), jnp.bfloat16),
            pltpu.VMEM((groups, FRAMES, GROUP, COLS), jnp.bfloat16),
            pltpu.VMEM((groups, FRAMES, GROUP, HEAD_DIM), jnp.bfloat16),
            pltpu.VMEM((COLS, ROWS), jnp.bfloat16),
            pltpu.VMEM((WIDTH, COLS), jnp.bfloat16),
            pltpu.VMEM((8, 3, CHUNK, HEAD_DIM), jnp.bfloat16),
            pltpu.SemaphoreType.DMA((24,)),
            pltpu.SemaphoreType.DMA((token_parts,)),
            pltpu.SemaphoreType.DMA((FRAMES,)),
            pltpu.SemaphoreType.DMA((token_parts - 2,)),
            pltpu.SemaphoreType.DMA((8,)),
        ],
        compiler_params=pltpu.CompilerParams(vmem_limit_bytes=44 * 2**20),
        cost_estimate=pl.CostEstimate(
            flops=2 * ROWS * WIDTH * COLS, bytes_accessed=2 * ROWS * WIDTH, transcendentals=0
        ),
    )(order, mask, w, g, grouped(proj_a), grouped(proj_b), *buffers)


def local(inputs, grad_attn, w_qkv):
    table = jnp.asarray(tables())[lax.axis_index(AXES)]
    to_worker = [(target, source) for source, target in owner_moves(0)]
    rows_w = lax.dynamic_slice(
        w_qkv.transpose(1, 0, 2), (0, table[40] * CHUNK, 0), (3, CHUNK, HEAD_DIM)
    )
    rows_w = lax.ppermute(rows_w.reshape(3 * CHUNK, HEAD_DIM), AXES, to_worker)
    w = lax.all_gather(rows_w, "z", axis=0, tiled=True).reshape(8, 3, CHUNK, HEAD_DIM)
    g = lax.ppermute(grad_attn[0], AXES, to_worker).reshape(FRAMES, PATCHES, HEAD_DIM)
    g = lax.all_to_all(g, TOK, split_axis=0, concat_axis=0, tiled=True)
    g = g.reshape(FRAMES, PATCHES // GROUP, GROUP, HEAD_DIM)
    steps = gather_frames(inputs[0])
    first, second_, third = (
        [buffer.reshape(-1, GROUP, WIDTH) for buffer in buffers] for buffers in steps
    )
    proj_a = project(w, first)
    proj_b = project(w, second_)
    share = weight_share(
        table[:24], visible(table[24:40]), w, g, proj_a, proj_b, first + second_ + third
    )
    mine = lax.psum_scatter(
        share.reshape(8 * 3 * CHUNK, HEAD_DIM), "z", scatter_dimension=0, tiled=True
    )
    mine = mine.reshape(3, 2, CHUNK // 2, HEAD_DIM)
    yh = lax.axis_index("yh")
    total = None
    for flip in range(2):
        part = lax.dynamic_index_in_dim(mine, (yh + flip) % 2, 1, keepdims=False)
        part = lax.ppermute(part, AXES, owner_moves(flip)).astype(jnp.float32)
        total = part if total is None else total + part
    return total.astype(jnp.bfloat16).transpose(1, 0, 2)


def solution(mesh):
    fine = Mesh(mesh.devices.reshape(SIZES), AXES)
    in_specs = (P(FRAME, TOK, None), P(FRAME, None, TOK), P(None, None, TOK))
    out_specs = P(FRAME, None, TOK)
    return jax.shard_map(local, mesh=fine, in_specs=in_specs, out_specs=out_specs, check_vma=False)
```

time: 284 us -> 291 us (1.025)
  the two profiles are of different devices: /device:TPU:31 before, /device:TPU:3 now
where the time goes in v2:
time: 291 us; the launch traced here: 288 us
  waiting for transfers between devices  154 us (53%)
  starting transfers between devices  55.1 us (19%)
  Pallas kernels  37.1 us (13%)
  local copies, waits for them, and re-layouts  21.4 us (7%)
  between operations  14.3 us (5%)
  other arithmetic  6.39 us (2%)
    ppermute x13, waiting for transfers between devices, shift(): lax.ppermute(value, axis, [(i, (i + by) % count) for i in range(count)])  60 us
    reduce_scatter x1, waiting for transfers between devices, local(): lax.psum_scatter(share.reshape(8 * 3 * CHUNK, HEAD_DIM), 'z', scatter_dim...  51.1 us
    ppermute x2, waiting for transfers between devices, local(): part = lax.ppermute(part, AXES, owner_moves(flip)).astype(jnp.float32)  40.4 us
    pallas_call x1, Pallas kernels, weight_share(): pl.pallas_call(functools.partial(share_kernel, count), out_shape=jax.Shap...  21.1 us
    ppermute x13, starting transfers between devices, shift(): lax.ppermute(value, axis, [(i, (i + by) % count) for i in range(count)])  20.3 us
    pallas_call x2, Pallas kernels, project(): pl.pallas_call(functools.partial(project_kernel, len(buffers)), out_shape...  16 us
    unnamed x32, local copies, waits for them, and re-layouts  14.5 us
    all_to_all x1, starting transfers between devices, local(): g = lax.all_to_all(g, TOK, split_axis=0, concat_axis=0, tiled=True)  13.7 us
  transfers between devices with their start and end apart: 20, of which 12 were waited for; matrix products, arithmetic and copies ran while one was open for 5% of the time, Pallas kernels for 6%

profile of v2, /device:TPU:3, one launch (start us, length us, event | category | flops | bytes accessed | tf_op | source)
XLA Modules:
  0.0 288.3 jit_solution(15057278935026286992)
XLA Ops:
  6.5 1.2 collective-permute-start.4
  7.8 0.3 collective-permute-start.3
  8.0 0.7 constant_dynamic-slice_fusion.1
  8.7 0.6 slice.43
  10.0 8.5 %collective-permute-start = (bf16[1536,128]{1,0:T(8,128)(2,1)S(1)}, bf16[1536,128]{1,0:T(8,128)(2,1)S(1)}, u32[]{:S(2)}, u32[]{:S(2)}) collective-permute-start(bf16[1536,128]{1,0:T(8,128)(2,1)S(1)} %bitcast.52), channel_id=1, source_target_pairs={{0,0},{32,1},{64,2},{96,3},{128,4},{160,5},{192,6},{224,7},{16,8},... | collective-permute-start | bytes 1179656 | tf_op jit(solution)/shard_map/ppermute | solution.py:325
  18.5 4.6 %collective-permute-start.5 = (bf16[128,4096]{1,0:T(8,128)(2,1)}, bf16[128,4096]{1,0:T(8,128)(2,1)}, u32[]{:S(2)}, u32[]{:S(2)}) collective-permute-start(bf16[128,4096]{1,0:T(8,128)(2,1)} %bitcast.10), channel_id=1, source_target_pairs={{0,128},{128,0},{1,129},{129,1},{2,130},{130,2},{3,131},{131,3},{4... | collective-permute-start | bytes 3145736 | tf_op jit(solution)/shard_map/ppermute | solution.py:53
  23.1 2.5 collective-permute-done
  25.6 0.7 copy-done.14
  26.4 4.2 %collective-permute-done.4 = bf16[128,4096]{1,0:T(8,128)(2,1)} collective-permute-done((bf16[128,4096]{1,0:T(8,128)(2,1)}, bf16[128,4096]{1,0:T(8,128)(2,1)}, u32[]{:S(2)}, u32[]{:S(2)}) %collective-permute-start.4) | collective-permute-done | bytes 1048608 | tf_op jit(solution)/shard_map/ppermute | solution.py:53
  30.6 1.1 slice.51
  31.7 0.1 collective-permute-done.3
  31.8 1.3 fusion.1
  33.1 16.0 %collective-permute-done.5 = bf16[128,4096]{1,0:T(8,128)(2,1)} collective-permute-done((bf16[128,4096]{1,0:T(8,128)(2,1)}, bf16[128,4096]{1,0:T(8,128)(2,1)}, u32[]{:S(2)}, u32[]{:S(2)}) %collective-permute-start.5) | collective-permute-done | bytes 1048608 | tf_op jit(solution)/shard_map/ppermute | solution.py:53
  49.0 1.1 slice.52
  50.1 0.4 pad_maximum_fusion.4
  50.5 0.3 collective-permute-start.7
  50.8 1.6 collective-permute-start.8
  52.4 1.4 collective-permute-start.9
  53.7 21.8 %collective-permute-done.7 = bf16[128,4096]{1,0:T(8,128)(2,1)S(1)} collective-permute-done((bf16[128,4096]{1,0:T(8,128)(2,1)S(1)}, bf16[128,4096]{1,0:T(8,128)(2,1)S(1)}, u32[]{:S(2)}, u32[]{:S(2)}) %collective-permute-start.7) | collective-permute-done | bytes 1048608 | tf_op jit(solution)/shard_map/ppermute | solution.py:53
  75.6 0.9 collective-permute-done.9
  76.5 1.8 pad_maximum_fusion.1
  78.4 0.2 copy-done.8
  78.5 1.4 collective-permute-start.10
  80.0 3.3 %pad_maximum_fusion = bf16[384,4096]{1,0:T(8,128)(2,1)} fusion(bf16[128,4096]{1,0:T(8,128)(2,1)} %collective-permute-done.5, bf16[128,4096]{1,0:T(8,128)(2,1)} %collective-permute-done.4, bf16[128,4096]{1,0:T(8,128)(2,1)} %collective-permute-done.3), kind=kLoop, calls=%fused_computation | loop fusion | flops 9437184 | bytes 6291456 | tf_op jit(solution)/shard_map/concatenate | solution.py:57
  83.3 1.7 collective-permute-start.11
  85.0 0.8 collective-permute-start.2
  85.7 4.0 %collective-permute-start.1 = (bf16[2048,128]{1,0:T(8,128)(2,1)}, bf16[2048,128]{1,0:T(8,128)(2,1)}, u32[]{:S(2)}, u32[]{:S(2)}) collective-permute-start(bf16[2048,128]{1,0:T(8,128)(2,1)} %bitcast.6), channel_id=1, source_target_pairs={{0,0},{32,1},{64,2},{96,3},{128,4},{160,5},{192,6},{224,7},{16,8},... | collective-permute-start | bytes 1572872 | tf_op jit(solution)/shard_map/ppermute | solution.py:327
  89.8 10.3 %collective-permute-done.11 = bf16[64,4096]{1,0:T(8,128)(2,1)S(1)} collective-permute-done((bf16[64,4096]{1,0:T(8,128)(2,1)S(1)}, bf16[64,4096]{1,0:T(8,128)(2,1)S(1)}, u32[]{:S(2)}, u32[]{:S(2)}) %collective-permute-start.11) | collective-permute-done | bytes 524320 | tf_op jit(solution)/shard_map/ppermute | solution.py:53
  100.2 0.3 collective-permute-start.12
  100.5 0.9 constant_dynamic-update-slice_fusion.2
  101.4 4.0 %collective-permute-done.12 = bf16[32,4096]{1,0:T(8,128)(2,1)S(1)} collective-permute-done((bf16[32,4096]{1,0:T(8,128)(2,1)S(1)}, bf16[32,4096]{1,0:T(8,128)(2,1)S(1)}, u32[]{:S(2)}, u32[]{:S(2)}) %collective-permute-start.12) | collective-permute-done | bytes 262176 | tf_op jit(solution)/shard_map/ppermute | solution.py:53
  105.4 2.4 collective-permute-start.13
  107.8 0.7 constant_dynamic-update-slice_fusion.1
  108.5 2.6 collective-permute-done.13
  111.1 0.7 constant_dynamic-update-slice_fusion
  111.8 4.4 %collective-permute-start.14 = (bf16[128,4096]{1,0:T(8,128)(2,1)}, bf16[128,4096]{1,0:T(8,128)(2,1)}, u32[]{:S(2)}, u32[]{:S(2)}) collective-permute-start(bf16[128,4096]{1,0:T(8,128)(2,1)} %constant_dynamic-update-slice_fusion), channel_id=1, source_target_pairs={{0,16},{16,0},{1,17},{17,1},{2,18},{18,2},{3,19},{19,3},{4,20},{20... | collective-permute-start | bytes 3145736 | tf_op jit(solution)/shard_map/ppermute | solution.py:53
  116.2 0.1 slice_bitcast_fusion
  116.3 0.1 broadcast_in_dim.3
  116.4 0.1 le.15
  116.5 0.1 eq.18
  116.6 13.7 %all-to-all-start = ((bf16[16,128,128]{2,1,0:T(8,128)(2,1)}), bf16[16,128,128]{2,1,0:T(8,128)(2,1)}, u32[]{:S(2)}, u32[]{:S(2)}) async-start(bf16[16,128,128]{2,1,0:T(8,128)(2,1)} %bitcast.7), calls=%async_computation | async-start | bytes 1048576 | tf_op jit(solution)/shard_map/all_to_all | solution.py:328
  130.3 0.2 reduce-scatter.2.cloned.1.call-start
  130.5 0.1 and_convert_fusion.mask
  130.7 0.0 all-gather.2.cloned.1.call-done
  130.7 1.9 copy-done.1
  132.6 1.2 copy-done.3
  133.8 1.2 copy-done.6
  135.1 1.2 copy-done.9
  136.3 6.7 %shard_map.47 = bf16[768,384]{1,0:T(8,128)(2,1)S(1)} custom-call(bf16[8,3,512,128]{3,2,1,0:T(8,128)(2,1)S(1)} %bitcast.40, bf16[8,16,4096]{2,1,0:T(8,128)(2,1)S(1)} %bitcast.42, bf16[8,16,4096]{2,1,0:T(8,128)(2,1)S(1)} %bitcast.44, bf16[8,16,4096]{2,1,0:T(8,128)(2,1)S(1)} %bitcast.47, bf16[24,16,4096]{2,1,0:T(8,128)(2,1)} %bitcast.20.refs_3_.refs_9_), custom_call_target="tpu_custom_call" | custom-call | flops 2415919104 | bytes 9437184 | tf_op jit(solution)/shard_map/pallas_call | solution.py:183
  143.0 0.8 copy-done.12
  143.8 9.3 %shard_map.46 = bf16[1024,384]{1,0:T(8,128)(2,1)S(1)} custom-call(bf16[8,3,512,128]{3,2,1,0:T(8,128)(2,1)S(1)} %bitcast.41, bf16[8,16,4096]{2,1,0:T(8,128)(2,1)} %bitcast.9.refs_0_, bf16[8,16,4096]{2,1,0:T(8,128)(2,1)} %bitcast.11.refs_1_, bf16[8,16,4096]{2,1,0:T(8,128)(2,1)} %bitcast.12.refs_2_, bf16[8,16,4096]{2,1,0:T(8,128)(2,1)} %bitcast.13.refs_3_, ...), custom_call_target="tpu_custom_call" | custom-call | flops 3221225472 | bytes 11534336 | tf_op jit(solution)/shard_map/pallas_call | solution.py:183
  153.2 0.9 copy-done.10
  154.1 1.2 copy-done.4
  155.3 1.2 copy-done.7
  156.5 1.1 copy-done.11
  157.7 1.1 copy-done.13
  158.7 21.1 %shard_map.48 = bf16[8,3,512,128]{3,2,1,0:T(8,128)(2,1)} custom-call(s32[24]{0:T(128)S(1)} %slice_bitcast_fusion.1.order, f32[256,256]{1,0:T(8,128)S(1)} %and_convert_fusion.mask, bf16[8,3,512,128]{3,2,1,0:T(8,128)(2,1)} %bitcast.39, bf16[16,8,16,128]{3,2,1,0:T(8,128)(2,1)} %bitcast.8.g_ref, bf16[64,16,384]{2,1,0:T(8,128)(2,1)S(1)} %bitcast.48, ...), custom_call_target="tpu_custom_call" | custom-call | flops 6442450944 | bytes 16777216 | tf_op jit(solution)/shard_map/pallas_call | solution.py:294
  179.9 51.1 %reduce-scatter.2.cloned.1.call-done = bf16[1536,128]{1,0:T(8,128)(2,1)} async-done(((bf16[12288,128]{1,0:T(8,128)(2,1)}), bf16[1536,128]{1,0:T(8,128)(2,1)}) %reduce-scatter.2.cloned.1.call-update) | async-done | bytes 393232 | tf_op jit(solution)/shard_map/reduce_scatter | solution.py:339
  231.0 1.0 dynamic-slice_bitcast_fusion.1
  232.1 8.2 %collective-permute-start.15 = (bf16[3,256,128]{2,1,0:T(8,128)(2,1)S(1)}, bf16[3,256,128]{2,1,0:T(8,128)(2,1)S(1)}, u32[]{:S(2)}, u32[]{:S(2)}) collective-permute-start(bf16[3,256,128]{2,1,0:T(8,128)(2,1)S(1)} %get-tuple-element.10), channel_id=1, source_target_pairs={{0,0},{1,32},{2,64},{3,96},{4,128},{5,160},{6,192},{7,224},{8,16},... | collective-permute-start | bytes 589832 | tf_op jit(solution)/shard_map/ppermute | solution.py:347
  240.3 0.1 collective-permute-start.16
  240.4 36.8 %collective-permute-done.15 = bf16[3,256,128]{2,1,0:T(8,128)(2,1)S(1)} collective-permute-done((bf16[3,256,128]{2,1,0:T(8,128)(2,1)S(1)}, bf16[3,256,128]{2,1,0:T(8,128)(2,1)S(1)}, u32[]{:S(2)}, u32[]{:S(2)}) %collective-permute-start.15) | collective-permute-done | bytes 196640 | tf_op jit(solution)/shard_map/ppermute | solution.py:347
  277.1 3.6 %collective-permute-done.16 = bf16[3,256,128]{2,1,0:T(8,128)(2,1)S(1)} collective-permute-done((bf16[3,256,128]{2,1,0:T(8,128)(2,1)S(1)}, bf16[3,256,128]{2,1,0:T(8,128)(2,1)S(1)}, u32[]{:S(2)}, u32[]{:S(2)}) %collective-permute-start.16) | collective-permute-done | bytes 196640 | tf_op jit(solution)/shard_map/ppermute | solution.py:347
  280.8 0.7 fusion
  (35 shorter events, 0.2 us)
Async XLA Ops:
  6.5 3.4 %copy-start = (bf16[4096,3,128]{2,0,1:T(8,128)(2,1)S(1)}, bf16[4096,3,128]{2,0,1:T(8,128)(2,1)}, u32[]{:S(2)}) copy-start(bf16[4096,3,128]{2,0,1:T(8,128)(2,1)} %param.6) | copy-start | bytes 9437188
  6.5 124.2 %all-gather.2.cloned.1.call-start = ((), (), s32[]{:S(2)}) async-start(), calls=%async_computation.2 | async-start | bytes 3538944 | tf_op jit(solution)/shard_map/all_gather | solution.py:326
  6.5 24.1 %collective-permute-start.4 = (bf16[128,4096]{1,0:T(8,128)(2,1)}, bf16[128,4096]{1,0:T(8,128)(2,1)}, u32[]{:S(2)}, u32[]{:S(2)}) collective-permute-start(bf16[128,4096]{1,0:T(8,128)(2,1)} %bitcast.10), channel_id=1, source_target_pairs={{0,32},{32,64},{64,96},{96,0},{1,33},{33,65},{65,97},{97,1},{2,34}... | collective-permute-start | bytes 3145736 | tf_op jit(solution)/shard_map/ppermute | solution.py:53
  7.8 24.0 %collective-permute-start.3 = (bf16[128,4096]{1,0:T(8,128)(2,1)}, bf16[128,4096]{1,0:T(8,128)(2,1)}, u32[]{:S(2)}, u32[]{:S(2)}) collective-permute-start(bf16[128,4096]{1,0:T(8,128)(2,1)} %bitcast.10), channel_id=1, source_target_pairs={{0,96},{32,0},{64,32},{96,64},{1,97},{33,1},{65,33},{97,65},{2,98}... | collective-permute-start | bytes 3145736 | tf_op jit(solution)/shard_map/ppermute | solution.py:53
  10.0 15.6 %collective-permute-start = (bf16[1536,128]{1,0:T(8,128)(2,1)S(1)}, bf16[1536,128]{1,0:T(8,128)(2,1)S(1)}, u32[]{:S(2)}, u32[]{:S(2)}) collective-permute-start(bf16[1536,128]{1,0:T(8,128)(2,1)S(1)} %bitcast.52), channel_id=1, source_target_pairs={{0,0},{32,1},{64,2},{96,3},{128,4},{160,5},{192,6},{224,7},{16,8},... | collective-permute-start | bytes 1179656 | tf_op jit(solution)/shard_map/ppermute | solution.py:325
  18.5 30.6 %collective-permute-start.5 = (bf16[128,4096]{1,0:T(8,128)(2,1)}, bf16[128,4096]{1,0:T(8,128)(2,1)}, u32[]{:S(2)}, u32[]{:S(2)}) collective-permute-start(bf16[128,4096]{1,0:T(8,128)(2,1)} %bitcast.10), channel_id=1, source_target_pairs={{0,128},{128,0},{1,129},{129,1},{2,130},{130,2},{3,131},{131,3},{4... | collective-permute-start | bytes 3145736 | tf_op jit(solution)/shard_map/ppermute | solution.py:53
  25.6 0.7 copy-start.14
  50.5 25.1 %collective-permute-start.7 = (bf16[128,4096]{1,0:T(8,128)(2,1)S(1)}, bf16[128,4096]{1,0:T(8,128)(2,1)S(1)}, u32[]{:S(2)}, u32[]{:S(2)}) collective-permute-start(bf16[128,4096]{1,0:T(8,128)(2,1)S(1)} %get-tuple-element.8), channel_id=1, source_target_pairs={{0,32},{32,64},{64,96},{96,0},{1,33},{33,65},{65,97},{97,1},{2,34}... | collective-permute-start | bytes 3145736 | tf_op jit(solution)/shard_map/ppermute | solution.py:53
  50.8 24.8 %collective-permute-start.8 = (bf16[128,4096]{1,0:T(8,128)(2,1)S(1)}, bf16[128,4096]{1,0:T(8,128)(2,1)S(1)}, u32[]{:S(2)}, u32[]{:S(2)}) collective-permute-start(bf16[128,4096]{1,0:T(8,128)(2,1)S(1)} %get-tuple-element.9), channel_id=1, source_target_pairs={{0,96},{32,0},{64,32},{96,64},{1,97},{33,1},{65,33},{97,65},{2,98}... | collective-permute-start | bytes 3145736 | tf_op jit(solution)/shard_map/ppermute | solution.py:53
  52.4 24.1 %collective-permute-start.9 = (bf16[128,4096]{1,0:T(8,128)(2,1)S(1)}, bf16[128,4096]{1,0:T(8,128)(2,1)S(1)}, u32[]{:S(2)}, u32[]{:S(2)}) collective-permute-start(bf16[128,4096]{1,0:T(8,128)(2,1)S(1)} %get-tuple-element.7), channel_id=1, source_target_pairs={{0,128},{128,0},{1,129},{129,1},{2,130},{130,2},{3,131},{131,3},{4... | collective-permute-start | bytes 3145736 | tf_op jit(solution)/shard_map/ppermute | solution.py:53
  75.6 14.2 %copy-start.2 = (bf16[128,4096]{1,0:T(8,128)(2,1)}, bf16[128,4096]{1,0:T(8,128)(2,1)S(1)}, u32[]{:S(2)}) copy-start(bf16[128,4096]{1,0:T(8,128)(2,1)S(1)} %collective-permute-done.7) | copy-start | bytes 3145732
  75.6 14.2 %copy-start.5 = (bf16[128,4096]{1,0:T(8,128)(2,1)}, bf16[128,4096]{1,0:T(8,128)(2,1)S(1)}, u32[]{:S(2)}) copy-start(bf16[128,4096]{1,0:T(8,128)(2,1)S(1)} %collective-permute-done.8) | copy-start | bytes 3145732
  76.5 2.0 copy-start.8
  78.5 52.2 %collective-permute-start.10 = (bf16[384,4096]{1,0:T(8,128)(2,1)}, bf16[384,4096]{1,0:T(8,128)(2,1)}, u32[]{:S(2)}, u32[]{:S(2)}) collective-permute-start(bf16[384,4096]{1,0:T(8,128)(2,1)} %pad_maximum_fusion.1), channel_id=1, source_target_pairs={{0,16},{16,0},{1,17},{17,1},{2,18},{18,2},{3,19},{19,3},{4,20},{20... | collective-permute-start | bytes 9437192 | tf_op jit(solution)/shard_map/ppermute | solution.py:53
  83.3 60.6 %collective-permute-start.6 = (bf16[384,4096]{1,0:T(8,128)(2,1)}, bf16[384,4096]{1,0:T(8,128)(2,1)}, u32[]{:S(2)}, u32[]{:S(2)}) collective-permute-start(bf16[384,4096]{1,0:T(8,128)(2,1)} %pad_maximum_fusion), channel_id=1, source_target_pairs={{0,16},{16,0},{1,17},{17,1},{2,18},{18,2},{3,19},{19,3},{4,20},{20... | collective-permute-start | bytes 9437192 | tf_op jit(solution)/shard_map/ppermute | solution.py:53
  83.3 16.9 %collective-permute-start.11 = (bf16[64,4096]{1,0:T(8,128)(2,1)S(1)}, bf16[64,4096]{1,0:T(8,128)(2,1)S(1)}, u32[]{:S(2)}, u32[]{:S(2)}) collective-permute-start(bf16[64,4096]{1,0:T(8,128)(2,1)S(1)} %slice.55), channel_id=1, source_target_pairs={{0,128},{128,0},{1,129},{129,1},{2,130},{130,2},{3,131},{131,3},{4... | collective-permute-start | bytes 1572872 | tf_op jit(solution)/shard_map/ppermute | solution.py:53
  85.0 58.9 %collective-permute-start.2 = (bf16[128,4096]{1,0:T(8,128)(2,1)}, bf16[128,4096]{1,0:T(8,128)(2,1)}, u32[]{:S(2)}, u32[]{:S(2)}) collective-permute-start(bf16[128,4096]{1,0:T(8,128)(2,1)} %bitcast.10), channel_id=1, source_target_pairs={{0,16},{16,0},{1,17},{17,1},{2,18},{18,2},{3,19},{19,3},{4,20},{20... | collective-permute-start | bytes 3145736 | tf_op jit(solution)/shard_map/ppermute | solution.py:53
  85.7 30.8 %collective-permute-start.1 = (bf16[2048,128]{1,0:T(8,128)(2,1)}, bf16[2048,128]{1,0:T(8,128)(2,1)}, u32[]{:S(2)}, u32[]{:S(2)}) collective-permute-start(bf16[2048,128]{1,0:T(8,128)(2,1)} %bitcast.6), channel_id=1, source_target_pairs={{0,0},{32,1},{64,2},{96,3},{128,4},{160,5},{192,6},{224,7},{16,8},... | collective-permute-start | bytes 1572872 | tf_op jit(solution)/shard_map/ppermute | solution.py:327
  100.2 5.2 %collective-permute-start.12 = (bf16[32,4096]{1,0:T(8,128)(2,1)S(1)}, bf16[32,4096]{1,0:T(8,128)(2,1)S(1)}, u32[]{:S(2)}, u32[]{:S(2)}) collective-permute-start(bf16[32,4096]{1,0:T(8,128)(2,1)S(1)} %slice.56), channel_id=1, source_target_pairs={{0,32},{32,64},{64,96},{96,0},{1,33},{33,65},{65,97},{97,1},{2,34}... | collective-permute-start | bytes 786440 | tf_op jit(solution)/shard_map/ppermute | solution.py:53
  105.4 5.7 %collective-permute-start.13 = (bf16[32,4096]{1,0:T(8,128)(2,1)S(1)}, bf16[32,4096]{1,0:T(8,128)(2,1)S(1)}, u32[]{:S(2)}, u32[]{:S(2)}) collective-permute-start(bf16[32,4096]{1,0:T(8,128)(2,1)S(1)} %slice.57), channel_id=1, source_target_pairs={{0,96},{32,0},{64,32},{96,64},{1,97},{33,1},{65,33},{97,65},{2,98}... | collective-permute-start | bytes 786440 | tf_op jit(solution)/shard_map/ppermute | solution.py:53
  111.8 42.3 %collective-permute-start.14 = (bf16[128,4096]{1,0:T(8,128)(2,1)}, bf16[128,4096]{1,0:T(8,128)(2,1)}, u32[]{:S(2)}, u32[]{:S(2)}) collective-permute-start(bf16[128,4096]{1,0:T(8,128)(2,1)} %constant_dynamic-update-slice_fusion), channel_id=1, source_target_pairs={{0,16},{16,0},{1,17},{17,1},{2,18},{18,2},{3,19},{19,3},{4,20},{20... | collective-permute-start | bytes 3145736 | tf_op jit(solution)/shard_map/ppermute | solution.py:53
  116.6 37.5 %all-to-all-start = ((bf16[16,128,128]{2,1,0:T(8,128)(2,1)}), bf16[16,128,128]{2,1,0:T(8,128)(2,1)}, u32[]{:S(2)}, u32[]{:S(2)}) async-start(bf16[16,128,128]{2,1,0:T(8,128)(2,1)} %bitcast.7), calls=%async_computation | async-start | bytes 1048576 | tf_op jit(solution)/shard_map/all_to_all | solution.py:328
  130.3 100.7 %reduce-scatter.2.cloned.1.call-start = ((), (), s32[]{:S(2)}) async-start(), calls=%async_computation.3 | async-start | bytes 3538944 | tf_op jit(solution)/shard_map/reduce_scatter | solution.py:339
  130.7 1.9 copy-start.1
  132.6 1.2 copy-start.3
  133.8 1.2 copy-start.6
  135.1 1.2 copy-start.9
  143.0 0.9 copy-start.12
  153.2 0.9 copy-start.10
  154.1 1.2 copy-start.4
  155.3 1.2 copy-start.7
  156.5 1.1 copy-start.11
  157.7 1.1 copy-start.13
  232.1 45.1 %collective-permute-start.15 = (bf16[3,256,128]{2,1,0:T(8,128)(2,1)S(1)}, bf16[3,256,128]{2,1,0:T(8,128)(2,1)S(1)}, u32[]{:S(2)}, u32[]{:S(2)}) collective-permute-start(bf16[3,256,128]{2,1,0:T(8,128)(2,1)S(1)} %get-tuple-element.10), channel_id=1, source_target_pairs={{0,0},{1,32},{2,64},{3,96},{4,128},{5,160},{6,192},{7,224},{8,16},... | collective-permute-start | bytes 589832 | tf_op jit(solution)/shard_map/ppermute | solution.py:347
  240.3 40.5 %collective-permute-start.16 = (bf16[3,256,128]{2,1,0:T(8,128)(2,1)S(1)}, bf16[3,256,128]{2,1,0:T(8,128)(2,1)S(1)}, u32[]{:S(2)}, u32[]{:S(2)}) collective-permute-start(bf16[3,256,128]{2,1,0:T(8,128)(2,1)S(1)} %get-tuple-element.11), channel_id=1, source_target_pairs={{0,16},{1,48},{2,80},{3,112},{4,144},{5,176},{6,208},{7,240},{8,0}... | collective-permute-start | bytes 589832 | tf_op jit(solution)/shard_map/ppermute | solution.py:347
Sparse Core Ops, SparseCore 0:
  26.5 66.2 all-gather.1
  180.0 50.9 reduce-scatter.1

commit v3 on v2

--- a/solution.py
+++ b/solution.py
@@ -16,8 +16,9 @@
 TOK = AXES[3:]
 FRAMES = 16
 PATCHES = 128
-HALF = PATCHES // 2
-QUARTER = PATCHES // 4
+CUT_A, CUT_B = 48, 96
+CUTS = ((0, CUT_A), (CUT_A, CUT_B), (CUT_B, PATCHES))
+CUT_FLOPS = 3 * 10**10
 WIDTH = 4096
 COLS = 3 * HEAD_DIM
 ROWS = FRAMES * PATCHES
@@ -43,7 +44,7 @@
                 for yh in range(2):
                     for z in range(8):
                         source = device(yl, x, core, yh, z)
-                        target = device(yl ^ (z // 4), x + z % 4, yh ^ flip, core, 4 * yl + x)
+                        target = device(yl ^ (z % 2), x + z // 2, yh ^ flip, core, 2 * x + yl)
                         pairs.append((source, target))
     return pairs
 
@@ -53,49 +54,63 @@
     return lax.ppermute(value, axis, [(i, (i + by) % count) for i in range(count)])
 
 
-def gather_frames(own):
-    join = lambda *parts: jnp.concatenate(parts, axis=0)
-    left = shift(own, "x", 1)
-    right = shift(own, "x", -1)
-    other = shift(own, "yl", 1)
-    twin = shift(own, "core", 1)
-    from_left = shift(join(left[:HALF], other[HALF:]), "x", 1)
-    from_right = shift(join(right[HALF:], other[HALF:]), "x", -1)
-    from_other = shift(join(right[:HALF], left[:HALF]), "yl", 1)
-    twin_a = shift(join(right, left, other), "core", 1)
-    last_left = shift(from_left[HALF : HALF + QUARTER], "x", 1)
-    last_right = shift(from_right[HALF + QUARTER :], "x", -1)
-    last_other = shift(from_left[:HALF], "yl", 1)
-    twin_b = shift(join(from_left, from_right, from_other), "core", 1)
-    last = join(last_other, last_left, last_right)
-    twin_c = shift(last, "core", 1)
+def after(values, *others):
+    return lax.optimization_barrier((values, *others))[0]
+
+
+def cut_kernel(*refs):
+    sems = refs[-1]
+    copies = []
+    for index, (first, last) in enumerate(CUTS):
+        source, target = refs[index], refs[3 + index]
+        copies.append(
+            pltpu.make_async_copy(source.at[pl.ds(first, last - first)], target, sems.at[index])
+        )
+        copies[-1].start()
+    for copy in copies:
+        copy.wait()
+
+
+def cut(*buffers):
+    hbm = pl.BlockSpec(memory_space=pltpu.HBM)
+    return pl.pallas_call(
+        cut_kernel,
+        out_shape=[
+            jax.ShapeDtypeStruct((last - first, WIDTH), jnp.bfloat16) for first, last in CUTS
+        ],
+        in_specs=[hbm] * 3,
+        out_specs=[hbm] * 3,
+        scratch_shapes=[pltpu.SemaphoreType.DMA((3,))],
+        cost_estimate=pl.CostEstimate(flops=CUT_FLOPS, bytes_accessed=0, transcendentals=0),
+    )(*buffers)
+
+
+def gather_frames(own, early, middle):
+    twin = lambda values: [shift(value, "core", 1) for value in values]
+    first = [shift(own, "x", 1), shift(own, "x", -1), shift(own, "yl", 1)]
+    own_twin = shift(own, "core", 1)
+    left, right, other = after(first, *early)
+    second = [shift(other, "x", 1), shift(right, "x", -1), shift(right, "yl", 1)]
+    first_twins = twin([left, right, other])
+    other_left, far, other_right = after(second, *middle)
+    cuts = cut(other_left, other_right, far)
+    third = [shift(cuts[0], "x", 1), shift(cuts[1], "x", -1), shift(cuts[2], "yl", 1)]
+    second_twins = twin([other_left, far, other_right])
+    third = after(third)
     return (
-        [own, twin, right, left, other, twin_a],
-        [from_left, from_right, from_other, twin_b],
-        [last, twin_c],
-    )
-
-
-FIRST = [
-    [(0, 0, PATCHES)],
-    [(1, 0, PATCHES)],
-    [(2, 0, PATCHES)],
-    [(4, 0, PATCHES)],
-    [(6, 0, PATCHES)],
-    [(3, 0, PATCHES), (5, 0, PATCHES), (7, 0, PATCHES)],
+        [own, own_twin, left, right, other, *first_twins],
+        [other_left, far, other_right, *second_twins],
+        [*third, *twin(third)],
+    )
+
+
+FIRST = [[(slot, 0, PATCHES)] for slot in (0, 1, 4, 2, 6, 5, 3, 7)]
+SECOND = [[(slot, 0, PATCHES)] for slot in (12, 8, 10, 13, 9, 11)]
+THIRD = [
+    [(14 + core, first, last - first)]
+    for core in (0, 1)
+    for first, last in CUTS
 ]
-
-
-def second(core):
-    return [
-        [(8 + core, 0, HALF), (12 + core, HALF, HALF)],
-        [(8 + core, HALF, HALF), (10 + core, HALF, HALF)],
-        [(10 + core, 0, HALF), (12 + core, 0, HALF)],
-    ]
-
-
-SECOND = second(0) + [[part for buffer in second(1) for part in buffer]]
-THIRD = [[(14, 0, PATCHES)], [(15, 0, PATCHES)]]
 
 
 def parts_of(places):
@@ -113,11 +128,11 @@
     for yl, x, core, yh, z in np.ndindex(*SIZES):
         row = out[device(yl, x, core, yh, z)]
         for slot, (dy, dx, dc) in enumerate(SLOTS):
-            row[slot] = (core ^ dc) * 8 + dy * 4 + dx % 4
+            row[slot] = (core ^ dc) * 8 + (x + dx) % 4 * 2 + (yl ^ dy)
             row[24 + slot] = ((yl ^ dy) * 4 + (x + dx) % 4) * 2 + (core ^ dc)
         for k in range(8):
-            row[16 + k] = (yl ^ (k // 4)) * 4 + (x + k % 4) % 4
-        row[40] = (yl ^ (z // 4)) * 4 + (x - z % 4) % 4
+            row[16 + k] = (yl ^ (k % 2)) * 4 + (x + k // 2) % 4
+        row[40] = (x - z // 2) % 4 * 2 + (yl ^ (z % 2))
     return out
 
 
@@ -130,7 +145,7 @@
 
 VMEM = pl.BlockSpec(memory_space=pltpu.VMEM)
 SMEM = pl.BlockSpec(memory_space=pltpu.SMEM)
-ANY = pl.BlockSpec(memory_space=pl.ANY)
+HBM = pl.BlockSpec(memory_space=pltpu.HBM)
 
 
 def load_weights(w_ref, w, sem):
@@ -155,26 +170,29 @@
 
 def project_kernel(count, w_ref, *refs):
     buffers, out = refs[:count], refs[count]
-    tokens, w, w_sem, sems = refs[count + 1 :]
+    tokens, result, w, w_sem, sems, o_sem = refs[count + 1 :]
     copies, at = [], 0
+    loads = load_weights(w_ref, w, w_sem)
     for index, ref in enumerate(buffers):
         rows = ref.shape[0]
         copies.append(pltpu.make_async_copy(ref, tokens.at[pl.ds(at, rows)], sems.at[index]))
+        copies[-1].start()
         at += rows
-    loads = load_weights(w_ref, w, w_sem)
-    for copy in copies:
-        copy.start()
-    for copy in loads + copies:
-        copy.wait()
-    block = 2 * PATCHES
-
-    def body(step, carry):
-        rows = pl.ds(pl.multiple_of(step * block, block), block)
-        groups = pl.ds(step * (block // GROUP), block // GROUP)
-        out[rows] = project_rows(tokens[groups].reshape(block, WIDTH), w)
-        return carry
-
-    lax.fori_loop(0, at * GROUP // block, body, 0)
+    for copy in loads:
+        copy.wait()
+    stores = []
+    for index in range(0, count, 2):
+        copies[index].wait()
+        copies[index + 1].wait()
+        groups = pl.ds(index * (PATCHES // GROUP), 2 * (PATCHES // GROUP))
+        rows = project_rows(tokens[groups].reshape(2 * PATCHES, WIDTH), w)
+        result[groups] = rows.reshape(-1, GROUP, COLS)
+        stores.append(
+            pltpu.make_async_copy(result.at[groups], out.at[groups], o_sem.at[index // 2])
+        )
+        stores[-1].start()
+    for store in stores:
+        store.wait()
 
 
 def project(w, buffers):
@@ -182,16 +200,18 @@
     rows = groups * GROUP
     return pl.pallas_call(
         functools.partial(project_kernel, len(buffers)),
-        out_shape=jax.ShapeDtypeStruct((rows, COLS), jnp.bfloat16),
-        in_specs=[ANY] * (1 + len(buffers)),
-        out_specs=VMEM,
+        out_shape=jax.ShapeDtypeStruct((groups, GROUP, COLS), jnp.bfloat16),
+        in_specs=[HBM] * (1 + len(buffers)),
+        out_specs=HBM,
         scratch_shapes=[
             pltpu.VMEM((groups, GROUP, WIDTH), jnp.bfloat16),
+            pltpu.VMEM((groups, GROUP, COLS), jnp.bfloat16),
             pltpu.VMEM((WIDTH, COLS), jnp.bfloat16),
             pltpu.SemaphoreType.DMA((24,)),
             pltpu.SemaphoreType.DMA((len(buffers),)),
+            pltpu.SemaphoreType.DMA((len(buffers) // 2,)),
         ],
-        compiler_params=pltpu.CompilerParams(vmem_limit_bytes=32 * 2**20),
+        compiler_params=pltpu.CompilerParams(vmem_limit_bytes=58 * 2**20),
         cost_estimate=pl.CostEstimate(
             flops=2 * rows * WIDTH * COLS, bytes_accessed=2 * (rows + COLS) * WIDTH, transcendentals=0
         ),
@@ -228,7 +248,7 @@
     lax.fori_loop(0, PATCHES // GROUP, body, 0)
 
 
-def share_kernel(count, order, mask, w_ref, g_ref, proj_a, proj_b, *refs):
+def share_kernel(count, order, mask, w_ref, g_ref, early, *refs):
     buffers, out = refs[:count], refs[count]
     tokens, proj, grads, turned, w, shares, w_sem, x_sem, g_sem, p_sem, o_sem = refs[count + 1 :]
     token_copies = []
@@ -240,28 +260,24 @@
                 x_sem.at[index],
             )
         )
-    for copy in token_copies[-2:]:
+    last = token_copies[-len(THIRD) :]
+    for copy in last:
         copy.start()
     loads = load_weights(w_ref, w, w_sem)
     small = []
     for slot in range(FRAMES):
         small.append(pltpu.make_async_copy(g_ref.at[order[slot]], grads.at[:, slot], g_sem.at[slot]))
-    index = 0
-    for source, places in ((proj_a, FIRST), (proj_b, SECOND)):
-        at = 0
-        for _, _, slot, first, groups in parts_of(places):
-            small.append(
-                pltpu.make_async_copy(
-                    source.at[pl.ds(at, groups)],
-                    proj.at[pl.ds(first, groups), slot],
-                    p_sem.at[index],
-                )
+    at = 0
+    for index, (_, _, slot, first, groups) in enumerate(parts_of(FIRST + SECOND)):
+        small.append(
+            pltpu.make_async_copy(
+                early.at[pl.ds(at, groups)], proj.at[pl.ds(first, groups), slot], p_sem.at[index]
             )
-            at += groups
-            index += 1
-    for copy in small + token_copies[:-2]:
+        )
+        at += groups
+    for copy in small + token_copies[: -len(THIRD)]:
         copy.start()
-    for copy in token_copies[-2:] + loads:
+    for copy in last + loads:
         copy.wait()
     for slot in (14, 15):
         rows = project_rows(tokens[:, slot].reshape(PATCHES, WIDTH), w)
@@ -269,7 +285,7 @@
     for copy in small:
         copy.wait()
     attend(proj, grads, mask, turned)
-    for copy in token_copies[:-2]:
+    for copy in token_copies[: -len(THIRD)]:
         copy.wait()
 
     def weigh(step, carry):
@@ -286,16 +302,15 @@
         pltpu.make_async_copy(shares.at[step], out.at[step], o_sem.at[step]).wait()
 
 
-def weight_share(order, mask, w, g, proj_a, proj_b, buffers):
+def weight_share(order, mask, w, g, early, buffers):
     count = len(buffers)
     groups = PATCHES // GROUP
     token_parts = len(parts_of(FIRST + SECOND + THIRD))
-    grouped = lambda value: value.reshape(-1, GROUP, COLS)
     return pl.pallas_call(
         functools.partial(share_kernel, count),
         out_shape=jax.ShapeDtypeStruct((8, 3, CHUNK, HEAD_DIM), jnp.bfloat16),
-        in_specs=[SMEM, VMEM] + [ANY] * (4 + count),
-        out_specs=ANY,
+        in_specs=[SMEM, VMEM] + [HBM] * (3 + count),
+        out_specs=HBM,
         scratch_shapes=[
             pltpu.VMEM((groups, FRAMES, GROUP, WIDTH), jnp.bfloat16),
             pltpu.VMEM((groups, FRAMES, GROUP, COLS), jnp.bfloat16),
@@ -306,14 +321,14 @@
             pltpu.SemaphoreType.DMA((24,)),
             pltpu.SemaphoreType.DMA((token_parts,)),
             pltpu.SemaphoreType.DMA((FRAMES,)),
-            pltpu.SemaphoreType.DMA((token_parts - 2,)),
+            pltpu.SemaphoreType.DMA((len(FIRST + SECOND),)),
             pltpu.SemaphoreType.DMA((8,)),
         ],
-        compiler_params=pltpu.CompilerParams(vmem_limit_bytes=44 * 2**20),
+        compiler_params=pltpu.CompilerParams(vmem_limit_bytes=58 * 2**20),
         cost_estimate=pl.CostEstimate(
             flops=2 * ROWS * WIDTH * COLS, bytes_accessed=2 * ROWS * WIDTH, transcendentals=0
         ),
-    )(order, mask, w, g, grouped(proj_a), grouped(proj_b), *buffers)
+    )(order, mask, w, g, early, *buffers)
 
 
 def local(inputs, grad_attn, w_qkv):
@@ -324,18 +339,18 @@
     )
     rows_w = lax.ppermute(rows_w.reshape(3 * CHUNK, HEAD_DIM), AXES, to_worker)
     w = lax.all_gather(rows_w, "z", axis=0, tiled=True).reshape(8, 3, CHUNK, HEAD_DIM)
-    g = lax.ppermute(grad_attn[0], AXES, to_worker).reshape(FRAMES, PATCHES, HEAD_DIM)
-    g = lax.all_to_all(g, TOK, split_axis=0, concat_axis=0, tiled=True)
-    g = g.reshape(FRAMES, PATCHES // GROUP, GROUP, HEAD_DIM)
-    steps = gather_frames(inputs[0])
-    first, second_, third = (
+    exchange = lambda value, axes: lax.all_to_all(
+        value, axes, split_axis=0, concat_axis=0, tiled=True
+    )
+    heads_g = exchange(grad_attn[0].reshape(FRAMES, PATCHES, HEAD_DIM), TOK)
+    frames_g = exchange(heads_g, ("core", "x", "yl"))
+    steps = gather_frames(inputs[0], (rows_w, heads_g), (frames_g,))
+    g = frames_g.reshape(FRAMES, PATCHES // GROUP, GROUP, HEAD_DIM)
+    first, second, third = (
         [buffer.reshape(-1, GROUP, WIDTH) for buffer in buffers] for buffers in steps
     )
-    proj_a = project(w, first)
-    proj_b = project(w, second_)
-    share = weight_share(
-        table[:24], visible(table[24:40]), w, g, proj_a, proj_b, first + second_ + third
-    )
+    early = project(w, first + second)
+    share = weight_share(table[:24], visible(table[24:40]), w, g, early, first + second + third)
     mine = lax.psum_scatter(
         share.reshape(8 * 3 * CHUNK, HEAD_DIM), "z", scatter_dimension=0, tiled=True
     )

time: 291 us -> 278 us (0.955)
  Pallas kernels: 37.1 us -> 74 us
  waiting for transfers between devices: 154 us -> 137 us
  local copies, waits for them, and re-layouts: 21.4 us -> 4.64 us
  starting transfers between devices: 55.1 us -> 46 us
  other arithmetic: 6.39 us -> 1.56 us
    ppermute x13 -> x19, waiting for transfers between devices: 60 us -> 7.17 us  [shift(): lax.ppermute(value, axis, [(i, (i + by) % count) for i in range(count)])]
    pallas_call x0 -> x1, Pallas kernels: none -> 32.9 us  [cut(): pl.pallas_call(cut_kernel, out_shape=[jax.ShapeDtypeStruct((last - first,...]
    all_to_all x1 -> x2, waiting for transfers between devices: 0.01 us -> 24.6 us  [local(): lax.all_to_all(value, axes, split_axis=0, concat_axis=0, tiled=True)]
    ppermute x1, waiting for transfers between devices: 2.53 us -> 22.1 us  [local(): rows_w = lax.ppermute(rows_w.reshape(3 * CHUNK, HEAD_DIM), AXES, to_worker)]
    unnamed x32 -> x10, local copies, waits for them, and re-layouts: 14.5 us -> 0.76 us
    reduce_scatter x1, waiting for transfers between devices: 51.1 us -> 42.7 us  [local(): lax.psum_scatter(share.reshape(8 * 3 * CHUNK, HEAD_DIM), 'z', scatter_dim...]
    ppermute x13 -> x19, starting transfers between devices: 20.3 us -> 12 us  [shift(): lax.ppermute(value, axis, [(i, (i + by) % count) for i in range(count)])]
    concatenate x3 -> x0, other arithmetic: 5.52 us -> none  [gather_frames(): join = lambda *parts: jnp.concatenate(parts, axis=0)]
  transfers between devices with their start and end apart: 20 -> 26, of which waited for: 12 -> 8; matrix products, arithmetic and copies ran while one was open for 5% -> 1% of each run, Pallas kernels for 6% -> 18%
where the time goes in v3:
time: 278 us; the launch traced here: 277 us
  waiting for transfers between devices  137 us (49%)
  Pallas kernels  74 us (27%)
  starting transfers between devices  46 us (17%)
  between operations  14.3 us (5%)
  local copies, waits for them, and re-layouts  4.64 us (2%)
    reduce_scatter x1, waiting for transfers between devices, local(): lax.psum_scatter(share.reshape(8 * 3 * CHUNK, HEAD_DIM), 'z', scatter_dim...  42.7 us
    ppermute x2, waiting for transfers between devices, local(): part = lax.ppermute(part, AXES, owner_moves(flip)).astype(jnp.float32)  40.1 us
    pallas_call x1, Pallas kernels, cut(): pl.pallas_call(cut_kernel, out_shape=[jax.ShapeDtypeStruct((last - first,...  32.9 us
    pallas_call x1, Pallas kernels, weight_share(): pl.pallas_call(functools.partial(share_kernel, count), out_shape=jax.Shap...  25.3 us
    all_to_all x2, waiting for transfers between devices, local(): lax.all_to_all(value, axes, split_axis=0, concat_axis=0, tiled=True)  24.6 us
    ppermute x1, waiting for transfers between devices, local(): rows_w = lax.ppermute(rows_w.reshape(3 * CHUNK, HEAD_DIM), AXES, to_worker)  22.1 us
    pallas_call x1, Pallas kernels, project(): pl.pallas_call(functools.partial(project_kernel, len(buffers)), out_shape...  15.7 us
    all_to_all x2, starting transfers between devices, local(): lax.all_to_all(value, axes, split_axis=0, concat_axis=0, tiled=True)  15.2 us
  transfers between devices with their start and end apart: 26, of which 8 were waited for; matrix products, arithmetic and copies ran while one was open for 1% of the time, Pallas kernels for 18%

profile of v3, /device:TPU:3, one launch (start us, length us, event | category | flops | bytes accessed | tf_op | source)
XLA Modules:
  0.0 277.2 jit_solution(17421234229366717430)
XLA Ops:
  6.5 1.2 collective-permute-start.2
  7.7 0.3 collective-permute-start.3
  8.0 1.3 collective-permute-start.4
  9.3 10.7 %all-to-all-start = ((bf16[16,128,128]{2,1,0:T(8,128)(2,1)}), bf16[16,128,128]{2,1,0:T(8,128)(2,1)}, u32[]{:S(2)}, u32[]{:S(2)}) async-start(bf16[16,128,128]{2,1,0:T(8,128)(2,1)} %bitcast.53), calls=%async_computation | async-start | bytes 1048576 | tf_op jit(solution)/shard_map/all_to_all | solution.py:342
  20.0 0.0 all-gather.2.cloned.1.call-start
  20.0 0.7 constant_dynamic-slice_fusion.1
  20.7 0.6 slice.20
  22.1 9.7 %collective-permute-start = (bf16[1536,128]{1,0:T(8,128)(2,1)S(1)}, bf16[1536,128]{1,0:T(8,128)(2,1)S(1)}, u32[]{:S(2)}, u32[]{:S(2)}) collective-permute-start(bf16[1536,128]{1,0:T(8,128)(2,1)S(1)} %bitcast.55), channel_id=1, source_target_pairs={{0,0},{128,1},{32,2},{160,3},{64,4},{192,5},{96,6},{224,7},{16,8},... | collective-permute-start | bytes 1179656 | tf_op jit(solution)/shard_map/ppermute | solution.py:340
  31.8 22.1 %collective-permute-done = bf16[1536,128]{1,0:T(8,128)(2,1)S(1)} collective-permute-done((bf16[1536,128]{1,0:T(8,128)(2,1)S(1)}, bf16[1536,128]{1,0:T(8,128)(2,1)S(1)}, u32[]{:S(2)}, u32[]{:S(2)}) %collective-permute-start) | collective-permute-done | bytes 393248 | tf_op jit(solution)/shard_map/ppermute | solution.py:340
  53.9 0.7 copy-done.1
  54.6 0.0 all-gather.2.cloned.1.call-update
  54.7 0.0 all-to-all-done
  54.7 0.0 collective-permute-done.2
  54.7 0.0 collective-permute-done.3
  54.7 0.0 collective-permute-done.4
  54.7 0.1 collective-permute-start.10
  54.8 0.1 collective-permute-start.8
  54.9 1.5 collective-permute-start.9
  56.4 4.5 %all-to-all-start.1 = ((bf16[16,128,128]{2,1,0:T(8,128)(2,1)}), bf16[16,128,128]{2,1,0:T(8,128)(2,1)}, u32[]{:S(2)}, u32[]{:S(2)}) async-start(bf16[16,128,128]{2,1,0:T(8,128)(2,1)} %all-to-all-done), calls=%async_computation.1 | async-start | bytes 1048576 | tf_op jit(solution)/shard_map/all_to_all | solution.py:342
  60.9 0.0 reduce-scatter.2.cloned.1.call-start
  60.9 0.4 collective-permute-start.1
  61.4 0.2 collective-permute-start.5
  61.5 24.6 %all-to-all-done.1 = bf16[16,128,128]{2,1,0:T(8,128)(2,1)} async-done(((bf16[16,128,128]{2,1,0:T(8,128)(2,1)}), bf16[16,128,128]{2,1,0:T(8,128)(2,1)}, u32[]{:S(2)}, u32[]{:S(2)}) %all-to-all-start.1) | async-done | bytes 524320 | tf_op jit(solution)/shard_map/all_to_all | solution.py:342
  86.2 0.0 collective-permute-done.10.refs_1_
  86.2 0.0 collective-permute-done.8.refs_0_
  86.2 0.0 collective-permute-done.9.refs_2_
  86.2 32.9 %shard_map.47 = (bf16[48,4096]{1,0:T(8,128)(2,1)}, bf16[48,4096]{1,0:T(8,128)(2,1)}, bf16[32,4096]{1,0:T(8,128)(2,1)}) custom-call(bf16[128,4096]{1,0:T(8,128)(2,1)} %collective-permute-done.8.refs_0_, bf16[128,4096]{1,0:T(8,128)(2,1)} %collective-permute-done.10.refs_1_, bf16[128,4096]{1,0:T(8,128)(2,1)} %collective-permute-done.9.refs_2_), custom_call_target="tpu_custom_call" | custom-call | flops 30000001024 | tf_op jit(solution)/shard_map/pallas_call | solution.py:76
  119.1 0.9 collective-permute-start.14
  120.0 0.9 collective-permute-start.15
  120.9 1.3 collective-permute-start.16
  122.3 0.0 collective-permute-done.1
  122.3 0.4 collective-permute-start.6
  122.7 0.0 collective-permute-done.5
  122.7 0.1 collective-permute-start.7
  122.8 5.9 %collective-permute-done.16 = bf16[32,4096]{1,0:T(8,128)(2,1)S(1)} collective-permute-done((bf16[32,4096]{1,0:T(8,128)(2,1)}, bf16[32,4096]{1,0:T(8,128)(2,1)S(1)}, u32[]{:S(2)}, u32[]{:S(2)}) %collective-permute-start.16) | collective-permute-done | bytes 262176 | tf_op jit(solution)/shard_map/ppermute | solution.py:54
  128.7 1.2 collective-permute-start.11
  129.9 0.7 collective-permute-done.14
  130.5 0.6 collective-permute-start.12
  131.1 0.0 collective-permute-done.15
  131.1 0.7 collective-permute-start.13
  131.8 0.1 slice_bitcast_fusion
  131.9 0.1 broadcast_in_dim.3
  132.0 0.1 le.15
  132.1 0.1 eq.18
  132.2 1.1 slice_bitcast_fusion.1.order
  133.3 0.8 and_convert_fusion.mask
  134.1 0.0 collective-permute-done.6
  134.1 0.0 collective-permute-start.17
  134.1 0.5 collective-permute-start.18
  134.7 0.0 collective-permute-done.11
  134.7 0.3 collective-permute-start.19
  134.9 0.0 collective-permute-done.12
  134.9 0.6 collective-permute-done.13
  135.5 15.7 %shard_map.46.early = bf16[112,16,384]{2,1,0:T(8,128)(2,1)} custom-call(bf16[8,3,512,128]{3,2,1,0:T(8,128)(2,1)} %bitcast.45, bf16[8,16,4096]{2,1,0:T(8,128)(2,1)} %bitcast.51, bf16[8,16,4096]{2,1,0:T(8,128)(2,1)} %bitcast.10.refs_1_, bf16[8,16,4096]{2,1,0:T(8,128)(2,1)} %bitcast.11.refs_2_, bf16[8,16,4096]{2,1,0:T(8,128)(2,1)} %bitcast.12.refs_3_, ...), custom_call_target="tpu_custom_call" | custom-call | flops 5637144576 | bytes 17825792 | tf_op jit(solution)/shard_map/pallas_call | solution.py:201
  151.3 0.0 collective-permute-done.19
  151.3 25.3 %shard_map.48 = bf16[8,3,512,128]{3,2,1,0:T(8,128)(2,1)} custom-call(s32[24]{0:T(128)} %slice_bitcast_fusion.1.order, f32[256,256]{1,0:T(8,128)} %and_convert_fusion.mask, bf16[8,3,512,128]{3,2,1,0:T(8,128)(2,1)} %bitcast.46, bf16[16,8,16,128]{3,2,1,0:T(8,128)(2,1)} %bitcast.7.g_ref, bf16[112,16,384]{2,1,0:T(8,128)(2,1)} %shard_map.46.early, ...), custom_call_target="tpu_custom_call" | custom-call | flops 6442450944 | bytes 16777216 | tf_op jit(solution)/shard_map/pallas_call | solution.py:309
  176.6 0.0 reduce-scatter.2.cloned.1.call-update
  176.7 42.7 %reduce-scatter.2.cloned.1.call-done = bf16[1536,128]{1,0:T(8,128)(2,1)} async-done(((bf16[12288,128]{1,0:T(8,128)(2,1)}), bf16[1536,128]{1,0:T(8,128)(2,1)}) %reduce-scatter.2.cloned.1.call-update) | async-done | bytes 393232 | tf_op jit(solution)/shard_map/reduce_scatter | solution.py:354
  219.3 1.0 dynamic-slice_bitcast_fusion.1
  220.4 9.0 %collective-permute-start.20 = (bf16[3,256,128]{2,1,0:T(8,128)(2,1)S(1)}, bf16[3,256,128]{2,1,0:T(8,128)(2,1)S(1)}, u32[]{:S(2)}, u32[]{:S(2)}) collective-permute-start(bf16[3,256,128]{2,1,0:T(8,128)(2,1)S(1)} %get-tuple-element.29), channel_id=1, source_target_pairs={{0,0},{1,128},{2,32},{3,160},{4,64},{5,192},{6,96},{7,224},{8,16},... | collective-permute-start | bytes 589832 | tf_op jit(solution)/shard_map/ppermute | solution.py:362
  229.4 0.1 collective-permute-start.21
  229.5 36.9 %collective-permute-done.20 = bf16[3,256,128]{2,1,0:T(8,128)(2,1)S(1)} collective-permute-done((bf16[3,256,128]{2,1,0:T(8,128)(2,1)S(1)}, bf16[3,256,128]{2,1,0:T(8,128)(2,1)S(1)}, u32[]{:S(2)}, u32[]{:S(2)}) %collective-permute-start.20) | collective-permute-done | bytes 196640 | tf_op jit(solution)/shard_map/ppermute | solution.py:362
  266.4 3.2 %collective-permute-done.21 = bf16[3,256,128]{2,1,0:T(8,128)(2,1)S(1)} collective-permute-done((bf16[3,256,128]{2,1,0:T(8,128)(2,1)S(1)}, bf16[3,256,128]{2,1,0:T(8,128)(2,1)S(1)}, u32[]{:S(2)}, u32[]{:S(2)}) %collective-permute-start.21) | collective-permute-done | bytes 196640 | tf_op jit(solution)/shard_map/ppermute | solution.py:362
  269.6 0.7 fusion
  (15 shorter events, 0.1 us)
Async XLA Ops:
  6.5 15.5 %copy-start = (bf16[4096,3,128]{2,0,1:T(8,128)(2,1)S(1)}, bf16[4096,3,128]{2,0,1:T(8,128)(2,1)}, u32[]{:S(2)}) copy-start(bf16[4096,3,128]{2,0,1:T(8,128)(2,1)} %param.6) | copy-start | bytes 9437188
  6.5 48.1 %collective-permute-start.2 = (bf16[128,4096]{1,0:T(8,128)(2,1)}, bf16[128,4096]{1,0:T(8,128)(2,1)}, u32[]{:S(2)}, u32[]{:S(2)}) collective-permute-start(bf16[128,4096]{1,0:T(8,128)(2,1)} %bitcast.47), channel_id=1, source_target_pairs={{0,32},{32,64},{64,96},{96,0},{1,33},{33,65},{65,97},{97,1},{2,34}... | collective-permute-start | bytes 3145736 | tf_op jit(solution)/shard_map/ppermute | solution.py:54
  7.7 46.9 %collective-permute-start.3 = (bf16[128,4096]{1,0:T(8,128)(2,1)}, bf16[128,4096]{1,0:T(8,128)(2,1)}, u32[]{:S(2)}, u32[]{:S(2)}) collective-permute-start(bf16[128,4096]{1,0:T(8,128)(2,1)} %bitcast.48), channel_id=1, source_target_pairs={{0,96},{32,0},{64,32},{96,64},{1,97},{33,1},{65,33},{97,65},{2,98}... | collective-permute-start | bytes 3145736 | tf_op jit(solution)/shard_map/ppermute | solution.py:54
  8.0 46.7 %collective-permute-start.4 = (bf16[128,4096]{1,0:T(8,128)(2,1)}, bf16[128,4096]{1,0:T(8,128)(2,1)}, u32[]{:S(2)}, u32[]{:S(2)}) collective-permute-start(bf16[128,4096]{1,0:T(8,128)(2,1)} %bitcast.49), channel_id=1, source_target_pairs={{0,128},{128,0},{1,129},{129,1},{2,130},{130,2},{3,131},{131,3},{4... | collective-permute-start | bytes 3145736 | tf_op jit(solution)/shard_map/ppermute | solution.py:54
  9.3 45.4 %all-to-all-start = ((bf16[16,128,128]{2,1,0:T(8,128)(2,1)}), bf16[16,128,128]{2,1,0:T(8,128)(2,1)}, u32[]{:S(2)}, u32[]{:S(2)}) async-start(bf16[16,128,128]{2,1,0:T(8,128)(2,1)} %bitcast.53), calls=%async_computation | async-start | bytes 1048576 | tf_op jit(solution)/shard_map/all_to_all | solution.py:342
  20.0 115.5 %all-gather.2.cloned.1.call-start = ((), (), s32[]{:S(2)}) async-start(), calls=%async_computation.3 | async-start | bytes 3538944 | tf_op jit(solution)/shard_map/all_gather | solution.py:341
  20.7 111.1 %copy-start.4 = (s32[1,48]{1,0:T(1,128)}, s32[1,48]{1,0:T(1,128)S(1)}, u32[]{:S(2)}) copy-start(s32[1,48]{1,0:T(1,128)S(1)} %constant_dynamic-slice_fusion.1) | copy-start | bytes 580
  22.1 31.8 %collective-permute-start = (bf16[1536,128]{1,0:T(8,128)(2,1)S(1)}, bf16[1536,128]{1,0:T(8,128)(2,1)S(1)}, u32[]{:S(2)}, u32[]{:S(2)}) collective-permute-start(bf16[1536,128]{1,0:T(8,128)(2,1)S(1)} %bitcast.55), channel_id=1, source_target_pairs={{0,0},{128,1},{32,2},{160,3},{64,4},{192,5},{96,6},{224,7},{16,8},... | collective-permute-start | bytes 1179656 | tf_op jit(solution)/shard_map/ppermute | solution.py:340
  53.9 0.7 copy-start.1
  54.7 31.5 %collective-permute-start.10 = (bf16[128,4096]{1,0:T(8,128)(2,1)}, bf16[128,4096]{1,0:T(8,128)(2,1)}, u32[]{:S(2)}, u32[]{:S(2)}) collective-permute-start(bf16[128,4096]{1,0:T(8,128)(2,1)} %collective-permute-done.3), channel_id=1, source_target_pairs={{0,128},{128,0},{1,129},{129,1},{2,130},{130,2},{3,131},{131,3},{4... | collective-permute-start | bytes 3145736 | tf_op jit(solution)/shard_map/ppermute | solution.py:54
  54.8 31.4 %collective-permute-start.8 = (bf16[128,4096]{1,0:T(8,128)(2,1)}, bf16[128,4096]{1,0:T(8,128)(2,1)}, u32[]{:S(2)}, u32[]{:S(2)}) collective-permute-start(bf16[128,4096]{1,0:T(8,128)(2,1)} %collective-permute-done.4), channel_id=1, source_target_pairs={{0,32},{32,64},{64,96},{96,0},{1,33},{33,65},{65,97},{97,1},{2,34}... | collective-permute-start | bytes 3145736 | tf_op jit(solution)/shard_map/ppermute | solution.py:54
  54.9 31.3 %collective-permute-start.9 = (bf16[128,4096]{1,0:T(8,128)(2,1)}, bf16[128,4096]{1,0:T(8,128)(2,1)}, u32[]{:S(2)}, u32[]{:S(2)}) collective-permute-start(bf16[128,4096]{1,0:T(8,128)(2,1)} %collective-permute-done.3), channel_id=1, source_target_pairs={{0,96},{32,0},{64,32},{96,64},{1,97},{33,1},{65,33},{97,65},{2,98}... | collective-permute-start | bytes 3145736 | tf_op jit(solution)/shard_map/ppermute | solution.py:54
  56.4 29.8 %all-to-all-start.1 = ((bf16[16,128,128]{2,1,0:T(8,128)(2,1)}), bf16[16,128,128]{2,1,0:T(8,128)(2,1)}, u32[]{:S(2)}, u32[]{:S(2)}) async-start(bf16[16,128,128]{2,1,0:T(8,128)(2,1)} %all-to-all-done), calls=%async_computation.1 | async-start | bytes 1048576 | tf_op jit(solution)/shard_map/all_to_all | solution.py:342
  60.9 158.4 %reduce-scatter.2.cloned.1.call-start = ((), (), s32[]{:S(2)}) async-start(), calls=%async_computation.4 | async-start | bytes 3538944 | tf_op jit(solution)/shard_map/reduce_scatter | solution.py:354
  60.9 61.3 %collective-permute-start.1 = (bf16[128,4096]{1,0:T(8,128)(2,1)}, bf16[128,4096]{1,0:T(8,128)(2,1)}, u32[]{:S(2)}, u32[]{:S(2)}) collective-permute-start(bf16[128,4096]{1,0:T(8,128)(2,1)} %bitcast.50), channel_id=1, source_target_pairs={{0,16},{16,0},{1,17},{17,1},{2,18},{18,2},{3,19},{19,3},{4,20},{20... | collective-permute-start | bytes 3145736 | tf_op jit(solution)/shard_map/ppermute | solution.py:54
  61.4 61.4 %collective-permute-start.5 = (bf16[128,4096]{1,0:T(8,128)(2,1)}, bf16[128,4096]{1,0:T(8,128)(2,1)}, u32[]{:S(2)}, u32[]{:S(2)}) collective-permute-start(bf16[128,4096]{1,0:T(8,128)(2,1)} %collective-permute-done.2), channel_id=1, source_target_pairs={{0,16},{16,0},{1,17},{17,1},{2,18},{18,2},{3,19},{19,3},{4,20},{20... | collective-permute-start | bytes 3145736 | tf_op jit(solution)/shard_map/ppermute | solution.py:54
  119.1 11.4 %collective-permute-start.14 = (bf16[48,4096]{1,0:T(8,128)(2,1)}, bf16[48,4096]{1,0:T(8,128)(2,1)S(1)}, u32[]{:S(2)}, u32[]{:S(2)}) collective-permute-start(bf16[48,4096]{1,0:T(8,128)(2,1)} %get-tuple-element.23), channel_id=1, source_target_pairs={{0,32},{32,64},{64,96},{96,0},{1,33},{33,65},{65,97},{97,1},{2,34}... | collective-permute-start | bytes 1179656 | tf_op jit(solution)/shard_map/ppermute | solution.py:54
  120.0 11.1 %collective-permute-start.15 = (bf16[48,4096]{1,0:T(8,128)(2,1)}, bf16[48,4096]{1,0:T(8,128)(2,1)}, u32[]{:S(2)}, u32[]{:S(2)}) collective-permute-start(bf16[48,4096]{1,0:T(8,128)(2,1)} %get-tuple-element.24), channel_id=1, source_target_pairs={{0,96},{32,0},{64,32},{96,64},{1,97},{33,1},{65,33},{97,65},{2,98}... | collective-permute-start | bytes 1179656 | tf_op jit(solution)/shard_map/ppermute | solution.py:54
  120.9 7.8 %collective-permute-start.16 = (bf16[32,4096]{1,0:T(8,128)(2,1)}, bf16[32,4096]{1,0:T(8,128)(2,1)S(1)}, u32[]{:S(2)}, u32[]{:S(2)}) collective-permute-start(bf16[32,4096]{1,0:T(8,128)(2,1)} %get-tuple-element.25), channel_id=1, source_target_pairs={{0,128},{128,0},{1,129},{129,1},{2,130},{130,2},{3,131},{131,3},{4... | collective-permute-start | bytes 786440 | tf_op jit(solution)/shard_map/ppermute | solution.py:54
  122.3 11.9 %collective-permute-start.6 = (bf16[128,4096]{1,0:T(8,128)(2,1)}, bf16[128,4096]{1,0:T(8,128)(2,1)}, u32[]{:S(2)}, u32[]{:S(2)}) collective-permute-start(bf16[128,4096]{1,0:T(8,128)(2,1)} %collective-permute-done.3), channel_id=1, source_target_pairs={{0,16},{16,0},{1,17},{17,1},{2,18},{18,2},{3,19},{19,3},{4,20},{20... | collective-permute-start | bytes 3145736 | tf_op jit(solution)/shard_map/ppermute | solution.py:54
  122.7 11.4 %collective-permute-start.7 = (bf16[128,4096]{1,0:T(8,128)(2,1)}, bf16[128,4096]{1,0:T(8,128)(2,1)}, u32[]{:S(2)}, u32[]{:S(2)}) collective-permute-start(bf16[128,4096]{1,0:T(8,128)(2,1)} %collective-permute-done.4), channel_id=1, source_target_pairs={{0,16},{16,0},{1,17},{17,1},{2,18},{18,2},{3,19},{19,3},{4,20},{20... | collective-permute-start | bytes 3145736 | tf_op jit(solution)/shard_map/ppermute | solution.py:54
  128.7 1.8 copy-start.3
  128.7 5.9 %collective-permute-start.11 = (bf16[128,4096]{1,0:T(8,128)(2,1)}, bf16[128,4096]{1,0:T(8,128)(2,1)}, u32[]{:S(2)}, u32[]{:S(2)}) collective-permute-start(bf16[128,4096]{1,0:T(8,128)(2,1)} %collective-permute-done.8.refs_0_), channel_id=1, source_target_pairs={{0,16},{16,0},{1,17},{17,1},{2,18},{18,2},{3,19},{19,3},{4,20},{20... | collective-permute-start | bytes 3145736 | tf_op jit(solution)/shard_map/ppermute | solution.py:54
  130.5 20.7 %copy-start.2 = (bf16[48,4096]{1,0:T(8,128)(2,1)}, bf16[48,4096]{1,0:T(8,128)(2,1)S(1)}, u32[]{:S(2)}) copy-start(bf16[48,4096]{1,0:T(8,128)(2,1)S(1)} %collective-permute-done.14) | copy-start | bytes 1179652
  130.5 4.4 %collective-permute-start.12 = (bf16[128,4096]{1,0:T(8,128)(2,1)}, bf16[128,4096]{1,0:T(8,128)(2,1)}, u32[]{:S(2)}, u32[]{:S(2)}) collective-permute-start(bf16[128,4096]{1,0:T(8,128)(2,1)} %collective-permute-done.9.refs_2_), channel_id=1, source_target_pairs={{0,16},{16,0},{1,17},{17,1},{2,18},{18,2},{3,19},{19,3},{4,20},{20... | collective-permute-start | bytes 3145736 | tf_op jit(solution)/shard_map/ppermute | solution.py:54
  131.1 4.4 %collective-permute-start.13 = (bf16[128,4096]{1,0:T(8,128)(2,1)}, bf16[128,4096]{1,0:T(8,128)(2,1)}, u32[]{:S(2)}, u32[]{:S(2)}) collective-permute-start(bf16[128,4096]{1,0:T(8,128)(2,1)} %collective-permute-done.10.refs_1_), channel_id=1, source_target_pairs={{0,16},{16,0},{1,17},{17,1},{2,18},{18,2},{3,19},{19,3},{4,20},{20... | collective-permute-start | bytes 3145736 | tf_op jit(solution)/shard_map/ppermute | solution.py:54
  134.1 17.1 %collective-permute-start.17 = (bf16[48,4096]{1,0:T(8,128)(2,1)S(1)}, bf16[48,4096]{1,0:T(8,128)(2,1)}, u32[]{:S(2)}, u32[]{:S(2)}) collective-permute-start(bf16[48,4096]{1,0:T(8,128)(2,1)S(1)} %collective-permute-done.14), channel_id=1, source_target_pairs={{0,16},{16,0},{1,17},{17,1},{2,18},{18,2},{3,19},{19,3},{4,20},{20... | collective-permute-start | bytes 1179656 | tf_op jit(solution)/shard_map/ppermute | solution.py:54
  134.1 17.1 %collective-permute-start.18 = (bf16[48,4096]{1,0:T(8,128)(2,1)}, bf16[48,4096]{1,0:T(8,128)(2,1)}, u32[]{:S(2)}, u32[]{:S(2)}) collective-permute-start(bf16[48,4096]{1,0:T(8,128)(2,1)} %collective-permute-done.15), channel_id=1, source_target_pairs={{0,16},{16,0},{1,17},{17,1},{2,18},{18,2},{3,19},{19,3},{4,20},{20... | collective-permute-start | bytes 1179656 | tf_op jit(solution)/shard_map/ppermute | solution.py:54
  134.7 16.6 %collective-permute-start.19 = (bf16[32,4096]{1,0:T(8,128)(2,1)}, bf16[32,4096]{1,0:T(8,128)(2,1)}, u32[]{:S(2)}, u32[]{:S(2)}) collective-permute-start(bf16[32,4096]{1,0:T(8,128)(2,1)} %copy-done.3), channel_id=1, source_target_pairs={{0,16},{16,0},{1,17},{17,1},{2,18},{18,2},{3,19},{19,3},{4,20},{20... | collective-permute-start | bytes 786440 | tf_op jit(solution)/shard_map/ppermute | solution.py:54
  220.4 46.1 %collective-permute-start.20 = (bf16[3,256,128]{2,1,0:T(8,128)(2,1)S(1)}, bf16[3,256,128]{2,1,0:T(8,128)(2,1)S(1)}, u32[]{:S(2)}, u32[]{:S(2)}) collective-permute-start(bf16[3,256,128]{2,1,0:T(8,128)(2,1)S(1)} %get-tuple-element.29), channel_id=1, source_target_pairs={{0,0},{1,128},{2,32},{3,160},{4,64},{5,192},{6,96},{7,224},{8,16},... | collective-permute-start | bytes 589832 | tf_op jit(solution)/shard_map/ppermute | solution.py:362
  229.4 40.2 %collective-permute-start.21 = (bf16[3,256,128]{2,1,0:T(8,128)(2,1)S(1)}, bf16[3,256,128]{2,1,0:T(8,128)(2,1)S(1)}, u32[]{:S(2)}, u32[]{:S(2)}) collective-permute-start(bf16[3,256,128]{2,1,0:T(8,128)(2,1)S(1)} %get-tuple-element.30), channel_id=1, source_target_pairs={{0,16},{1,144},{2,48},{3,176},{4,80},{5,208},{6,112},{7,240},{8,0}... | collective-permute-start | bytes 589832 | tf_op jit(solution)/shard_map/ppermute | solution.py:362
Sparse Core Ops, SparseCore 0:
  54.8 41.8 all-gather.1
  176.8 42.5 reduce-scatter.1

commit v4 on v3

--- a/solution.py
+++ b/solution.py
@@ -18,6 +18,7 @@
 PATCHES = 128
 CUT_A, CUT_B = 48, 96
 CUTS = ((0, CUT_A), (CUT_A, CUT_B), (CUT_B, PATCHES))
+STEP = 4
 CUT_FLOPS = 3 * 10**10
 WIDTH = 4096
 COLS = 3 * HEAD_DIM
@@ -36,16 +37,27 @@
     return place
 
 
-def owner_moves(flip):
+def worker_moves():
     pairs = []
-    for yl in range(2):
-        for x in range(4):
-            for core in range(2):
-                for yh in range(2):
-                    for z in range(8):
-                        source = device(yl, x, core, yh, z)
-                        target = device(yl ^ (z % 2), x + z // 2, yh ^ flip, core, 2 * x + yl)
-                        pairs.append((source, target))
+    for yl, x, core, yh, z in np.ndindex(*SIZES):
+        owner = device(yl ^ (z % 2), x + z // 2, yh, core, 2 * x + yl)
+        pairs.append((owner, device(yl, x, core, yh, z)))
+    return pairs
+
+
+def plane_moves(flip):
+    pairs = []
+    for yl, x, core, yh, z in np.ndindex(*SIZES):
+        target = device(yl ^ (z % 2), x + z // 2, yh ^ flip, core, z)
+        pairs.append((device(yl, x, core, yh, z), target))
+    return pairs
+
+
+def line_moves():
+    pairs = []
+    for yl, x, core, yh, z in np.ndindex(*SIZES):
+        target = device(yl, x, core, yh, 2 * ((x - z // 2) % 4) + (yl ^ (z % 2)))
+        pairs.append((device(yl, x, core, yh, z), target))
     return pairs
 
 
@@ -79,7 +91,7 @@
             jax.ShapeDtypeStruct((last - first, WIDTH), jnp.bfloat16) for first, last in CUTS
         ],
         in_specs=[hbm] * 3,
-        out_specs=[hbm] * 3,
+        out_specs=[pl.BlockSpec(memory_space=pltpu.VMEM)] * 3,
         scratch_shapes=[pltpu.SemaphoreType.DMA((3,))],
         cost_estimate=pl.CostEstimate(flops=CUT_FLOPS, bytes_accessed=0, transcendentals=0),
     )(*buffers)
@@ -148,74 +160,25 @@
 HBM = pl.BlockSpec(memory_space=pltpu.HBM)
 
 
-def load_weights(w_ref, w, sem):
+def take_kernel(start, w_ref, out, sem):
     copies = []
-    for chunk in range(8):
-        for j in range(3):
-            copies.append(
-                pltpu.make_async_copy(
-                    w_ref.at[chunk, j],
-                    w.at[pl.ds(chunk * CHUNK, CHUNK), pl.ds(j * HEAD_DIM, HEAD_DIM)],
-                    sem.at[chunk * 3 + j],
-                )
-            )
+    for j in range(3):
+        rows = pl.ds(pl.multiple_of(start[0] * CHUNK, CHUNK), CHUNK)
+        columns = pl.ds(j * HEAD_DIM, HEAD_DIM)
+        copies.append(pltpu.make_async_copy(w_ref.at[j, rows], out.at[:, columns], sem.at[j]))
+        copies[-1].start()
     for copy in copies:
-        copy.start()
-    return copies
-
-
-def project_rows(rows, w):
-    return jnp.dot(rows, w[...], preferred_element_type=jnp.float32).astype(jnp.bfloat16)
-
-
-def project_kernel(count, w_ref, *refs):
-    buffers, out = refs[:count], refs[count]
-    tokens, result, w, w_sem, sems, o_sem = refs[count + 1 :]
-    copies, at = [], 0
-    loads = load_weights(w_ref, w, w_sem)
-    for index, ref in enumerate(buffers):
-        rows = ref.shape[0]
-        copies.append(pltpu.make_async_copy(ref, tokens.at[pl.ds(at, rows)], sems.at[index]))
-        copies[-1].start()
-        at += rows
-    for copy in loads:
         copy.wait()
-    stores = []
-    for index in range(0, count, 2):
-        copies[index].wait()
-        copies[index + 1].wait()
-        groups = pl.ds(index * (PATCHES // GROUP), 2 * (PATCHES // GROUP))
-        rows = project_rows(tokens[groups].reshape(2 * PATCHES, WIDTH), w)
-        result[groups] = rows.reshape(-1, GROUP, COLS)
-        stores.append(
-            pltpu.make_async_copy(result.at[groups], out.at[groups], o_sem.at[index // 2])
-        )
-        stores[-1].start()
-    for store in stores:
-        store.wait()
-
-
-def project(w, buffers):
-    groups = sum(buffer.shape[0] for buffer in buffers)
-    rows = groups * GROUP
+
+
+def take_rows(start, w):
     return pl.pallas_call(
-        functools.partial(project_kernel, len(buffers)),
-        out_shape=jax.ShapeDtypeStruct((groups, GROUP, COLS), jnp.bfloat16),
-        in_specs=[HBM] * (1 + len(buffers)),
-        out_specs=HBM,
-        scratch_shapes=[
-            pltpu.VMEM((groups, GROUP, WIDTH), jnp.bfloat16),
-            pltpu.VMEM((groups, GROUP, COLS), jnp.bfloat16),
-            pltpu.VMEM((WIDTH, COLS), jnp.bfloat16),
-            pltpu.SemaphoreType.DMA((24,)),
-            pltpu.SemaphoreType.DMA((len(buffers),)),
-            pltpu.SemaphoreType.DMA((len(buffers) // 2,)),
-        ],
-        compiler_params=pltpu.CompilerParams(vmem_limit_bytes=58 * 2**20),
-        cost_estimate=pl.CostEstimate(
-            flops=2 * rows * WIDTH * COLS, bytes_accessed=2 * (rows + COLS) * WIDTH, transcendentals=0
-        ),
-    )(w, *buffers)
+        take_kernel,
+        out_shape=jax.ShapeDtypeStruct((CHUNK, COLS), jnp.bfloat16),
+        in_specs=[SMEM, HBM],
+        out_specs=VMEM,
+        scratch_shapes=[pltpu.SemaphoreType.DMA((3,))],
+    )(start, w)
 
 
 def attend(proj, grads, mask, turned):
@@ -248,45 +211,45 @@
     lax.fori_loop(0, PATCHES // GROUP, body, 0)
 
 
-def share_kernel(count, order, mask, w_ref, g_ref, early, *refs):
+def share_kernel(count, order, mask, w_ref, g_ref, *refs):
     buffers, out = refs[:count], refs[count]
-    tokens, proj, grads, turned, w, shares, w_sem, x_sem, g_sem, p_sem, o_sem = refs[count + 1 :]
-    token_copies = []
+    tokens, proj, grads, turned, w, shares, w_sem, x_sem, g_sem, o_sem = refs[count + 1 :]
+    arrivals = [[] for _ in range(FRAMES)]
     for index, (buffer, at, slot, first, groups) in enumerate(parts_of(FIRST + SECOND + THIRD)):
-        token_copies.append(
+        arrivals[slot].append(
             pltpu.make_async_copy(
                 buffers[buffer].at[pl.ds(at, groups)],
                 tokens.at[pl.ds(first, groups), slot],
                 x_sem.at[index],
             )
         )
-    last = token_copies[-len(THIRD) :]
-    for copy in last:
+    cotangents = []
+    for slot in range(FRAMES):
+        cotangents.append(
+            pltpu.make_async_copy(g_ref.at[order[slot]], grads.at[:, slot], g_sem.at[slot])
+        )
+    weights = pltpu.make_async_copy(w_ref, w, w_sem.at[0])
+
+    def step_copies(step):
+        return [copy for slot in range(STEP * step, STEP * step + STEP) for copy in arrivals[slot]]
+
+    weights.start()
+    for copy in step_copies(0):
         copy.start()
-    loads = load_weights(w_ref, w, w_sem)
-    small = []
-    for slot in range(FRAMES):
-        small.append(pltpu.make_async_copy(g_ref.at[order[slot]], grads.at[:, slot], g_sem.at[slot]))
-    at = 0
-    for index, (_, _, slot, first, groups) in enumerate(parts_of(FIRST + SECOND)):
-        small.append(
-            pltpu.make_async_copy(
-                early.at[pl.ds(at, groups)], proj.at[pl.ds(first, groups), slot], p_sem.at[index]
-            )
-        )
-        at += groups
-    for copy in small + token_copies[: -len(THIRD)]:
-        copy.start()
-    for copy in last + loads:
-        copy.wait()
-    for slot in (14, 15):
-        rows = project_rows(tokens[:, slot].reshape(PATCHES, WIDTH), w)
-        proj[:, slot] = rows.reshape(PATCHES // GROUP, GROUP, COLS)
-    for copy in small:
+    weights.wait()
+    steps = FRAMES // STEP
+    for step in range(steps):
+        for copy in step_copies(step):
+            copy.wait()
+        for copy in step_copies(step + 1) if step + 1 < steps else cotangents:
+            copy.start()
+        slots = slice(STEP * step, STEP * step + STEP)
+        rows = tokens[:, slots].reshape(STEP * PATCHES, WIDTH)
+        result = jnp.dot(rows, w[...], preferred_element_type=jnp.float32)
+        proj[:, slots] = result.astype(jnp.bfloat16).reshape(-1, STEP, GROUP, COLS)
+    for copy in cotangents:
         copy.wait()
     attend(proj, grads, mask, turned)
-    for copy in token_copies[: -len(THIRD)]:
-        copy.wait()
 
     def weigh(step, carry):
         columns = pl.ds(pl.multiple_of(order[16 + step] * CHUNK, CHUNK), CHUNK)
@@ -302,14 +265,13 @@
         pltpu.make_async_copy(shares.at[step], out.at[step], o_sem.at[step]).wait()
 
 
-def weight_share(order, mask, w, g, early, buffers):
+def weight_share(order, mask, w, g, buffers):
     count = len(buffers)
     groups = PATCHES // GROUP
-    token_parts = len(parts_of(FIRST + SECOND + THIRD))
     return pl.pallas_call(
         functools.partial(share_kernel, count),
         out_shape=jax.ShapeDtypeStruct((8, 3, CHUNK, HEAD_DIM), jnp.bfloat16),
-        in_specs=[SMEM, VMEM] + [HBM] * (3 + count),
+        in_specs=[SMEM, VMEM] + [HBM] * (2 + count),
         out_specs=HBM,
         scratch_shapes=[
             pltpu.VMEM((groups, FRAMES, GROUP, WIDTH), jnp.bfloat16),
@@ -318,39 +280,34 @@
             pltpu.VMEM((COLS, ROWS), jnp.bfloat16),
             pltpu.VMEM((WIDTH, COLS), jnp.bfloat16),
             pltpu.VMEM((8, 3, CHUNK, HEAD_DIM), jnp.bfloat16),
-            pltpu.SemaphoreType.DMA((24,)),
-            pltpu.SemaphoreType.DMA((token_parts,)),
+            pltpu.SemaphoreType.DMA((1,)),
+            pltpu.SemaphoreType.DMA((len(parts_of(FIRST + SECOND + THIRD)),)),
             pltpu.SemaphoreType.DMA((FRAMES,)),
-            pltpu.SemaphoreType.DMA((len(FIRST + SECOND),)),
             pltpu.SemaphoreType.DMA((8,)),
         ],
         compiler_params=pltpu.CompilerParams(vmem_limit_bytes=58 * 2**20),
         cost_estimate=pl.CostEstimate(
-            flops=2 * ROWS * WIDTH * COLS, bytes_accessed=2 * ROWS * WIDTH, transcendentals=0
+            flops=4 * ROWS * WIDTH * COLS, bytes_accessed=2 * ROWS * WIDTH, transcendentals=0
         ),
-    )(order, mask, w, g, early, *buffers)
+    )(order, mask, w, g, *buffers)
 
 
 def local(inputs, grad_attn, w_qkv):
     table = jnp.asarray(tables())[lax.axis_index(AXES)]
-    to_worker = [(target, source) for source, target in owner_moves(0)]
-    rows_w = lax.dynamic_slice(
-        w_qkv.transpose(1, 0, 2), (0, table[40] * CHUNK, 0), (3, CHUNK, HEAD_DIM)
-    )
-    rows_w = lax.ppermute(rows_w.reshape(3 * CHUNK, HEAD_DIM), AXES, to_worker)
-    w = lax.all_gather(rows_w, "z", axis=0, tiled=True).reshape(8, 3, CHUNK, HEAD_DIM)
+    rows_w = take_rows(table[40:41], w_qkv.transpose(1, 0, 2))
+    rows_w = lax.ppermute(rows_w, AXES, worker_moves())
+    w = lax.all_gather(rows_w, "z", axis=0, tiled=True)
     exchange = lambda value, axes: lax.all_to_all(
         value, axes, split_axis=0, concat_axis=0, tiled=True
     )
-    heads_g = exchange(grad_attn[0].reshape(FRAMES, PATCHES, HEAD_DIM), TOK)
+    heads_g = exchange(after(grad_attn[0], rows_w).reshape(FRAMES, PATCHES, HEAD_DIM), TOK)
     frames_g = exchange(heads_g, ("core", "x", "yl"))
-    steps = gather_frames(inputs[0], (rows_w, heads_g), (frames_g,))
+    steps = gather_frames(inputs[0], (rows_w,), (heads_g,))
     g = frames_g.reshape(FRAMES, PATCHES // GROUP, GROUP, HEAD_DIM)
     first, second, third = (
         [buffer.reshape(-1, GROUP, WIDTH) for buffer in buffers] for buffers in steps
     )
-    early = project(w, first + second)
-    share = weight_share(table[:24], visible(table[24:40]), w, g, early, first + second + third)
+    share = weight_share(table[:24], visible(table[24:40]), w, g, first + second + third)
     mine = lax.psum_scatter(
         share.reshape(8 * 3 * CHUNK, HEAD_DIM), "z", scatter_dimension=0, tiled=True
     )
@@ -359,9 +316,9 @@
     total = None
     for flip in range(2):
         part = lax.dynamic_index_in_dim(mine, (yh + flip) % 2, 1, keepdims=False)
-        part = lax.ppermute(part, AXES, owner_moves(flip)).astype(jnp.float32)
+        part = lax.ppermute(part, AXES, plane_moves(flip)).astype(jnp.float32)
         total = part if total is None else total + part
-    return total.astype(jnp.bfloat16).transpose(1, 0, 2)
+    return lax.ppermute(total.astype(jnp.bfloat16), AXES, line_moves()).transpose(1, 0, 2)
 
 
 def solution(mesh):

time: 278 us -> 219 us (0.79)
  Pallas kernels: 74 us -> 34.2 us
  waiting for transfers between devices: 137 us -> 99.4 us
  starting transfers between devices: 46 us -> 64.2 us
    ppermute x3 -> x4, waiting for transfers between devices: 62.2 us -> 29.6 us  [the longest x1 15.5 us: local(): rows_w = lax.ppermute(rows_w, AXES, worker_moves())]
    pallas_call x1, Pallas kernels: 32.9 us -> 2.24 us  [cut(): pl.pallas_call(cut_kernel, out_shape=[jax.ShapeDtypeStruct((last - first,...]
    all_to_all x2, waiting for transfers between devices: 24.6 us -> 11 us  [local(): lax.all_to_all(value, axes, split_axis=0, concat_axis=0, tiled=True)]
    pallas_call x1, Pallas kernels: 15.7 us -> 2.45 us  [take_rows(): pl.pallas_call(take_kernel, out_shape=jax.ShapeDtypeStruct((CHUNK, COLS),...]
    ppermute x19, starting transfers between devices: 12 us -> 22.9 us  [shift(): lax.ppermute(value, axis, [(i, (i + by) % count) for i in range(count)])]
    ppermute x19, waiting for transfers between devices: 7.17 us -> 15.1 us  [shift(): lax.ppermute(value, axis, [(i, (i + by) % count) for i in range(count)])]
    ppermute x3 -> x4, starting transfers between devices: 18.8 us -> 24.5 us  [the longest x1 9.82 us: local(): rows_w = lax.ppermute(rows_w, AXES, worker_moves())]
    pallas_call x1, Pallas kernels: 25.3 us -> 29.6 us  [weight_share(): pl.pallas_call(functools.partial(share_kernel, count), out_shape=jax.Shap...]
  transfers between devices with their start and end apart: 26 -> 27, of which waited for: 8 -> 9; matrix products, arithmetic and copies ran while one was open for 1% -> 1% of each run, Pallas kernels for 18% -> 2%
where the time goes in v4:
time: 219 us; the launch traced here: 218 us
  waiting for transfers between devices  99.4 us (45%)
  starting transfers between devices  64.2 us (29%)
  Pallas kernels  34.2 us (16%)
  between operations  13.6 us (6%)
  local copies, waits for them, and re-layouts  5.93 us (3%)
    reduce_scatter x1, waiting for transfers between devices, local(): lax.psum_scatter(share.reshape(8 * 3 * CHUNK, HEAD_DIM), 'z', scatter_dim...  43.6 us
    pallas_call x1, Pallas kernels, weight_share(): pl.pallas_call(functools.partial(share_kernel, count), out_shape=jax.Shap...  29.6 us
    ppermute x19, starting transfers between devices, shift(): lax.ppermute(value, axis, [(i, (i + by) % count) for i in range(count)])  22.9 us
    all_to_all x2, starting transfers between devices, local(): lax.all_to_all(value, axes, split_axis=0, concat_axis=0, tiled=True)  16.9 us
    ppermute x1, waiting for transfers between devices, local(): rows_w = lax.ppermute(rows_w, AXES, worker_moves())  15.5 us
    ppermute x19, waiting for transfers between devices, shift(): lax.ppermute(value, axis, [(i, (i + by) % count) for i in range(count)])  15.1 us
    all_to_all x2, waiting for transfers between devices, local(): lax.all_to_all(value, axes, split_axis=0, concat_axis=0, tiled=True)  11 us
    ppermute x1, starting transfers between devices, local(): rows_w = lax.ppermute(rows_w, AXES, worker_moves())  9.82 us
  transfers between devices with their start and end apart: 27, of which 9 were waited for; matrix products, arithmetic and copies ran while one was open for 1% of the time, Pallas kernels for 2%

profile of v4, /device:TPU:3, one launch (start us, length us, event | category | flops | bytes accessed | tf_op | source)
XLA Modules:
  0.0 218.3 jit_solution(13223094367917671697)
XLA Ops:
  6.5 1.2 collective-permute-start.2
  7.8 0.3 collective-permute-start.3
  8.0 1.3 collective-permute-start.4
  9.3 0.7 constant_dynamic-slice_fusion
  10.0 0.6 slice.22
  10.6 2.4 %shard_map.46 = bf16[512,384]{1,0:T(8,128)(2,1)} custom-call(s32[1]{0:T(128)} %bitcast.2.start, bf16[3,4096,128]{2,1,0:T(8,128)(2,1)} %bitcast.42), custom_call_target="tpu_custom_call" | custom-call | tf_op jit(solution)/shard_map/pallas_call | solution.py:175
  13.0 9.8 %collective-permute-start = (bf16[512,384]{1,0:T(8,128)(2,1)}, bf16[512,384]{1,0:T(8,128)(2,1)S(1)}, u32[]{:S(2)}, u32[]{:S(2)}) collective-permute-start(bf16[512,384]{1,0:T(8,128)(2,1)} %shard_map.46), channel_id=1, source_target_pairs={{0,0},{128,1},{32,2},{160,3},{64,4},{192,5},{96,6},{224,7},{16,8},... | collective-permute-start | bytes 1179656 | tf_op jit(solution)/shard_map/ppermute | solution.py:298
  22.9 15.5 %collective-permute-done = bf16[512,384]{1,0:T(8,128)(2,1)S(1)} collective-permute-done((bf16[512,384]{1,0:T(8,128)(2,1)}, bf16[512,384]{1,0:T(8,128)(2,1)S(1)}, u32[]{:S(2)}, u32[]{:S(2)}) %collective-permute-start) | collective-permute-done | bytes 393248 | tf_op jit(solution)/shard_map/ppermute | solution.py:298
  38.4 0.7 copy-done.1
  39.1 0.0 all-gather.2.cloned.1.call-update
  39.2 0.0 collective-permute-done.3
  39.2 0.0 collective-permute-done.4
  39.2 0.1 collective-permute-start.10
  39.3 2.9 %collective-permute-start.9 = (bf16[128,4096]{1,0:T(8,128)(2,1)}, bf16[128,4096]{1,0:T(8,128)(2,1)}, u32[]{:S(2)}, u32[]{:S(2)}) collective-permute-start(bf16[128,4096]{1,0:T(8,128)(2,1)} %collective-permute-done.3), channel_id=1, source_target_pairs={{0,96},{32,0},{64,32},{96,64},{1,97},{33,1},{65,33},{97,65},{2,98}... | collective-permute-start | bytes 3145736 | tf_op jit(solution)/shard_map/ppermute | solution.py:66
  42.2 0.0 collective-permute-start.8
  42.2 11.4 %all-to-all-start = ((bf16[16,128,128]{2,1,0:T(8,128)(2,1)}), bf16[16,128,128]{2,1,0:T(8,128)(2,1)}, u32[]{:S(2)}, u32[]{:S(2)}) async-start(bf16[16,128,128]{2,1,0:T(8,128)(2,1)} %bitcast.5), calls=%async_computation | async-start | bytes 1048576 | tf_op jit(solution)/shard_map/all_to_all | solution.py:300
  53.7 3.1 %collective-permute-start.1 = (bf16[128,4096]{1,0:T(8,128)(2,1)S(1)}, bf16[128,4096]{1,0:T(8,128)(2,1)}, u32[]{:S(2)}, u32[]{:S(2)}) collective-permute-start(bf16[128,4096]{1,0:T(8,128)(2,1)S(1)} %bitcast.50), channel_id=1, source_target_pairs={{0,16},{16,0},{1,17},{17,1},{2,18},{18,2},{3,19},{19,3},{4,20},{20... | collective-permute-start | bytes 3145736 | tf_op jit(solution)/shard_map/ppermute | solution.py:66
  56.7 0.1 collective-permute-start.6
  56.8 10.6 %collective-permute-done.10.refs_1_ = bf16[128,4096]{1,0:T(8,128)(2,1)} collective-permute-done((bf16[128,4096]{1,0:T(8,128)(2,1)}, bf16[128,4096]{1,0:T(8,128)(2,1)}, u32[]{:S(2)}, u32[]{:S(2)}) %collective-permute-start.10) | collective-permute-done | bytes 1048608 | tf_op jit(solution)/shard_map/ppermute | solution.py:66
  67.5 0.5 collective-permute-start.5
  68.0 5.0 %all-to-all-done = bf16[16,128,128]{2,1,0:T(8,128)(2,1)} async-done(((bf16[16,128,128]{2,1,0:T(8,128)(2,1)}), bf16[16,128,128]{2,1,0:T(8,128)(2,1)}, u32[]{:S(2)}, u32[]{:S(2)}) %all-to-all-start) | async-done | bytes 524320 | tf_op jit(solution)/shard_map/all_to_all | solution.py:300
  73.0 0.0 collective-permute-done.8.refs_0_
  73.0 2.2 %shard_map.47 = (bf16[48,4096]{1,0:T(8,128)(2,1)}, bf16[48,4096]{1,0:T(8,128)(2,1)}, bf16[32,4096]{1,0:T(8,128)(2,1)}) custom-call(bf16[128,4096]{1,0:T(8,128)(2,1)} %collective-permute-done.8.refs_0_, bf16[128,4096]{1,0:T(8,128)(2,1)} %collective-permute-done.10.refs_1_, bf16[128,4096]{1,0:T(8,128)(2,1)} %collective-permute-done.9.refs_2_), custom_call_target="tpu_custom_call" | custom-call | flops 30000001024 | tf_op jit(solution)/shard_map/pallas_call | solution.py:88
  75.2 0.7 collective-permute-start.14
  76.0 0.0 collective-permute-done.1
  76.0 3.3 %collective-permute-start.15 = (bf16[48,4096]{1,0:T(8,128)(2,1)}, bf16[48,4096]{1,0:T(8,128)(2,1)S(1)}, u32[]{:S(2)}, u32[]{:S(2)}) collective-permute-start(bf16[48,4096]{1,0:T(8,128)(2,1)} %get-tuple-element.26), channel_id=1, source_target_pairs={{0,96},{32,0},{64,32},{96,64},{1,97},{33,1},{65,33},{97,65},{2,98}... | collective-permute-start | bytes 1179656 | tf_op jit(solution)/shard_map/ppermute | solution.py:66
  79.2 0.0 collective-permute-done.6
  79.2 2.3 %collective-permute-start.16 = (bf16[32,4096]{1,0:T(8,128)(2,1)}, bf16[32,4096]{1,0:T(8,128)(2,1)}, u32[]{:S(2)}, u32[]{:S(2)}) collective-permute-start(bf16[32,4096]{1,0:T(8,128)(2,1)} %get-tuple-element.27), channel_id=1, source_target_pairs={{0,128},{128,0},{1,129},{129,1},{2,130},{130,2},{3,131},{131,3},{4... | collective-permute-start | bytes 786440 | tf_op jit(solution)/shard_map/ppermute | solution.py:66
  81.5 4.4 %collective-permute-done.16 = bf16[32,4096]{1,0:T(8,128)(2,1)} collective-permute-done((bf16[32,4096]{1,0:T(8,128)(2,1)}, bf16[32,4096]{1,0:T(8,128)(2,1)}, u32[]{:S(2)}, u32[]{:S(2)}) %collective-permute-start.16) | collective-permute-done | bytes 262176 | tf_op jit(solution)/shard_map/ppermute | solution.py:66
  85.9 4.6 %collective-permute-start.11 = (bf16[128,4096]{1,0:T(8,128)(2,1)}, bf16[128,4096]{1,0:T(8,128)(2,1)S(1)}, u32[]{:S(2)}, u32[]{:S(2)}) collective-permute-start(bf16[128,4096]{1,0:T(8,128)(2,1)} %collective-permute-done.8.refs_0_), channel_id=1, source_target_pairs={{0,16},{16,0},{1,17},{17,1},{2,18},{18,2},{3,19},{19,3},{4,20},{20... | collective-permute-start | bytes 3145736 | tf_op jit(solution)/shard_map/ppermute | solution.py:66
  90.5 0.0 collective-permute-done.14
  90.5 0.1 collective-permute-start.12
  90.6 0.0 collective-permute-done.15
  90.6 1.6 collective-permute-start.13
  92.2 0.1 collective-permute-start.19
  92.3 5.4 %all-to-all-start.1 = ((bf16[16,128,128]{2,1,0:T(8,128)(2,1)}), bf16[16,128,128]{2,1,0:T(8,128)(2,1)S(1)}, u32[]{:S(2)}, u32[]{:S(2)}) async-start(bf16[16,128,128]{2,1,0:T(8,128)(2,1)} %all-to-all-done), calls=%async_computation.1 | async-start | bytes 1048576 | tf_op jit(solution)/shard_map/all_to_all | solution.py:300
  97.7 0.0 reduce-scatter.2.cloned.1.call-start
  97.7 0.1 slice_bitcast_fusion
  97.8 0.1 broadcast_in_dim.3
  97.9 0.1 le.15
  98.0 0.1 eq.18
  98.1 0.0 collective-permute-done.5
  98.1 0.6 collective-permute-start.17
  98.7 0.2 collective-permute-start.18
  98.9 0.5 slice_bitcast_fusion.1.order
  99.4 0.8 and_convert_fusion.mask
  100.2 6.0 %all-to-all-done.1 = bf16[16,128,128]{2,1,0:T(8,128)(2,1)S(1)} async-done(((bf16[16,128,128]{2,1,0:T(8,128)(2,1)}), bf16[16,128,128]{2,1,0:T(8,128)(2,1)S(1)}, u32[]{:S(2)}, u32[]{:S(2)}) %all-to-all-start.1) | async-done | bytes 524320 | tf_op jit(solution)/shard_map/all_to_all | solution.py:300
  106.3 0.0 all-gather.2.cloned.1.call-done.w_ref
  106.4 0.7 copy-done
  107.0 0.2 copy-done.7
  107.2 0.1 copy-done.8
  107.3 0.4 copy-done.4
  107.7 29.6 %shard_map.48 = bf16[8,3,512,128]{3,2,1,0:T(8,128)(2,1)} custom-call(s32[24]{0:T(128)} %slice_bitcast_fusion.1.order, f32[256,256]{1,0:T(8,128)} %and_convert_fusion.mask, bf16[4096,384]{1,0:T(8,128)(2,1)} %all-gather.2.cloned.1.call-done.w_ref, bf16[16,8,16,128]{3,2,1,0:T(8,128)(2,1)} %bitcast.43, bf16[8,16,4096]{2,1,0:T(8,128)(2,1)} %bitcast.49, ...), custom_call_target="tpu_custom_call" | custom-call | flops 12884901888 | bytes 16777216 | tf_op jit(solution)/shard_map/pallas_call | solution.py:271
  137.3 0.0 reduce-scatter.2.cloned.1.call-update
  137.3 43.6 %reduce-scatter.2.cloned.1.call-done = bf16[1536,128]{1,0:T(8,128)(2,1)} async-done(((bf16[12288,128]{1,0:T(8,128)(2,1)}), bf16[1536,128]{1,0:T(8,128)(2,1)}) %reduce-scatter.2.cloned.1.call-update) | async-done | bytes 393232 | tf_op jit(solution)/shard_map/reduce_scatter | solution.py:311
  180.9 1.0 dynamic-slice_bitcast_fusion.1
  181.9 7.6 %collective-permute-start.20 = (bf16[3,256,128]{2,1,0:T(8,128)(2,1)S(1)}, bf16[3,256,128]{2,1,0:T(8,128)(2,1)S(1)}, u32[]{:S(2)}, u32[]{:S(2)}) collective-permute-start(bf16[3,256,128]{2,1,0:T(8,128)(2,1)S(1)} %get-tuple-element.31), channel_id=1, source_target_pairs={{0,0},{1,129},{2,34},{3,163},{4,68},{5,197},{6,102},{7,231},{8,16}... | collective-permute-start | bytes 589832 | tf_op jit(solution)/shard_map/ppermute | solution.py:319
  189.6 0.1 collective-permute-start.21
  189.7 3.2 %collective-permute-done.20 = bf16[3,256,128]{2,1,0:T(8,128)(2,1)S(1)} collective-permute-done((bf16[3,256,128]{2,1,0:T(8,128)(2,1)S(1)}, bf16[3,256,128]{2,1,0:T(8,128)(2,1)S(1)}, u32[]{:S(2)}, u32[]{:S(2)}) %collective-permute-start.20) | collective-permute-done | bytes 196640 | tf_op jit(solution)/shard_map/ppermute | solution.py:319
  192.9 1.4 collective-permute-done.21
  194.3 0.1 add_convert_fusion
  194.3 6.9 %collective-permute-start.22 = (bf16[3,256,128]{2,1,0:T(8,128)(2,1)S(1)}, bf16[3,256,128]{2,1,0:T(8,128)(2,1)S(1)}, u32[]{:S(2)}, u32[]{:S(2)}) collective-permute-start(bf16[3,256,128]{2,1,0:T(8,128)(2,1)S(1)} %add_convert_fusion), channel_id=1, source_target_pairs={{0,0},{1,1},{2,6},{3,7},{4,4},{5,5},{6,2},{7,3},{8,8},{9,9},{10,14... | collective-permute-start | bytes 589832 | tf_op jit(solution)/shard_map/ppermute | solution.py:321
  201.3 9.5 %collective-permute-done.22 = bf16[3,256,128]{2,1,0:T(8,128)(2,1)S(1)} collective-permute-done((bf16[3,256,128]{2,1,0:T(8,128)(2,1)S(1)}, bf16[3,256,128]{2,1,0:T(8,128)(2,1)S(1)}, u32[]{:S(2)}, u32[]{:S(2)}) %collective-permute-start.22) | collective-permute-done | bytes 196640 | tf_op jit(solution)/shard_map/ppermute | solution.py:321
  210.8 0.7 copy.10
  (25 shorter events, 0.1 us)
Async XLA Ops:
  6.5 47.1 %copy-start.2 = (bf16[1,128,4096]{2,1,0:T(8,128)(2,1)S(1)}, bf16[1,128,4096]{2,1,0:T(8,128)(2,1)}, u32[]{:S(2)}) copy-start(bf16[1,128,4096]{2,1,0:T(8,128)(2,1)} %param.4) | copy-start | bytes 3145732
  6.5 99.8 %all-gather.2.cloned.1.call-start = ((), (), s32[]{:S(2)}) async-start(), calls=%async_computation.3 | async-start | bytes 3538944 | tf_op jit(solution)/shard_map/all_gather | solution.py:299
  6.5 32.6 %collective-permute-start.2 = (bf16[128,4096]{1,0:T(8,128)(2,1)}, bf16[128,4096]{1,0:T(8,128)(2,1)S(1)}, u32[]{:S(2)}, u32[]{:S(2)}) collective-permute-start(bf16[128,4096]{1,0:T(8,128)(2,1)} %bitcast.46), channel_id=1, source_target_pairs={{0,32},{32,64},{64,96},{96,0},{1,33},{33,65},{65,97},{97,1},{2,34}... | collective-permute-start | bytes 3145736 | tf_op jit(solution)/shard_map/ppermute | solution.py:66
  7.8 31.4 %collective-permute-start.3 = (bf16[128,4096]{1,0:T(8,128)(2,1)}, bf16[128,4096]{1,0:T(8,128)(2,1)}, u32[]{:S(2)}, u32[]{:S(2)}) collective-permute-start(bf16[128,4096]{1,0:T(8,128)(2,1)} %bitcast.47), channel_id=1, source_target_pairs={{0,96},{32,0},{64,32},{96,64},{1,97},{33,1},{65,33},{97,65},{2,98}... | collective-permute-start | bytes 3145736 | tf_op jit(solution)/shard_map/ppermute | solution.py:66
  8.0 31.2 %collective-permute-start.4 = (bf16[128,4096]{1,0:T(8,128)(2,1)}, bf16[128,4096]{1,0:T(8,128)(2,1)}, u32[]{:S(2)}, u32[]{:S(2)}) collective-permute-start(bf16[128,4096]{1,0:T(8,128)(2,1)} %bitcast.48), channel_id=1, source_target_pairs={{0,128},{128,0},{1,129},{129,1},{2,130},{130,2},{3,131},{131,3},{4... | collective-permute-start | bytes 3145736 | tf_op jit(solution)/shard_map/ppermute | solution.py:66
  13.0 25.4 %collective-permute-start = (bf16[512,384]{1,0:T(8,128)(2,1)}, bf16[512,384]{1,0:T(8,128)(2,1)S(1)}, u32[]{:S(2)}, u32[]{:S(2)}) collective-permute-start(bf16[512,384]{1,0:T(8,128)(2,1)} %shard_map.46), channel_id=1, source_target_pairs={{0,0},{128,1},{32,2},{160,3},{64,4},{192,5},{96,6},{224,7},{16,8},... | collective-permute-start | bytes 1179656 | tf_op jit(solution)/shard_map/ppermute | solution.py:298
  38.4 0.8 copy-start.1
  39.2 36.0 %copy-start.3 = (bf16[128,4096]{1,0:T(8,128)(2,1)}, bf16[128,4096]{1,0:T(8,128)(2,1)S(1)}, u32[]{:S(2)}) copy-start(bf16[128,4096]{1,0:T(8,128)(2,1)S(1)} %collective-permute-done.2) | copy-start | bytes 3145732
  39.2 28.3 %collective-permute-start.10 = (bf16[128,4096]{1,0:T(8,128)(2,1)}, bf16[128,4096]{1,0:T(8,128)(2,1)}, u32[]{:S(2)}, u32[]{:S(2)}) collective-permute-start(bf16[128,4096]{1,0:T(8,128)(2,1)} %collective-permute-done.3), channel_id=1, source_target_pairs={{0,128},{128,0},{1,129},{129,1},{2,130},{130,2},{3,131},{131,3},{4... | collective-permute-start | bytes 3145736 | tf_op jit(solution)/shard_map/ppermute | solution.py:66
  39.3 28.2 %collective-permute-start.9 = (bf16[128,4096]{1,0:T(8,128)(2,1)}, bf16[128,4096]{1,0:T(8,128)(2,1)}, u32[]{:S(2)}, u32[]{:S(2)}) collective-permute-start(bf16[128,4096]{1,0:T(8,128)(2,1)} %collective-permute-done.3), channel_id=1, source_target_pairs={{0,96},{32,0},{64,32},{96,64},{1,97},{33,1},{65,33},{97,65},{2,98}... | collective-permute-start | bytes 3145736 | tf_op jit(solution)/shard_map/ppermute | solution.py:66
  42.2 30.7 %collective-permute-start.8 = (bf16[128,4096]{1,0:T(8,128)(2,1)}, bf16[128,4096]{1,0:T(8,128)(2,1)}, u32[]{:S(2)}, u32[]{:S(2)}) collective-permute-start(bf16[128,4096]{1,0:T(8,128)(2,1)} %collective-permute-done.4), channel_id=1, source_target_pairs={{0,32},{32,64},{64,96},{96,0},{1,33},{33,65},{65,97},{97,1},{2,34}... | collective-permute-start | bytes 3145736 | tf_op jit(solution)/shard_map/ppermute | solution.py:66
  42.2 30.7 %all-to-all-start = ((bf16[16,128,128]{2,1,0:T(8,128)(2,1)}), bf16[16,128,128]{2,1,0:T(8,128)(2,1)}, u32[]{:S(2)}, u32[]{:S(2)}) async-start(bf16[16,128,128]{2,1,0:T(8,128)(2,1)} %bitcast.5), calls=%async_computation | async-start | bytes 1048576 | tf_op jit(solution)/shard_map/all_to_all | solution.py:300
  53.7 22.3 %collective-permute-start.1 = (bf16[128,4096]{1,0:T(8,128)(2,1)S(1)}, bf16[128,4096]{1,0:T(8,128)(2,1)}, u32[]{:S(2)}, u32[]{:S(2)}) collective-permute-start(bf16[128,4096]{1,0:T(8,128)(2,1)S(1)} %bitcast.50), channel_id=1, source_target_pairs={{0,16},{16,0},{1,17},{17,1},{2,18},{18,2},{3,19},{19,3},{4,20},{20... | collective-permute-start | bytes 3145736 | tf_op jit(solution)/shard_map/ppermute | solution.py:66
  56.7 22.5 %collective-permute-start.6 = (bf16[128,4096]{1,0:T(8,128)(2,1)}, bf16[128,4096]{1,0:T(8,128)(2,1)}, u32[]{:S(2)}, u32[]{:S(2)}) collective-permute-start(bf16[128,4096]{1,0:T(8,128)(2,1)} %collective-permute-done.3), channel_id=1, source_target_pairs={{0,16},{16,0},{1,17},{17,1},{2,18},{18,2},{3,19},{19,3},{4,20},{20... | collective-permute-start | bytes 3145736 | tf_op jit(solution)/shard_map/ppermute | solution.py:66
  67.5 24.7 %collective-permute-start.7 = (bf16[128,4096]{1,0:T(8,128)(2,1)}, bf16[128,4096]{1,0:T(8,128)(2,1)}, u32[]{:S(2)}, u32[]{:S(2)}) collective-permute-start(bf16[128,4096]{1,0:T(8,128)(2,1)} %collective-permute-done.4), channel_id=1, source_target_pairs={{0,16},{16,0},{1,17},{17,1},{2,18},{18,2},{3,19},{19,3},{4,20},{20... | collective-permute-start | bytes 3145736 | tf_op jit(solution)/shard_map/ppermute | solution.py:66
  67.5 30.6 %collective-permute-start.5 = (bf16[128,4096]{1,0:T(8,128)(2,1)S(1)}, bf16[128,4096]{1,0:T(8,128)(2,1)}, u32[]{:S(2)}, u32[]{:S(2)}) collective-permute-start(bf16[128,4096]{1,0:T(8,128)(2,1)S(1)} %collective-permute-done.2), channel_id=1, source_target_pairs={{0,16},{16,0},{1,17},{17,1},{2,18},{18,2},{3,19},{19,3},{4,20},{20... | collective-permute-start | bytes 3145736 | tf_op jit(solution)/shard_map/ppermute | solution.py:66
  75.2 15.3 %collective-permute-start.14 = (bf16[48,4096]{1,0:T(8,128)(2,1)}, bf16[48,4096]{1,0:T(8,128)(2,1)S(1)}, u32[]{:S(2)}, u32[]{:S(2)}) collective-permute-start(bf16[48,4096]{1,0:T(8,128)(2,1)} %get-tuple-element.25), channel_id=1, source_target_pairs={{0,32},{32,64},{64,96},{96,0},{1,33},{33,65},{65,97},{97,1},{2,34}... | collective-permute-start | bytes 1179656 | tf_op jit(solution)/shard_map/ppermute | solution.py:66
  76.0 14.6 %collective-permute-start.15 = (bf16[48,4096]{1,0:T(8,128)(2,1)}, bf16[48,4096]{1,0:T(8,128)(2,1)S(1)}, u32[]{:S(2)}, u32[]{:S(2)}) collective-permute-start(bf16[48,4096]{1,0:T(8,128)(2,1)} %get-tuple-element.26), channel_id=1, source_target_pairs={{0,96},{32,0},{64,32},{96,64},{1,97},{33,1},{65,33},{97,65},{2,98}... | collective-permute-start | bytes 1179656 | tf_op jit(solution)/shard_map/ppermute | solution.py:66
  79.2 6.7 %collective-permute-start.16 = (bf16[32,4096]{1,0:T(8,128)(2,1)}, bf16[32,4096]{1,0:T(8,128)(2,1)}, u32[]{:S(2)}, u32[]{:S(2)}) collective-permute-start(bf16[32,4096]{1,0:T(8,128)(2,1)} %get-tuple-element.27), channel_id=1, source_target_pairs={{0,128},{128,0},{1,129},{129,1},{2,130},{130,2},{3,131},{131,3},{4... | collective-permute-start | bytes 786440 | tf_op jit(solution)/shard_map/ppermute | solution.py:66
  85.9 20.4 %collective-permute-start.11 = (bf16[128,4096]{1,0:T(8,128)(2,1)}, bf16[128,4096]{1,0:T(8,128)(2,1)S(1)}, u32[]{:S(2)}, u32[]{:S(2)}) collective-permute-start(bf16[128,4096]{1,0:T(8,128)(2,1)} %collective-permute-done.8.refs_0_), channel_id=1, source_target_pairs={{0,16},{16,0},{1,17},{17,1},{2,18},{18,2},{3,19},{19,3},{4,20},{20... | collective-permute-start | bytes 3145736 | tf_op jit(solution)/shard_map/ppermute | solution.py:66
  90.5 15.8 %copy-start.5 = (bf16[48,4096]{1,0:T(8,128)(2,1)}, bf16[48,4096]{1,0:T(8,128)(2,1)S(1)}, u32[]{:S(2)}) copy-start(bf16[48,4096]{1,0:T(8,128)(2,1)S(1)} %collective-permute-done.14) | copy-start | bytes 1179652
  90.5 15.8 %collective-permute-start.12 = (bf16[128,4096]{1,0:T(8,128)(2,1)}, bf16[128,4096]{1,0:T(8,128)(2,1)}, u32[]{:S(2)}, u32[]{:S(2)}) collective-permute-start(bf16[128,4096]{1,0:T(8,128)(2,1)} %collective-permute-done.9.refs_2_), channel_id=1, source_target_pairs={{0,16},{16,0},{1,17},{17,1},{2,18},{18,2},{3,19},{19,3},{4,20},{20... | collective-permute-start | bytes 3145736 | tf_op jit(solution)/shard_map/ppermute | solution.py:66
  90.6 15.7 %copy-start.6 = (bf16[48,4096]{1,0:T(8,128)(2,1)}, bf16[48,4096]{1,0:T(8,128)(2,1)S(1)}, u32[]{:S(2)}) copy-start(bf16[48,4096]{1,0:T(8,128)(2,1)S(1)} %collective-permute-done.15) | copy-start | bytes 1179652
  90.6 15.7 %collective-permute-start.13 = (bf16[128,4096]{1,0:T(8,128)(2,1)}, bf16[128,4096]{1,0:T(8,128)(2,1)}, u32[]{:S(2)}, u32[]{:S(2)}) collective-permute-start(bf16[128,4096]{1,0:T(8,128)(2,1)} %collective-permute-done.10.refs_1_), channel_id=1, source_target_pairs={{0,16},{16,0},{1,17},{17,1},{2,18},{18,2},{3,19},{19,3},{4,20},{20... | collective-permute-start | bytes 3145736 | tf_op jit(solution)/shard_map/ppermute | solution.py:66
  92.2 6.5 %collective-permute-start.19 = (bf16[32,4096]{1,0:T(8,128)(2,1)}, bf16[32,4096]{1,0:T(8,128)(2,1)}, u32[]{:S(2)}, u32[]{:S(2)}) collective-permute-start(bf16[32,4096]{1,0:T(8,128)(2,1)} %collective-permute-done.16), channel_id=1, source_target_pairs={{0,16},{16,0},{1,17},{17,1},{2,18},{18,2},{3,19},{19,3},{4,20},{20... | collective-permute-start | bytes 786440 | tf_op jit(solution)/shard_map/ppermute | solution.py:66
  92.3 14.0 %all-to-all-start.1 = ((bf16[16,128,128]{2,1,0:T(8,128)(2,1)}), bf16[16,128,128]{2,1,0:T(8,128)(2,1)S(1)}, u32[]{:S(2)}, u32[]{:S(2)}) async-start(bf16[16,128,128]{2,1,0:T(8,128)(2,1)} %all-to-all-done), calls=%async_computation.1 | async-start | bytes 1048576 | tf_op jit(solution)/shard_map/all_to_all | solution.py:300
  97.7 83.2 %reduce-scatter.2.cloned.1.call-start = ((), (), s32[]{:S(2)}) async-start(), calls=%async_computation.4 | async-start | bytes 3538944 | tf_op jit(solution)/shard_map/reduce_scatter | solution.py:311
  98.1 8.2 %collective-permute-start.17 = (bf16[48,4096]{1,0:T(8,128)(2,1)S(1)}, bf16[48,4096]{1,0:T(8,128)(2,1)S(1)}, u32[]{:S(2)}, u32[]{:S(2)}) collective-permute-start(bf16[48,4096]{1,0:T(8,128)(2,1)S(1)} %collective-permute-done.14), channel_id=1, source_target_pairs={{0,16},{16,0},{1,17},{17,1},{2,18},{18,2},{3,19},{19,3},{4,20},{20... | collective-permute-start | bytes 1179656 | tf_op jit(solution)/shard_map/ppermute | solution.py:66
  98.7 7.6 %collective-permute-start.18 = (bf16[48,4096]{1,0:T(8,128)(2,1)S(1)}, bf16[48,4096]{1,0:T(8,128)(2,1)S(1)}, u32[]{:S(2)}, u32[]{:S(2)}) collective-permute-start(bf16[48,4096]{1,0:T(8,128)(2,1)S(1)} %collective-permute-done.15), channel_id=1, source_target_pairs={{0,16},{16,0},{1,17},{17,1},{2,18},{18,2},{3,19},{19,3},{4,20},{20... | collective-permute-start | bytes 1179656 | tf_op jit(solution)/shard_map/ppermute | solution.py:66
  106.2 0.8 copy-start
  106.3 0.9 copy-start.7
  106.3 1.1 copy-start.8
  106.3 1.4 copy-start.4
  181.9 11.0 %collective-permute-start.20 = (bf16[3,256,128]{2,1,0:T(8,128)(2,1)S(1)}, bf16[3,256,128]{2,1,0:T(8,128)(2,1)S(1)}, u32[]{:S(2)}, u32[]{:S(2)}) collective-permute-start(bf16[3,256,128]{2,1,0:T(8,128)(2,1)S(1)} %get-tuple-element.31), channel_id=1, source_target_pairs={{0,0},{1,129},{2,34},{3,163},{4,68},{5,197},{6,102},{7,231},{8,16}... | collective-permute-start | bytes 589832 | tf_op jit(solution)/shard_map/ppermute | solution.py:319
  189.6 4.7 %collective-permute-start.21 = (bf16[3,256,128]{2,1,0:T(8,128)(2,1)S(1)}, bf16[3,256,128]{2,1,0:T(8,128)(2,1)S(1)}, u32[]{:S(2)}, u32[]{:S(2)}) collective-permute-start(bf16[3,256,128]{2,1,0:T(8,128)(2,1)S(1)} %get-tuple-element.32), channel_id=1, source_target_pairs={{0,16},{1,145},{2,50},{3,179},{4,84},{5,213},{6,118},{7,247},{8,0}... | collective-permute-start | bytes 589832 | tf_op jit(solution)/shard_map/ppermute | solution.py:319
  194.3 16.5 %collective-permute-start.22 = (bf16[3,256,128]{2,1,0:T(8,128)(2,1)S(1)}, bf16[3,256,128]{2,1,0:T(8,128)(2,1)S(1)}, u32[]{:S(2)}, u32[]{:S(2)}) collective-permute-start(bf16[3,256,128]{2,1,0:T(8,128)(2,1)S(1)} %add_convert_fusion), channel_id=1, source_target_pairs={{0,0},{1,1},{2,6},{3,7},{4,4},{5,5},{6,2},{7,3},{8,8},{9,9},{10,14... | collective-permute-start | bytes 589832 | tf_op jit(solution)/shard_map/ppermute | solution.py:321
Sparse Core Ops, SparseCore 0:
  39.3 59.1 all-gather.1
  137.4 43.4 reduce-scatter.1

commit v5 on v4

--- a/solution.py
+++ b/solution.py
@@ -19,6 +19,8 @@
 CUT_A, CUT_B = 48, 96
 CUTS = ((0, CUT_A), (CUT_A, CUT_B), (CUT_B, PATCHES))
 STEP = 4
+FAR = (4, 5)
+NEAR = (3, 6, 2, 7, 1, 0)
 CUT_FLOPS = 3 * 10**10
 WIDTH = 4096
 COLS = 3 * HEAD_DIM
@@ -97,7 +99,7 @@
     )(*buffers)
 
 
-def gather_frames(own, early, middle):
+def gather_frames(own, early, middle, late):
     twin = lambda values: [shift(value, "core", 1) for value in values]
     first = [shift(own, "x", 1), shift(own, "x", -1), shift(own, "yl", 1)]
     own_twin = shift(own, "core", 1)
@@ -108,7 +110,7 @@
     cuts = cut(other_left, other_right, far)
     third = [shift(cuts[0], "x", 1), shift(cuts[1], "x", -1), shift(cuts[2], "yl", 1)]
     second_twins = twin([other_left, far, other_right])
-    third = after(third)
+    third = after(third, *late)
     return (
         [own, own_twin, left, right, other, *first_twins],
         [other_left, far, other_right, *second_twins],
@@ -135,6 +137,9 @@
     return out
 
 
+PARTS = parts_of(FIRST + SECOND + THIRD)
+
+
 def tables():
     out = np.zeros((256, 48), np.int32)
     for yl, x, core, yh, z in np.ndindex(*SIZES):
@@ -143,7 +148,8 @@
             row[slot] = (core ^ dc) * 8 + (x + dx) % 4 * 2 + (yl ^ dy)
             row[24 + slot] = ((yl ^ dy) * 4 + (x + dx) % 4) * 2 + (core ^ dc)
         for k in range(8):
-            row[16 + k] = (yl ^ (k % 2)) * 4 + (x + k // 2) % 4
+            at = (z + k) % 8
+            row[16 + k] = (yl ^ (at % 2)) * 4 + (x + at // 2) % 4
         row[40] = (x - z // 2) % 4 * 2 + (yl ^ (z % 2))
     return out
 
@@ -212,10 +218,10 @@
 
 
 def share_kernel(count, order, mask, w_ref, g_ref, *refs):
-    buffers, out = refs[:count], refs[count]
-    tokens, proj, grads, turned, w, shares, w_sem, x_sem, g_sem, o_sem = refs[count + 1 :]
+    buffers, turned_out, out = refs[:count], refs[count], refs[count + 1 : count + 1 + len(FAR)]
+    tokens, proj, grads, turned, w, w_sem, x_sem, g_sem = refs[count + 1 + len(FAR) :]
     arrivals = [[] for _ in range(FRAMES)]
-    for index, (buffer, at, slot, first, groups) in enumerate(parts_of(FIRST + SECOND + THIRD)):
+    for index, (buffer, at, slot, first, groups) in enumerate(PARTS):
         arrivals[slot].append(
             pltpu.make_async_copy(
                 buffers[buffer].at[pl.ds(at, groups)],
@@ -250,46 +256,101 @@
     for copy in cotangents:
         copy.wait()
     attend(proj, grads, mask, turned)
-
-    def weigh(step, carry):
-        columns = pl.ds(pl.multiple_of(order[16 + step] * CHUNK, CHUNK), CHUNK)
+    store = pltpu.make_async_copy(turned, turned_out, w_sem.at[1])
+    store.start()
+    for index, ahead in enumerate(FAR):
+        columns = pl.ds(pl.multiple_of(order[16 + ahead] * CHUNK, CHUNK), CHUNK)
         rows = tokens[:, :, :, columns].reshape(ROWS, CHUNK)
-        value = jnp.dot(turned[...], rows, preferred_element_type=jnp.float32)
-        for j in range(3):
-            shares[step, j] = value[j * HEAD_DIM : (j + 1) * HEAD_DIM].T.astype(jnp.bfloat16)
-        pltpu.make_async_copy(shares.at[step], out.at[step], o_sem.at[step]).start()
-        return carry
-
-    lax.fori_loop(0, 8, weigh, 0)
-    for step in range(8):
-        pltpu.make_async_copy(shares.at[step], out.at[step], o_sem.at[step]).wait()
-
-
-def weight_share(order, mask, w, g, buffers):
+        weigh(turned, rows, out[index])
+    store.wait()
+
+
+def weigh(turned, rows, out):
+    value = jnp.dot(turned[...], rows, preferred_element_type=jnp.float32)
+    for j in range(3):
+        out[j] = value[j * HEAD_DIM : (j + 1) * HEAD_DIM].T.astype(jnp.bfloat16)
+
+
+def near_kernel(count, order, turned_ref, *refs):
+    buffers, out = refs[:count], refs[count : count + len(NEAR)]
+    tokens, turned, t_sem, x_sem = refs[count + len(NEAR) :]
+    load = pltpu.make_async_copy(turned_ref, turned, t_sem.at[0])
+    load.start()
+    copies = []
+    for index, ahead in enumerate(NEAR):
+        columns = pl.ds(pl.multiple_of(order[16 + ahead] * CHUNK, CHUNK), CHUNK)
+        copies.append([])
+        for part, (buffer, at, slot, first, groups) in enumerate(PARTS):
+            copies[-1].append(
+                pltpu.make_async_copy(
+                    buffers[buffer].at[pl.ds(at, groups), :, columns],
+                    tokens.at[index, pl.ds(first, groups), slot],
+                    x_sem.at[index, part],
+                )
+            )
+    for copy in copies[0] + copies[1]:
+        copy.start()
+    load.wait()
+    for index in range(len(NEAR)):
+        for copy in copies[index]:
+            copy.wait()
+        if index + 2 < len(NEAR):
+            for copy in copies[index + 2]:
+                copy.start()
+        weigh(turned, tokens[index].reshape(ROWS, CHUNK), out[index])
+
+
+def near_shares(order, turned, buffers):
+    count = len(buffers)
+    share = jax.ShapeDtypeStruct((3, CHUNK, HEAD_DIM), jnp.bfloat16)
+    return pl.pallas_call(
+        functools.partial(near_kernel, count),
+        out_shape=[share] * len(NEAR),
+        in_specs=[SMEM] + [HBM] * (1 + count),
+        out_specs=[VMEM] * len(NEAR),
+        scratch_shapes=[
+            pltpu.VMEM((len(NEAR), PATCHES // GROUP, FRAMES, GROUP, CHUNK), jnp.bfloat16),
+            pltpu.VMEM((COLS, ROWS), jnp.bfloat16),
+            pltpu.SemaphoreType.DMA((1,)),
+            pltpu.SemaphoreType.DMA((len(NEAR), len(PARTS))),
+        ],
+        compiler_params=pltpu.CompilerParams(vmem_limit_bytes=44 * 2**20),
+        cost_estimate=pl.CostEstimate(
+            flops=2 * ROWS * len(NEAR) * CHUNK * COLS,
+            bytes_accessed=2 * ROWS * len(NEAR) * CHUNK,
+            transcendentals=0,
+        ),
+    )(order, turned, *buffers)
+
+
+def far_shares(order, mask, w, g, buffers):
     count = len(buffers)
     groups = PATCHES // GROUP
+    share = jax.ShapeDtypeStruct((3, CHUNK, HEAD_DIM), jnp.bfloat16)
     return pl.pallas_call(
         functools.partial(share_kernel, count),
-        out_shape=jax.ShapeDtypeStruct((8, 3, CHUNK, HEAD_DIM), jnp.bfloat16),
+        out_shape=[jax.ShapeDtypeStruct((COLS, ROWS), jnp.bfloat16)] + [share] * len(FAR),
         in_specs=[SMEM, VMEM] + [HBM] * (2 + count),
-        out_specs=HBM,
+        out_specs=[HBM] + [VMEM] * len(FAR),
         scratch_shapes=[
             pltpu.VMEM((groups, FRAMES, GROUP, WIDTH), jnp.bfloat16),
             pltpu.VMEM((groups, FRAMES, GROUP, COLS), jnp.bfloat16),
             pltpu.VMEM((groups, FRAMES, GROUP, HEAD_DIM), jnp.bfloat16),
             pltpu.VMEM((COLS, ROWS), jnp.bfloat16),
             pltpu.VMEM((WIDTH, COLS), jnp.bfloat16),
-            pltpu.VMEM((8, 3, CHUNK, HEAD_DIM), jnp.bfloat16),
-            pltpu.SemaphoreType.DMA((1,)),
-            pltpu.SemaphoreType.DMA((len(parts_of(FIRST + SECOND + THIRD)),)),
+            pltpu.SemaphoreType.DMA((2,)),
+            pltpu.SemaphoreType.DMA((len(PARTS),)),
             pltpu.SemaphoreType.DMA((FRAMES,)),
-            pltpu.SemaphoreType.DMA((8,)),
         ],
-        compiler_params=pltpu.CompilerParams(vmem_limit_bytes=58 * 2**20),
+        compiler_params=pltpu.CompilerParams(vmem_limit_bytes=44 * 2**20),
         cost_estimate=pl.CostEstimate(
-            flops=4 * ROWS * WIDTH * COLS, bytes_accessed=2 * ROWS * WIDTH, transcendentals=0
+            flops=2 * ROWS * WIDTH * COLS, bytes_accessed=2 * ROWS * WIDTH, transcendentals=0
         ),
     )(order, mask, w, g, *buffers)
+
+
+def add(*parts):
+    return sum(part.astype(jnp.float32) for part in parts).astype(jnp.bfloat16)
 
 
 def local(inputs, grad_attn, w_qkv):
@@ -302,15 +363,21 @@
     )
     heads_g = exchange(after(grad_attn[0], rows_w).reshape(FRAMES, PATCHES, HEAD_DIM), TOK)
     frames_g = exchange(heads_g, ("core", "x", "yl"))
-    steps = gather_frames(inputs[0], (rows_w,), (heads_g,))
+    steps = gather_frames(inputs[0], (rows_w,), (heads_g,), (frames_g,))
     g = frames_g.reshape(FRAMES, PATCHES // GROUP, GROUP, HEAD_DIM)
     first, second, third = (
         [buffer.reshape(-1, GROUP, WIDTH) for buffer in buffers] for buffers in steps
     )
-    share = weight_share(table[:24], visible(table[24:40]), w, g, first + second + third)
-    mine = lax.psum_scatter(
-        share.reshape(8 * 3 * CHUNK, HEAD_DIM), "z", scatter_dimension=0, tiled=True
+    order, buffers = table[:24], first + second + third
+    turned, up, down = far_shares(order, visible(table[24:40]), w, g, buffers)
+    up, down, near = lax.optimization_barrier(
+        (shift(up, "z", 1), shift(down, "z", -1), near_shares(order, turned, buffers))
     )
+    for step in (0, 2):
+        up = shift(add(up, near[step]), "z", 1)
+        down = shift(add(down, near[step + 1]), "z", -1)
+    up = shift(add(up, near[4]), "z", 1)
+    mine = add(up, down, near[5])
     mine = mine.reshape(3, 2, CHUNK // 2, HEAD_DIM)
     yh = lax.axis_index("yh")
     total = None

time: 219 us -> 210 us (0.959)
  waiting for transfers between devices: 99.4 us -> 77.9 us
  starting transfers between devices: 64.2 us -> 69.4 us
  local copies, waits for them, and re-layouts: 5.93 us -> 9.15 us
  Pallas kernels: 34.2 us -> 37.3 us
    reduce_scatter x1 -> x0, waiting for transfers between devices: 43.6 us -> none  [local(): lax.psum_scatter(share.reshape(8 * 3 * CHUNK, HEAD_DIM), 'z', scatter_dim...]
    ppermute x19 -> x26, waiting for transfers between devices: 15.1 us -> 36.5 us  [shift(): lax.ppermute(value, axis, [(i, (i + by) % count) for i in range(count)])]
    ppermute x19 -> x26, starting transfers between devices: 22.9 us -> 27.7 us  [shift(): lax.ppermute(value, axis, [(i, (i + by) % count) for i in range(count)])]
    unnamed x19 -> x23, local copies, waits for them, and re-layouts: 2.79 us -> 6.88 us
    all_to_all x2, starting transfers between devices: 16.9 us -> 20.9 us  [local(): lax.all_to_all(value, axes, split_axis=0, concat_axis=0, tiled=True)]
    pallas_call x1 -> x2, Pallas kernels: 29.6 us -> 32.7 us  [the longest x1 22.3 us: far_shares(): pl.pallas_call(functools.partial(share_kernel, count), out_shape=[jax.Sha...]
  transfers between devices with their start and end apart: 27 -> 33, of which waited for: 9 -> 11; matrix products, arithmetic and copies ran while one was open for 1% -> 2% of each run, Pallas kernels for 2% -> 7%
where the time goes in v5:
time: 210 us; the launch traced here: 209 us
  waiting for transfers between devices  77.9 us (37%)
  starting transfers between devices  69.4 us (33%)
  Pallas kernels  37.3 us (18%)
  between operations  13.7 us (7%)
  local copies, waits for them, and re-layouts  9.15 us (4%)
    ppermute x26, waiting for transfers between devices, shift(): lax.ppermute(value, axis, [(i, (i + by) % count) for i in range(count)])  36.5 us
    ppermute x26, starting transfers between devices, shift(): lax.ppermute(value, axis, [(i, (i + by) % count) for i in range(count)])  27.7 us
    pallas_call x1, Pallas kernels, far_shares(): pl.pallas_call(functools.partial(share_kernel, count), out_shape=[jax.Sha...  22.3 us
    all_to_all x2, starting transfers between devices, local(): lax.all_to_all(value, axes, split_axis=0, concat_axis=0, tiled=True)  20.9 us
    ppermute x1, waiting for transfers between devices, local(): rows_w = lax.ppermute(rows_w, AXES, worker_moves())  15.5 us
    all_to_all x2, waiting for transfers between devices, local(): lax.all_to_all(value, axes, split_axis=0, concat_axis=0, tiled=True)  12.2 us
    pallas_call x1, Pallas kernels, near_shares(): pl.pallas_call(functools.partial(near_kernel, count), out_shape=[share] *...  10.5 us
    ppermute x1, starting transfers between devices, local(): rows_w = lax.ppermute(rows_w, AXES, worker_moves())  9.82 us
  transfers between devices with their start and end apart: 33, of which 11 were waited for; matrix products, arithmetic and copies ran while one was open for 2% of the time, Pallas kernels for 7%

profile of v5, /device:TPU:3, one launch (start us, length us, event | category | flops | bytes accessed | tf_op | source)
XLA Modules:
  0.0 209.0 jit_solution(11818061068708972917)
XLA Ops:
  6.5 1.2 collective-permute-start.2
  7.8 0.3 collective-permute-start.3
  8.0 1.3 collective-permute-start.4
  9.3 0.7 constant_dynamic-slice_fusion
  10.0 0.6 slice.22
  10.6 2.4 %shard_map.46 = bf16[512,384]{1,0:T(8,128)(2,1)} custom-call(s32[1]{0:T(128)} %bitcast.2.start, bf16[3,4096,128]{2,1,0:T(8,128)(2,1)} %bitcast.52), custom_call_target="tpu_custom_call" | custom-call | tf_op jit(solution)/shard_map/pallas_call | solution.py:181
  12.9 9.8 %collective-permute-start = (bf16[512,384]{1,0:T(8,128)(2,1)}, bf16[512,384]{1,0:T(8,128)(2,1)S(1)}, u32[]{:S(2)}, u32[]{:S(2)}) collective-permute-start(bf16[512,384]{1,0:T(8,128)(2,1)} %shard_map.46), channel_id=1, source_target_pairs={{0,0},{128,1},{32,2},{160,3},{64,4},{192,5},{96,6},{224,7},{16,8},... | collective-permute-start | bytes 1179656 | tf_op jit(solution)/shard_map/ppermute | solution.py:359
  22.8 15.5 %collective-permute-done = bf16[512,384]{1,0:T(8,128)(2,1)S(1)} collective-permute-done((bf16[512,384]{1,0:T(8,128)(2,1)}, bf16[512,384]{1,0:T(8,128)(2,1)S(1)}, u32[]{:S(2)}, u32[]{:S(2)}) %collective-permute-start) | collective-permute-done | bytes 393248 | tf_op jit(solution)/shard_map/ppermute | solution.py:359
  38.3 0.8 copy-done.9
  39.1 0.1 collective-permute-start.10
  39.2 3.0 %collective-permute-start.9 = (bf16[128,4096]{1,0:T(8,128)(2,1)S(1)}, bf16[128,4096]{1,0:T(8,128)(2,1)}, u32[]{:S(2)}, u32[]{:S(2)}) collective-permute-start(bf16[128,4096]{1,0:T(8,128)(2,1)S(1)} %collective-permute-done.3), channel_id=1, source_target_pairs={{0,96},{32,0},{64,32},{96,64},{1,97},{33,1},{65,33},{97,65},{2,98}... | collective-permute-start | bytes 3145736 | tf_op jit(solution)/shard_map/ppermute | solution.py:68
  42.2 11.3 %all-to-all-start = ((bf16[16,128,128]{2,1,0:T(8,128)(2,1)}), bf16[16,128,128]{2,1,0:T(8,128)(2,1)}, u32[]{:S(2)}, u32[]{:S(2)}) async-start(bf16[16,128,128]{2,1,0:T(8,128)(2,1)} %bitcast.54), calls=%async_computation | async-start | bytes 1048576 | tf_op jit(solution)/shard_map/all_to_all | solution.py:361
  53.6 3.1 %collective-permute-start.1 = (bf16[128,4096]{1,0:T(8,128)(2,1)S(1)}, bf16[128,4096]{1,0:T(8,128)(2,1)}, u32[]{:S(2)}, u32[]{:S(2)}) collective-permute-start(bf16[128,4096]{1,0:T(8,128)(2,1)S(1)} %bitcast.39), channel_id=1, source_target_pairs={{0,16},{16,0},{1,17},{17,1},{2,18},{18,2},{3,19},{19,3},{4,20},{20... | collective-permute-start | bytes 3145736 | tf_op jit(solution)/shard_map/ppermute | solution.py:68
  56.6 0.1 collective-permute-start.6
  56.7 10.5 %collective-permute-done.10.refs_1_ = bf16[128,4096]{1,0:T(8,128)(2,1)} collective-permute-done((bf16[128,4096]{1,0:T(8,128)(2,1)S(1)}, bf16[128,4096]{1,0:T(8,128)(2,1)}, u32[]{:S(2)}, u32[]{:S(2)}) %collective-permute-start.10) | collective-permute-done | bytes 1048608 | tf_op jit(solution)/shard_map/ppermute | solution.py:68
  67.2 0.5 collective-permute-start.5
  67.7 4.7 %all-to-all-done = bf16[16,128,128]{2,1,0:T(8,128)(2,1)} async-done(((bf16[16,128,128]{2,1,0:T(8,128)(2,1)}), bf16[16,128,128]{2,1,0:T(8,128)(2,1)}, u32[]{:S(2)}, u32[]{:S(2)}) %all-to-all-start) | async-done | bytes 524320 | tf_op jit(solution)/shard_map/all_to_all | solution.py:361
  72.4 2.2 %shard_map.47 = (bf16[48,4096]{1,0:T(8,128)(2,1)}, bf16[48,4096]{1,0:T(8,128)(2,1)}, bf16[32,4096]{1,0:T(8,128)(2,1)}) custom-call(bf16[128,4096]{1,0:T(8,128)(2,1)} %collective-permute-done.8.refs_0_, bf16[128,4096]{1,0:T(8,128)(2,1)} %collective-permute-done.10.refs_1_, bf16[128,4096]{1,0:T(8,128)(2,1)} %collective-permute-done.9.refs_2_), custom_call_target="tpu_custom_call" | custom-call | flops 30000001024 | tf_op jit(solution)/shard_map/pallas_call | solution.py:90
  74.6 1.4 collective-permute-start.14
  76.0 3.0 %collective-permute-start.15 = (bf16[48,4096]{1,0:T(8,128)(2,1)}, bf16[48,4096]{1,0:T(8,128)(2,1)}, u32[]{:S(2)}, u32[]{:S(2)}) collective-permute-start(bf16[48,4096]{1,0:T(8,128)(2,1)} %get-tuple-element.43), channel_id=1, source_target_pairs={{0,96},{32,0},{64,32},{96,64},{1,97},{33,1},{65,33},{97,65},{2,98}... | collective-permute-start | bytes 1179656 | tf_op jit(solution)/shard_map/ppermute | solution.py:68
  79.1 2.5 %collective-permute-start.16 = (bf16[32,4096]{1,0:T(8,128)(2,1)}, bf16[32,4096]{1,0:T(8,128)(2,1)}, u32[]{:S(2)}, u32[]{:S(2)}) collective-permute-start(bf16[32,4096]{1,0:T(8,128)(2,1)} %get-tuple-element.44), channel_id=1, source_target_pairs={{0,128},{128,0},{1,129},{129,1},{2,130},{130,2},{3,131},{131,3},{4... | collective-permute-start | bytes 786440 | tf_op jit(solution)/shard_map/ppermute | solution.py:68
  81.6 9.6 %all-to-all-start.1 = ((bf16[16,128,128]{2,1,0:T(8,128)(2,1)}), bf16[16,128,128]{2,1,0:T(8,128)(2,1)}, u32[]{:S(2)}, u32[]{:S(2)}) async-start(bf16[16,128,128]{2,1,0:T(8,128)(2,1)} %all-to-all-done), calls=%async_computation.1 | async-start | bytes 1048576 | tf_op jit(solution)/shard_map/all_to_all | solution.py:361
  91.1 0.4 collective-permute-start.11
  91.6 0.1 collective-permute-start.12
  91.7 0.4 collective-permute-start.13
  92.2 7.5 %all-to-all-done.1 = bf16[16,128,128]{2,1,0:T(8,128)(2,1)} async-done(((bf16[16,128,128]{2,1,0:T(8,128)(2,1)}), bf16[16,128,128]{2,1,0:T(8,128)(2,1)}, u32[]{:S(2)}, u32[]{:S(2)}) %all-to-all-start.1) | async-done | bytes 524320 | tf_op jit(solution)/shard_map/all_to_all | solution.py:361
  99.7 1.3 collective-permute-start.19
  101.2 0.1 le.15
  101.3 0.1 collective-permute-start.17
  101.4 1.1 collective-permute-done.19
  102.5 0.4 collective-permute-start.18
  102.9 0.7 slice_bitcast_fusion.1.order
  103.6 0.8 and_convert_fusion.mask
  104.4 0.7 copy-done.3
  105.1 0.8 copy-done.6
  106.0 1.0 copy-done.4
  106.9 1.0 copy-done.7
  107.9 0.9 copy-done.8
  108.9 22.3 %shard_map.48 = (bf16[384,2048]{1,0:T(8,128)(2,1)}, bf16[3,512,128]{2,1,0:T(8,128)(2,1)S(1)}, bf16[3,512,128]{2,1,0:T(8,128)(2,1)S(1)}) custom-call(s32[24]{0:T(128)S(1)} %slice_bitcast_fusion.1.order, f32[256,256]{1,0:T(8,128)S(1)} %copy-done.8, bf16[4096,384]{1,0:T(8,128)(2,1)} %all-gather.2.cloned.1.call-done.w_ref, ...), custom_call_target="tpu_custom_call" | custom-call | flops 6442450944 | bytes 16777216 | tf_op jit(solution)/shard_map/pallas_call | solution.py:330
  131.2 0.1 collective-permute-start.20
  131.3 2.7 %collective-permute-start.21 = (bf16[3,512,128]{2,1,0:T(8,128)(2,1)S(1)}, bf16[3,512,128]{2,1,0:T(8,128)(2,1)S(1)}, u32[]{:S(2)}, u32[]{:S(2)}) collective-permute-start(bf16[3,512,128]{2,1,0:T(8,128)(2,1)S(1)} %get-tuple-element.49), channel_id=1, source_target_pairs={{0,7},{1,0},{2,1},{3,2},{4,3},{5,4},{6,5},{7,6},{8,15},{9,8},{10,9... | collective-permute-start | bytes 1179656 | tf_op jit(solution)/shard_map/ppermute | solution.py:68
  133.9 1.0 copy-done.2
  134.9 10.5 %shard_map.49 = (bf16[3,512,128]{2,1,0:T(8,128)(2,1)S(1)}, bf16[3,512,128]{2,1,0:T(8,128)(2,1)S(1)}, bf16[3,512,128]{2,1,0:T(8,128)(2,1)S(1)}, bf16[3,512,128]{2...) custom-call(s32[24]{0:T(128)S(1)} %slice_bitcast_fusion.1.order, ...), custom_call_target="tpu_custom_call" | custom-call | flops 4831838208 | bytes 12582912 | tf_op jit(solution)/shard_map/pallas_call | solution.py:306
  145.4 0.1 add_convert_fusion.5
  145.5 0.1 collective-permute-start.22
  145.6 0.1 add_convert_fusion.2
  145.8 2.7 %collective-permute-start.25 = (bf16[3,512,128]{2,1,0:T(8,128)(2,1)S(1)}, bf16[3,512,128]{2,1,0:T(8,128)(2,1)S(1)}, u32[]{:S(2)}, u32[]{:S(2)}) collective-permute-start(bf16[3,512,128]{2,1,0:T(8,128)(2,1)S(1)} %add_convert_fusion.2), channel_id=1, source_target_pairs={{0,7},{1,0},{2,1},{3,2},{4,3},{5,4},{6,5},{7,6},{8,15},{9,8},{10,9... | collective-permute-start | bytes 1179656 | tf_op jit(solution)/shard_map/ppermute | solution.py:68
  148.5 8.3 %collective-permute-done.22 = bf16[3,512,128]{2,1,0:T(8,128)(2,1)S(1)} collective-permute-done((bf16[3,512,128]{2,1,0:T(8,128)(2,1)S(1)}, bf16[3,512,128]{2,1,0:T(8,128)(2,1)S(1)}, u32[]{:S(2)}, u32[]{:S(2)}) %collective-permute-start.22) | collective-permute-done | bytes 393248 | tf_op jit(solution)/shard_map/ppermute | solution.py:68
  156.8 0.1 add_convert_fusion.4
  156.9 0.1 collective-permute-start.23
  157.0 0.1 add_convert_fusion.1
  157.1 2.7 %collective-permute-start.26 = (bf16[3,512,128]{2,1,0:T(8,128)(2,1)S(1)}, bf16[3,512,128]{2,1,0:T(8,128)(2,1)S(1)}, u32[]{:S(2)}, u32[]{:S(2)}) collective-permute-start(bf16[3,512,128]{2,1,0:T(8,128)(2,1)S(1)} %add_convert_fusion.1), channel_id=1, source_target_pairs={{0,7},{1,0},{2,1},{3,2},{4,3},{5,4},{6,5},{7,6},{8,15},{9,8},{10,9... | collective-permute-start | bytes 1179656 | tf_op jit(solution)/shard_map/ppermute | solution.py:68
  159.8 7.4 %collective-permute-done.23 = bf16[3,512,128]{2,1,0:T(8,128)(2,1)S(1)} collective-permute-done((bf16[3,512,128]{2,1,0:T(8,128)(2,1)S(1)}, bf16[3,512,128]{2,1,0:T(8,128)(2,1)S(1)}, u32[]{:S(2)}, u32[]{:S(2)}) %collective-permute-start.23) | collective-permute-done | bytes 393248 | tf_op jit(solution)/shard_map/ppermute | solution.py:68
  167.2 0.1 add_convert_fusion.3
  167.3 0.1 collective-permute-start.24
  167.4 9.3 %collective-permute-done.24 = bf16[3,512,128]{2,1,0:T(8,128)(2,1)S(1)} collective-permute-done((bf16[3,512,128]{2,1,0:T(8,128)(2,1)S(1)}, bf16[3,512,128]{2,1,0:T(8,128)(2,1)S(1)}, u32[]{:S(2)}, u32[]{:S(2)}) %collective-permute-start.24) | collective-permute-done | bytes 393248 | tf_op jit(solution)/shard_map/ppermute | solution.py:68
  176.7 0.2 add_convert_fusion
  176.9 5.5 %collective-permute-start.27 = (bf16[3,256,128]{2,1,0:T(8,128)(2,1)S(1)}, bf16[3,256,128]{2,1,0:T(8,128)(2,1)S(1)}, u32[]{:S(2)}, u32[]{:S(2)}) collective-permute-start(bf16[3,256,128]{2,1,0:T(8,128)(2,1)S(1)} %get-tuple-element.65), channel_id=1, source_target_pairs={{0,0},{1,129},{2,34},{3,163},{4,68},{5,197},{6,102},{7,231},{8,16}... | collective-permute-start | bytes 589832 | tf_op jit(solution)/shard_map/ppermute | solution.py:386
  182.4 0.1 collective-permute-start.28
  182.5 3.2 %collective-permute-done.27 = bf16[3,256,128]{2,1,0:T(8,128)(2,1)S(1)} collective-permute-done((bf16[3,256,128]{2,1,0:T(8,128)(2,1)S(1)}, bf16[3,256,128]{2,1,0:T(8,128)(2,1)S(1)}, u32[]{:S(2)}, u32[]{:S(2)}) %collective-permute-start.27) | collective-permute-done | bytes 196640 | tf_op jit(solution)/shard_map/ppermute | solution.py:386
  185.7 1.4 collective-permute-done.28
  187.1 5.3 %collective-permute-start.29 = (bf16[3,256,128]{2,1,0:T(8,128)(2,1)S(1)}, bf16[3,256,128]{2,1,0:T(8,128)(2,1)S(1)}, u32[]{:S(2)}, u32[]{:S(2)}) collective-permute-start(bf16[3,256,128]{2,1,0:T(8,128)(2,1)S(1)} %add_convert_fusion.6), channel_id=1, source_target_pairs={{0,0},{1,1},{2,6},{3,7},{4,4},{5,5},{6,2},{7,3},{8,8},{9,9},{10,14... | collective-permute-start | bytes 589832 | tf_op jit(solution)/shard_map/ppermute | solution.py:388
  192.5 9.0 %collective-permute-done.29 = bf16[3,256,128]{2,1,0:T(8,128)(2,1)S(1)} collective-permute-done((bf16[3,256,128]{2,1,0:T(8,128)(2,1)S(1)}, bf16[3,256,128]{2,1,0:T(8,128)(2,1)S(1)}, u32[]{:S(2)}, u32[]{:S(2)}) %collective-permute-start.29) | collective-permute-done | bytes 196640 | tf_op jit(solution)/shard_map/ppermute | solution.py:388
  201.4 0.7 copy.6
  (47 shorter events, 0.4 us)
Async XLA Ops:
  6.5 47.0 %copy-start = (bf16[1,128,4096]{2,1,0:T(8,128)(2,1)S(1)}, bf16[1,128,4096]{2,1,0:T(8,128)(2,1)}, u32[]{:S(2)}) copy-start(bf16[1,128,4096]{2,1,0:T(8,128)(2,1)} %param.4) | copy-start | bytes 3145732
  6.5 99.4 %all-gather.2.cloned.1.call-start = ((), (), s32[]{:S(2)}) async-start(), calls=%async_computation.2 | async-start | bytes 3538944 | tf_op jit(solution)/shard_map/all_gather | solution.py:360
  6.5 32.5 %collective-permute-start.2 = (bf16[128,4096]{1,0:T(8,128)(2,1)}, bf16[128,4096]{1,0:T(8,128)(2,1)S(1)}, u32[]{:S(2)}, u32[]{:S(2)}) collective-permute-start(bf16[128,4096]{1,0:T(8,128)(2,1)} %bitcast.36), channel_id=1, source_target_pairs={{0,32},{32,64},{64,96},{96,0},{1,33},{33,65},{65,97},{97,1},{2,34}... | collective-permute-start | bytes 3145736 | tf_op jit(solution)/shard_map/ppermute | solution.py:68
  7.8 31.3 %collective-permute-start.3 = (bf16[128,4096]{1,0:T(8,128)(2,1)}, bf16[128,4096]{1,0:T(8,128)(2,1)S(1)}, u32[]{:S(2)}, u32[]{:S(2)}) collective-permute-start(bf16[128,4096]{1,0:T(8,128)(2,1)} %bitcast.37), channel_id=1, source_target_pairs={{0,96},{32,0},{64,32},{96,64},{1,97},{33,1},{65,33},{97,65},{2,98}... | collective-permute-start | bytes 3145736 | tf_op jit(solution)/shard_map/ppermute | solution.py:68
  8.0 31.1 %collective-permute-start.4 = (bf16[128,4096]{1,0:T(8,128)(2,1)}, bf16[128,4096]{1,0:T(8,128)(2,1)}, u32[]{:S(2)}, u32[]{:S(2)}) collective-permute-start(bf16[128,4096]{1,0:T(8,128)(2,1)} %bitcast.38), channel_id=1, source_target_pairs={{0,128},{128,0},{1,129},{129,1},{2,130},{130,2},{3,131},{131,3},{4... | collective-permute-start | bytes 3145736 | tf_op jit(solution)/shard_map/ppermute | solution.py:68
  10.0 91.0 %copy-start.10 = (s32[1,48]{1,0:T(1,128)}, s32[1,48]{1,0:T(1,128)S(1)}, u32[]{:S(2)}) copy-start(s32[1,48]{1,0:T(1,128)S(1)} %constant_dynamic-slice_fusion) | copy-start | bytes 580
  12.9 25.4 %collective-permute-start = (bf16[512,384]{1,0:T(8,128)(2,1)}, bf16[512,384]{1,0:T(8,128)(2,1)S(1)}, u32[]{:S(2)}, u32[]{:S(2)}) collective-permute-start(bf16[512,384]{1,0:T(8,128)(2,1)} %shard_map.46), channel_id=1, source_target_pairs={{0,0},{128,1},{32,2},{160,3},{64,4},{192,5},{96,6},{224,7},{16,8},... | collective-permute-start | bytes 1179656 | tf_op jit(solution)/shard_map/ppermute | solution.py:359
  38.3 0.8 copy-start.9
  39.1 28.1 %collective-permute-start.10 = (bf16[128,4096]{1,0:T(8,128)(2,1)S(1)}, bf16[128,4096]{1,0:T(8,128)(2,1)}, u32[]{:S(2)}, u32[]{:S(2)}) collective-permute-start(bf16[128,4096]{1,0:T(8,128)(2,1)S(1)} %collective-permute-done.3), channel_id=1, source_target_pairs={{0,128},{128,0},{1,129},{129,1},{2,130},{130,2},{3,131},{131,3},{4... | collective-permute-start | bytes 3145736 | tf_op jit(solution)/shard_map/ppermute | solution.py:68
  39.2 28.0 %collective-permute-start.9 = (bf16[128,4096]{1,0:T(8,128)(2,1)S(1)}, bf16[128,4096]{1,0:T(8,128)(2,1)}, u32[]{:S(2)}, u32[]{:S(2)}) collective-permute-start(bf16[128,4096]{1,0:T(8,128)(2,1)S(1)} %collective-permute-done.3), channel_id=1, source_target_pairs={{0,96},{32,0},{64,32},{96,64},{1,97},{33,1},{65,33},{97,65},{2,98}... | collective-permute-start | bytes 3145736 | tf_op jit(solution)/shard_map/ppermute | solution.py:68
  42.2 30.2 %collective-permute-start.8 = (bf16[128,4096]{1,0:T(8,128)(2,1)}, bf16[128,4096]{1,0:T(8,128)(2,1)}, u32[]{:S(2)}, u32[]{:S(2)}) collective-permute-start(bf16[128,4096]{1,0:T(8,128)(2,1)} %collective-permute-done.4), channel_id=1, source_target_pairs={{0,32},{32,64},{64,96},{96,0},{1,33},{33,65},{65,97},{97,1},{2,34}... | collective-permute-start | bytes 3145736 | tf_op jit(solution)/shard_map/ppermute | solution.py:68
  42.2 30.2 %all-to-all-start = ((bf16[16,128,128]{2,1,0:T(8,128)(2,1)}), bf16[16,128,128]{2,1,0:T(8,128)(2,1)}, u32[]{:S(2)}, u32[]{:S(2)}) async-start(bf16[16,128,128]{2,1,0:T(8,128)(2,1)} %bitcast.54), calls=%async_computation | async-start | bytes 1048576 | tf_op jit(solution)/shard_map/all_to_all | solution.py:361
  53.6 22.5 %collective-permute-start.1 = (bf16[128,4096]{1,0:T(8,128)(2,1)S(1)}, bf16[128,4096]{1,0:T(8,128)(2,1)}, u32[]{:S(2)}, u32[]{:S(2)}) collective-permute-start(bf16[128,4096]{1,0:T(8,128)(2,1)S(1)} %bitcast.39), channel_id=1, source_target_pairs={{0,16},{16,0},{1,17},{17,1},{2,18},{18,2},{3,19},{19,3},{4,20},{20... | collective-permute-start | bytes 3145736 | tf_op jit(solution)/shard_map/ppermute | solution.py:68
  56.6 22.4 %collective-permute-start.6 = (bf16[128,4096]{1,0:T(8,128)(2,1)S(1)}, bf16[128,4096]{1,0:T(8,128)(2,1)}, u32[]{:S(2)}, u32[]{:S(2)}) collective-permute-start(bf16[128,4096]{1,0:T(8,128)(2,1)S(1)} %collective-permute-done.3), channel_id=1, source_target_pairs={{0,16},{16,0},{1,17},{17,1},{2,18},{18,2},{3,19},{19,3},{4,20},{20... | collective-permute-start | bytes 3145736 | tf_op jit(solution)/shard_map/ppermute | solution.py:68
  67.2 32.5 %collective-permute-start.7 = (bf16[128,4096]{1,0:T(8,128)(2,1)}, bf16[128,4096]{1,0:T(8,128)(2,1)}, u32[]{:S(2)}, u32[]{:S(2)}) collective-permute-start(bf16[128,4096]{1,0:T(8,128)(2,1)} %collective-permute-done.4), channel_id=1, source_target_pairs={{0,16},{16,0},{1,17},{17,1},{2,18},{18,2},{3,19},{19,3},{4,20},{20... | collective-permute-start | bytes 3145736 | tf_op jit(solution)/shard_map/ppermute | solution.py:68
  67.2 34.1 %collective-permute-start.5 = (bf16[128,4096]{1,0:T(8,128)(2,1)S(1)}, bf16[128,4096]{1,0:T(8,128)(2,1)}, u32[]{:S(2)}, u32[]{:S(2)}) collective-permute-start(bf16[128,4096]{1,0:T(8,128)(2,1)S(1)} %collective-permute-done.2), channel_id=1, source_target_pairs={{0,16},{16,0},{1,17},{17,1},{2,18},{18,2},{3,19},{19,3},{4,20},{20... | collective-permute-start | bytes 3145736 | tf_op jit(solution)/shard_map/ppermute | solution.py:68
  74.6 16.9 %collective-permute-start.14 = (bf16[48,4096]{1,0:T(8,128)(2,1)}, bf16[48,4096]{1,0:T(8,128)(2,1)S(1)}, u32[]{:S(2)}, u32[]{:S(2)}) collective-permute-start(bf16[48,4096]{1,0:T(8,128)(2,1)} %get-tuple-element.42), channel_id=1, source_target_pairs={{0,32},{32,64},{64,96},{96,0},{1,33},{33,65},{65,97},{97,1},{2,34}... | collective-permute-start | bytes 1179656 | tf_op jit(solution)/shard_map/ppermute | solution.py:68
  76.0 15.7 %collective-permute-start.15 = (bf16[48,4096]{1,0:T(8,128)(2,1)}, bf16[48,4096]{1,0:T(8,128)(2,1)}, u32[]{:S(2)}, u32[]{:S(2)}) collective-permute-start(bf16[48,4096]{1,0:T(8,128)(2,1)} %get-tuple-element.43), channel_id=1, source_target_pairs={{0,96},{32,0},{64,32},{96,64},{1,97},{33,1},{65,33},{97,65},{2,98}... | collective-permute-start | bytes 1179656 | tf_op jit(solution)/shard_map/ppermute | solution.py:68
  79.1 12.1 %collective-permute-start.16 = (bf16[32,4096]{1,0:T(8,128)(2,1)}, bf16[32,4096]{1,0:T(8,128)(2,1)}, u32[]{:S(2)}, u32[]{:S(2)}) collective-permute-start(bf16[32,4096]{1,0:T(8,128)(2,1)} %get-tuple-element.44), channel_id=1, source_target_pairs={{0,128},{128,0},{1,129},{129,1},{2,130},{130,2},{3,131},{131,3},{4... | collective-permute-start | bytes 786440 | tf_op jit(solution)/shard_map/ppermute | solution.py:68
  81.6 18.1 %all-to-all-start.1 = ((bf16[16,128,128]{2,1,0:T(8,128)(2,1)}), bf16[16,128,128]{2,1,0:T(8,128)(2,1)}, u32[]{:S(2)}, u32[]{:S(2)}) async-start(bf16[16,128,128]{2,1,0:T(8,128)(2,1)} %all-to-all-done), calls=%async_computation.1 | async-start | bytes 1048576 | tf_op jit(solution)/shard_map/all_to_all | solution.py:361
  91.1 14.8 %collective-permute-start.11 = (bf16[128,4096]{1,0:T(8,128)(2,1)}, bf16[128,4096]{1,0:T(8,128)(2,1)}, u32[]{:S(2)}, u32[]{:S(2)}) collective-permute-start(bf16[128,4096]{1,0:T(8,128)(2,1)} %collective-permute-done.8.refs_0_), channel_id=1, source_target_pairs={{0,16},{16,0},{1,17},{17,1},{2,18},{18,2},{3,19},{19,3},{4,20},{20... | collective-permute-start | bytes 3145736 | tf_op jit(solution)/shard_map/ppermute | solution.py:68
  91.6 39.6 %copy-start.1 = (bf16[48,4096]{1,0:T(8,128)(2,1)}, bf16[48,4096]{1,0:T(8,128)(2,1)S(1)}, u32[]{:S(2)}) copy-start(bf16[48,4096]{1,0:T(8,128)(2,1)S(1)} %collective-permute-done.14) | copy-start | bytes 1179652
  91.6 14.3 %collective-permute-start.12 = (bf16[128,4096]{1,0:T(8,128)(2,1)}, bf16[128,4096]{1,0:T(8,128)(2,1)}, u32[]{:S(2)}, u32[]{:S(2)}) collective-permute-start(bf16[128,4096]{1,0:T(8,128)(2,1)} %collective-permute-done.9.refs_2_), channel_id=1, source_target_pairs={{0,16},{16,0},{1,17},{17,1},{2,18},{18,2},{3,19},{19,3},{4,20},{20... | collective-permute-start | bytes 3145736 | tf_op jit(solution)/shard_map/ppermute | solution.py:68
  91.7 14.2 %collective-permute-start.13 = (bf16[128,4096]{1,0:T(8,128)(2,1)}, bf16[128,4096]{1,0:T(8,128)(2,1)}, u32[]{:S(2)}, u32[]{:S(2)}) collective-permute-start(bf16[128,4096]{1,0:T(8,128)(2,1)} %collective-permute-done.10.refs_1_), channel_id=1, source_target_pairs={{0,16},{16,0},{1,17},{17,1},{2,18},{18,2},{3,19},{19,3},{4,20},{20... | collective-permute-start | bytes 3145736 | tf_op jit(solution)/shard_map/ppermute | solution.py:68
  99.7 2.8 %collective-permute-start.19 = (bf16[32,4096]{1,0:T(8,128)(2,1)}, bf16[32,4096]{1,0:T(8,128)(2,1)}, u32[]{:S(2)}, u32[]{:S(2)}) collective-permute-start(bf16[32,4096]{1,0:T(8,128)(2,1)} %collective-permute-done.16), channel_id=1, source_target_pairs={{0,16},{16,0},{1,17},{17,1},{2,18},{18,2},{3,19},{19,3},{4,20},{20... | collective-permute-start | bytes 786440 | tf_op jit(solution)/shard_map/ppermute | solution.py:68
  101.3 3.1 %collective-permute-start.17 = (bf16[48,4096]{1,0:T(8,128)(2,1)S(1)}, bf16[48,4096]{1,0:T(8,128)(2,1)S(1)}, u32[]{:S(2)}, u32[]{:S(2)}) collective-permute-start(bf16[48,4096]{1,0:T(8,128)(2,1)S(1)} %collective-permute-done.14), channel_id=1, source_target_pairs={{0,16},{16,0},{1,17},{17,1},{2,18},{18,2},{3,19},{19,3},{4,20},{20... | collective-permute-start | bytes 1179656 | tf_op jit(solution)/shard_map/ppermute | solution.py:68
  102.5 2.6 %collective-permute-start.18 = (bf16[48,4096]{1,0:T(8,128)(2,1)}, bf16[48,4096]{1,0:T(8,128)(2,1)S(1)}, u32[]{:S(2)}, u32[]{:S(2)}) collective-permute-start(bf16[48,4096]{1,0:T(8,128)(2,1)} %collective-permute-done.15), channel_id=1, source_target_pairs={{0,16},{16,0},{1,17},{17,1},{2,18},{18,2},{3,19},{19,3},{4,20},{20... | collective-permute-start | bytes 1179656 | tf_op jit(solution)/shard_map/ppermute | solution.py:68
  104.4 0.7 copy-start.3
  105.1 0.8 copy-start.6
  105.9 1.0 copy-start.4
  106.9 1.0 copy-start.7
  107.9 0.9 copy-start.8
  108.9 25.0 %copy-start.5 = (bf16[48,4096]{1,0:T(8,128)(2,1)S(1)}, bf16[48,4096]{1,0:T(8,128)(2,1)}, u32[]{:S(2)}) copy-start(bf16[48,4096]{1,0:T(8,128)(2,1)} %copy-done.3) | copy-start | bytes 1179652
  131.2 14.2 %collective-permute-start.20 = (bf16[3,512,128]{2,1,0:T(8,128)(2,1)S(1)}, bf16[3,512,128]{2,1,0:T(8,128)(2,1)S(1)}, u32[]{:S(2)}, u32[]{:S(2)}) collective-permute-start(bf16[3,512,128]{2,1,0:T(8,128)(2,1)S(1)} %get-tuple-element.48), channel_id=1, source_target_pairs={{0,1},{1,2},{2,3},{3,4},{4,5},{5,6},{6,7},{7,0},{8,9},{9,10},{10,1... | collective-permute-start | bytes 1179656 | tf_op jit(solution)/shard_map/ppermute | solution.py:68
  131.3 14.2 %collective-permute-start.21 = (bf16[3,512,128]{2,1,0:T(8,128)(2,1)S(1)}, bf16[3,512,128]{2,1,0:T(8,128)(2,1)S(1)}, u32[]{:S(2)}, u32[]{:S(2)}) collective-permute-start(bf16[3,512,128]{2,1,0:T(8,128)(2,1)S(1)} %get-tuple-element.49), channel_id=1, source_target_pairs={{0,7},{1,0},{2,1},{3,2},{4,3},{5,4},{6,5},{7,6},{8,15},{9,8},{10,9... | collective-permute-start | bytes 1179656 | tf_op jit(solution)/shard_map/ppermute | solution.py:68
  133.9 1.0 copy-start.2
  145.5 11.2 %collective-permute-start.22 = (bf16[3,512,128]{2,1,0:T(8,128)(2,1)S(1)}, bf16[3,512,128]{2,1,0:T(8,128)(2,1)S(1)}, u32[]{:S(2)}, u32[]{:S(2)}) collective-permute-start(bf16[3,512,128]{2,1,0:T(8,128)(2,1)S(1)} %add_convert_fusion.5), channel_id=1, source_target_pairs={{0,1},{1,2},{2,3},{3,4},{4,5},{5,6},{6,7},{7,0},{8,9},{9,10},{10,1... | collective-permute-start | bytes 1179656 | tf_op jit(solution)/shard_map/ppermute | solution.py:68
  145.8 11.2 %collective-permute-start.25 = (bf16[3,512,128]{2,1,0:T(8,128)(2,1)S(1)}, bf16[3,512,128]{2,1,0:T(8,128)(2,1)S(1)}, u32[]{:S(2)}, u32[]{:S(2)}) collective-permute-start(bf16[3,512,128]{2,1,0:T(8,128)(2,1)S(1)} %add_convert_fusion.2), channel_id=1, source_target_pairs={{0,7},{1,0},{2,1},{3,2},{4,3},{5,4},{6,5},{7,6},{8,15},{9,8},{10,9... | collective-permute-start | bytes 1179656 | tf_op jit(solution)/shard_map/ppermute | solution.py:68
  156.9 10.3 %collective-permute-start.23 = (bf16[3,512,128]{2,1,0:T(8,128)(2,1)S(1)}, bf16[3,512,128]{2,1,0:T(8,128)(2,1)S(1)}, u32[]{:S(2)}, u32[]{:S(2)}) collective-permute-start(bf16[3,512,128]{2,1,0:T(8,128)(2,1)S(1)} %add_convert_fusion.4), channel_id=1, source_target_pairs={{0,1},{1,2},{2,3},{3,4},{4,5},{5,6},{6,7},{7,0},{8,9},{9,10},{10,1... | collective-permute-start | bytes 1179656 | tf_op jit(solution)/shard_map/ppermute | solution.py:68
  157.1 10.3 %collective-permute-start.26 = (bf16[3,512,128]{2,1,0:T(8,128)(2,1)S(1)}, bf16[3,512,128]{2,1,0:T(8,128)(2,1)S(1)}, u32[]{:S(2)}, u32[]{:S(2)}) collective-permute-start(bf16[3,512,128]{2,1,0:T(8,128)(2,1)S(1)} %add_convert_fusion.1), channel_id=1, source_target_pairs={{0,7},{1,0},{2,1},{3,2},{4,3},{5,4},{6,5},{7,6},{8,15},{9,8},{10,9... | collective-permute-start | bytes 1179656 | tf_op jit(solution)/shard_map/ppermute | solution.py:68
  167.3 9.4 %collective-permute-start.24 = (bf16[3,512,128]{2,1,0:T(8,128)(2,1)S(1)}, bf16[3,512,128]{2,1,0:T(8,128)(2,1)S(1)}, u32[]{:S(2)}, u32[]{:S(2)}) collective-permute-start(bf16[3,512,128]{2,1,0:T(8,128)(2,1)S(1)} %add_convert_fusion.3), channel_id=1, source_target_pairs={{0,1},{1,2},{2,3},{3,4},{4,5},{5,6},{6,7},{7,0},{8,9},{9,10},{10,1... | collective-permute-start | bytes 1179656 | tf_op jit(solution)/shard_map/ppermute | solution.py:68
  176.9 8.8 %collective-permute-start.27 = (bf16[3,256,128]{2,1,0:T(8,128)(2,1)S(1)}, bf16[3,256,128]{2,1,0:T(8,128)(2,1)S(1)}, u32[]{:S(2)}, u32[]{:S(2)}) collective-permute-start(bf16[3,256,128]{2,1,0:T(8,128)(2,1)S(1)} %get-tuple-element.65), channel_id=1, source_target_pairs={{0,0},{1,129},{2,34},{3,163},{4,68},{5,197},{6,102},{7,231},{8,16}... | collective-permute-start | bytes 589832 | tf_op jit(solution)/shard_map/ppermute | solution.py:386
  182.4 4.7 %collective-permute-start.28 = (bf16[3,256,128]{2,1,0:T(8,128)(2,1)S(1)}, bf16[3,256,128]{2,1,0:T(8,128)(2,1)S(1)}, u32[]{:S(2)}, u32[]{:S(2)}) collective-permute-start(bf16[3,256,128]{2,1,0:T(8,128)(2,1)S(1)} %get-tuple-element.66), channel_id=1, source_target_pairs={{0,16},{1,145},{2,50},{3,179},{4,84},{5,213},{6,118},{7,247},{8,0}... | collective-permute-start | bytes 589832 | tf_op jit(solution)/shard_map/ppermute | solution.py:386
  187.1 14.3 %collective-permute-start.29 = (bf16[3,256,128]{2,1,0:T(8,128)(2,1)S(1)}, bf16[3,256,128]{2,1,0:T(8,128)(2,1)S(1)}, u32[]{:S(2)}, u32[]{:S(2)}) collective-permute-start(bf16[3,256,128]{2,1,0:T(8,128)(2,1)S(1)} %add_convert_fusion.6), channel_id=1, source_target_pairs={{0,0},{1,1},{2,6},{3,7},{4,4},{5,5},{6,2},{7,3},{8,8},{9,9},{10,14... | collective-permute-start | bytes 589832 | tf_op jit(solution)/shard_map/ppermute | solution.py:388
Sparse Core Ops, SparseCore 0:
  39.2 59.0 all-gather.1

commit v6 on v5

--- a/solution.py
+++ b/solution.py
@@ -19,14 +19,16 @@
 CUT_A, CUT_B = 48, 96
 CUTS = ((0, CUT_A), (CUT_A, CUT_B), (CUT_B, PATCHES))
 STEP = 4
-FAR = (4, 5)
-NEAR = (3, 6, 2, 7, 1, 0)
+FAR = (4,)
+NEAR_A = (3, 5)
+NEAR_B = (2, 6, 1, 7, 0)
 CUT_FLOPS = 3 * 10**10
 WIDTH = 4096
 COLS = 3 * HEAD_DIM
 ROWS = FRAMES * PATCHES
 GROUP = 16
 CHUNK = WIDTH // 8
+SHARE = jax.ShapeDtypeStruct((2, 3, CHUNK // 2, HEAD_DIM), jnp.bfloat16)
 
 SAME_CORE = ((0, 0), (0, 1), (0, -1), (1, 0), (0, 2), (1, 1), (1, -1), (1, 2))
 SLOTS = [(dy, dx, dc) for dy, dx in SAME_CORE for dc in (0, 1)]
@@ -267,17 +269,20 @@
 
 def weigh(turned, rows, out):
     value = jnp.dot(turned[...], rows, preferred_element_type=jnp.float32)
-    for j in range(3):
-        out[j] = value[j * HEAD_DIM : (j + 1) * HEAD_DIM].T.astype(jnp.bfloat16)
-
-
-def near_kernel(count, order, turned_ref, *refs):
-    buffers, out = refs[:count], refs[count : count + len(NEAR)]
-    tokens, turned, t_sem, x_sem = refs[count + len(NEAR) :]
+    for half in range(2):
+        rows = slice(half * CHUNK // 2, (half + 1) * CHUNK // 2)
+        for j in range(3):
+            part = value[j * HEAD_DIM : (j + 1) * HEAD_DIM, rows]
+            out[half, j] = part.T.astype(jnp.bfloat16)
+
+
+def near_kernel(count, near, order, turned_ref, *refs):
+    buffers, out = refs[:count], refs[count : count + len(near)]
+    tokens, turned, t_sem, x_sem = refs[count + len(near) :]
     load = pltpu.make_async_copy(turned_ref, turned, t_sem.at[0])
     load.start()
     copies = []
-    for index, ahead in enumerate(NEAR):
+    for index, ahead in enumerate(near):
         columns = pl.ds(pl.multiple_of(order[16 + ahead] * CHUNK, CHUNK), CHUNK)
         copies.append([])
         for part, (buffer, at, slot, first, groups) in enumerate(PARTS):
@@ -291,33 +296,32 @@
     for copy in copies[0] + copies[1]:
         copy.start()
     load.wait()
-    for index in range(len(NEAR)):
+    for index in range(len(near)):
         for copy in copies[index]:
             copy.wait()
-        if index + 2 < len(NEAR):
+        if index + 2 < len(near):
             for copy in copies[index + 2]:
                 copy.start()
         weigh(turned, tokens[index].reshape(ROWS, CHUNK), out[index])
 
 
-def near_shares(order, turned, buffers):
+def near_shares(order, turned, buffers, near):
     count = len(buffers)
-    share = jax.ShapeDtypeStruct((3, CHUNK, HEAD_DIM), jnp.bfloat16)
     return pl.pallas_call(
-        functools.partial(near_kernel, count),
-        out_shape=[share] * len(NEAR),
+        functools.partial(near_kernel, count, near),
+        out_shape=[SHARE] * len(near),
         in_specs=[SMEM] + [HBM] * (1 + count),
-        out_specs=[VMEM] * len(NEAR),
+        out_specs=[VMEM] * len(near),
         scratch_shapes=[
-            pltpu.VMEM((len(NEAR), PATCHES // GROUP, FRAMES, GROUP, CHUNK), jnp.bfloat16),
+            pltpu.VMEM((len(near), PATCHES // GROUP, FRAMES, GROUP, CHUNK), jnp.bfloat16),
             pltpu.VMEM((COLS, ROWS), jnp.bfloat16),
             pltpu.SemaphoreType.DMA((1,)),
-            pltpu.SemaphoreType.DMA((len(NEAR), len(PARTS))),
+            pltpu.SemaphoreType.DMA((len(near), len(PARTS))),
         ],
         compiler_params=pltpu.CompilerParams(vmem_limit_bytes=44 * 2**20),
         cost_estimate=pl.CostEstimate(
-            flops=2 * ROWS * len(NEAR) * CHUNK * COLS,
-            bytes_accessed=2 * ROWS * len(NEAR) * CHUNK,
+            flops=2 * ROWS * len(near) * CHUNK * COLS,
+            bytes_accessed=2 * ROWS * len(near) * CHUNK,
             transcendentals=0,
         ),
     )(order, turned, *buffers)
@@ -326,10 +330,9 @@
 def far_shares(order, mask, w, g, buffers):
     count = len(buffers)
     groups = PATCHES // GROUP
-    share = jax.ShapeDtypeStruct((3, CHUNK, HEAD_DIM), jnp.bfloat16)
     return pl.pallas_call(
         functools.partial(share_kernel, count),
-        out_shape=[jax.ShapeDtypeStruct((COLS, ROWS), jnp.bfloat16)] + [share] * len(FAR),
+        out_shape=[jax.ShapeDtypeStruct((COLS, ROWS), jnp.bfloat16)] + [SHARE] * len(FAR),
         in_specs=[SMEM, VMEM] + [HBM] * (2 + count),
         out_specs=[HBM] + [VMEM] * len(FAR),
         scratch_shapes=[
@@ -369,20 +372,23 @@
         [buffer.reshape(-1, GROUP, WIDTH) for buffer in buffers] for buffers in steps
     )
     order, buffers = table[:24], first + second + third
-    turned, up, down = far_shares(order, visible(table[24:40]), w, g, buffers)
-    up, down, near = lax.optimization_barrier(
-        (shift(up, "z", 1), shift(down, "z", -1), near_shares(order, turned, buffers))
+    turned, far = far_shares(order, visible(table[24:40]), w, g, buffers)
+    beside = lax.optimization_barrier
+    shares = lambda near: near_shares(order, turned, buffers, near)
+    up, down, (share_3, share_5) = beside(
+        (shift(far[0], "z", 1), shift(far[1], "z", -1), shares(NEAR_A))
     )
+    up = jnp.stack((add(up, share_3[0]), share_3[1]))
+    down = jnp.stack((share_5[0], add(down, share_5[1])))
+    up, down, near = beside((shift(up, "z", 1), shift(down, "z", -1), shares(NEAR_B)))
     for step in (0, 2):
         up = shift(add(up, near[step]), "z", 1)
         down = shift(add(down, near[step + 1]), "z", -1)
-    up = shift(add(up, near[4]), "z", 1)
-    mine = add(up, down, near[5])
-    mine = mine.reshape(3, 2, CHUNK // 2, HEAD_DIM)
+    mine = add(up, down, near[4])
     yh = lax.axis_index("yh")
     total = None
     for flip in range(2):
-        part = lax.dynamic_index_in_dim(mine, (yh + flip) % 2, 1, keepdims=False)
+        part = lax.dynamic_index_in_dim(mine, (yh + flip) % 2, 0, keepdims=False)
         part = lax.ppermute(part, AXES, plane_moves(flip)).astype(jnp.float32)
         total = part if total is None else total + part
     return lax.ppermute(total.astype(jnp.bfloat16), AXES, line_moves()).transpose(1, 0, 2)

time: 210 us -> 207 us (0.986)
  waiting for transfers between devices: 77.9 us -> 65 us
  starting transfers between devices: 69.4 us -> 74.5 us
  Pallas kernels: 37.3 us -> 40 us
    ppermute x26 -> x27, waiting for transfers between devices: 36.5 us -> 23.9 us  [shift(): lax.ppermute(value, axis, [(i, (i + by) % count) for i in range(count)])]
    pallas_call x1 -> x2, Pallas kernels: 10.5 us -> 14.2 us  [near_shares(): pl.pallas_call(functools.partial(near_kernel, count, near), out_shape=[SH...]
    ppermute x26 -> x27, starting transfers between devices: 27.7 us -> 30.2 us  [shift(): lax.ppermute(value, axis, [(i, (i + by) % count) for i in range(count)])]
    unnamed x23 -> x25, local copies, waits for them, and re-layouts: 6.88 us -> 6.65 us
  transfers between devices with their start and end apart: 33 -> 34, of which waited for: 11 -> 11; matrix products, arithmetic and copies ran while one was open for 2% -> 2% of each run, Pallas kernels for 7% -> 9%
where the time goes in v6:
time: 207 us; the launch traced here: 204 us
  starting transfers between devices  74.5 us (36%)
  waiting for transfers between devices  65 us (31%)
  Pallas kernels  40 us (19%)
  between operations  13.7 us (7%)
  local copies, waits for them, and re-layouts  9.01 us (4%)
    ppermute x27, starting transfers between devices, shift(): lax.ppermute(value, axis, [(i, (i + by) % count) for i in range(count)])  30.2 us
    ppermute x27, waiting for transfers between devices, shift(): lax.ppermute(value, axis, [(i, (i + by) % count) for i in range(count)])  23.9 us
    pallas_call x1, Pallas kernels, far_shares(): pl.pallas_call(functools.partial(share_kernel, count), out_shape=[jax.Sha...  21.2 us
    all_to_all x2, starting transfers between devices, local(): lax.all_to_all(value, axes, split_axis=0, concat_axis=0, tiled=True)  20.9 us
    ppermute x1, waiting for transfers between devices, local(): rows_w = lax.ppermute(rows_w, AXES, worker_moves())  15.5 us
    pallas_call x2, Pallas kernels, near_shares(): pl.pallas_call(functools.partial(near_kernel, count, near), out_shape=[SH...  14.2 us
    all_to_all x2, waiting for transfers between devices, local(): lax.all_to_all(value, axes, split_axis=0, concat_axis=0, tiled=True)  12.2 us
    ppermute x1, starting transfers between devices, local(): rows_w = lax.ppermute(rows_w, AXES, worker_moves())  9.82 us
  transfers between devices with their start and end apart: 34, of which 11 were waited for; matrix products, arithmetic and copies ran while one was open for 2% of the time, Pallas kernels for 9%

profile of v6, /device:TPU:3, one launch (start us, length us, event | category | flops | bytes accessed | tf_op | source)
XLA Modules:
  0.0 204.0 jit_solution(536887722469049516)
XLA Ops:
  6.5 1.2 collective-permute-start.2
  7.8 0.3 collective-permute-start.3
  8.0 1.3 collective-permute-start.4
  9.3 0.7 constant_dynamic-slice_fusion
  10.0 0.6 slice.40
  10.6 2.4 %shard_map.46 = bf16[512,384]{1,0:T(8,128)(2,1)} custom-call(s32[1]{0:T(128)} %bitcast.2.start, bf16[3,4096,128]{2,1,0:T(8,128)(2,1)} %bitcast.71), custom_call_target="tpu_custom_call" | custom-call | tf_op jit(solution)/shard_map/pallas_call | solution.py:183
  13.1 9.8 %collective-permute-start = (bf16[512,384]{1,0:T(8,128)(2,1)}, bf16[512,384]{1,0:T(8,128)(2,1)S(1)}, u32[]{:S(2)}, u32[]{:S(2)}) collective-permute-start(bf16[512,384]{1,0:T(8,128)(2,1)} %shard_map.46), channel_id=1, source_target_pairs={{0,0},{128,1},{32,2},{160,3},{64,4},{192,5},{96,6},{224,7},{16,8},... | collective-permute-start | bytes 1179656 | tf_op jit(solution)/shard_map/ppermute | solution.py:362
  22.9 15.5 %collective-permute-done = bf16[512,384]{1,0:T(8,128)(2,1)S(1)} collective-permute-done((bf16[512,384]{1,0:T(8,128)(2,1)}, bf16[512,384]{1,0:T(8,128)(2,1)S(1)}, u32[]{:S(2)}, u32[]{:S(2)}) %collective-permute-start) | collective-permute-done | bytes 393248 | tf_op jit(solution)/shard_map/ppermute | solution.py:362
  38.4 0.7 copy-done.10
  39.2 0.1 collective-permute-start.10
  39.3 2.9 %collective-permute-start.9 = (bf16[128,4096]{1,0:T(8,128)(2,1)S(1)}, bf16[128,4096]{1,0:T(8,128)(2,1)}, u32[]{:S(2)}, u32[]{:S(2)}) collective-permute-start(bf16[128,4096]{1,0:T(8,128)(2,1)S(1)} %collective-permute-done.3), channel_id=1, source_target_pairs={{0,96},{32,0},{64,32},{96,64},{1,97},{33,1},{65,33},{97,65},{2,98}... | collective-permute-start | bytes 3145736 | tf_op jit(solution)/shard_map/ppermute | solution.py:70
  42.2 11.3 %all-to-all-start = ((bf16[16,128,128]{2,1,0:T(8,128)(2,1)}), bf16[16,128,128]{2,1,0:T(8,128)(2,1)}, u32[]{:S(2)}, u32[]{:S(2)}) async-start(bf16[16,128,128]{2,1,0:T(8,128)(2,1)} %bitcast.72), calls=%async_computation | async-start | bytes 1048576 | tf_op jit(solution)/shard_map/all_to_all | solution.py:364
  53.6 3.1 %collective-permute-start.1 = (bf16[128,4096]{1,0:T(8,128)(2,1)S(1)}, bf16[128,4096]{1,0:T(8,128)(2,1)}, u32[]{:S(2)}, u32[]{:S(2)}) collective-permute-start(bf16[128,4096]{1,0:T(8,128)(2,1)S(1)} %bitcast.52), channel_id=1, source_target_pairs={{0,16},{16,0},{1,17},{17,1},{2,18},{18,2},{3,19},{19,3},{4,20},{20... | collective-permute-start | bytes 3145736 | tf_op jit(solution)/shard_map/ppermute | solution.py:70
  56.6 0.1 collective-permute-start.6
  56.7 10.5 %collective-permute-done.10.refs_1_ = bf16[128,4096]{1,0:T(8,128)(2,1)} collective-permute-done((bf16[128,4096]{1,0:T(8,128)(2,1)S(1)}, bf16[128,4096]{1,0:T(8,128)(2,1)}, u32[]{:S(2)}, u32[]{:S(2)}) %collective-permute-start.10) | collective-permute-done | bytes 1048608 | tf_op jit(solution)/shard_map/ppermute | solution.py:70
  67.2 0.5 collective-permute-start.5
  67.7 4.7 %all-to-all-done = bf16[16,128,128]{2,1,0:T(8,128)(2,1)} async-done(((bf16[16,128,128]{2,1,0:T(8,128)(2,1)}), bf16[16,128,128]{2,1,0:T(8,128)(2,1)}, u32[]{:S(2)}, u32[]{:S(2)}) %all-to-all-start) | async-done | bytes 524320 | tf_op jit(solution)/shard_map/all_to_all | solution.py:364
  72.4 2.2 %shard_map.47 = (bf16[48,4096]{1,0:T(8,128)(2,1)}, bf16[48,4096]{1,0:T(8,128)(2,1)}, bf16[32,4096]{1,0:T(8,128)(2,1)}) custom-call(bf16[128,4096]{1,0:T(8,128)(2,1)} %collective-permute-done.8.refs_0_, bf16[128,4096]{1,0:T(8,128)(2,1)} %collective-permute-done.10.refs_1_, bf16[128,4096]{1,0:T(8,128)(2,1)} %collective-permute-done.9.refs_2_), custom_call_target="tpu_custom_call" | custom-call | flops 30000001024 | tf_op jit(solution)/shard_map/pallas_call | solution.py:92
  74.6 1.2 collective-permute-start.14
  75.9 3.1 %collective-permute-start.15 = (bf16[48,4096]{1,0:T(8,128)(2,1)}, bf16[48,4096]{1,0:T(8,128)(2,1)}, u32[]{:S(2)}, u32[]{:S(2)}) collective-permute-start(bf16[48,4096]{1,0:T(8,128)(2,1)} %get-tuple-element.46), channel_id=1, source_target_pairs={{0,96},{32,0},{64,32},{96,64},{1,97},{33,1},{65,33},{97,65},{2,98}... | collective-permute-start | bytes 1179656 | tf_op jit(solution)/shard_map/ppermute | solution.py:70
  79.0 2.5 %collective-permute-start.16 = (bf16[32,4096]{1,0:T(8,128)(2,1)}, bf16[32,4096]{1,0:T(8,128)(2,1)}, u32[]{:S(2)}, u32[]{:S(2)}) collective-permute-start(bf16[32,4096]{1,0:T(8,128)(2,1)} %get-tuple-element.47), channel_id=1, source_target_pairs={{0,128},{128,0},{1,129},{129,1},{2,130},{130,2},{3,131},{131,3},{4... | collective-permute-start | bytes 786440 | tf_op jit(solution)/shard_map/ppermute | solution.py:70
  81.5 9.6 %all-to-all-start.1 = ((bf16[16,128,128]{2,1,0:T(8,128)(2,1)}), bf16[16,128,128]{2,1,0:T(8,128)(2,1)}, u32[]{:S(2)}, u32[]{:S(2)}) async-start(bf16[16,128,128]{2,1,0:T(8,128)(2,1)} %all-to-all-done), calls=%async_computation.1 | async-start | bytes 1048576 | tf_op jit(solution)/shard_map/all_to_all | solution.py:364
  91.1 0.4 collective-permute-start.11
  91.6 0.1 collective-permute-start.12
  91.7 0.4 collective-permute-start.13
  92.2 7.5 %all-to-all-done.1 = bf16[16,128,128]{2,1,0:T(8,128)(2,1)} async-done(((bf16[16,128,128]{2,1,0:T(8,128)(2,1)}), bf16[16,128,128]{2,1,0:T(8,128)(2,1)}, u32[]{:S(2)}, u32[]{:S(2)}) %all-to-all-start.1) | async-done | bytes 524320 | tf_op jit(solution)/shard_map/all_to_all | solution.py:364
  99.7 1.3 collective-permute-start.19
  101.3 0.1 collective-permute-start.17
  101.4 1.1 collective-permute-done.19
  102.5 0.4 collective-permute-start.18
  102.9 0.7 slice_bitcast_fusion.3.order
  103.6 0.8 and_convert_fusion.mask
  104.4 0.8 copy-done.1
  105.1 0.8 copy-done.4
  105.9 1.0 copy-done.2
  106.9 1.0 copy-done.5
  107.9 0.9 copy-done.9
  108.9 21.2 %shard_map.48 = (bf16[384,2048]{1,0:T(8,128)(2,1)}, bf16[2,3,256,128]{3,2,1,0:T(8,128)(2,1)S(1)}) custom-call(s32[24]{0:T(128)S(1)} %slice_bitcast_fusion.3.order, f32[256,256]{1,0:T(8,128)S(1)} %copy-done.9, bf16[4096,384]{1,0:T(8,128)(2,1)} %all-gather.2.cloned.1.call-done.w_ref, bf16[16,8,16,128]{3,2,1,0:T(8,128)(2,1)} %bitcast.6.g_ref, ...), custom_call_target="tpu_custom_call" | custom-call | flops 6442450944 | bytes 16777216 | tf_op jit(solution)/shard_map/pallas_call | solution.py:333
  130.2 0.1 collective-permute-start.20
  130.3 2.7 %collective-permute-start.21 = (bf16[3,256,128]{2,1,0:T(8,128)(2,1)S(1)}, bf16[3,256,128]{2,1,0:T(8,128)(2,1)S(1)}, u32[]{:S(2)}, u32[]{:S(2)}) collective-permute-start(bf16[3,256,128]{2,1,0:T(8,128)(2,1)S(1)} %get-tuple-element.73), channel_id=1, source_target_pairs={{0,7},{1,0},{2,1},{3,2},{4,3},{5,4},{6,5},{7,6},{8,15},{9,8},{10,9... | collective-permute-start | bytes 589832 | tf_op jit(solution)/shard_map/ppermute | solution.py:70
  132.9 4.9 %shard_map.49 = (bf16[2,3,256,128]{3,2,1,0:T(8,128)(2,1)S(1)}, bf16[2,3,256,128]{3,2,1,0:T(8,128)(2,1)S(1)}) custom-call(s32[24]{0:T(128)S(1)} %slice_bitcast_fusion.3.order, bf16[384,2048]{1,0:T(8,128)(2,1)} %get-tuple-element.52.turned_ref, bf16[8,16,4096]{2,1,0:T(8,128)(2,1)S(1)} %bitcast.54, bf16[8,16,4096]{2,1,0:T(8,128)(2,1)} %bitcast.9.refs_1_, ...), custom_call_target="tpu_custom_call" | custom-call | flops 1610612736 | bytes 4194304 | tf_op jit(solution)/shard_map/pallas_call | solution.py:310
  138.0 2.4 %collective-permute-start.23 = (bf16[2,3,256,128]{3,2,1,0:T(8,128)(2,1)S(1)}, bf16[2,3,256,128]{3,2,1,0:T(8,128)(2,1)S(1)}, u32[]{:S(2)}, u32[]{:S(2)}) collective-permute-start(bf16[2,3,256,128]{3,2,1,0:T(8,128)(2,1)S(1)} %pad_maximum_fusion.1), channel_id=1, source_target_pairs={{0,7},{1,0},{2,1},{3,2},{4,3},{5,4},{6,5},{7,6},{8,15},{9,8},{10,9... | collective-permute-start | bytes 1179656 | tf_op jit(solution)/shard_map/ppermute | solution.py:70
  140.5 0.3 collective-permute-start.22
  140.8 9.2 %shard_map.50 = (bf16[2,3,256,128]{3,2,1,0:T(8,128)(2,1)S(1)}, bf16[2,3,256,128]{3,2,1,0:T(8,128)(2,1)S(1)}, bf16[2,3,256,128]{3,2,1,0:T(8,128)(2,1)S(1)}, bf16[...) custom-call(s32[24]{0:T(128)S(1)} %slice_bitcast_fusion.3.order, ...), custom_call_target="tpu_custom_call" | custom-call | flops 4026531840 | bytes 10485760 | tf_op jit(solution)/shard_map/pallas_call | solution.py:310
  150.1 0.8 copy-done.7
  150.8 0.2 collective-permute-done.22
  151.1 0.1 add_convert_fusion.4
  151.2 0.1 collective-permute-start.24
  151.3 0.1 add_convert_fusion.2
  151.4 2.7 %collective-permute-start.26 = (bf16[2,3,256,128]{3,2,1,0:T(8,128)(2,1)S(1)}, bf16[2,3,256,128]{3,2,1,0:T(8,128)(2,1)S(1)}, u32[]{:S(2)}, u32[]{:S(2)}) collective-permute-start(bf16[2,3,256,128]{3,2,1,0:T(8,128)(2,1)S(1)} %add_convert_fusion.2), channel_id=1, source_target_pairs={{0,7},{1,0},{2,1},{3,2},{4,3},{5,4},{6,5},{7,6},{8,15},{9,8},{10,9... | collective-permute-start | bytes 1179656 | tf_op jit(solution)/shard_map/ppermute | solution.py:70
  154.1 6.5 %collective-permute-done.24 = bf16[2,3,256,128]{3,2,1,0:T(8,128)(2,1)S(1)} collective-permute-done((bf16[2,3,256,128]{3,2,1,0:T(8,128)(2,1)S(1)}, bf16[2,3,256,128]{3,2,1,0:T(8,128)(2,1)S(1)}, u32[]{:S(2)}, u32[]{:S(2)}) %collective-permute-start.24) | collective-permute-done | bytes 393248 | tf_op jit(solution)/shard_map/ppermute | solution.py:70
  160.6 0.1 add_convert_fusion.3
  160.7 0.1 collective-permute-start.25
  160.8 0.1 add_convert_fusion.1
  160.9 2.7 %collective-permute-start.27 = (bf16[2,3,256,128]{3,2,1,0:T(8,128)(2,1)S(1)}, bf16[2,3,256,128]{3,2,1,0:T(8,128)(2,1)S(1)}, u32[]{:S(2)}, u32[]{:S(2)}) collective-permute-start(bf16[2,3,256,128]{3,2,1,0:T(8,128)(2,1)S(1)} %add_convert_fusion.1), channel_id=1, source_target_pairs={{0,7},{1,0},{2,1},{3,2},{4,3},{5,4},{6,5},{7,6},{8,15},{9,8},{10,9... | collective-permute-start | bytes 1179656 | tf_op jit(solution)/shard_map/ppermute | solution.py:70
  163.6 5.6 %collective-permute-done.25 = bf16[2,3,256,128]{3,2,1,0:T(8,128)(2,1)S(1)} collective-permute-done((bf16[2,3,256,128]{3,2,1,0:T(8,128)(2,1)S(1)}, bf16[2,3,256,128]{3,2,1,0:T(8,128)(2,1)S(1)}, u32[]{:S(2)}, u32[]{:S(2)}) %collective-permute-start.25) | collective-permute-done | bytes 393248 | tf_op jit(solution)/shard_map/ppermute | solution.py:70
  169.2 0.2 add_convert_fusion
  169.4 6.4 %collective-permute-start.28 = (bf16[3,256,128]{2,1,0:T(8,128)(2,1)S(1)}, bf16[3,256,128]{2,1,0:T(8,128)(2,1)S(1)}, u32[]{:S(2)}, u32[]{:S(2)}) collective-permute-start(bf16[3,256,128]{2,1,0:T(8,128)(2,1)S(1)} %get-tuple-element.71), channel_id=1, source_target_pairs={{0,0},{1,129},{2,34},{3,163},{4,68},{5,197},{6,102},{7,231},{8,16}... | collective-permute-start | bytes 589832 | tf_op jit(solution)/shard_map/ppermute | solution.py:392
  175.8 0.1 collective-permute-start.29
  175.9 3.2 %collective-permute-done.28 = bf16[3,256,128]{2,1,0:T(8,128)(2,1)S(1)} collective-permute-done((bf16[3,256,128]{2,1,0:T(8,128)(2,1)S(1)}, bf16[3,256,128]{2,1,0:T(8,128)(2,1)S(1)}, u32[]{:S(2)}, u32[]{:S(2)}) %collective-permute-start.28) | collective-permute-done | bytes 196640 | tf_op jit(solution)/shard_map/ppermute | solution.py:392
  179.1 1.4 collective-permute-done.29
  180.6 7.1 %collective-permute-start.30 = (bf16[3,256,128]{2,1,0:T(8,128)(2,1)S(1)}, bf16[3,256,128]{2,1,0:T(8,128)(2,1)S(1)}, u32[]{:S(2)}, u32[]{:S(2)}) collective-permute-start(bf16[3,256,128]{2,1,0:T(8,128)(2,1)S(1)} %add_convert_fusion.5), channel_id=1, source_target_pairs={{0,0},{1,1},{2,6},{3,7},{4,4},{5,5},{6,2},{7,3},{8,8},{9,9},{10,14... | collective-permute-start | bytes 589832 | tf_op jit(solution)/shard_map/ppermute | solution.py:394
  187.7 8.8 %collective-permute-done.30 = bf16[3,256,128]{2,1,0:T(8,128)(2,1)S(1)} collective-permute-done((bf16[3,256,128]{2,1,0:T(8,128)(2,1)S(1)}, bf16[3,256,128]{2,1,0:T(8,128)(2,1)S(1)}, u32[]{:S(2)}, u32[]{:S(2)}) %collective-permute-start.30) | collective-permute-done | bytes 196640 | tf_op jit(solution)/shard_map/ppermute | solution.py:394
  196.4 0.7 copy.6
  (58 shorter events, 0.8 us)
Async XLA Ops:
  6.5 47.0 %copy-start = (bf16[1,128,4096]{2,1,0:T(8,128)(2,1)S(1)}, bf16[1,128,4096]{2,1,0:T(8,128)(2,1)}, u32[]{:S(2)}) copy-start(bf16[1,128,4096]{2,1,0:T(8,128)(2,1)} %param.4) | copy-start | bytes 3145732
  6.5 99.4 %all-gather.2.cloned.1.call-start = ((), (), s32[]{:S(2)}) async-start(), calls=%async_computation.2 | async-start | bytes 3538944 | tf_op jit(solution)/shard_map/all_gather | solution.py:363
  6.5 32.7 %collective-permute-start.2 = (bf16[128,4096]{1,0:T(8,128)(2,1)}, bf16[128,4096]{1,0:T(8,128)(2,1)S(1)}, u32[]{:S(2)}, u32[]{:S(2)}) collective-permute-start(bf16[128,4096]{1,0:T(8,128)(2,1)} %bitcast.49), channel_id=1, source_target_pairs={{0,32},{32,64},{64,96},{96,0},{1,33},{33,65},{65,97},{97,1},{2,34}... | collective-permute-start | bytes 3145736 | tf_op jit(solution)/shard_map/ppermute | solution.py:70
  7.8 31.5 %collective-permute-start.3 = (bf16[128,4096]{1,0:T(8,128)(2,1)}, bf16[128,4096]{1,0:T(8,128)(2,1)S(1)}, u32[]{:S(2)}, u32[]{:S(2)}) collective-permute-start(bf16[128,4096]{1,0:T(8,128)(2,1)} %bitcast.50), channel_id=1, source_target_pairs={{0,96},{32,0},{64,32},{96,64},{1,97},{33,1},{65,33},{97,65},{2,98}... | collective-permute-start | bytes 3145736 | tf_op jit(solution)/shard_map/ppermute | solution.py:70
  8.0 31.2 %collective-permute-start.4 = (bf16[128,4096]{1,0:T(8,128)(2,1)}, bf16[128,4096]{1,0:T(8,128)(2,1)}, u32[]{:S(2)}, u32[]{:S(2)}) collective-permute-start(bf16[128,4096]{1,0:T(8,128)(2,1)} %bitcast.51), channel_id=1, source_target_pairs={{0,128},{128,0},{1,129},{129,1},{2,130},{130,2},{3,131},{131,3},{4... | collective-permute-start | bytes 3145736 | tf_op jit(solution)/shard_map/ppermute | solution.py:70
  10.0 91.0 %copy-start.11 = (s32[1,48]{1,0:T(1,128)}, s32[1,48]{1,0:T(1,128)S(1)}, u32[]{:S(2)}) copy-start(s32[1,48]{1,0:T(1,128)S(1)} %constant_dynamic-slice_fusion) | copy-start | bytes 580
  13.1 25.4 %collective-permute-start = (bf16[512,384]{1,0:T(8,128)(2,1)}, bf16[512,384]{1,0:T(8,128)(2,1)S(1)}, u32[]{:S(2)}, u32[]{:S(2)}) collective-permute-start(bf16[512,384]{1,0:T(8,128)(2,1)} %shard_map.46), channel_id=1, source_target_pairs={{0,0},{128,1},{32,2},{160,3},{64,4},{192,5},{96,6},{224,7},{16,8},... | collective-permute-start | bytes 1179656 | tf_op jit(solution)/shard_map/ppermute | solution.py:362
  38.4 0.7 copy-start.10
  39.2 28.0 %collective-permute-start.10 = (bf16[128,4096]{1,0:T(8,128)(2,1)S(1)}, bf16[128,4096]{1,0:T(8,128)(2,1)}, u32[]{:S(2)}, u32[]{:S(2)}) collective-permute-start(bf16[128,4096]{1,0:T(8,128)(2,1)S(1)} %collective-permute-done.3), channel_id=1, source_target_pairs={{0,128},{128,0},{1,129},{129,1},{2,130},{130,2},{3,131},{131,3},{4... | collective-permute-start | bytes 3145736 | tf_op jit(solution)/shard_map/ppermute | solution.py:70
  39.3 27.9 %collective-permute-start.9 = (bf16[128,4096]{1,0:T(8,128)(2,1)S(1)}, bf16[128,4096]{1,0:T(8,128)(2,1)}, u32[]{:S(2)}, u32[]{:S(2)}) collective-permute-start(bf16[128,4096]{1,0:T(8,128)(2,1)S(1)} %collective-permute-done.3), channel_id=1, source_target_pairs={{0,96},{32,0},{64,32},{96,64},{1,97},{33,1},{65,33},{97,65},{2,98}... | collective-permute-start | bytes 3145736 | tf_op jit(solution)/shard_map/ppermute | solution.py:70
  42.2 30.2 %collective-permute-start.8 = (bf16[128,4096]{1,0:T(8,128)(2,1)}, bf16[128,4096]{1,0:T(8,128)(2,1)}, u32[]{:S(2)}, u32[]{:S(2)}) collective-permute-start(bf16[128,4096]{1,0:T(8,128)(2,1)} %collective-permute-done.4), channel_id=1, source_target_pairs={{0,32},{32,64},{64,96},{96,0},{1,33},{33,65},{65,97},{97,1},{2,34}... | collective-permute-start | bytes 3145736 | tf_op jit(solution)/shard_map/ppermute | solution.py:70
  42.2 30.2 %all-to-all-start = ((bf16[16,128,128]{2,1,0:T(8,128)(2,1)}), bf16[16,128,128]{2,1,0:T(8,128)(2,1)}, u32[]{:S(2)}, u32[]{:S(2)}) async-start(bf16[16,128,128]{2,1,0:T(8,128)(2,1)} %bitcast.72), calls=%async_computation | async-start | bytes 1048576 | tf_op jit(solution)/shard_map/all_to_all | solution.py:364
  53.6 22.3 %collective-permute-start.1 = (bf16[128,4096]{1,0:T(8,128)(2,1)S(1)}, bf16[128,4096]{1,0:T(8,128)(2,1)}, u32[]{:S(2)}, u32[]{:S(2)}) collective-permute-start(bf16[128,4096]{1,0:T(8,128)(2,1)S(1)} %bitcast.52), channel_id=1, source_target_pairs={{0,16},{16,0},{1,17},{17,1},{2,18},{18,2},{3,19},{19,3},{4,20},{20... | collective-permute-start | bytes 3145736 | tf_op jit(solution)/shard_map/ppermute | solution.py:70
  56.6 22.4 %collective-permute-start.6 = (bf16[128,4096]{1,0:T(8,128)(2,1)S(1)}, bf16[128,4096]{1,0:T(8,128)(2,1)}, u32[]{:S(2)}, u32[]{:S(2)}) collective-permute-start(bf16[128,4096]{1,0:T(8,128)(2,1)S(1)} %collective-permute-done.3), channel_id=1, source_target_pairs={{0,16},{16,0},{1,17},{17,1},{2,18},{18,2},{3,19},{19,3},{4,20},{20... | collective-permute-start | bytes 3145736 | tf_op jit(solution)/shard_map/ppermute | solution.py:70
  67.2 32.5 %collective-permute-start.7 = (bf16[128,4096]{1,0:T(8,128)(2,1)}, bf16[128,4096]{1,0:T(8,128)(2,1)}, u32[]{:S(2)}, u32[]{:S(2)}) collective-permute-start(bf16[128,4096]{1,0:T(8,128)(2,1)} %collective-permute-done.4), channel_id=1, source_target_pairs={{0,16},{16,0},{1,17},{17,1},{2,18},{18,2},{3,19},{19,3},{4,20},{20... | collective-permute-start | bytes 3145736 | tf_op jit(solution)/shard_map/ppermute | solution.py:70
  67.2 34.1 %collective-permute-start.5 = (bf16[128,4096]{1,0:T(8,128)(2,1)S(1)}, bf16[128,4096]{1,0:T(8,128)(2,1)}, u32[]{:S(2)}, u32[]{:S(2)}) collective-permute-start(bf16[128,4096]{1,0:T(8,128)(2,1)S(1)} %collective-permute-done.2), channel_id=1, source_target_pairs={{0,16},{16,0},{1,17},{17,1},{2,18},{18,2},{3,19},{19,3},{4,20},{20... | collective-permute-start | bytes 3145736 | tf_op jit(solution)/shard_map/ppermute | solution.py:70
  74.6 16.9 %collective-permute-start.14 = (bf16[48,4096]{1,0:T(8,128)(2,1)}, bf16[48,4096]{1,0:T(8,128)(2,1)S(1)}, u32[]{:S(2)}, u32[]{:S(2)}) collective-permute-start(bf16[48,4096]{1,0:T(8,128)(2,1)} %get-tuple-element.45), channel_id=1, source_target_pairs={{0,32},{32,64},{64,96},{96,0},{1,33},{33,65},{65,97},{97,1},{2,34}... | collective-permute-start | bytes 1179656 | tf_op jit(solution)/shard_map/ppermute | solution.py:70
  75.9 15.8 %collective-permute-start.15 = (bf16[48,4096]{1,0:T(8,128)(2,1)}, bf16[48,4096]{1,0:T(8,128)(2,1)}, u32[]{:S(2)}, u32[]{:S(2)}) collective-permute-start(bf16[48,4096]{1,0:T(8,128)(2,1)} %get-tuple-element.46), channel_id=1, source_target_pairs={{0,96},{32,0},{64,32},{96,64},{1,97},{33,1},{65,33},{97,65},{2,98}... | collective-permute-start | bytes 1179656 | tf_op jit(solution)/shard_map/ppermute | solution.py:70
  79.0 12.1 %collective-permute-start.16 = (bf16[32,4096]{1,0:T(8,128)(2,1)}, bf16[32,4096]{1,0:T(8,128)(2,1)}, u32[]{:S(2)}, u32[]{:S(2)}) collective-permute-start(bf16[32,4096]{1,0:T(8,128)(2,1)} %get-tuple-element.47), channel_id=1, source_target_pairs={{0,128},{128,0},{1,129},{129,1},{2,130},{130,2},{3,131},{131,3},{4... | collective-permute-start | bytes 786440 | tf_op jit(solution)/shard_map/ppermute | solution.py:70
  81.5 18.1 %all-to-all-start.1 = ((bf16[16,128,128]{2,1,0:T(8,128)(2,1)}), bf16[16,128,128]{2,1,0:T(8,128)(2,1)}, u32[]{:S(2)}, u32[]{:S(2)}) async-start(bf16[16,128,128]{2,1,0:T(8,128)(2,1)} %all-to-all-done), calls=%async_computation.1 | async-start | bytes 1048576 | tf_op jit(solution)/shard_map/all_to_all | solution.py:364
  91.1 14.8 %collective-permute-start.11 = (bf16[128,4096]{1,0:T(8,128)(2,1)}, bf16[128,4096]{1,0:T(8,128)(2,1)}, u32[]{:S(2)}, u32[]{:S(2)}) collective-permute-start(bf16[128,4096]{1,0:T(8,128)(2,1)} %collective-permute-done.8.refs_0_), channel_id=1, source_target_pairs={{0,16},{16,0},{1,17},{17,1},{2,18},{18,2},{3,19},{19,3},{4,20},{20... | collective-permute-start | bytes 3145736 | tf_op jit(solution)/shard_map/ppermute | solution.py:70
  91.6 14.3 %collective-permute-start.12 = (bf16[128,4096]{1,0:T(8,128)(2,1)}, bf16[128,4096]{1,0:T(8,128)(2,1)}, u32[]{:S(2)}, u32[]{:S(2)}) collective-permute-start(bf16[128,4096]{1,0:T(8,128)(2,1)} %collective-permute-done.9.refs_2_), channel_id=1, source_target_pairs={{0,16},{16,0},{1,17},{17,1},{2,18},{18,2},{3,19},{19,3},{4,20},{20... | collective-permute-start | bytes 3145736 | tf_op jit(solution)/shard_map/ppermute | solution.py:70
  91.7 14.2 %collective-permute-start.13 = (bf16[128,4096]{1,0:T(8,128)(2,1)}, bf16[128,4096]{1,0:T(8,128)(2,1)}, u32[]{:S(2)}, u32[]{:S(2)}) collective-permute-start(bf16[128,4096]{1,0:T(8,128)(2,1)} %collective-permute-done.10.refs_1_), channel_id=1, source_target_pairs={{0,16},{16,0},{1,17},{17,1},{2,18},{18,2},{3,19},{19,3},{4,20},{20... | collective-permute-start | bytes 3145736 | tf_op jit(solution)/shard_map/ppermute | solution.py:70
  99.7 2.8 %collective-permute-start.19 = (bf16[32,4096]{1,0:T(8,128)(2,1)}, bf16[32,4096]{1,0:T(8,128)(2,1)}, u32[]{:S(2)}, u32[]{:S(2)}) collective-permute-start(bf16[32,4096]{1,0:T(8,128)(2,1)} %collective-permute-done.16), channel_id=1, source_target_pairs={{0,16},{16,0},{1,17},{17,1},{2,18},{18,2},{3,19},{19,3},{4,20},{20... | collective-permute-start | bytes 786440 | tf_op jit(solution)/shard_map/ppermute | solution.py:70
  101.3 3.0 %collective-permute-start.17 = (bf16[48,4096]{1,0:T(8,128)(2,1)S(1)}, bf16[48,4096]{1,0:T(8,128)(2,1)S(1)}, u32[]{:S(2)}, u32[]{:S(2)}) collective-permute-start(bf16[48,4096]{1,0:T(8,128)(2,1)S(1)} %collective-permute-done.14), channel_id=1, source_target_pairs={{0,16},{16,0},{1,17},{17,1},{2,18},{18,2},{3,19},{19,3},{4,20},{20... | collective-permute-start | bytes 1179656 | tf_op jit(solution)/shard_map/ppermute | solution.py:70
  102.5 2.6 %collective-permute-start.18 = (bf16[48,4096]{1,0:T(8,128)(2,1)}, bf16[48,4096]{1,0:T(8,128)(2,1)S(1)}, u32[]{:S(2)}, u32[]{:S(2)}) collective-permute-start(bf16[48,4096]{1,0:T(8,128)(2,1)} %collective-permute-done.15), channel_id=1, source_target_pairs={{0,16},{16,0},{1,17},{17,1},{2,18},{18,2},{3,19},{19,3},{4,20},{20... | collective-permute-start | bytes 1179656 | tf_op jit(solution)/shard_map/ppermute | solution.py:70
  104.4 0.8 copy-start.1
  105.1 0.8 copy-start.4
  105.9 1.0 copy-start.2
  106.9 1.0 copy-start.5
  107.9 0.9 copy-start.9
  108.9 24.0 %copy-start.3 = (bf16[48,4096]{1,0:T(8,128)(2,1)S(1)}, bf16[48,4096]{1,0:T(8,128)(2,1)}, u32[]{:S(2)}) copy-start(bf16[48,4096]{1,0:T(8,128)(2,1)} %copy-done.1) | copy-start | bytes 1179652
  108.9 24.0 %copy-start.6 = (bf16[48,4096]{1,0:T(8,128)(2,1)S(1)}, bf16[48,4096]{1,0:T(8,128)(2,1)}, u32[]{:S(2)}) copy-start(bf16[48,4096]{1,0:T(8,128)(2,1)} %copy-done.4) | copy-start | bytes 1179652
  130.2 7.7 %collective-permute-start.20 = (bf16[3,256,128]{2,1,0:T(8,128)(2,1)S(1)}, bf16[3,256,128]{2,1,0:T(8,128)(2,1)S(1)}, u32[]{:S(2)}, u32[]{:S(2)}) collective-permute-start(bf16[3,256,128]{2,1,0:T(8,128)(2,1)S(1)} %get-tuple-element.74), channel_id=1, source_target_pairs={{0,1},{1,2},{2,3},{3,4},{4,5},{5,6},{6,7},{7,0},{8,9},{9,10},{10,1... | collective-permute-start | bytes 589832 | tf_op jit(solution)/shard_map/ppermute | solution.py:70
  130.3 7.6 %collective-permute-start.21 = (bf16[3,256,128]{2,1,0:T(8,128)(2,1)S(1)}, bf16[3,256,128]{2,1,0:T(8,128)(2,1)S(1)}, u32[]{:S(2)}, u32[]{:S(2)}) collective-permute-start(bf16[3,256,128]{2,1,0:T(8,128)(2,1)S(1)} %get-tuple-element.73), channel_id=1, source_target_pairs={{0,7},{1,0},{2,1},{3,2},{4,3},{5,4},{6,5},{7,6},{8,15},{9,8},{10,9... | collective-permute-start | bytes 589832 | tf_op jit(solution)/shard_map/ppermute | solution.py:70
  138.0 12.8 %collective-permute-start.23 = (bf16[2,3,256,128]{3,2,1,0:T(8,128)(2,1)S(1)}, bf16[2,3,256,128]{3,2,1,0:T(8,128)(2,1)S(1)}, u32[]{:S(2)}, u32[]{:S(2)}) collective-permute-start(bf16[2,3,256,128]{3,2,1,0:T(8,128)(2,1)S(1)} %pad_maximum_fusion.1), channel_id=1, source_target_pairs={{0,7},{1,0},{2,1},{3,2},{4,3},{5,4},{6,5},{7,6},{8,15},{9,8},{10,9... | collective-permute-start | bytes 1179656 | tf_op jit(solution)/shard_map/ppermute | solution.py:70
  140.5 10.6 %collective-permute-start.22 = (bf16[2,3,256,128]{3,2,1,0:T(8,128)(2,1)S(1)}, bf16[2,3,256,128]{3,2,1,0:T(8,128)(2,1)S(1)}, u32[]{:S(2)}, u32[]{:S(2)}) collective-permute-start(bf16[2,3,256,128]{3,2,1,0:T(8,128)(2,1)S(1)} %pad_maximum_fusion), channel_id=1, source_target_pairs={{0,1},{1,2},{2,3},{3,4},{4,5},{5,6},{6,7},{7,0},{8,9},{9,10},{10,1... | collective-permute-start | bytes 1179656 | tf_op jit(solution)/shard_map/ppermute | solution.py:70
  150.1 0.8 copy-start.7
  150.8 18.4 %copy-start.8 = (bf16[2,3,256,128]{3,2,1,0:T(8,128)(2,1)S(1)}, bf16[2,3,256,128]{3,2,1,0:T(8,128)(2,1)}, u32[]{:S(2)}) copy-start(bf16[2,3,256,128]{3,2,1,0:T(8,128)(2,1)} %copy-done.7) | copy-start | bytes 1179652
  151.2 9.4 %collective-permute-start.24 = (bf16[2,3,256,128]{3,2,1,0:T(8,128)(2,1)S(1)}, bf16[2,3,256,128]{3,2,1,0:T(8,128)(2,1)S(1)}, u32[]{:S(2)}, u32[]{:S(2)}) collective-permute-start(bf16[2,3,256,128]{3,2,1,0:T(8,128)(2,1)S(1)} %add_convert_fusion.4), channel_id=1, source_target_pairs={{0,1},{1,2},{2,3},{3,4},{4,5},{5,6},{6,7},{7,0},{8,9},{9,10},{10,1... | collective-permute-start | bytes 1179656 | tf_op jit(solution)/shard_map/ppermute | solution.py:70
  151.4 9.4 %collective-permute-start.26 = (bf16[2,3,256,128]{3,2,1,0:T(8,128)(2,1)S(1)}, bf16[2,3,256,128]{3,2,1,0:T(8,128)(2,1)S(1)}, u32[]{:S(2)}, u32[]{:S(2)}) collective-permute-start(bf16[2,3,256,128]{3,2,1,0:T(8,128)(2,1)S(1)} %add_convert_fusion.2), channel_id=1, source_target_pairs={{0,7},{1,0},{2,1},{3,2},{4,3},{5,4},{6,5},{7,6},{8,15},{9,8},{10,9... | collective-permute-start | bytes 1179656 | tf_op jit(solution)/shard_map/ppermute | solution.py:70
  160.7 8.5 %collective-permute-start.25 = (bf16[2,3,256,128]{3,2,1,0:T(8,128)(2,1)S(1)}, bf16[2,3,256,128]{3,2,1,0:T(8,128)(2,1)S(1)}, u32[]{:S(2)}, u32[]{:S(2)}) collective-permute-start(bf16[2,3,256,128]{3,2,1,0:T(8,128)(2,1)S(1)} %add_convert_fusion.3), channel_id=1, source_target_pairs={{0,1},{1,2},{2,3},{3,4},{4,5},{5,6},{6,7},{7,0},{8,9},{9,10},{10,1... | collective-permute-start | bytes 1179656 | tf_op jit(solution)/shard_map/ppermute | solution.py:70
  160.9 8.3 %collective-permute-start.27 = (bf16[2,3,256,128]{3,2,1,0:T(8,128)(2,1)S(1)}, bf16[2,3,256,128]{3,2,1,0:T(8,128)(2,1)S(1)}, u32[]{:S(2)}, u32[]{:S(2)}) collective-permute-start(bf16[2,3,256,128]{3,2,1,0:T(8,128)(2,1)S(1)} %add_convert_fusion.1), channel_id=1, source_target_pairs={{0,7},{1,0},{2,1},{3,2},{4,3},{5,4},{6,5},{7,6},{8,15},{9,8},{10,9... | collective-permute-start | bytes 1179656 | tf_op jit(solution)/shard_map/ppermute | solution.py:70
  169.4 9.7 %collective-permute-start.28 = (bf16[3,256,128]{2,1,0:T(8,128)(2,1)S(1)}, bf16[3,256,128]{2,1,0:T(8,128)(2,1)S(1)}, u32[]{:S(2)}, u32[]{:S(2)}) collective-permute-start(bf16[3,256,128]{2,1,0:T(8,128)(2,1)S(1)} %get-tuple-element.71), channel_id=1, source_target_pairs={{0,0},{1,129},{2,34},{3,163},{4,68},{5,197},{6,102},{7,231},{8,16}... | collective-permute-start | bytes 589832 | tf_op jit(solution)/shard_map/ppermute | solution.py:392
  175.8 4.7 %collective-permute-start.29 = (bf16[3,256,128]{2,1,0:T(8,128)(2,1)S(1)}, bf16[3,256,128]{2,1,0:T(8,128)(2,1)S(1)}, u32[]{:S(2)}, u32[]{:S(2)}) collective-permute-start(bf16[3,256,128]{2,1,0:T(8,128)(2,1)S(1)} %get-tuple-element.72), channel_id=1, source_target_pairs={{0,16},{1,145},{2,50},{3,179},{4,84},{5,213},{6,118},{7,247},{8,0}... | collective-permute-start | bytes 589832 | tf_op jit(solution)/shard_map/ppermute | solution.py:392
  180.6 15.9 %collective-permute-start.30 = (bf16[3,256,128]{2,1,0:T(8,128)(2,1)S(1)}, bf16[3,256,128]{2,1,0:T(8,128)(2,1)S(1)}, u32[]{:S(2)}, u32[]{:S(2)}) collective-permute-start(bf16[3,256,128]{2,1,0:T(8,128)(2,1)S(1)} %add_convert_fusion.5), channel_id=1, source_target_pairs={{0,0},{1,1},{2,6},{3,7},{4,4},{5,5},{6,2},{7,3},{8,8},{9,9},{10,14... | collective-permute-start | bytes 589832 | tf_op jit(solution)/shard_map/ppermute | solution.py:394
Sparse Core Ops, SparseCore 0:
  39.3 58.9 all-gather.1

commit v7 on v6

--- a/solution.py
+++ b/solution.py
@@ -22,7 +22,7 @@
 FAR = (4,)
 NEAR_A = (3, 5)
 NEAR_B = (2, 6, 1, 7, 0)
-CUT_FLOPS = 3 * 10**10
+CUT_FLOPS = 2 * 10**10
 WIDTH = 4096
 COLS = 3 * HEAD_DIM
 ROWS = FRAMES * PATCHES
@@ -101,7 +101,7 @@
     )(*buffers)
 
 
-def gather_frames(own, early, middle, late):
+def gather_frames(own, early, middle, late, beside_third):
     twin = lambda values: [shift(value, "core", 1) for value in values]
     first = [shift(own, "x", 1), shift(own, "x", -1), shift(own, "yl", 1)]
     own_twin = shift(own, "core", 1)
@@ -112,12 +112,11 @@
     cuts = cut(other_left, other_right, far)
     third = [shift(cuts[0], "x", 1), shift(cuts[1], "x", -1), shift(cuts[2], "yl", 1)]
     second_twins = twin([other_left, far, other_right])
-    third = after(third, *late)
-    return (
-        [own, own_twin, left, right, other, *first_twins],
-        [other_left, far, other_right, *second_twins],
-        [*third, *twin(third)],
-    )
+    whole = [own, own_twin, left, right, other, *first_twins]
+    whole += [other_left, far, other_right, *second_twins]
+    result = beside_third(whole)
+    third = after(third, result, *late)
+    return whole, [*third, *twin(third)], result
 
 
 FIRST = [[(slot, 0, PATCHES)] for slot in (0, 1, 4, 2, 6, 5, 3, 7)]
@@ -216,50 +215,102 @@
             turned[j * HEAD_DIM : (j + 1) * HEAD_DIM, columns] = result.T.astype(jnp.bfloat16)
         return carry
 
-    lax.fori_loop(0, PATCHES // GROUP, body, 0)
-
-
-def share_kernel(count, order, mask, w_ref, g_ref, *refs):
+    lax.fori_loop(0, PATCHES // GROUP, body, 0, unroll=4)
+
+
+def project_kernel(count, w_ref, *refs):
+    buffers, out = refs[:count], refs[count]
+    tokens, result, w, w_sem, x_sem, o_sem = refs[count + 1 :]
+    groups = PATCHES // GROUP
+    weights = pltpu.make_async_copy(w_ref, w, w_sem.at[0])
+    copies = []
+    for index, ref in enumerate(buffers):
+        rows = pl.ds(index * groups, groups)
+        copies.append(pltpu.make_async_copy(ref, tokens.at[rows], x_sem.at[index]))
+    steps = [copies[at : at + STEP] for at in range(0, count, STEP)]
+    weights.start()
+    for copy in steps[0]:
+        copy.start()
+    weights.wait()
+    stores = []
+    for step, here in enumerate(steps):
+        for copy in here:
+            copy.wait()
+        for copy in steps[step + 1] if step + 1 < len(steps) else ():
+            copy.start()
+        rows = pl.ds(step * STEP * groups, len(here) * groups)
+        value = tokens[rows].reshape(len(here) * PATCHES, WIDTH)
+        value = jnp.dot(value, w[...], preferred_element_type=jnp.float32)
+        result[rows] = value.astype(jnp.bfloat16).reshape(-1, GROUP, COLS)
+        stores.append(pltpu.make_async_copy(result.at[rows], out.at[rows], o_sem.at[step]))
+        stores[-1].start()
+    for store in stores:
+        store.wait()
+
+
+def project(w, buffers):
+    count = len(buffers)
+    groups = count * PATCHES // GROUP
+    return pl.pallas_call(
+        functools.partial(project_kernel, count),
+        out_shape=jax.ShapeDtypeStruct((groups, GROUP, COLS), jnp.bfloat16),
+        in_specs=[HBM] * (1 + count),
+        out_specs=HBM,
+        scratch_shapes=[
+            pltpu.VMEM((groups, GROUP, WIDTH), jnp.bfloat16),
+            pltpu.VMEM((groups, GROUP, COLS), jnp.bfloat16),
+            pltpu.VMEM((WIDTH, COLS), jnp.bfloat16),
+            pltpu.SemaphoreType.DMA((1,)),
+            pltpu.SemaphoreType.DMA((count,)),
+            pltpu.SemaphoreType.DMA((count,)),
+        ],
+        compiler_params=pltpu.CompilerParams(vmem_limit_bytes=48 * 2**20),
+        cost_estimate=pl.CostEstimate(
+            flops=2 * groups * GROUP * WIDTH * COLS,
+            bytes_accessed=2 * groups * GROUP * WIDTH,
+            transcendentals=0,
+        ),
+    )(w, *buffers)
+
+
+def share_kernel(count, order, mask, w_ref, g_ref, early, *refs):
     buffers, turned_out, out = refs[:count], refs[count], refs[count + 1 : count + 1 + len(FAR)]
-    tokens, proj, grads, turned, w, w_sem, x_sem, g_sem = refs[count + 1 + len(FAR) :]
-    arrivals = [[] for _ in range(FRAMES)]
+    tokens, proj, grads, turned, w, w_sem, x_sem, g_sem, p_sem = refs[count + 1 + len(FAR) :]
+    copies = []
     for index, (buffer, at, slot, first, groups) in enumerate(PARTS):
-        arrivals[slot].append(
+        copies.append(
             pltpu.make_async_copy(
                 buffers[buffer].at[pl.ds(at, groups)],
                 tokens.at[pl.ds(first, groups), slot],
                 x_sem.at[index],
             )
         )
-    cotangents = []
+    copies, last = copies[: -len(THIRD)], copies[-len(THIRD) :]
+    small = []
     for slot in range(FRAMES):
-        cotangents.append(
+        small.append(
             pltpu.make_async_copy(g_ref.at[order[slot]], grads.at[:, slot], g_sem.at[slot])
         )
+    for index, (buffer, _, slot, _, groups) in enumerate(parts_of(FIRST + SECOND)):
+        source = early.at[pl.ds(buffer * groups, groups)]
+        small.append(pltpu.make_async_copy(source, proj.at[:, slot], p_sem.at[index]))
     weights = pltpu.make_async_copy(w_ref, w, w_sem.at[0])
-
-    def step_copies(step):
-        return [copy for slot in range(STEP * step, STEP * step + STEP) for copy in arrivals[slot]]
-
-    weights.start()
-    for copy in step_copies(0):
+    for copy in [weights] + last + small:
         copy.start()
-    weights.wait()
-    steps = FRAMES // STEP
-    for step in range(steps):
-        for copy in step_copies(step):
-            copy.wait()
-        for copy in step_copies(step + 1) if step + 1 < steps else cotangents:
-            copy.start()
-        slots = slice(STEP * step, STEP * step + STEP)
-        rows = tokens[:, slots].reshape(STEP * PATCHES, WIDTH)
-        result = jnp.dot(rows, w[...], preferred_element_type=jnp.float32)
-        proj[:, slots] = result.astype(jnp.bfloat16).reshape(-1, STEP, GROUP, COLS)
-    for copy in cotangents:
+    for copy in [weights] + last:
+        copy.wait()
+    for copy in copies:
+        copy.start()
+    rows = tokens[:, FRAMES - 2 :].reshape(2 * PATCHES, WIDTH)
+    result = jnp.dot(rows, w[...], preferred_element_type=jnp.float32)
+    proj[:, FRAMES - 2 :] = result.astype(jnp.bfloat16).reshape(-1, 2, GROUP, COLS)
+    for copy in small:
         copy.wait()
     attend(proj, grads, mask, turned)
     store = pltpu.make_async_copy(turned, turned_out, w_sem.at[1])
     store.start()
+    for copy in copies:
+        copy.wait()
     for index, ahead in enumerate(FAR):
         columns = pl.ds(pl.multiple_of(order[16 + ahead] * CHUNK, CHUNK), CHUNK)
         rows = tokens[:, :, :, columns].reshape(ROWS, CHUNK)
@@ -318,7 +369,7 @@
             pltpu.SemaphoreType.DMA((1,)),
             pltpu.SemaphoreType.DMA((len(near), len(PARTS))),
         ],
-        compiler_params=pltpu.CompilerParams(vmem_limit_bytes=44 * 2**20),
+        compiler_params=pltpu.CompilerParams(vmem_limit_bytes=48 * 2**20),
         cost_estimate=pl.CostEstimate(
             flops=2 * ROWS * len(near) * CHUNK * COLS,
             bytes_accessed=2 * ROWS * len(near) * CHUNK,
@@ -327,13 +378,13 @@
     )(order, turned, *buffers)
 
 
-def far_shares(order, mask, w, g, buffers):
+def far_shares(order, mask, w, g, early, buffers):
     count = len(buffers)
     groups = PATCHES // GROUP
     return pl.pallas_call(
         functools.partial(share_kernel, count),
         out_shape=[jax.ShapeDtypeStruct((COLS, ROWS), jnp.bfloat16)] + [SHARE] * len(FAR),
-        in_specs=[SMEM, VMEM] + [HBM] * (2 + count),
+        in_specs=[SMEM, VMEM] + [HBM] * (3 + count),
         out_specs=[HBM] + [VMEM] * len(FAR),
         scratch_shapes=[
             pltpu.VMEM((groups, FRAMES, GROUP, WIDTH), jnp.bfloat16),
@@ -344,12 +395,13 @@
             pltpu.SemaphoreType.DMA((2,)),
             pltpu.SemaphoreType.DMA((len(PARTS),)),
             pltpu.SemaphoreType.DMA((FRAMES,)),
+            pltpu.SemaphoreType.DMA((len(FIRST + SECOND),)),
         ],
-        compiler_params=pltpu.CompilerParams(vmem_limit_bytes=44 * 2**20),
+        compiler_params=pltpu.CompilerParams(vmem_limit_bytes=48 * 2**20),
         cost_estimate=pl.CostEstimate(
             flops=2 * ROWS * WIDTH * COLS, bytes_accessed=2 * ROWS * WIDTH, transcendentals=0
         ),
-    )(order, mask, w, g, *buffers)
+    )(order, mask, w, g, early, *buffers)
 
 
 def add(*parts):
@@ -366,13 +418,13 @@
     )
     heads_g = exchange(after(grad_attn[0], rows_w).reshape(FRAMES, PATCHES, HEAD_DIM), TOK)
     frames_g = exchange(heads_g, ("core", "x", "yl"))
-    steps = gather_frames(inputs[0], (rows_w,), (heads_g,), (frames_g,))
+    grouped = lambda buffers: [buffer.reshape(-1, GROUP, WIDTH) for buffer in buffers]
+    whole, third, early = gather_frames(
+        inputs[0], (rows_w,), (heads_g,), (frames_g,), lambda whole: project(w, grouped(whole))
+    )
     g = frames_g.reshape(FRAMES, PATCHES // GROUP, GROUP, HEAD_DIM)
-    first, second, third = (
-        [buffer.reshape(-1, GROUP, WIDTH) for buffer in buffers] for buffers in steps
-    )
-    order, buffers = table[:24], first + second + third
-    turned, far = far_shares(order, visible(table[24:40]), w, g, buffers)
+    order, buffers = table[:24], grouped(whole + third)
+    turned, far = far_shares(order, visible(table[24:40]), w, g, early, buffers)
     beside = lax.optimization_barrier
     shares = lambda near: near_shares(order, turned, buffers, near)
     up, down, (share_3, share_5) = beside(

time: 207 us -> 216 us (1.043)
  waiting for transfers between devices: 65 us -> 91.1 us
  starting transfers between devices: 74.5 us -> 63.9 us
  local copies, waits for them, and re-layouts: 9.01 us -> 3.23 us
    ppermute x27, waiting for transfers between devices: 23.9 us -> 41.5 us  [shift(): lax.ppermute(value, axis, [(i, (i + by) % count) for i in range(count)])]
    pallas_call x0 -> x1, Pallas kernels: none -> 11.4 us  [project(): pl.pallas_call(functools.partial(project_kernel, count), out_shape=jax.Sh...]
    pallas_call x1, Pallas kernels: 21.2 us -> 10.5 us  [far_shares(): pl.pallas_call(functools.partial(share_kernel, count), out_shape=[jax.Sha...]
    ppermute x27, starting transfers between devices: 30.2 us -> 22.4 us  [shift(): lax.ppermute(value, axis, [(i, (i + by) % count) for i in range(count)])]
    all_to_all x2, waiting for transfers between devices: 12.2 us -> 18.5 us  [local(): lax.all_to_all(value, axes, split_axis=0, concat_axis=0, tiled=True)]
    unnamed x25 -> x11, local copies, waits for them, and re-layouts: 6.65 us -> 1.46 us
    ppermute x2, starting transfers between devices: 6.48 us -> 10.5 us  [local(): part = lax.ppermute(part, AXES, plane_moves(flip)).astype(jnp.float32)]
    all_to_all x2, starting transfers between devices: 20.9 us -> 17 us  [local(): lax.all_to_all(value, axes, split_axis=0, concat_axis=0, tiled=True)]
  transfers between devices with their start and end apart: 34 -> 34, of which waited for: 11 -> 15; matrix products, arithmetic and copies ran while one was open for 2% -> 0% of each run, Pallas kernels for 9% -> 13%
where the time goes in v7:
time: 216 us; the launch traced here: 214 us
  waiting for transfers between devices  91.1 us (42%)
  starting transfers between devices  63.9 us (30%)
  Pallas kernels  40.7 us (19%)
  between operations  13.7 us (6%)
  local copies, waits for them, and re-layouts  3.23 us (1%)
    ppermute x27, waiting for transfers between devices, shift(): lax.ppermute(value, axis, [(i, (i + by) % count) for i in range(count)])  41.5 us
    ppermute x27, starting transfers between devices, shift(): lax.ppermute(value, axis, [(i, (i + by) % count) for i in range(count)])  22.4 us
    all_to_all x2, waiting for transfers between devices, local(): lax.all_to_all(value, axes, split_axis=0, concat_axis=0, tiled=True)  18.5 us
    ppermute x1, waiting for transfers between devices, local(): rows_w = lax.ppermute(rows_w, AXES, worker_moves())  17.5 us
    all_to_all x2, starting transfers between devices, local(): lax.all_to_all(value, axes, split_axis=0, concat_axis=0, tiled=True)  17 us
    pallas_call x2, Pallas kernels, near_shares(): pl.pallas_call(functools.partial(near_kernel, count, near), out_shape=[SH...  14.2 us
    pallas_call x1, Pallas kernels, project(): pl.pallas_call(functools.partial(project_kernel, count), out_shape=jax.Sh...  11.4 us
    pallas_call x1, Pallas kernels, far_shares(): pl.pallas_call(functools.partial(share_kernel, count), out_shape=[jax.Sha...  10.5 us
  transfers between devices with their start and end apart: 34, of which 15 were waited for; matrix products, arithmetic and copies ran while one was open for 0% of the time, Pallas kernels for 13%

profile of v7, /device:TPU:3, one launch (start us, length us, event | category | flops | bytes accessed | tf_op | source)
XLA Modules:
  0.0 213.7 jit_solution(16777591176874514542)
XLA Ops:
  6.5 0.8 constant_dynamic-slice_fusion
  7.3 0.6 slice.40
  7.9 2.4 %shard_map.46 = bf16[512,384]{1,0:T(8,128)(2,1)} custom-call(s32[1]{0:T(128)} %bitcast.2.start, bf16[3,4096,128]{2,1,0:T(8,128)(2,1)} %bitcast.77), custom_call_target="tpu_custom_call" | custom-call | tf_op jit(solution)/shard_map/pallas_call | solution.py:182
  10.4 8.1 %collective-permute-start = (bf16[512,384]{1,0:T(8,128)(2,1)}, bf16[512,384]{1,0:T(8,128)(2,1)S(1)}, u32[]{:S(2)}, u32[]{:S(2)}) collective-permute-start(bf16[512,384]{1,0:T(8,128)(2,1)} %shard_map.46), channel_id=1, source_target_pairs={{0,0},{128,1},{32,2},{160,3},{64,4},{192,5},{96,6},{224,7},{16,8},... | collective-permute-start | bytes 1179656 | tf_op jit(solution)/shard_map/ppermute | solution.py:414
  18.4 17.5 %collective-permute-done = bf16[512,384]{1,0:T(8,128)(2,1)S(1)} collective-permute-done((bf16[512,384]{1,0:T(8,128)(2,1)}, bf16[512,384]{1,0:T(8,128)(2,1)S(1)}, u32[]{:S(2)}, u32[]{:S(2)}) %collective-permute-start) | collective-permute-done | bytes 393248 | tf_op jit(solution)/shard_map/ppermute | solution.py:414
  35.9 0.8 copy-done.4
  36.7 0.1 collective-permute-start.2
  36.8 1.5 collective-permute-start.3
  38.2 21.4 %collective-permute-done.2 = bf16[128,4096]{1,0:T(8,128)(2,1)S(1)} collective-permute-done((bf16[128,4096]{1,0:T(8,128)(2,1)S(1)}, bf16[128,4096]{1,0:T(8,128)(2,1)S(1)}, u32[]{:S(2)}, u32[]{:S(2)}) %collective-permute-start.2) | collective-permute-done | bytes 1048608 | tf_op jit(solution)/shard_map/ppermute | solution.py:70
  59.7 3.4 %collective-permute-done.3 = bf16[128,4096]{1,0:T(8,128)(2,1)S(1)} collective-permute-done((bf16[128,4096]{1,0:T(8,128)(2,1)S(1)}, bf16[128,4096]{1,0:T(8,128)(2,1)S(1)}, u32[]{:S(2)}, u32[]{:S(2)}) %collective-permute-start.3) | collective-permute-done | bytes 1048608 | tf_op jit(solution)/shard_map/ppermute | solution.py:70
  63.0 2.1 collective-permute-start.10
  65.1 2.4 %collective-permute-start.9 = (bf16[128,4096]{1,0:T(8,128)(2,1)S(1)}, bf16[128,4096]{1,0:T(8,128)(2,1)}, u32[]{:S(2)}, u32[]{:S(2)}) collective-permute-start(bf16[128,4096]{1,0:T(8,128)(2,1)S(1)} %collective-permute-done.3), channel_id=1, source_target_pairs={{0,96},{32,0},{64,32},{96,64},{1,97},{33,1},{65,33},{97,65},{2,98}... | collective-permute-start | bytes 3145736 | tf_op jit(solution)/shard_map/ppermute | solution.py:70
  67.6 0.6 collective-permute-start.1
  68.2 10.8 %all-to-all-start = ((bf16[16,128,128]{2,1,0:T(8,128)(2,1)}), bf16[16,128,128]{2,1,0:T(8,128)(2,1)}, u32[]{:S(2)}, u32[]{:S(2)}) async-start(bf16[16,128,128]{2,1,0:T(8,128)(2,1)} %bitcast.78), calls=%async_computation | async-start | bytes 1048576 | tf_op jit(solution)/shard_map/all_to_all | solution.py:416
  79.0 18.5 %all-to-all-done = bf16[16,128,128]{2,1,0:T(8,128)(2,1)} async-done(((bf16[16,128,128]{2,1,0:T(8,128)(2,1)}), bf16[16,128,128]{2,1,0:T(8,128)(2,1)}, u32[]{:S(2)}, u32[]{:S(2)}) %all-to-all-start) | async-done | bytes 524320 | tf_op jit(solution)/shard_map/all_to_all | solution.py:416
  97.6 6.2 %all-to-all-start.1 = ((bf16[16,128,128]{2,1,0:T(8,128)(2,1)}), bf16[16,128,128]{2,1,0:T(8,128)(2,1)}, u32[]{:S(2)}, u32[]{:S(2)}) async-start(bf16[16,128,128]{2,1,0:T(8,128)(2,1)} %all-to-all-done), calls=%async_computation.1 | async-start | bytes 1048576 | tf_op jit(solution)/shard_map/all_to_all | solution.py:416
  103.8 0.4 collective-permute-start.7
  104.2 0.1 collective-permute-start.5
  104.4 0.4 collective-permute-start.11
  104.7 0.1 collective-permute-start.12
  104.9 0.4 collective-permute-start.13
  105.3 2.2 %shard_map.48 = (bf16[48,4096]{1,0:T(8,128)(2,1)}, bf16[48,4096]{1,0:T(8,128)(2,1)}, bf16[32,4096]{1,0:T(8,128)(2,1)}) custom-call(bf16[128,4096]{1,0:T(8,128)(2,1)} %collective-permute-done.8.refs_0_, bf16[128,4096]{1,0:T(8,128)(2,1)} %collective-permute-done.10.refs_1_, bf16[128,4096]{1,0:T(8,128)(2,1)} %collective-permute-done.9.refs_2_), custom_call_target="tpu_custom_call" | custom-call | flops 20000000000 | tf_op jit(solution)/shard_map/pallas_call | solution.py:92
  107.5 1.3 collective-permute-start.14
  108.8 0.9 collective-permute-done.5
  109.7 0.1 collective-permute-start.15
  109.7 0.1 collective-permute-done.11
  109.9 1.3 collective-permute-start.16
  111.1 0.2 collective-permute-done.12
  111.4 1.5 collective-permute-done.13
  112.9 11.4 %shard_map.47.early = bf16[112,16,384]{2,1,0:T(8,128)(2,1)} custom-call(bf16[4096,384]{1,0:T(8,128)(2,1)} %all-gather.2.cloned.1.call-done.w_ref, bf16[8,16,4096]{2,1,0:T(8,128)(2,1)S(1)} %bitcast.53, bf16[8,16,4096]{2,1,0:T(8,128)(2,1)} %bitcast.9.refs_1_, bf16[8,16,4096]{2,1,0:T(8,128)(2,1)S(1)} %bitcast.57, bf16[8,16,4096]{2,1,0:T(8,128)(2,1)S(1)} %bitcast.61, ...), custom_call_target="tpu_custom_call" | custom-call | flops 5637144576 | bytes 14680064 | tf_op jit(solution)/shard_map/pallas_call | solution.py:254
  124.3 0.4 collective-permute-start.17
  124.7 0.1 collective-permute-start.18
  124.9 0.4 collective-permute-start.19
  125.3 0.1 broadcast_in_dim.3
  125.4 0.1 le.15
  125.5 0.1 eq.18
  125.6 0.1 and_convert_fusion.mask
  125.7 1.5 collective-permute-done.19
  127.3 10.5 %shard_map.49 = (bf16[384,2048]{1,0:T(8,128)(2,1)}, bf16[2,3,256,128]{3,2,1,0:T(8,128)(2,1)S(1)}) custom-call(s32[24]{0:T(128)S(1)} %slice_bitcast_fusion.3.order, f32[256,256]{1,0:T(8,128)S(1)} %and_convert_fusion.mask, bf16[4096,384]{1,0:T(8,128)(2,1)} %all-gather.2.cloned.1.call-done.w_ref, bf16[16,8,16,128]{3,2,1,0:T(8,128)(2,1)} %bitcast.6.g_ref, ...), custom_call_target="tpu_custom_call" | custom-call | flops 6442450944 | bytes 16777216 | tf_op jit(solution)/shard_map/pallas_call | solution.py:384
  137.8 0.1 collective-permute-start.20
  137.9 2.7 %collective-permute-start.21 = (bf16[3,256,128]{2,1,0:T(8,128)(2,1)S(1)}, bf16[3,256,128]{2,1,0:T(8,128)(2,1)S(1)}, u32[]{:S(2)}, u32[]{:S(2)}) collective-permute-start(bf16[3,256,128]{2,1,0:T(8,128)(2,1)S(1)} %get-tuple-element.73), channel_id=1, source_target_pairs={{0,7},{1,0},{2,1},{3,2},{4,3},{5,4},{6,5},{7,6},{8,15},{9,8},{10,9... | collective-permute-start | bytes 589832 | tf_op jit(solution)/shard_map/ppermute | solution.py:70
  140.6 4.9 %shard_map.50 = (bf16[2,3,256,128]{3,2,1,0:T(8,128)(2,1)S(1)}, bf16[2,3,256,128]{3,2,1,0:T(8,128)(2,1)S(1)}) custom-call(s32[24]{0:T(128)S(1)} %slice_bitcast_fusion.3.order, bf16[384,2048]{1,0:T(8,128)(2,1)} %get-tuple-element.52.turned_ref, bf16[8,16,4096]{2,1,0:T(8,128)(2,1)S(1)} %bitcast.55, bf16[8,16,4096]{2,1,0:T(8,128)(2,1)} %bitcast.9.refs_1_, ...), custom_call_target="tpu_custom_call" | custom-call | flops 1610612736 | bytes 4194304 | tf_op jit(solution)/shard_map/pallas_call | solution.py:361
  145.7 2.2 %collective-permute-start.23 = (bf16[2,3,256,128]{3,2,1,0:T(8,128)(2,1)S(1)}, bf16[2,3,256,128]{3,2,1,0:T(8,128)(2,1)S(1)}, u32[]{:S(2)}, u32[]{:S(2)}) collective-permute-start(bf16[2,3,256,128]{3,2,1,0:T(8,128)(2,1)S(1)} %pad_maximum_fusion.1), channel_id=1, source_target_pairs={{0,7},{1,0},{2,1},{3,2},{4,3},{5,4},{6,5},{7,6},{8,15},{9,8},{10,9... | collective-permute-start | bytes 1179656 | tf_op jit(solution)/shard_map/ppermute | solution.py:70
  148.0 0.1 collective-permute-start.22
  148.1 9.2 %shard_map.51 = (bf16[2,3,256,128]{3,2,1,0:T(8,128)(2,1)S(1)}, bf16[2,3,256,128]{3,2,1,0:T(8,128)(2,1)S(1)}, bf16[2,3,256,128]{3,2,1,0:T(8,128)(2,1)S(1)}, bf16[...) custom-call(s32[24]{0:T(128)S(1)} %slice_bitcast_fusion.3.order, ...), custom_call_target="tpu_custom_call" | custom-call | flops 4026531840 | bytes 10485760 | tf_op jit(solution)/shard_map/pallas_call | solution.py:361
  157.3 0.8 collective-permute-done.22
  158.1 0.1 add_convert_fusion.4
  158.2 0.1 collective-permute-start.24
  158.3 0.1 add_convert_fusion.2
  158.4 2.7 %collective-permute-start.26 = (bf16[2,3,256,128]{3,2,1,0:T(8,128)(2,1)S(1)}, bf16[2,3,256,128]{3,2,1,0:T(8,128)(2,1)S(1)}, u32[]{:S(2)}, u32[]{:S(2)}) collective-permute-start(bf16[2,3,256,128]{3,2,1,0:T(8,128)(2,1)S(1)} %add_convert_fusion.2), channel_id=1, source_target_pairs={{0,7},{1,0},{2,1},{3,2},{4,3},{5,4},{6,5},{7,6},{8,15},{9,8},{10,9... | collective-permute-start | bytes 1179656 | tf_op jit(solution)/shard_map/ppermute | solution.py:70
  161.2 6.3 %collective-permute-done.24 = bf16[2,3,256,128]{3,2,1,0:T(8,128)(2,1)S(1)} collective-permute-done((bf16[2,3,256,128]{3,2,1,0:T(8,128)(2,1)S(1)}, bf16[2,3,256,128]{3,2,1,0:T(8,128)(2,1)S(1)}, u32[]{:S(2)}, u32[]{:S(2)}) %collective-permute-start.24) | collective-permute-done | bytes 393248 | tf_op jit(solution)/shard_map/ppermute | solution.py:70
  167.5 0.1 add_convert_fusion.3
  167.6 0.1 collective-permute-start.25
  167.7 0.1 add_convert_fusion.1
  167.8 2.7 %collective-permute-start.27 = (bf16[2,3,256,128]{3,2,1,0:T(8,128)(2,1)S(1)}, bf16[2,3,256,128]{3,2,1,0:T(8,128)(2,1)S(1)}, u32[]{:S(2)}, u32[]{:S(2)}) collective-permute-start(bf16[2,3,256,128]{3,2,1,0:T(8,128)(2,1)S(1)} %add_convert_fusion.1), channel_id=1, source_target_pairs={{0,7},{1,0},{2,1},{3,2},{4,3},{5,4},{6,5},{7,6},{8,15},{9,8},{10,9... | collective-permute-start | bytes 1179656 | tf_op jit(solution)/shard_map/ppermute | solution.py:70
  170.5 5.4 %collective-permute-done.25 = bf16[2,3,256,128]{3,2,1,0:T(8,128)(2,1)S(1)} collective-permute-done((bf16[2,3,256,128]{3,2,1,0:T(8,128)(2,1)S(1)}, bf16[2,3,256,128]{3,2,1,0:T(8,128)(2,1)S(1)}, u32[]{:S(2)}, u32[]{:S(2)}) %collective-permute-start.25) | collective-permute-done | bytes 393248 | tf_op jit(solution)/shard_map/ppermute | solution.py:70
  175.9 0.2 add_convert_fusion
  176.1 10.4 %collective-permute-start.28 = (bf16[3,256,128]{2,1,0:T(8,128)(2,1)S(1)}, bf16[3,256,128]{2,1,0:T(8,128)(2,1)S(1)}, u32[]{:S(2)}, u32[]{:S(2)}) collective-permute-start(bf16[3,256,128]{2,1,0:T(8,128)(2,1)S(1)} %get-tuple-element.71), channel_id=1, source_target_pairs={{0,0},{1,129},{2,34},{3,163},{4,68},{5,197},{6,102},{7,231},{8,16}... | collective-permute-start | bytes 589832 | tf_op jit(solution)/shard_map/ppermute | solution.py:444
  186.5 0.1 collective-permute-start.29
  186.6 3.2 %collective-permute-done.28 = bf16[3,256,128]{2,1,0:T(8,128)(2,1)S(1)} collective-permute-done((bf16[3,256,128]{2,1,0:T(8,128)(2,1)S(1)}, bf16[3,256,128]{2,1,0:T(8,128)(2,1)S(1)}, u32[]{:S(2)}, u32[]{:S(2)}) %collective-permute-start.28) | collective-permute-done | bytes 196640 | tf_op jit(solution)/shard_map/ppermute | solution.py:444
  189.8 1.4 collective-permute-done.29
  191.2 6.0 %collective-permute-start.30 = (bf16[3,256,128]{2,1,0:T(8,128)(2,1)S(1)}, bf16[3,256,128]{2,1,0:T(8,128)(2,1)S(1)}, u32[]{:S(2)}, u32[]{:S(2)}) collective-permute-start(bf16[3,256,128]{2,1,0:T(8,128)(2,1)S(1)} %add_convert_fusion.5), channel_id=1, source_target_pairs={{0,0},{1,1},{2,6},{3,7},{4,4},{5,5},{6,2},{7,3},{8,8},{9,9},{10,14... | collective-permute-start | bytes 589832 | tf_op jit(solution)/shard_map/ppermute | solution.py:446
  197.2 9.0 %collective-permute-done.30 = bf16[3,256,128]{2,1,0:T(8,128)(2,1)S(1)} collective-permute-done((bf16[3,256,128]{2,1,0:T(8,128)(2,1)S(1)}, bf16[3,256,128]{2,1,0:T(8,128)(2,1)S(1)}, u32[]{:S(2)}, u32[]{:S(2)}) %collective-permute-start.30) | collective-permute-done | bytes 196640 | tf_op jit(solution)/shard_map/ppermute | solution.py:446
  206.2 0.7 copy.6
  (45 shorter events, 0.5 us)
Async XLA Ops:
  6.5 30.2 %copy-start = (bf16[1,128,4096]{2,1,0:T(8,128)(2,1)S(1)}, bf16[1,128,4096]{2,1,0:T(8,128)(2,1)}, u32[]{:S(2)}) copy-start(bf16[1,128,4096]{2,1,0:T(8,128)(2,1)} %param.4) | copy-start | bytes 3145732
  6.5 106.3 %all-gather.2.cloned.1.call-start = ((), (), s32[]{:S(2)}) async-start(), calls=%async_computation.2 | async-start | bytes 3538944 | tf_op jit(solution)/shard_map/all_gather | solution.py:415
  10.4 25.5 %collective-permute-start = (bf16[512,384]{1,0:T(8,128)(2,1)}, bf16[512,384]{1,0:T(8,128)(2,1)S(1)}, u32[]{:S(2)}, u32[]{:S(2)}) collective-permute-start(bf16[512,384]{1,0:T(8,128)(2,1)} %shard_map.46), channel_id=1, source_target_pairs={{0,0},{128,1},{32,2},{160,3},{64,4},{192,5},{96,6},{224,7},{16,8},... | collective-permute-start | bytes 1179656 | tf_op jit(solution)/shard_map/ppermute | solution.py:414
  35.9 0.8 copy-start.4
  36.7 23.0 %collective-permute-start.2 = (bf16[128,4096]{1,0:T(8,128)(2,1)S(1)}, bf16[128,4096]{1,0:T(8,128)(2,1)S(1)}, u32[]{:S(2)}, u32[]{:S(2)}) collective-permute-start(bf16[128,4096]{1,0:T(8,128)(2,1)S(1)} %bitcast.49), channel_id=1, source_target_pairs={{0,32},{32,64},{64,96},{96,0},{1,33},{33,65},{65,97},{97,1},{2,34}... | collective-permute-start | bytes 3145736 | tf_op jit(solution)/shard_map/ppermute | solution.py:70
  36.8 26.3 %collective-permute-start.3 = (bf16[128,4096]{1,0:T(8,128)(2,1)S(1)}, bf16[128,4096]{1,0:T(8,128)(2,1)S(1)}, u32[]{:S(2)}, u32[]{:S(2)}) collective-permute-start(bf16[128,4096]{1,0:T(8,128)(2,1)S(1)} %bitcast.50), channel_id=1, source_target_pairs={{0,96},{32,0},{64,32},{96,64},{1,97},{33,1},{65,33},{97,65},{2,98}... | collective-permute-start | bytes 3145736 | tf_op jit(solution)/shard_map/ppermute | solution.py:70
  38.2 24.8 %collective-permute-start.4 = (bf16[128,4096]{1,0:T(8,128)(2,1)S(1)}, bf16[128,4096]{1,0:T(8,128)(2,1)}, u32[]{:S(2)}, u32[]{:S(2)}) collective-permute-start(bf16[128,4096]{1,0:T(8,128)(2,1)S(1)} %bitcast.51), channel_id=1, source_target_pairs={{0,128},{128,0},{1,129},{129,1},{2,130},{130,2},{3,131},{131,3},{4... | collective-permute-start | bytes 3145736 | tf_op jit(solution)/shard_map/ppermute | solution.py:70
  59.7 53.2 %copy-start.1 = (bf16[128,4096]{1,0:T(8,128)(2,1)}, bf16[128,4096]{1,0:T(8,128)(2,1)S(1)}, u32[]{:S(2)}) copy-start(bf16[128,4096]{1,0:T(8,128)(2,1)S(1)} %collective-permute-done.2) | copy-start | bytes 3145732
  63.0 49.8 %copy-start.3 = (bf16[128,4096]{1,0:T(8,128)(2,1)}, bf16[128,4096]{1,0:T(8,128)(2,1)S(1)}, u32[]{:S(2)}) copy-start(bf16[128,4096]{1,0:T(8,128)(2,1)S(1)} %collective-permute-done.3) | copy-start | bytes 3145732
  63.0 40.7 %collective-permute-start.10 = (bf16[128,4096]{1,0:T(8,128)(2,1)S(1)}, bf16[128,4096]{1,0:T(8,128)(2,1)}, u32[]{:S(2)}, u32[]{:S(2)}) collective-permute-start(bf16[128,4096]{1,0:T(8,128)(2,1)S(1)} %collective-permute-done.3), channel_id=1, source_target_pairs={{0,128},{128,0},{1,129},{129,1},{2,130},{130,2},{3,131},{131,3},{4... | collective-permute-start | bytes 3145736 | tf_op jit(solution)/shard_map/ppermute | solution.py:70
  65.1 39.1 %collective-permute-start.9 = (bf16[128,4096]{1,0:T(8,128)(2,1)S(1)}, bf16[128,4096]{1,0:T(8,128)(2,1)}, u32[]{:S(2)}, u32[]{:S(2)}) collective-permute-start(bf16[128,4096]{1,0:T(8,128)(2,1)S(1)} %collective-permute-done.3), channel_id=1, source_target_pairs={{0,96},{32,0},{64,32},{96,64},{1,97},{33,1},{65,33},{97,65},{2,98}... | collective-permute-start | bytes 3145736 | tf_op jit(solution)/shard_map/ppermute | solution.py:70
  67.6 36.8 %collective-permute-start.8 = (bf16[128,4096]{1,0:T(8,128)(2,1)}, bf16[128,4096]{1,0:T(8,128)(2,1)}, u32[]{:S(2)}, u32[]{:S(2)}) collective-permute-start(bf16[128,4096]{1,0:T(8,128)(2,1)} %collective-permute-done.4), channel_id=1, source_target_pairs={{0,32},{32,64},{64,96},{96,0},{1,33},{33,65},{65,97},{97,1},{2,34}... | collective-permute-start | bytes 3145736 | tf_op jit(solution)/shard_map/ppermute | solution.py:70
  67.6 37.2 %collective-permute-start.1 = (bf16[128,4096]{1,0:T(8,128)(2,1)S(1)}, bf16[128,4096]{1,0:T(8,128)(2,1)}, u32[]{:S(2)}, u32[]{:S(2)}) collective-permute-start(bf16[128,4096]{1,0:T(8,128)(2,1)S(1)} %bitcast.52), channel_id=1, source_target_pairs={{0,16},{16,0},{1,17},{17,1},{2,18},{18,2},{3,19},{19,3},{4,20},{20... | collective-permute-start | bytes 3145736 | tf_op jit(solution)/shard_map/ppermute | solution.py:70
  68.2 36.7 %collective-permute-start.6 = (bf16[128,4096]{1,0:T(8,128)(2,1)S(1)}, bf16[128,4096]{1,0:T(8,128)(2,1)}, u32[]{:S(2)}, u32[]{:S(2)}) collective-permute-start(bf16[128,4096]{1,0:T(8,128)(2,1)S(1)} %collective-permute-done.3), channel_id=1, source_target_pairs={{0,16},{16,0},{1,17},{17,1},{2,18},{18,2},{3,19},{19,3},{4,20},{20... | collective-permute-start | bytes 3145736 | tf_op jit(solution)/shard_map/ppermute | solution.py:70
  68.2 29.4 %all-to-all-start = ((bf16[16,128,128]{2,1,0:T(8,128)(2,1)}), bf16[16,128,128]{2,1,0:T(8,128)(2,1)}, u32[]{:S(2)}, u32[]{:S(2)}) async-start(bf16[16,128,128]{2,1,0:T(8,128)(2,1)} %bitcast.78), calls=%async_computation | async-start | bytes 1048576 | tf_op jit(solution)/shard_map/all_to_all | solution.py:416
  97.6 26.7 %all-to-all-start.1 = ((bf16[16,128,128]{2,1,0:T(8,128)(2,1)}), bf16[16,128,128]{2,1,0:T(8,128)(2,1)}, u32[]{:S(2)}, u32[]{:S(2)}) async-start(bf16[16,128,128]{2,1,0:T(8,128)(2,1)} %all-to-all-done), calls=%async_computation.1 | async-start | bytes 1048576 | tf_op jit(solution)/shard_map/all_to_all | solution.py:416
  103.8 3.7 %collective-permute-start.7 = (bf16[128,4096]{1,0:T(8,128)(2,1)}, bf16[128,4096]{1,0:T(8,128)(2,1)}, u32[]{:S(2)}, u32[]{:S(2)}) collective-permute-start(bf16[128,4096]{1,0:T(8,128)(2,1)} %collective-permute-done.4), channel_id=1, source_target_pairs={{0,16},{16,0},{1,17},{17,1},{2,18},{18,2},{3,19},{19,3},{4,20},{20... | collective-permute-start | bytes 3145736 | tf_op jit(solution)/shard_map/ppermute | solution.py:70
  104.2 5.4 %collective-permute-start.5 = (bf16[128,4096]{1,0:T(8,128)(2,1)S(1)}, bf16[128,4096]{1,0:T(8,128)(2,1)}, u32[]{:S(2)}, u32[]{:S(2)}) collective-permute-start(bf16[128,4096]{1,0:T(8,128)(2,1)S(1)} %collective-permute-done.2), channel_id=1, source_target_pairs={{0,16},{16,0},{1,17},{17,1},{2,18},{18,2},{3,19},{19,3},{4,20},{20... | collective-permute-start | bytes 3145736 | tf_op jit(solution)/shard_map/ppermute | solution.py:70
  104.4 5.5 %collective-permute-start.11 = (bf16[128,4096]{1,0:T(8,128)(2,1)}, bf16[128,4096]{1,0:T(8,128)(2,1)}, u32[]{:S(2)}, u32[]{:S(2)}) collective-permute-start(bf16[128,4096]{1,0:T(8,128)(2,1)} %collective-permute-done.8.refs_0_), channel_id=1, source_target_pairs={{0,16},{16,0},{1,17},{17,1},{2,18},{18,2},{3,19},{19,3},{4,20},{20... | collective-permute-start | bytes 3145736 | tf_op jit(solution)/shard_map/ppermute | solution.py:70
  104.7 6.6 %collective-permute-start.12 = (bf16[128,4096]{1,0:T(8,128)(2,1)}, bf16[128,4096]{1,0:T(8,128)(2,1)}, u32[]{:S(2)}, u32[]{:S(2)}) collective-permute-start(bf16[128,4096]{1,0:T(8,128)(2,1)} %collective-permute-done.9.refs_2_), channel_id=1, source_target_pairs={{0,16},{16,0},{1,17},{17,1},{2,18},{18,2},{3,19},{19,3},{4,20},{20... | collective-permute-start | bytes 3145736 | tf_op jit(solution)/shard_map/ppermute | solution.py:70
  104.9 8.0 %collective-permute-start.13 = (bf16[128,4096]{1,0:T(8,128)(2,1)}, bf16[128,4096]{1,0:T(8,128)(2,1)}, u32[]{:S(2)}, u32[]{:S(2)}) collective-permute-start(bf16[128,4096]{1,0:T(8,128)(2,1)} %collective-permute-done.10.refs_1_), channel_id=1, source_target_pairs={{0,16},{16,0},{1,17},{17,1},{2,18},{18,2},{3,19},{19,3},{4,20},{20... | collective-permute-start | bytes 3145736 | tf_op jit(solution)/shard_map/ppermute | solution.py:70
  107.5 16.8 %collective-permute-start.14 = (bf16[48,4096]{1,0:T(8,128)(2,1)}, bf16[48,4096]{1,0:T(8,128)(2,1)S(1)}, u32[]{:S(2)}, u32[]{:S(2)}) collective-permute-start(bf16[48,4096]{1,0:T(8,128)(2,1)} %get-tuple-element.45), channel_id=1, source_target_pairs={{0,32},{32,64},{64,96},{96,0},{1,33},{33,65},{65,97},{97,1},{2,34}... | collective-permute-start | bytes 1179656 | tf_op jit(solution)/shard_map/ppermute | solution.py:70
  109.7 14.6 %collective-permute-start.15 = (bf16[48,4096]{1,0:T(8,128)(2,1)}, bf16[48,4096]{1,0:T(8,128)(2,1)}, u32[]{:S(2)}, u32[]{:S(2)}) collective-permute-start(bf16[48,4096]{1,0:T(8,128)(2,1)} %get-tuple-element.46), channel_id=1, source_target_pairs={{0,96},{32,0},{64,32},{96,64},{1,97},{33,1},{65,33},{97,65},{2,98}... | collective-permute-start | bytes 1179656 | tf_op jit(solution)/shard_map/ppermute | solution.py:70
  109.9 14.4 %collective-permute-start.16 = (bf16[32,4096]{1,0:T(8,128)(2,1)}, bf16[32,4096]{1,0:T(8,128)(2,1)}, u32[]{:S(2)}, u32[]{:S(2)}) collective-permute-start(bf16[32,4096]{1,0:T(8,128)(2,1)} %get-tuple-element.47), channel_id=1, source_target_pairs={{0,128},{128,0},{1,129},{129,1},{2,130},{130,2},{3,131},{131,3},{4... | collective-permute-start | bytes 786440 | tf_op jit(solution)/shard_map/ppermute | solution.py:70
  124.3 3.0 %collective-permute-start.17 = (bf16[48,4096]{1,0:T(8,128)(2,1)S(1)}, bf16[48,4096]{1,0:T(8,128)(2,1)S(1)}, u32[]{:S(2)}, u32[]{:S(2)}) collective-permute-start(bf16[48,4096]{1,0:T(8,128)(2,1)S(1)} %collective-permute-done.14), channel_id=1, source_target_pairs={{0,16},{16,0},{1,17},{17,1},{2,18},{18,2},{3,19},{19,3},{4,20},{20... | collective-permute-start | bytes 1179656 | tf_op jit(solution)/shard_map/ppermute | solution.py:70
  124.7 2.5 %collective-permute-start.18 = (bf16[48,4096]{1,0:T(8,128)(2,1)}, bf16[48,4096]{1,0:T(8,128)(2,1)S(1)}, u32[]{:S(2)}, u32[]{:S(2)}) collective-permute-start(bf16[48,4096]{1,0:T(8,128)(2,1)} %collective-permute-done.15), channel_id=1, source_target_pairs={{0,16},{16,0},{1,17},{17,1},{2,18},{18,2},{3,19},{19,3},{4,20},{20... | collective-permute-start | bytes 1179656 | tf_op jit(solution)/shard_map/ppermute | solution.py:70
  124.9 2.4 %collective-permute-start.19 = (bf16[32,4096]{1,0:T(8,128)(2,1)}, bf16[32,4096]{1,0:T(8,128)(2,1)S(1)}, u32[]{:S(2)}, u32[]{:S(2)}) collective-permute-start(bf16[32,4096]{1,0:T(8,128)(2,1)} %collective-permute-done.16), channel_id=1, source_target_pairs={{0,16},{16,0},{1,17},{17,1},{2,18},{18,2},{3,19},{19,3},{4,20},{20... | collective-permute-start | bytes 786440 | tf_op jit(solution)/shard_map/ppermute | solution.py:70
  127.3 13.3 %copy-start.2 = (bf16[128,4096]{1,0:T(8,128)(2,1)S(1)}, bf16[128,4096]{1,0:T(8,128)(2,1)}, u32[]{:S(2)}) copy-start(bf16[128,4096]{1,0:T(8,128)(2,1)} %copy-done.1) | copy-start | bytes 3145732
  137.8 7.8 %collective-permute-start.20 = (bf16[3,256,128]{2,1,0:T(8,128)(2,1)S(1)}, bf16[3,256,128]{2,1,0:T(8,128)(2,1)S(1)}, u32[]{:S(2)}, u32[]{:S(2)}) collective-permute-start(bf16[3,256,128]{2,1,0:T(8,128)(2,1)S(1)} %get-tuple-element.74), channel_id=1, source_target_pairs={{0,1},{1,2},{2,3},{3,4},{4,5},{5,6},{6,7},{7,0},{8,9},{9,10},{10,1... | collective-permute-start | bytes 589832 | tf_op jit(solution)/shard_map/ppermute | solution.py:70
  137.9 7.6 %collective-permute-start.21 = (bf16[3,256,128]{2,1,0:T(8,128)(2,1)S(1)}, bf16[3,256,128]{2,1,0:T(8,128)(2,1)S(1)}, u32[]{:S(2)}, u32[]{:S(2)}) collective-permute-start(bf16[3,256,128]{2,1,0:T(8,128)(2,1)S(1)} %get-tuple-element.73), channel_id=1, source_target_pairs={{0,7},{1,0},{2,1},{3,2},{4,3},{5,4},{6,5},{7,6},{8,15},{9,8},{10,9... | collective-permute-start | bytes 589832 | tf_op jit(solution)/shard_map/ppermute | solution.py:70
  145.7 11.6 %collective-permute-start.23 = (bf16[2,3,256,128]{3,2,1,0:T(8,128)(2,1)S(1)}, bf16[2,3,256,128]{3,2,1,0:T(8,128)(2,1)S(1)}, u32[]{:S(2)}, u32[]{:S(2)}) collective-permute-start(bf16[2,3,256,128]{3,2,1,0:T(8,128)(2,1)S(1)} %pad_maximum_fusion.1), channel_id=1, source_target_pairs={{0,7},{1,0},{2,1},{3,2},{4,3},{5,4},{6,5},{7,6},{8,15},{9,8},{10,9... | collective-permute-start | bytes 1179656 | tf_op jit(solution)/shard_map/ppermute | solution.py:70
  148.0 10.1 %collective-permute-start.22 = (bf16[2,3,256,128]{3,2,1,0:T(8,128)(2,1)S(1)}, bf16[2,3,256,128]{3,2,1,0:T(8,128)(2,1)S(1)}, u32[]{:S(2)}, u32[]{:S(2)}) collective-permute-start(bf16[2,3,256,128]{3,2,1,0:T(8,128)(2,1)S(1)} %pad_maximum_fusion), channel_id=1, source_target_pairs={{0,1},{1,2},{2,3},{3,4},{4,5},{5,6},{6,7},{7,0},{8,9},{9,10},{10,1... | collective-permute-start | bytes 1179656 | tf_op jit(solution)/shard_map/ppermute | solution.py:70
  158.2 9.2 %collective-permute-start.24 = (bf16[2,3,256,128]{3,2,1,0:T(8,128)(2,1)S(1)}, bf16[2,3,256,128]{3,2,1,0:T(8,128)(2,1)S(1)}, u32[]{:S(2)}, u32[]{:S(2)}) collective-permute-start(bf16[2,3,256,128]{3,2,1,0:T(8,128)(2,1)S(1)} %add_convert_fusion.4), channel_id=1, source_target_pairs={{0,1},{1,2},{2,3},{3,4},{4,5},{5,6},{6,7},{7,0},{8,9},{9,10},{10,1... | collective-permute-start | bytes 1179656 | tf_op jit(solution)/shard_map/ppermute | solution.py:70
  158.4 9.2 %collective-permute-start.26 = (bf16[2,3,256,128]{3,2,1,0:T(8,128)(2,1)S(1)}, bf16[2,3,256,128]{3,2,1,0:T(8,128)(2,1)S(1)}, u32[]{:S(2)}, u32[]{:S(2)}) collective-permute-start(bf16[2,3,256,128]{3,2,1,0:T(8,128)(2,1)S(1)} %add_convert_fusion.2), channel_id=1, source_target_pairs={{0,7},{1,0},{2,1},{3,2},{4,3},{5,4},{6,5},{7,6},{8,15},{9,8},{10,9... | collective-permute-start | bytes 1179656 | tf_op jit(solution)/shard_map/ppermute | solution.py:70
  167.6 8.3 %collective-permute-start.25 = (bf16[2,3,256,128]{3,2,1,0:T(8,128)(2,1)S(1)}, bf16[2,3,256,128]{3,2,1,0:T(8,128)(2,1)S(1)}, u32[]{:S(2)}, u32[]{:S(2)}) collective-permute-start(bf16[2,3,256,128]{3,2,1,0:T(8,128)(2,1)S(1)} %add_convert_fusion.3), channel_id=1, source_target_pairs={{0,1},{1,2},{2,3},{3,4},{4,5},{5,6},{6,7},{7,0},{8,9},{9,10},{10,1... | collective-permute-start | bytes 1179656 | tf_op jit(solution)/shard_map/ppermute | solution.py:70
  167.8 8.1 %collective-permute-start.27 = (bf16[2,3,256,128]{3,2,1,0:T(8,128)(2,1)S(1)}, bf16[2,3,256,128]{3,2,1,0:T(8,128)(2,1)S(1)}, u32[]{:S(2)}, u32[]{:S(2)}) collective-permute-start(bf16[2,3,256,128]{3,2,1,0:T(8,128)(2,1)S(1)} %add_convert_fusion.1), channel_id=1, source_target_pairs={{0,7},{1,0},{2,1},{3,2},{4,3},{5,4},{6,5},{7,6},{8,15},{9,8},{10,9... | collective-permute-start | bytes 1179656 | tf_op jit(solution)/shard_map/ppermute | solution.py:70
  176.1 13.7 %collective-permute-start.28 = (bf16[3,256,128]{2,1,0:T(8,128)(2,1)S(1)}, bf16[3,256,128]{2,1,0:T(8,128)(2,1)S(1)}, u32[]{:S(2)}, u32[]{:S(2)}) collective-permute-start(bf16[3,256,128]{2,1,0:T(8,128)(2,1)S(1)} %get-tuple-element.71), channel_id=1, source_target_pairs={{0,0},{1,129},{2,34},{3,163},{4,68},{5,197},{6,102},{7,231},{8,16}... | collective-permute-start | bytes 589832 | tf_op jit(solution)/shard_map/ppermute | solution.py:444
  186.5 4.7 %collective-permute-start.29 = (bf16[3,256,128]{2,1,0:T(8,128)(2,1)S(1)}, bf16[3,256,128]{2,1,0:T(8,128)(2,1)S(1)}, u32[]{:S(2)}, u32[]{:S(2)}) collective-permute-start(bf16[3,256,128]{2,1,0:T(8,128)(2,1)S(1)} %get-tuple-element.72), channel_id=1, source_target_pairs={{0,16},{1,145},{2,50},{3,179},{4,84},{5,213},{6,118},{7,247},{8,0}... | collective-permute-start | bytes 589832 | tf_op jit(solution)/shard_map/ppermute | solution.py:444
  191.2 14.9 %collective-permute-start.30 = (bf16[3,256,128]{2,1,0:T(8,128)(2,1)S(1)}, bf16[3,256,128]{2,1,0:T(8,128)(2,1)S(1)}, u32[]{:S(2)}, u32[]{:S(2)}) collective-permute-start(bf16[3,256,128]{2,1,0:T(8,128)(2,1)S(1)} %add_convert_fusion.5), channel_id=1, source_target_pairs={{0,0},{1,1},{2,6},{3,7},{4,4},{5,5},{6,2},{7,3},{8,8},{9,9},{10,14... | collective-permute-start | bytes 589832 | tf_op jit(solution)/shard_map/ppermute | solution.py:446
Sparse Core Ops, SparseCore 0:
  36.8 48.7 all-gather.1

commit v8 on v6

--- a/solution.py
+++ b/solution.py
@@ -20,8 +20,7 @@
 CUTS = ((0, CUT_A), (CUT_A, CUT_B), (CUT_B, PATCHES))
 STEP = 4
 FAR = (4,)
-NEAR_A = (3, 5)
-NEAR_B = (2, 6, 1, 7, 0)
+NEAR = ((3, 5), (2, 6), (1, 7, 0))
 CUT_FLOPS = 3 * 10**10
 WIDTH = 4096
 COLS = 3 * HEAD_DIM
@@ -216,7 +215,7 @@
             turned[j * HEAD_DIM : (j + 1) * HEAD_DIM, columns] = result.T.astype(jnp.bfloat16)
         return carry
 
-    lax.fori_loop(0, PATCHES // GROUP, body, 0)
+    lax.fori_loop(0, PATCHES // GROUP, body, 0, unroll=4)
 
 
 def share_kernel(count, order, mask, w_ref, g_ref, *refs):
@@ -318,7 +317,7 @@
             pltpu.SemaphoreType.DMA((1,)),
             pltpu.SemaphoreType.DMA((len(near), len(PARTS))),
         ],
-        compiler_params=pltpu.CompilerParams(vmem_limit_bytes=44 * 2**20),
+        compiler_params=pltpu.CompilerParams(vmem_limit_bytes=48 * 2**20),
         cost_estimate=pl.CostEstimate(
             flops=2 * ROWS * len(near) * CHUNK * COLS,
             bytes_accessed=2 * ROWS * len(near) * CHUNK,
@@ -345,7 +344,7 @@
             pltpu.SemaphoreType.DMA((len(PARTS),)),
             pltpu.SemaphoreType.DMA((FRAMES,)),
         ],
-        compiler_params=pltpu.CompilerParams(vmem_limit_bytes=44 * 2**20),
+        compiler_params=pltpu.CompilerParams(vmem_limit_bytes=48 * 2**20),
         cost_estimate=pl.CostEstimate(
             flops=2 * ROWS * WIDTH * COLS, bytes_accessed=2 * ROWS * WIDTH, transcendentals=0
         ),
@@ -375,16 +374,13 @@
     turned, far = far_shares(order, visible(table[24:40]), w, g, buffers)
     beside = lax.optimization_barrier
     shares = lambda near: near_shares(order, turned, buffers, near)
-    up, down, (share_3, share_5) = beside(
-        (shift(far[0], "z", 1), shift(far[1], "z", -1), shares(NEAR_A))
-    )
-    up = jnp.stack((add(up, share_3[0]), share_3[1]))
-    down = jnp.stack((share_5[0], add(down, share_5[1])))
-    up, down, near = beside((shift(up, "z", 1), shift(down, "z", -1), shares(NEAR_B)))
-    for step in (0, 2):
-        up = shift(add(up, near[step]), "z", 1)
-        down = shift(add(down, near[step + 1]), "z", -1)
-    mine = add(up, down, near[4])
+    up, down, near = beside((shift(far[0], "z", 1), shift(far[1], "z", -1), shares(NEAR[0])))
+    up = jnp.stack((add(up, near[0][0]), near[0][1]))
+    down = jnp.stack((near[1][0], add(down, near[1][1])))
+    for step in NEAR[1:]:
+        up, down, near = beside((shift(up, "z", 1), shift(down, "z", -1), shares(step)))
+        up, down = add(up, near[0]), add(down, near[1])
+    mine = add(shift(up, "z", 1), shift(down, "z", -1), near[2])
     yh = lax.axis_index("yh")
     total = None
     for flip in range(2):

time: 207 us -> 201 us (0.971)
  local copies, waits for them, and re-layouts: 9.01 us -> 4.54 us
  starting transfers between devices: 74.5 us -> 72.4 us
    unnamed x25 -> x13, local copies, waits for them, and re-layouts: 6.65 us -> 2.18 us
    pallas_call x2 -> x3, Pallas kernels: 14.2 us -> 16.2 us  [near_shares(): pl.pallas_call(functools.partial(near_kernel, count, near), out_shape=[SH...]
  transfers between devices with their start and end apart: 34 -> 34, of which waited for: 11 -> 13; matrix products, arithmetic and copies ran while one was open for 2% -> 1% of each run, Pallas kernels for 9% -> 11%
where the time goes in v8:
time: 201 us; the launch traced here: 198 us
  starting transfers between devices  72.4 us (36%)
  waiting for transfers between devices  64.7 us (32%)
  Pallas kernels  40.6 us (20%)
  between operations  13.7 us (7%)
  local copies, waits for them, and re-layouts  4.54 us (2%)
    ppermute x27, starting transfers between devices, shift(): lax.ppermute(value, axis, [(i, (i + by) % count) for i in range(count)])  28.2 us
    ppermute x27, waiting for transfers between devices, shift(): lax.ppermute(value, axis, [(i, (i + by) % count) for i in range(count)])  23.3 us
    all_to_all x2, starting transfers between devices, local(): lax.all_to_all(value, axes, split_axis=0, concat_axis=0, tiled=True)  21.1 us
    pallas_call x1, Pallas kernels, far_shares(): pl.pallas_call(functools.partial(share_kernel, count), out_shape=[jax.Sha...  19.7 us
    pallas_call x3, Pallas kernels, near_shares(): pl.pallas_call(functools.partial(near_kernel, count, near), out_shape=[SH...  16.2 us
    ppermute x1, waiting for transfers between devices, local(): rows_w = lax.ppermute(rows_w, AXES, worker_moves())  15.5 us
    all_to_all x2, waiting for transfers between devices, local(): lax.all_to_all(value, axes, split_axis=0, concat_axis=0, tiled=True)  12.4 us
    ppermute x1, starting transfers between devices, local(): rows_w = lax.ppermute(rows_w, AXES, worker_moves())  9.82 us
  transfers between devices with their start and end apart: 34, of which 13 were waited for; matrix products, arithmetic and copies ran while one was open for 1% of the time, Pallas kernels for 11%

profile of v8, /device:TPU:3, one launch (start us, length us, event | category | flops | bytes accessed | tf_op | source)
XLA Modules:
  0.0 197.9 jit_solution(11997784627896646407)
XLA Ops:
  6.5 1.2 collective-permute-start.2
  7.8 0.3 collective-permute-start.3
  8.0 1.3 collective-permute-start.4
  9.3 0.7 constant_dynamic-slice_fusion
  10.0 0.6 slice.40
  10.6 2.4 %shard_map.46 = bf16[512,384]{1,0:T(8,128)(2,1)} custom-call(s32[1]{0:T(128)} %bitcast.2.start, bf16[3,4096,128]{2,1,0:T(8,128)(2,1)} %bitcast.77), custom_call_target="tpu_custom_call" | custom-call | tf_op jit(solution)/shard_map/pallas_call | solution.py:182
  13.0 9.8 %collective-permute-start = (bf16[512,384]{1,0:T(8,128)(2,1)}, bf16[512,384]{1,0:T(8,128)(2,1)S(1)}, u32[]{:S(2)}, u32[]{:S(2)}) collective-permute-start(bf16[512,384]{1,0:T(8,128)(2,1)} %shard_map.46), channel_id=1, source_target_pairs={{0,0},{128,1},{32,2},{160,3},{64,4},{192,5},{96,6},{224,7},{16,8},... | collective-permute-start | bytes 1179656 | tf_op jit(solution)/shard_map/ppermute | solution.py:361
  22.9 15.5 %collective-permute-done = bf16[512,384]{1,0:T(8,128)(2,1)S(1)} collective-permute-done((bf16[512,384]{1,0:T(8,128)(2,1)}, bf16[512,384]{1,0:T(8,128)(2,1)S(1)}, u32[]{:S(2)}, u32[]{:S(2)}) %collective-permute-start) | collective-permute-done | bytes 393248 | tf_op jit(solution)/shard_map/ppermute | solution.py:361
  38.4 0.8 copy-done.4
  39.2 0.1 collective-permute-start.10
  39.3 2.9 %collective-permute-start.9 = (bf16[128,4096]{1,0:T(8,128)(2,1)}, bf16[128,4096]{1,0:T(8,128)(2,1)}, u32[]{:S(2)}, u32[]{:S(2)}) collective-permute-start(bf16[128,4096]{1,0:T(8,128)(2,1)} %collective-permute-done.3), channel_id=1, source_target_pairs={{0,96},{32,0},{64,32},{96,64},{1,97},{33,1},{65,33},{97,65},{2,98}... | collective-permute-start | bytes 3145736 | tf_op jit(solution)/shard_map/ppermute | solution.py:69
  42.2 11.4 %all-to-all-start = ((bf16[16,128,128]{2,1,0:T(8,128)(2,1)}), bf16[16,128,128]{2,1,0:T(8,128)(2,1)}, u32[]{:S(2)}, u32[]{:S(2)}) async-start(bf16[16,128,128]{2,1,0:T(8,128)(2,1)} %bitcast.5), calls=%async_computation | async-start | bytes 1048576 | tf_op jit(solution)/shard_map/all_to_all | solution.py:363
  53.7 3.1 %collective-permute-start.1 = (bf16[128,4096]{1,0:T(8,128)(2,1)S(1)}, bf16[128,4096]{1,0:T(8,128)(2,1)S(1)}, u32[]{:S(2)}, u32[]{:S(2)}) collective-permute-start(bf16[128,4096]{1,0:T(8,128)(2,1)S(1)} %bitcast.52), channel_id=1, source_target_pairs={{0,16},{16,0},{1,17},{17,1},{2,18},{18,2},{3,19},{19,3},{4,20},{20... | collective-permute-start | bytes 3145736 | tf_op jit(solution)/shard_map/ppermute | solution.py:69
  56.7 0.1 collective-permute-start.6
  56.8 10.7 %collective-permute-done.10.refs_1_ = bf16[128,4096]{1,0:T(8,128)(2,1)} collective-permute-done((bf16[128,4096]{1,0:T(8,128)(2,1)}, bf16[128,4096]{1,0:T(8,128)(2,1)}, u32[]{:S(2)}, u32[]{:S(2)}) %collective-permute-start.10) | collective-permute-done | bytes 1048608 | tf_op jit(solution)/shard_map/ppermute | solution.py:69
  67.5 0.5 collective-permute-start.5
  68.0 4.9 %all-to-all-done = bf16[16,128,128]{2,1,0:T(8,128)(2,1)} async-done(((bf16[16,128,128]{2,1,0:T(8,128)(2,1)}), bf16[16,128,128]{2,1,0:T(8,128)(2,1)}, u32[]{:S(2)}, u32[]{:S(2)}) %all-to-all-start) | async-done | bytes 524320 | tf_op jit(solution)/shard_map/all_to_all | solution.py:363
  72.9 2.3 %shard_map.47 = (bf16[48,4096]{1,0:T(8,128)(2,1)}, bf16[48,4096]{1,0:T(8,128)(2,1)}, bf16[32,4096]{1,0:T(8,128)(2,1)}) custom-call(bf16[128,4096]{1,0:T(8,128)(2,1)} %collective-permute-done.8.refs_0_, bf16[128,4096]{1,0:T(8,128)(2,1)} %collective-permute-done.10.refs_1_, bf16[128,4096]{1,0:T(8,128)(2,1)} %collective-permute-done.9.refs_2_), custom_call_target="tpu_custom_call" | custom-call | flops 30000001024 | tf_op jit(solution)/shard_map/pallas_call | solution.py:91
  75.2 0.8 collective-permute-start.14
  76.0 3.2 %collective-permute-start.15 = (bf16[48,4096]{1,0:T(8,128)(2,1)}, bf16[48,4096]{1,0:T(8,128)(2,1)}, u32[]{:S(2)}, u32[]{:S(2)}) collective-permute-start(bf16[48,4096]{1,0:T(8,128)(2,1)} %get-tuple-element.48), channel_id=1, source_target_pairs={{0,96},{32,0},{64,32},{96,64},{1,97},{33,1},{65,33},{97,65},{2,98}... | collective-permute-start | bytes 1179656 | tf_op jit(solution)/shard_map/ppermute | solution.py:69
  79.2 2.3 %collective-permute-start.16 = (bf16[32,4096]{1,0:T(8,128)(2,1)}, bf16[32,4096]{1,0:T(8,128)(2,1)}, u32[]{:S(2)}, u32[]{:S(2)}) collective-permute-start(bf16[32,4096]{1,0:T(8,128)(2,1)} %get-tuple-element.49), channel_id=1, source_target_pairs={{0,128},{128,0},{1,129},{129,1},{2,130},{130,2},{3,131},{131,3},{4... | collective-permute-start | bytes 786440 | tf_op jit(solution)/shard_map/ppermute | solution.py:69
  81.6 9.7 %all-to-all-start.1 = ((bf16[16,128,128]{2,1,0:T(8,128)(2,1)}), bf16[16,128,128]{2,1,0:T(8,128)(2,1)}, u32[]{:S(2)}, u32[]{:S(2)}) async-start(bf16[16,128,128]{2,1,0:T(8,128)(2,1)} %all-to-all-done), calls=%async_computation.1 | async-start | bytes 1048576 | tf_op jit(solution)/shard_map/all_to_all | solution.py:363
  91.2 0.4 collective-permute-start.11
  91.7 0.1 collective-permute-start.12
  91.8 0.4 collective-permute-start.13
  92.3 7.5 %all-to-all-done.1 = bf16[16,128,128]{2,1,0:T(8,128)(2,1)} async-done(((bf16[16,128,128]{2,1,0:T(8,128)(2,1)}), bf16[16,128,128]{2,1,0:T(8,128)(2,1)}, u32[]{:S(2)}, u32[]{:S(2)}) %all-to-all-start.1) | async-done | bytes 524320 | tf_op jit(solution)/shard_map/all_to_all | solution.py:363
  99.8 1.3 collective-permute-start.19
  101.3 0.1 le.15
  101.4 0.1 eq.18
  101.5 0.3 collective-permute-start.17
  101.8 0.9 collective-permute-done.19
  102.7 0.4 collective-permute-start.18
  103.0 0.7 slice_bitcast_fusion.3.order
  103.7 0.1 and_convert_fusion.mask
  103.8 0.8 collective-permute-done.18
  104.6 19.7 %shard_map.48 = (bf16[384,2048]{1,0:T(8,128)(2,1)}, bf16[2,3,256,128]{3,2,1,0:T(8,128)(2,1)S(1)}) custom-call(s32[24]{0:T(128)S(1)} %slice_bitcast_fusion.3.order, f32[256,256]{1,0:T(8,128)S(1)} %and_convert_fusion.mask, bf16[4096,384]{1,0:T(8,128)(2,1)} %all-gather.2.cloned.1.call-done.w_ref, bf16[16,8,16,128]{3,2,1,0:T(8,128)(2,1)} %bitcast.6.g_ref, ...), custom_call_target="tpu_custom_call" | custom-call | flops 6442450944 | bytes 16777216 | tf_op jit(solution)/shard_map/pallas_call | solution.py:332
  124.4 0.1 collective-permute-start.20
  124.5 2.7 %collective-permute-start.21 = (bf16[3,256,128]{2,1,0:T(8,128)(2,1)S(1)}, bf16[3,256,128]{2,1,0:T(8,128)(2,1)S(1)}, u32[]{:S(2)}, u32[]{:S(2)}) collective-permute-start(bf16[3,256,128]{2,1,0:T(8,128)(2,1)S(1)} %get-tuple-element.77), channel_id=1, source_target_pairs={{0,7},{1,0},{2,1},{3,2},{4,3},{5,4},{6,5},{7,6},{8,15},{9,8},{10,9... | collective-permute-start | bytes 589832 | tf_op jit(solution)/shard_map/ppermute | solution.py:69
  127.2 4.9 %shard_map.49 = (bf16[2,3,256,128]{3,2,1,0:T(8,128)(2,1)S(1)}, bf16[2,3,256,128]{3,2,1,0:T(8,128)(2,1)S(1)}) custom-call(s32[24]{0:T(128)S(1)} %slice_bitcast_fusion.3.order, bf16[384,2048]{1,0:T(8,128)(2,1)} %get-tuple-element.54.turned_ref, bf16[8,16,4096]{2,1,0:T(8,128)(2,1)S(1)} %bitcast.54, bf16[8,16,4096]{2,1,0:T(8,128)(2,1)S(1)} %bitcast.62, ...), custom_call_target="tpu_custom_call" | custom-call | flops 1610612736 | bytes 4194304 | tf_op jit(solution)/shard_map/pallas_call | solution.py:309
  132.2 2.1 %collective-permute-start.23 = (bf16[2,3,256,128]{3,2,1,0:T(8,128)(2,1)S(1)}, bf16[2,3,256,128]{3,2,1,0:T(8,128)(2,1)S(1)}, u32[]{:S(2)}, u32[]{:S(2)}) collective-permute-start(bf16[2,3,256,128]{3,2,1,0:T(8,128)(2,1)S(1)} %pad_maximum_fusion.1), channel_id=1, source_target_pairs={{0,7},{1,0},{2,1},{3,2},{4,3},{5,4},{6,5},{7,6},{8,15},{9,8},{10,9... | collective-permute-start | bytes 1179656 | tf_op jit(solution)/shard_map/ppermute | solution.py:69
  134.5 0.1 collective-permute-start.22
  134.6 4.9 %shard_map.50 = (bf16[2,3,256,128]{3,2,1,0:T(8,128)(2,1)S(1)}, bf16[2,3,256,128]{3,2,1,0:T(8,128)(2,1)S(1)}) custom-call(s32[24]{0:T(128)S(1)} %slice_bitcast_fusion.3.order, bf16[384,2048]{1,0:T(8,128)(2,1)} %get-tuple-element.54.turned_ref, bf16[8,16,4096]{2,1,0:T(8,128)(2,1)S(1)} %bitcast.55, bf16[8,16,4096]{2,1,0:T(8,128)(2,1)S(1)} %bitcast.63, ...), custom_call_target="tpu_custom_call" | custom-call | flops 1610612736 | bytes 4194304 | tf_op jit(solution)/shard_map/pallas_call | solution.py:309
  139.5 2.5 %collective-permute-done.23 = bf16[2,3,256,128]{3,2,1,0:T(8,128)(2,1)S(1)} collective-permute-done((bf16[2,3,256,128]{3,2,1,0:T(8,128)(2,1)S(1)}, bf16[2,3,256,128]{3,2,1,0:T(8,128)(2,1)S(1)}, u32[]{:S(2)}, u32[]{:S(2)}) %collective-permute-start.23) | collective-permute-done | bytes 393248 | tf_op jit(solution)/shard_map/ppermute | solution.py:69
  142.0 2.6 %collective-permute-done.22 = bf16[2,3,256,128]{3,2,1,0:T(8,128)(2,1)S(1)} collective-permute-done((bf16[2,3,256,128]{3,2,1,0:T(8,128)(2,1)S(1)}, bf16[2,3,256,128]{3,2,1,0:T(8,128)(2,1)S(1)}, u32[]{:S(2)}, u32[]{:S(2)}) %collective-permute-start.22) | collective-permute-done | bytes 393248 | tf_op jit(solution)/shard_map/ppermute | solution.py:69
  144.6 0.1 add_convert_fusion.3
  144.7 0.2 collective-permute-start.25
  144.9 0.1 add_convert_fusion.4
  145.0 1.5 collective-permute-start.24
  146.4 6.4 %shard_map.51 = (bf16[2,3,256,128]{3,2,1,0:T(8,128)(2,1)S(1)}, bf16[2,3,256,128]{3,2,1,0:T(8,128)(2,1)S(1)}, bf16[2,3,256,128]{3,2,1,0:T(8,128)(2,1)S(1)}) custom-call(s32[24]{0:T(128)S(1)} %slice_bitcast_fusion.3.order, bf16[384,2048]{1,0:T(8,128)(2,1)} %get-tuple-element.54.turned_ref, bf16[8,16,4096]{2,1,0:T(8,128)(2,1)S(1)} %bitcast.56, ...), custom_call_target="tpu_custom_call" | custom-call | flops 2415919104 | bytes 6291456 | tf_op jit(solution)/shard_map/pallas_call | solution.py:309
  152.8 0.7 copy-done.3
  153.5 0.6 collective-permute-done.24
  154.1 0.1 add_convert_fusion.2
  154.2 0.1 collective-permute-start.26
  154.3 0.1 add_convert_fusion.1
  154.5 2.7 %collective-permute-start.27 = (bf16[2,3,256,128]{3,2,1,0:T(8,128)(2,1)S(1)}, bf16[2,3,256,128]{3,2,1,0:T(8,128)(2,1)S(1)}, u32[]{:S(2)}, u32[]{:S(2)}) collective-permute-start(bf16[2,3,256,128]{3,2,1,0:T(8,128)(2,1)S(1)} %add_convert_fusion.1), channel_id=1, source_target_pairs={{0,7},{1,0},{2,1},{3,2},{4,3},{5,4},{6,5},{7,6},{8,15},{9,8},{10,9... | collective-permute-start | bytes 1179656 | tf_op jit(solution)/shard_map/ppermute | solution.py:69
  157.2 5.3 %collective-permute-done.26 = bf16[2,3,256,128]{3,2,1,0:T(8,128)(2,1)S(1)} collective-permute-done((bf16[2,3,256,128]{3,2,1,0:T(8,128)(2,1)S(1)}, bf16[2,3,256,128]{3,2,1,0:T(8,128)(2,1)S(1)}, u32[]{:S(2)}, u32[]{:S(2)}) %collective-permute-start.26) | collective-permute-done | bytes 393248 | tf_op jit(solution)/shard_map/ppermute | solution.py:69
  162.5 1.2 add_convert_fusion
  163.7 6.6 %collective-permute-start.28 = (bf16[3,256,128]{2,1,0:T(8,128)(2,1)S(1)}, bf16[3,256,128]{2,1,0:T(8,128)(2,1)S(1)}, u32[]{:S(2)}, u32[]{:S(2)}) collective-permute-start(bf16[3,256,128]{2,1,0:T(8,128)(2,1)S(1)} %get-tuple-element.75), channel_id=1, source_target_pairs={{0,0},{1,129},{2,34},{3,163},{4,68},{5,197},{6,102},{7,231},{8,16}... | collective-permute-start | bytes 589832 | tf_op jit(solution)/shard_map/ppermute | solution.py:388
  170.3 0.1 collective-permute-start.29
  170.4 3.2 %collective-permute-done.28 = bf16[3,256,128]{2,1,0:T(8,128)(2,1)S(1)} collective-permute-done((bf16[3,256,128]{2,1,0:T(8,128)(2,1)S(1)}, bf16[3,256,128]{2,1,0:T(8,128)(2,1)S(1)}, u32[]{:S(2)}, u32[]{:S(2)}) %collective-permute-start.28) | collective-permute-done | bytes 196640 | tf_op jit(solution)/shard_map/ppermute | solution.py:388
  173.7 1.4 collective-permute-done.29
  175.1 6.6 %collective-permute-start.30 = (bf16[3,256,128]{2,1,0:T(8,128)(2,1)S(1)}, bf16[3,256,128]{2,1,0:T(8,128)(2,1)S(1)}, u32[]{:S(2)}, u32[]{:S(2)}) collective-permute-start(bf16[3,256,128]{2,1,0:T(8,128)(2,1)S(1)} %add_convert_fusion.5), channel_id=1, source_target_pairs={{0,0},{1,1},{2,6},{3,7},{4,4},{5,5},{6,2},{7,3},{8,8},{9,9},{10,14... | collective-permute-start | bytes 589832 | tf_op jit(solution)/shard_map/ppermute | solution.py:390
  181.7 8.7 %collective-permute-done.30 = bf16[3,256,128]{2,1,0:T(8,128)(2,1)S(1)} collective-permute-done((bf16[3,256,128]{2,1,0:T(8,128)(2,1)S(1)}, bf16[3,256,128]{2,1,0:T(8,128)(2,1)S(1)}, u32[]{:S(2)}, u32[]{:S(2)}) %collective-permute-start.30) | collective-permute-done | bytes 196640 | tf_op jit(solution)/shard_map/ppermute | solution.py:390
  190.4 0.7 copy.6
  (47 shorter events, 0.6 us)
Async XLA Ops:
  6.5 47.1 %copy-start = (bf16[1,128,4096]{2,1,0:T(8,128)(2,1)S(1)}, bf16[1,128,4096]{2,1,0:T(8,128)(2,1)}, u32[]{:S(2)}) copy-start(bf16[1,128,4096]{2,1,0:T(8,128)(2,1)} %param.4) | copy-start | bytes 3145732
  6.5 98.1 %all-gather.2.cloned.1.call-start = ((), (), s32[]{:S(2)}) async-start(), calls=%async_computation.2 | async-start | bytes 3538944 | tf_op jit(solution)/shard_map/all_gather | solution.py:362
  6.5 32.6 %collective-permute-start.2 = (bf16[128,4096]{1,0:T(8,128)(2,1)}, bf16[128,4096]{1,0:T(8,128)(2,1)S(1)}, u32[]{:S(2)}, u32[]{:S(2)}) collective-permute-start(bf16[128,4096]{1,0:T(8,128)(2,1)} %bitcast.49), channel_id=1, source_target_pairs={{0,32},{32,64},{64,96},{96,0},{1,33},{33,65},{65,97},{97,1},{2,34}... | collective-permute-start | bytes 3145736 | tf_op jit(solution)/shard_map/ppermute | solution.py:69
  7.8 31.4 %collective-permute-start.3 = (bf16[128,4096]{1,0:T(8,128)(2,1)}, bf16[128,4096]{1,0:T(8,128)(2,1)}, u32[]{:S(2)}, u32[]{:S(2)}) collective-permute-start(bf16[128,4096]{1,0:T(8,128)(2,1)} %bitcast.50), channel_id=1, source_target_pairs={{0,96},{32,0},{64,32},{96,64},{1,97},{33,1},{65,33},{97,65},{2,98}... | collective-permute-start | bytes 3145736 | tf_op jit(solution)/shard_map/ppermute | solution.py:69
  8.0 31.2 %collective-permute-start.4 = (bf16[128,4096]{1,0:T(8,128)(2,1)}, bf16[128,4096]{1,0:T(8,128)(2,1)}, u32[]{:S(2)}, u32[]{:S(2)}) collective-permute-start(bf16[128,4096]{1,0:T(8,128)(2,1)} %bitcast.51), channel_id=1, source_target_pairs={{0,128},{128,0},{1,129},{129,1},{2,130},{130,2},{3,131},{131,3},{4... | collective-permute-start | bytes 3145736 | tf_op jit(solution)/shard_map/ppermute | solution.py:69
  10.0 91.2 %copy-start.5 = (s32[1,48]{1,0:T(1,128)}, s32[1,48]{1,0:T(1,128)S(1)}, u32[]{:S(2)}) copy-start(s32[1,48]{1,0:T(1,128)S(1)} %constant_dynamic-slice_fusion) | copy-start | bytes 580
  13.0 25.4 %collective-permute-start = (bf16[512,384]{1,0:T(8,128)(2,1)}, bf16[512,384]{1,0:T(8,128)(2,1)S(1)}, u32[]{:S(2)}, u32[]{:S(2)}) collective-permute-start(bf16[512,384]{1,0:T(8,128)(2,1)} %shard_map.46), channel_id=1, source_target_pairs={{0,0},{128,1},{32,2},{160,3},{64,4},{192,5},{96,6},{224,7},{16,8},... | collective-permute-start | bytes 1179656 | tf_op jit(solution)/shard_map/ppermute | solution.py:361
  38.4 0.8 copy-start.4
  39.2 36.0 %copy-start.1 = (bf16[128,4096]{1,0:T(8,128)(2,1)}, bf16[128,4096]{1,0:T(8,128)(2,1)S(1)}, u32[]{:S(2)}) copy-start(bf16[128,4096]{1,0:T(8,128)(2,1)S(1)} %collective-permute-done.2) | copy-start | bytes 3145732
  39.2 28.3 %collective-permute-start.10 = (bf16[128,4096]{1,0:T(8,128)(2,1)}, bf16[128,4096]{1,0:T(8,128)(2,1)}, u32[]{:S(2)}, u32[]{:S(2)}) collective-permute-start(bf16[128,4096]{1,0:T(8,128)(2,1)} %collective-permute-done.3), channel_id=1, source_target_pairs={{0,128},{128,0},{1,129},{129,1},{2,130},{130,2},{3,131},{131,3},{4... | collective-permute-start | bytes 3145736 | tf_op jit(solution)/shard_map/ppermute | solution.py:69
  39.3 28.2 %collective-permute-start.9 = (bf16[128,4096]{1,0:T(8,128)(2,1)}, bf16[128,4096]{1,0:T(8,128)(2,1)}, u32[]{:S(2)}, u32[]{:S(2)}) collective-permute-start(bf16[128,4096]{1,0:T(8,128)(2,1)} %collective-permute-done.3), channel_id=1, source_target_pairs={{0,96},{32,0},{64,32},{96,64},{1,97},{33,1},{65,33},{97,65},{2,98}... | collective-permute-start | bytes 3145736 | tf_op jit(solution)/shard_map/ppermute | solution.py:69
  42.2 30.7 %collective-permute-start.8 = (bf16[128,4096]{1,0:T(8,128)(2,1)}, bf16[128,4096]{1,0:T(8,128)(2,1)}, u32[]{:S(2)}, u32[]{:S(2)}) collective-permute-start(bf16[128,4096]{1,0:T(8,128)(2,1)} %collective-permute-done.4), channel_id=1, source_target_pairs={{0,32},{32,64},{64,96},{96,0},{1,33},{33,65},{65,97},{97,1},{2,34}... | collective-permute-start | bytes 3145736 | tf_op jit(solution)/shard_map/ppermute | solution.py:69
  42.2 30.7 %all-to-all-start = ((bf16[16,128,128]{2,1,0:T(8,128)(2,1)}), bf16[16,128,128]{2,1,0:T(8,128)(2,1)}, u32[]{:S(2)}, u32[]{:S(2)}) async-start(bf16[16,128,128]{2,1,0:T(8,128)(2,1)} %bitcast.5), calls=%async_computation | async-start | bytes 1048576 | tf_op jit(solution)/shard_map/all_to_all | solution.py:363
  53.7 22.3 %collective-permute-start.1 = (bf16[128,4096]{1,0:T(8,128)(2,1)S(1)}, bf16[128,4096]{1,0:T(8,128)(2,1)S(1)}, u32[]{:S(2)}, u32[]{:S(2)}) collective-permute-start(bf16[128,4096]{1,0:T(8,128)(2,1)S(1)} %bitcast.52), channel_id=1, source_target_pairs={{0,16},{16,0},{1,17},{17,1},{2,18},{18,2},{3,19},{19,3},{4,20},{20... | collective-permute-start | bytes 3145736 | tf_op jit(solution)/shard_map/ppermute | solution.py:69
  56.7 22.5 %collective-permute-start.6 = (bf16[128,4096]{1,0:T(8,128)(2,1)}, bf16[128,4096]{1,0:T(8,128)(2,1)}, u32[]{:S(2)}, u32[]{:S(2)}) collective-permute-start(bf16[128,4096]{1,0:T(8,128)(2,1)} %collective-permute-done.3), channel_id=1, source_target_pairs={{0,16},{16,0},{1,17},{17,1},{2,18},{18,2},{3,19},{19,3},{4,20},{20... | collective-permute-start | bytes 3145736 | tf_op jit(solution)/shard_map/ppermute | solution.py:69
  67.5 32.3 %collective-permute-start.7 = (bf16[128,4096]{1,0:T(8,128)(2,1)}, bf16[128,4096]{1,0:T(8,128)(2,1)}, u32[]{:S(2)}, u32[]{:S(2)}) collective-permute-start(bf16[128,4096]{1,0:T(8,128)(2,1)} %collective-permute-done.4), channel_id=1, source_target_pairs={{0,16},{16,0},{1,17},{17,1},{2,18},{18,2},{3,19},{19,3},{4,20},{20... | collective-permute-start | bytes 3145736 | tf_op jit(solution)/shard_map/ppermute | solution.py:69
  67.5 34.0 %collective-permute-start.5 = (bf16[128,4096]{1,0:T(8,128)(2,1)S(1)}, bf16[128,4096]{1,0:T(8,128)(2,1)}, u32[]{:S(2)}, u32[]{:S(2)}) collective-permute-start(bf16[128,4096]{1,0:T(8,128)(2,1)S(1)} %collective-permute-done.2), channel_id=1, source_target_pairs={{0,16},{16,0},{1,17},{17,1},{2,18},{18,2},{3,19},{19,3},{4,20},{20... | collective-permute-start | bytes 3145736 | tf_op jit(solution)/shard_map/ppermute | solution.py:69
  75.2 16.5 %collective-permute-start.14 = (bf16[48,4096]{1,0:T(8,128)(2,1)}, bf16[48,4096]{1,0:T(8,128)(2,1)S(1)}, u32[]{:S(2)}, u32[]{:S(2)}) collective-permute-start(bf16[48,4096]{1,0:T(8,128)(2,1)} %get-tuple-element.47), channel_id=1, source_target_pairs={{0,32},{32,64},{64,96},{96,0},{1,33},{33,65},{65,97},{97,1},{2,34}... | collective-permute-start | bytes 1179656 | tf_op jit(solution)/shard_map/ppermute | solution.py:69
  76.0 15.8 %collective-permute-start.15 = (bf16[48,4096]{1,0:T(8,128)(2,1)}, bf16[48,4096]{1,0:T(8,128)(2,1)}, u32[]{:S(2)}, u32[]{:S(2)}) collective-permute-start(bf16[48,4096]{1,0:T(8,128)(2,1)} %get-tuple-element.48), channel_id=1, source_target_pairs={{0,96},{32,0},{64,32},{96,64},{1,97},{33,1},{65,33},{97,65},{2,98}... | collective-permute-start | bytes 1179656 | tf_op jit(solution)/shard_map/ppermute | solution.py:69
  79.2 12.0 %collective-permute-start.16 = (bf16[32,4096]{1,0:T(8,128)(2,1)}, bf16[32,4096]{1,0:T(8,128)(2,1)}, u32[]{:S(2)}, u32[]{:S(2)}) collective-permute-start(bf16[32,4096]{1,0:T(8,128)(2,1)} %get-tuple-element.49), channel_id=1, source_target_pairs={{0,128},{128,0},{1,129},{129,1},{2,130},{130,2},{3,131},{131,3},{4... | collective-permute-start | bytes 786440 | tf_op jit(solution)/shard_map/ppermute | solution.py:69
  81.6 18.3 %all-to-all-start.1 = ((bf16[16,128,128]{2,1,0:T(8,128)(2,1)}), bf16[16,128,128]{2,1,0:T(8,128)(2,1)}, u32[]{:S(2)}, u32[]{:S(2)}) async-start(bf16[16,128,128]{2,1,0:T(8,128)(2,1)} %all-to-all-done), calls=%async_computation.1 | async-start | bytes 1048576 | tf_op jit(solution)/shard_map/all_to_all | solution.py:363
  91.2 13.3 %collective-permute-start.11 = (bf16[128,4096]{1,0:T(8,128)(2,1)}, bf16[128,4096]{1,0:T(8,128)(2,1)}, u32[]{:S(2)}, u32[]{:S(2)}) collective-permute-start(bf16[128,4096]{1,0:T(8,128)(2,1)} %collective-permute-done.8.refs_0_), channel_id=1, source_target_pairs={{0,16},{16,0},{1,17},{17,1},{2,18},{18,2},{3,19},{19,3},{4,20},{20... | collective-permute-start | bytes 3145736 | tf_op jit(solution)/shard_map/ppermute | solution.py:69
  91.7 12.9 %collective-permute-start.12 = (bf16[128,4096]{1,0:T(8,128)(2,1)}, bf16[128,4096]{1,0:T(8,128)(2,1)}, u32[]{:S(2)}, u32[]{:S(2)}) collective-permute-start(bf16[128,4096]{1,0:T(8,128)(2,1)} %collective-permute-done.9.refs_2_), channel_id=1, source_target_pairs={{0,16},{16,0},{1,17},{17,1},{2,18},{18,2},{3,19},{19,3},{4,20},{20... | collective-permute-start | bytes 3145736 | tf_op jit(solution)/shard_map/ppermute | solution.py:69
  91.8 12.7 %collective-permute-start.13 = (bf16[128,4096]{1,0:T(8,128)(2,1)}, bf16[128,4096]{1,0:T(8,128)(2,1)}, u32[]{:S(2)}, u32[]{:S(2)}) collective-permute-start(bf16[128,4096]{1,0:T(8,128)(2,1)} %collective-permute-done.10.refs_1_), channel_id=1, source_target_pairs={{0,16},{16,0},{1,17},{17,1},{2,18},{18,2},{3,19},{19,3},{4,20},{20... | collective-permute-start | bytes 3145736 | tf_op jit(solution)/shard_map/ppermute | solution.py:69
  99.8 2.8 %collective-permute-start.19 = (bf16[32,4096]{1,0:T(8,128)(2,1)}, bf16[32,4096]{1,0:T(8,128)(2,1)}, u32[]{:S(2)}, u32[]{:S(2)}) collective-permute-start(bf16[32,4096]{1,0:T(8,128)(2,1)} %collective-permute-done.16), channel_id=1, source_target_pairs={{0,16},{16,0},{1,17},{17,1},{2,18},{18,2},{3,19},{19,3},{4,20},{20... | collective-permute-start | bytes 786440 | tf_op jit(solution)/shard_map/ppermute | solution.py:69
  101.5 2.4 %collective-permute-start.17 = (bf16[48,4096]{1,0:T(8,128)(2,1)S(1)}, bf16[48,4096]{1,0:T(8,128)(2,1)S(1)}, u32[]{:S(2)}, u32[]{:S(2)}) collective-permute-start(bf16[48,4096]{1,0:T(8,128)(2,1)S(1)} %collective-permute-done.14), channel_id=1, source_target_pairs={{0,16},{16,0},{1,17},{17,1},{2,18},{18,2},{3,19},{19,3},{4,20},{20... | collective-permute-start | bytes 1179656 | tf_op jit(solution)/shard_map/ppermute | solution.py:69
  102.7 1.9 collective-permute-start.18
  104.6 22.5 %copy-start.2 = (bf16[128,4096]{1,0:T(8,128)(2,1)S(1)}, bf16[128,4096]{1,0:T(8,128)(2,1)}, u32[]{:S(2)}) copy-start(bf16[128,4096]{1,0:T(8,128)(2,1)} %copy-done.1) | copy-start | bytes 3145732
  124.4 7.7 %collective-permute-start.20 = (bf16[3,256,128]{2,1,0:T(8,128)(2,1)S(1)}, bf16[3,256,128]{2,1,0:T(8,128)(2,1)S(1)}, u32[]{:S(2)}, u32[]{:S(2)}) collective-permute-start(bf16[3,256,128]{2,1,0:T(8,128)(2,1)S(1)} %get-tuple-element.78), channel_id=1, source_target_pairs={{0,1},{1,2},{2,3},{3,4},{4,5},{5,6},{6,7},{7,0},{8,9},{9,10},{10,1... | collective-permute-start | bytes 589832 | tf_op jit(solution)/shard_map/ppermute | solution.py:69
  124.5 7.6 %collective-permute-start.21 = (bf16[3,256,128]{2,1,0:T(8,128)(2,1)S(1)}, bf16[3,256,128]{2,1,0:T(8,128)(2,1)S(1)}, u32[]{:S(2)}, u32[]{:S(2)}) collective-permute-start(bf16[3,256,128]{2,1,0:T(8,128)(2,1)S(1)} %get-tuple-element.77), channel_id=1, source_target_pairs={{0,7},{1,0},{2,1},{3,2},{4,3},{5,4},{6,5},{7,6},{8,15},{9,8},{10,9... | collective-permute-start | bytes 589832 | tf_op jit(solution)/shard_map/ppermute | solution.py:69
  132.2 9.8 %collective-permute-start.23 = (bf16[2,3,256,128]{3,2,1,0:T(8,128)(2,1)S(1)}, bf16[2,3,256,128]{3,2,1,0:T(8,128)(2,1)S(1)}, u32[]{:S(2)}, u32[]{:S(2)}) collective-permute-start(bf16[2,3,256,128]{3,2,1,0:T(8,128)(2,1)S(1)} %pad_maximum_fusion.1), channel_id=1, source_target_pairs={{0,7},{1,0},{2,1},{3,2},{4,3},{5,4},{6,5},{7,6},{8,15},{9,8},{10,9... | collective-permute-start | bytes 1179656 | tf_op jit(solution)/shard_map/ppermute | solution.py:69
  134.5 10.1 %collective-permute-start.22 = (bf16[2,3,256,128]{3,2,1,0:T(8,128)(2,1)S(1)}, bf16[2,3,256,128]{3,2,1,0:T(8,128)(2,1)S(1)}, u32[]{:S(2)}, u32[]{:S(2)}) collective-permute-start(bf16[2,3,256,128]{3,2,1,0:T(8,128)(2,1)S(1)} %pad_maximum_fusion), channel_id=1, source_target_pairs={{0,1},{1,2},{2,3},{3,4},{4,5},{5,6},{6,7},{7,0},{8,9},{9,10},{10,1... | collective-permute-start | bytes 1179656 | tf_op jit(solution)/shard_map/ppermute | solution.py:69
  144.7 8.8 %collective-permute-start.25 = (bf16[2,3,256,128]{3,2,1,0:T(8,128)(2,1)S(1)}, bf16[2,3,256,128]{3,2,1,0:T(8,128)(2,1)S(1)}, u32[]{:S(2)}, u32[]{:S(2)}) collective-permute-start(bf16[2,3,256,128]{3,2,1,0:T(8,128)(2,1)S(1)} %add_convert_fusion.3), channel_id=1, source_target_pairs={{0,7},{1,0},{2,1},{3,2},{4,3},{5,4},{6,5},{7,6},{8,15},{9,8},{10,9... | collective-permute-start | bytes 1179656 | tf_op jit(solution)/shard_map/ppermute | solution.py:69
  145.0 9.2 %collective-permute-start.24 = (bf16[2,3,256,128]{3,2,1,0:T(8,128)(2,1)S(1)}, bf16[2,3,256,128]{3,2,1,0:T(8,128)(2,1)S(1)}, u32[]{:S(2)}, u32[]{:S(2)}) collective-permute-start(bf16[2,3,256,128]{3,2,1,0:T(8,128)(2,1)S(1)} %add_convert_fusion.4), channel_id=1, source_target_pairs={{0,1},{1,2},{2,3},{3,4},{4,5},{5,6},{6,7},{7,0},{8,9},{9,10},{10,1... | collective-permute-start | bytes 1179656 | tf_op jit(solution)/shard_map/ppermute | solution.py:69
  152.8 0.7 copy-start.3
  154.2 8.2 %collective-permute-start.26 = (bf16[2,3,256,128]{3,2,1,0:T(8,128)(2,1)S(1)}, bf16[2,3,256,128]{3,2,1,0:T(8,128)(2,1)S(1)}, u32[]{:S(2)}, u32[]{:S(2)}) collective-permute-start(bf16[2,3,256,128]{3,2,1,0:T(8,128)(2,1)S(1)} %add_convert_fusion.2), channel_id=1, source_target_pairs={{0,1},{1,2},{2,3},{3,4},{4,5},{5,6},{6,7},{7,0},{8,9},{9,10},{10,1... | collective-permute-start | bytes 1179656 | tf_op jit(solution)/shard_map/ppermute | solution.py:69
  154.5 8.0 %collective-permute-start.27 = (bf16[2,3,256,128]{3,2,1,0:T(8,128)(2,1)S(1)}, bf16[2,3,256,128]{3,2,1,0:T(8,128)(2,1)S(1)}, u32[]{:S(2)}, u32[]{:S(2)}) collective-permute-start(bf16[2,3,256,128]{3,2,1,0:T(8,128)(2,1)S(1)} %add_convert_fusion.1), channel_id=1, source_target_pairs={{0,7},{1,0},{2,1},{3,2},{4,3},{5,4},{6,5},{7,6},{8,15},{9,8},{10,9... | collective-permute-start | bytes 1179656 | tf_op jit(solution)/shard_map/ppermute | solution.py:69
  163.7 10.0 %collective-permute-start.28 = (bf16[3,256,128]{2,1,0:T(8,128)(2,1)S(1)}, bf16[3,256,128]{2,1,0:T(8,128)(2,1)S(1)}, u32[]{:S(2)}, u32[]{:S(2)}) collective-permute-start(bf16[3,256,128]{2,1,0:T(8,128)(2,1)S(1)} %get-tuple-element.75), channel_id=1, source_target_pairs={{0,0},{1,129},{2,34},{3,163},{4,68},{5,197},{6,102},{7,231},{8,16}... | collective-permute-start | bytes 589832 | tf_op jit(solution)/shard_map/ppermute | solution.py:388
  170.3 4.7 %collective-permute-start.29 = (bf16[3,256,128]{2,1,0:T(8,128)(2,1)S(1)}, bf16[3,256,128]{2,1,0:T(8,128)(2,1)S(1)}, u32[]{:S(2)}, u32[]{:S(2)}) collective-permute-start(bf16[3,256,128]{2,1,0:T(8,128)(2,1)S(1)} %get-tuple-element.76), channel_id=1, source_target_pairs={{0,16},{1,145},{2,50},{3,179},{4,84},{5,213},{6,118},{7,247},{8,0}... | collective-permute-start | bytes 589832 | tf_op jit(solution)/shard_map/ppermute | solution.py:388
  175.1 15.3 %collective-permute-start.30 = (bf16[3,256,128]{2,1,0:T(8,128)(2,1)S(1)}, bf16[3,256,128]{2,1,0:T(8,128)(2,1)S(1)}, u32[]{:S(2)}, u32[]{:S(2)}) collective-permute-start(bf16[3,256,128]{2,1,0:T(8,128)(2,1)S(1)} %add_convert_fusion.5), channel_id=1, source_target_pairs={{0,0},{1,1},{2,6},{3,7},{4,4},{5,5},{6,2},{7,3},{8,8},{9,9},{10,14... | collective-permute-start | bytes 589832 | tf_op jit(solution)/shard_map/ppermute | solution.py:390
Sparse Core Ops, SparseCore 0:
  39.3 59.0 all-gather.1

commit v9 on v8

--- a/solution.py
+++ b/solution.py
@@ -48,10 +48,14 @@
     return pairs
 
 
-def plane_moves(flip):
+def cross_moves(by):
+    return [(yh * 8 + z, (1 - yh) * 8 + (z + by) % 8) for yh in range(2) for z in range(8)]
+
+
+def plane_moves():
     pairs = []
     for yl, x, core, yh, z in np.ndindex(*SIZES):
-        target = device(yl ^ (z % 2), x + z // 2, yh ^ flip, core, z)
+        target = device(yl ^ (z % 2), x + z // 2, yh, core, z)
         pairs.append((device(yl, x, core, yh, z), target))
     return pairs
 
@@ -317,7 +321,7 @@
             pltpu.SemaphoreType.DMA((1,)),
             pltpu.SemaphoreType.DMA((len(near), len(PARTS))),
         ],
-        compiler_params=pltpu.CompilerParams(vmem_limit_bytes=48 * 2**20),
+        compiler_params=pltpu.CompilerParams(vmem_limit_bytes=50 * 2**20),
         cost_estimate=pl.CostEstimate(
             flops=2 * ROWS * len(near) * CHUNK * COLS,
             bytes_accessed=2 * ROWS * len(near) * CHUNK,
@@ -344,7 +348,7 @@
             pltpu.SemaphoreType.DMA((len(PARTS),)),
             pltpu.SemaphoreType.DMA((FRAMES,)),
         ],
-        compiler_params=pltpu.CompilerParams(vmem_limit_bytes=48 * 2**20),
+        compiler_params=pltpu.CompilerParams(vmem_limit_bytes=49 * 2**20),
         cost_estimate=pl.CostEstimate(
             flops=2 * ROWS * WIDTH * COLS, bytes_accessed=2 * ROWS * WIDTH, transcendentals=0
         ),
@@ -380,14 +384,18 @@
     for step in NEAR[1:]:
         up, down, near = beside((shift(up, "z", 1), shift(down, "z", -1), shares(step)))
         up, down = add(up, near[0]), add(down, near[1])
-    mine = add(shift(up, "z", 1), shift(down, "z", -1), near[2])
     yh = lax.axis_index("yh")
-    total = None
-    for flip in range(2):
-        part = lax.dynamic_index_in_dim(mine, (yh + flip) % 2, 0, keepdims=False)
-        part = lax.ppermute(part, AXES, plane_moves(flip)).astype(jnp.float32)
-        total = part if total is None else total + part
-    return lax.ppermute(total.astype(jnp.bfloat16), AXES, line_moves()).transpose(1, 0, 2)
+    half = lambda value, flip: lax.dynamic_index_in_dim(value, (yh + flip) % 2, 0, keepdims=False)
+    parts = [
+        half(near[2], 0),
+        shift(half(near[2], 1), "yh", 1),
+        shift(half(up, 0), "z", 1),
+        shift(half(down, 0), "z", -1),
+        lax.ppermute(half(up, 1), TOK, cross_moves(1)),
+        lax.ppermute(half(down, 1), TOK, cross_moves(-1)),
+    ]
+    mine = lax.ppermute(add(*parts), AXES, plane_moves())
+    return lax.ppermute(mine, AXES, line_moves()).transpose(1, 0, 2)
 
 
 def solution(mesh):

time: 201 us -> 207 us (1.030); the launches traced: 198 us -> 206 us
  waiting for transfers between devices: 64.7 us -> 72.9 us
    ppermute x3 -> x4, waiting for transfers between devices: 13.3 us -> 17.7 us  [the longest x1 11 us: local(): return lax.ppermute(mine, AXES, line_moves()).transpose(1, 0, 2)]
    ppermute x27 -> x28, waiting for transfers between devices: 23.3 us -> 26.8 us  [shift(): lax.ppermute(value, axis, [(i, (i + by) % count) for i in range(count)])]
    ppermute x3 -> x4, starting transfers between devices: 13.3 us -> 12.2 us  [the longest x1 5.37 us: local(): mine = lax.ppermute(add(*parts), AXES, plane_moves())]
    ppermute x27 -> x28, starting transfers between devices: 28.2 us -> 27.8 us  [shift(): lax.ppermute(value, axis, [(i, (i + by) % count) for i in range(count)])]
  transfers between devices with their start and end apart: 34 -> 36, of which waited for: 13 -> 15; matrix products, arithmetic and copies ran while one was open for 1% -> 1% of each run, Pallas kernels for 11% -> 10%
where the time goes in v9:
time: 207 us; the launch traced here: 206 us
  waiting for transfers between devices  72.9 us (35%)
  starting transfers between devices  70.9 us (34%)
  Pallas kernels  41.2 us (20%)
  between operations  13.7 us (7%)
  local copies, waits for them, and re-layouts  4.97 us (2%)
  other arithmetic  2.43 us (1%)
    ppermute x28, starting transfers between devices, shift(): lax.ppermute(value, axis, [(i, (i + by) % count) for i in range(count)])  27.8 us
    ppermute x28, waiting for transfers between devices, shift(): lax.ppermute(value, axis, [(i, (i + by) % count) for i in range(count)])  26.8 us
    all_to_all x2, starting transfers between devices, local(): lax.all_to_all(value, axes, split_axis=0, concat_axis=0, tiled=True)  21 us
    pallas_call x1, Pallas kernels, far_shares(): pl.pallas_call(functools.partial(share_kernel, count), out_shape=[jax.Sha...  20.2 us
    pallas_call x3, Pallas kernels, near_shares(): pl.pallas_call(functools.partial(near_kernel, count, near), out_shape=[SH...  16.4 us
    ppermute x1, waiting for transfers between devices, local(): rows_w = lax.ppermute(rows_w, AXES, worker_moves())  15.5 us
    all_to_all x2, waiting for transfers between devices, local(): lax.all_to_all(value, axes, split_axis=0, concat_axis=0, tiled=True)  12.8 us
    ppermute x1, waiting for transfers between devices, local(): return lax.ppermute(mine, AXES, line_moves()).transpose(1, 0, 2)  11 us
  transfers between devices with their start and end apart: 36, of which 15 were waited for; matrix products, arithmetic and copies ran while one was open for 1% of the time, Pallas kernels for 10%

profile of v9, /device:TPU:3, one launch (start us, length us, event | category | flops | bytes accessed | tf_op | source)
XLA Modules:
  0.0 206.1 jit_solution(6736785694721105819)
XLA Ops:
  6.5 1.2 collective-permute-start.2
  7.8 0.3 collective-permute-start.3
  8.0 1.3 collective-permute-start.4
  9.3 0.7 constant_dynamic-slice_fusion
  10.0 0.6 slice.40
  10.6 2.5 %shard_map.46 = bf16[512,384]{1,0:T(8,128)(2,1)} custom-call(s32[1]{0:T(128)} %bitcast.2.start, bf16[3,4096,128]{2,1,0:T(8,128)(2,1)} %bitcast.95), custom_call_target="tpu_custom_call" | custom-call | tf_op jit(solution)/shard_map/pallas_call | solution.py:186
  13.0 9.8 %collective-permute-start = (bf16[512,384]{1,0:T(8,128)(2,1)}, bf16[512,384]{1,0:T(8,128)(2,1)S(1)}, u32[]{:S(2)}, u32[]{:S(2)}) collective-permute-start(bf16[512,384]{1,0:T(8,128)(2,1)} %shard_map.46), channel_id=1, source_target_pairs={{0,0},{128,1},{32,2},{160,3},{64,4},{192,5},{96,6},{224,7},{16,8},... | collective-permute-start | bytes 1179656 | tf_op jit(solution)/shard_map/ppermute | solution.py:365
  22.9 15.5 %collective-permute-done = bf16[512,384]{1,0:T(8,128)(2,1)S(1)} collective-permute-done((bf16[512,384]{1,0:T(8,128)(2,1)}, bf16[512,384]{1,0:T(8,128)(2,1)S(1)}, u32[]{:S(2)}, u32[]{:S(2)}) %collective-permute-start) | collective-permute-done | bytes 393248 | tf_op jit(solution)/shard_map/ppermute | solution.py:365
  38.4 0.7 copy-done.4
  39.2 0.1 collective-permute-start.10
  39.3 2.9 %collective-permute-start.9 = (bf16[128,4096]{1,0:T(8,128)(2,1)S(1)}, bf16[128,4096]{1,0:T(8,128)(2,1)}, u32[]{:S(2)}, u32[]{:S(2)}) collective-permute-start(bf16[128,4096]{1,0:T(8,128)(2,1)S(1)} %collective-permute-done.3), channel_id=1, source_target_pairs={{0,96},{32,0},{64,32},{96,64},{1,97},{33,1},{65,33},{97,65},{2,98}... | collective-permute-start | bytes 3145736 | tf_op jit(solution)/shard_map/ppermute | solution.py:73
  42.2 11.4 %all-to-all-start = ((bf16[16,128,128]{2,1,0:T(8,128)(2,1)}), bf16[16,128,128]{2,1,0:T(8,128)(2,1)}, u32[]{:S(2)}, u32[]{:S(2)}) async-start(bf16[16,128,128]{2,1,0:T(8,128)(2,1)} %bitcast.5), calls=%async_computation | async-start | bytes 1048576 | tf_op jit(solution)/shard_map/all_to_all | solution.py:367
  53.7 3.0 %collective-permute-start.1 = (bf16[128,4096]{1,0:T(8,128)(2,1)S(1)}, bf16[128,4096]{1,0:T(8,128)(2,1)}, u32[]{:S(2)}, u32[]{:S(2)}) collective-permute-start(bf16[128,4096]{1,0:T(8,128)(2,1)S(1)} %bitcast.62), channel_id=1, source_target_pairs={{0,16},{16,0},{1,17},{17,1},{2,18},{18,2},{3,19},{19,3},{4,20},{20... | collective-permute-start | bytes 3145736 | tf_op jit(solution)/shard_map/ppermute | solution.py:73
  56.6 0.1 collective-permute-start.6
  56.7 10.5 %collective-permute-done.10.refs_1_ = bf16[128,4096]{1,0:T(8,128)(2,1)} collective-permute-done((bf16[128,4096]{1,0:T(8,128)(2,1)S(1)}, bf16[128,4096]{1,0:T(8,128)(2,1)}, u32[]{:S(2)}, u32[]{:S(2)}) %collective-permute-start.10) | collective-permute-done | bytes 1048608 | tf_op jit(solution)/shard_map/ppermute | solution.py:73
  67.2 0.5 collective-permute-start.5
  67.7 5.3 %all-to-all-done = bf16[16,128,128]{2,1,0:T(8,128)(2,1)} async-done(((bf16[16,128,128]{2,1,0:T(8,128)(2,1)}), bf16[16,128,128]{2,1,0:T(8,128)(2,1)}, u32[]{:S(2)}, u32[]{:S(2)}) %all-to-all-start) | async-done | bytes 524320 | tf_op jit(solution)/shard_map/all_to_all | solution.py:367
  73.0 2.2 %shard_map.47 = (bf16[48,4096]{1,0:T(8,128)(2,1)}, bf16[48,4096]{1,0:T(8,128)(2,1)}, bf16[32,4096]{1,0:T(8,128)(2,1)}) custom-call(bf16[128,4096]{1,0:T(8,128)(2,1)} %collective-permute-done.8.refs_0_, bf16[128,4096]{1,0:T(8,128)(2,1)} %collective-permute-done.10.refs_1_, bf16[128,4096]{1,0:T(8,128)(2,1)} %collective-permute-done.9.refs_2_), custom_call_target="tpu_custom_call" | custom-call | flops 30000001024 | tf_op jit(solution)/shard_map/pallas_call | solution.py:95
  75.2 0.8 collective-permute-start.14
  76.1 2.9 %collective-permute-start.15 = (bf16[48,4096]{1,0:T(8,128)(2,1)}, bf16[48,4096]{1,0:T(8,128)(2,1)S(1)}, u32[]{:S(2)}, u32[]{:S(2)}) collective-permute-start(bf16[48,4096]{1,0:T(8,128)(2,1)} %get-tuple-element.48), channel_id=1, source_target_pairs={{0,96},{32,0},{64,32},{96,64},{1,97},{33,1},{65,33},{97,65},{2,98}... | collective-permute-start | bytes 1179656 | tf_op jit(solution)/shard_map/ppermute | solution.py:73
  79.0 2.5 %collective-permute-start.16 = (bf16[32,4096]{1,0:T(8,128)(2,1)}, bf16[32,4096]{1,0:T(8,128)(2,1)S(1)}, u32[]{:S(2)}, u32[]{:S(2)}) collective-permute-start(bf16[32,4096]{1,0:T(8,128)(2,1)} %get-tuple-element.49), channel_id=1, source_target_pairs={{0,128},{128,0},{1,129},{129,1},{2,130},{130,2},{3,131},{131,3},{4... | collective-permute-start | bytes 786440 | tf_op jit(solution)/shard_map/ppermute | solution.py:73
  81.5 9.6 %all-to-all-start.1 = ((bf16[16,128,128]{2,1,0:T(8,128)(2,1)}), bf16[16,128,128]{2,1,0:T(8,128)(2,1)S(1)}, u32[]{:S(2)}, u32[]{:S(2)}) async-start(bf16[16,128,128]{2,1,0:T(8,128)(2,1)} %all-to-all-done), calls=%async_computation.1 | async-start | bytes 1048576 | tf_op jit(solution)/shard_map/all_to_all | solution.py:367
  91.1 0.4 collective-permute-start.11
  91.6 0.1 collective-permute-start.12
  91.7 0.4 collective-permute-start.13
  92.1 7.5 %all-to-all-done.1 = bf16[16,128,128]{2,1,0:T(8,128)(2,1)S(1)} async-done(((bf16[16,128,128]{2,1,0:T(8,128)(2,1)}), bf16[16,128,128]{2,1,0:T(8,128)(2,1)S(1)}, u32[]{:S(2)}, u32[]{:S(2)}) %all-to-all-start.1) | async-done | bytes 524320 | tf_op jit(solution)/shard_map/all_to_all | solution.py:367
  99.6 0.8 copy-done.1
  100.4 1.3 collective-permute-start.19
  102.0 0.1 collective-permute-start.17
  102.1 0.7 collective-permute-done.19
  102.9 0.4 collective-permute-start.18
  103.2 0.1 and_convert_fusion.mask
  103.4 0.5 collective-permute-done.17
  103.8 0.8 collective-permute-done.18
  104.6 1.0 copy-done.2
  105.7 20.2 %shard_map.48 = (bf16[384,2048]{1,0:T(8,128)(2,1)}, bf16[2,3,256,128]{3,2,1,0:T(8,128)(2,1)S(1)}) custom-call(s32[24]{0:T(128)S(1)} %slice_bitcast_fusion.3.order, f32[256,256]{1,0:T(8,128)S(1)} %and_convert_fusion.mask, bf16[4096,384]{1,0:T(8,128)(2,1)} %all-gather.2.cloned.1.call-done.w_ref, bf16[16,8,16,128]{3,2,1,0:T(8,128)(2,1)S(1)} %bitcast.90, ...), custom_call_target="tpu_custom_call" | custom-call | flops 6442450944 | bytes 16777216 | tf_op jit(solution)/shard_map/pallas_call | solution.py:336
  125.9 0.1 collective-permute-start.20
  126.0 2.7 %collective-permute-start.21 = (bf16[3,256,128]{2,1,0:T(8,128)(2,1)S(1)}, bf16[3,256,128]{2,1,0:T(8,128)(2,1)S(1)}, u32[]{:S(2)}, u32[]{:S(2)}) collective-permute-start(bf16[3,256,128]{2,1,0:T(8,128)(2,1)S(1)} %get-tuple-element.79), channel_id=1, source_target_pairs={{0,7},{1,0},{2,1},{3,2},{4,3},{5,4},{6,5},{7,6},{8,15},{9,8},{10,9... | collective-permute-start | bytes 589832 | tf_op jit(solution)/shard_map/ppermute | solution.py:73
  128.7 5.0 %shard_map.49 = (bf16[2,3,256,128]{3,2,1,0:T(8,128)(2,1)S(1)}, bf16[2,3,256,128]{3,2,1,0:T(8,128)(2,1)S(1)}) custom-call(s32[24]{0:T(128)S(1)} %slice_bitcast_fusion.3.order, bf16[384,2048]{1,0:T(8,128)(2,1)} %get-tuple-element.54.turned_ref, bf16[8,16,4096]{2,1,0:T(8,128)(2,1)S(1)} %bitcast.64, bf16[8,16,4096]{2,1,0:T(8,128)(2,1)} %bitcast.9.refs_1_, ...), custom_call_target="tpu_custom_call" | custom-call | flops 1610612736 | bytes 4194304 | tf_op jit(solution)/shard_map/pallas_call | solution.py:313
  133.8 2.1 collective-permute-start.23
  136.0 0.1 collective-permute-start.22
  136.1 5.0 %shard_map.50 = (bf16[2,3,256,128]{3,2,1,0:T(8,128)(2,1)S(1)}, bf16[2,3,256,128]{3,2,1,0:T(8,128)(2,1)S(1)}) custom-call(s32[24]{0:T(128)S(1)} %slice_bitcast_fusion.3.order, bf16[384,2048]{1,0:T(8,128)(2,1)} %get-tuple-element.54.turned_ref, bf16[8,16,4096]{2,1,0:T(8,128)(2,1)S(1)} %bitcast.65, bf16[8,16,4096]{2,1,0:T(8,128)(2,1)} %bitcast.9.refs_1_, ...), custom_call_target="tpu_custom_call" | custom-call | flops 1610612736 | bytes 4194304 | tf_op jit(solution)/shard_map/pallas_call | solution.py:313
  141.1 2.5 %collective-permute-done.23 = bf16[2,3,256,128]{3,2,1,0:T(8,128)(2,1)S(1)} collective-permute-done((bf16[2,3,256,128]{3,2,1,0:T(8,128)(2,1)S(1)}, bf16[2,3,256,128]{3,2,1,0:T(8,128)(2,1)S(1)}, u32[]{:S(2)}, u32[]{:S(2)}) %collective-permute-start.23) | collective-permute-done | bytes 393248 | tf_op jit(solution)/shard_map/ppermute | solution.py:73
  143.6 2.5 %collective-permute-done.22 = bf16[2,3,256,128]{3,2,1,0:T(8,128)(2,1)S(1)} collective-permute-done((bf16[2,3,256,128]{3,2,1,0:T(8,128)(2,1)S(1)}, bf16[2,3,256,128]{3,2,1,0:T(8,128)(2,1)S(1)}, u32[]{:S(2)}, u32[]{:S(2)}) %collective-permute-start.22) | collective-permute-done | bytes 393248 | tf_op jit(solution)/shard_map/ppermute | solution.py:73
  146.1 0.9 add_convert_fusion.2
  147.0 0.9 add_convert_fusion.3
  147.9 1.4 collective-permute-start.24
  149.3 6.4 %shard_map.51 = (bf16[2,3,256,128]{3,2,1,0:T(8,128)(2,1)S(1)}, bf16[2,3,256,128]{3,2,1,0:T(8,128)(2,1)S(1)}, bf16[2,3,256,128]{3,2,1,0:T(8,128)(2,1)S(1)}) custom-call(s32[24]{0:T(128)S(1)} %slice_bitcast_fusion.3.order, bf16[384,2048]{1,0:T(8,128)(2,1)} %get-tuple-element.54.turned_ref, bf16[8,16,4096]{2,1,0:T(8,128)(2,1)} %bitcast.61, ...), custom_call_target="tpu_custom_call" | custom-call | flops 2415919104 | bytes 6291456 | tf_op jit(solution)/shard_map/pallas_call | solution.py:313
  155.7 1.5 collective-permute-done.24
  157.2 0.2 add_convert_fusion
  157.5 0.1 collective-permute-start.27
  157.6 0.1 collective-permute-start.29
  157.7 2.7 %collective-permute-start.28 = (bf16[3,256,128]{2,1,0:T(8,128)(2,1)S(1)}, bf16[3,256,128]{2,1,0:T(8,128)(2,1)S(1)}, u32[]{:S(2)}, u32[]{:S(2)}) collective-permute-start(bf16[3,256,128]{2,1,0:T(8,128)(2,1)S(1)} %get-tuple-element.77), channel_id=1, source_target_pairs={{0,7},{1,0},{2,1},{3,2},{4,3},{5,4},{6,5},{7,6},{8,15},{9,8},{10,9... | collective-permute-start | bytes 589832 | tf_op jit(solution)/shard_map/ppermute | solution.py:73
  160.4 3.8 %collective-permute-start.30 = (bf16[3,256,128]{2,1,0:T(8,128)(2,1)S(1)}, bf16[3,256,128]{2,1,0:T(8,128)(2,1)S(1)}, u32[]{:S(2)}, u32[]{:S(2)}) collective-permute-start(bf16[3,256,128]{2,1,0:T(8,128)(2,1)S(1)} %get-tuple-element.78), channel_id=1, source_target_pairs={{0,15},{1,8},{2,9},{3,10},{4,11},{5,12},{6,13},{7,14},{8,7},{9,0},... | collective-permute-start | bytes 589832 | tf_op jit(solution)/shard_map/ppermute | solution.py:395
  164.2 0.3 collective-permute-start.26
  164.6 2.2 %collective-permute-done.29 = bf16[3,256,128]{2,1,0:T(8,128)(2,1)S(1)} collective-permute-done((bf16[3,256,128]{2,1,0:T(8,128)(2,1)S(1)}, bf16[3,256,128]{2,1,0:T(8,128)(2,1)S(1)}, u32[]{:S(2)}, u32[]{:S(2)}) %collective-permute-start.29) | collective-permute-done | bytes 196640 | tf_op jit(solution)/shard_map/ppermute | solution.py:394
  166.8 1.2 collective-permute-done.30
  168.0 7.8 %collective-permute-done.26 = bf16[3,256,128]{2,1,0:T(8,128)(2,1)S(1)} collective-permute-done((bf16[3,256,128]{2,1,0:T(8,128)(2,1)S(1)}, bf16[3,256,128]{2,1,0:T(8,128)(2,1)S(1)}, u32[]{:S(2)}, u32[]{:S(2)}) %collective-permute-start.26) | collective-permute-done | bytes 196640 | tf_op jit(solution)/shard_map/ppermute | solution.py:73
  175.9 0.2 fusion.4
  176.0 5.4 %collective-permute-start.31 = (bf16[3,256,128]{2,1,0:T(8,128)(2,1)S(1)}, bf16[3,256,128]{2,1,0:T(8,128)(2,1)S(1)}, u32[]{:S(2)}, u32[]{:S(2)}) collective-permute-start(bf16[3,256,128]{2,1,0:T(8,128)(2,1)S(1)} %fusion.4), channel_id=1, source_target_pairs={{0,0},{1,129},{2,34},{3,163},{4,68},{5,197},{6,102},{7,231},{8,16}... | collective-permute-start | bytes 589832 | tf_op jit(solution)/shard_map/ppermute | solution.py:397
  181.4 3.3 %collective-permute-done.31 = bf16[3,256,128]{2,1,0:T(8,128)(2,1)S(1)} collective-permute-done((bf16[3,256,128]{2,1,0:T(8,128)(2,1)S(1)}, bf16[3,256,128]{2,1,0:T(8,128)(2,1)S(1)}, u32[]{:S(2)}, u32[]{:S(2)}) %collective-permute-start.31) | collective-permute-done | bytes 196640 | tf_op jit(solution)/shard_map/ppermute | solution.py:397
  184.7 2.9 %collective-permute-start.32 = (bf16[3,256,128]{2,1,0:T(8,128)(2,1)S(1)}, bf16[3,256,128]{2,1,0:T(8,128)(2,1)S(1)}, u32[]{:S(2)}, u32[]{:S(2)}) collective-permute-start(bf16[3,256,128]{2,1,0:T(8,128)(2,1)S(1)} %collective-permute-done.31), channel_id=1, source_target_pairs={{0,0},{1,1},{2,6},{3,7},{4,4},{5,5},{6,2},{7,3},{8,8},{9,9},{10,14... | collective-permute-start | bytes 589832 | tf_op jit(solution)/shard_map/ppermute | solution.py:398
  187.6 11.0 %collective-permute-done.32 = bf16[3,256,128]{2,1,0:T(8,128)(2,1)S(1)} collective-permute-done((bf16[3,256,128]{2,1,0:T(8,128)(2,1)S(1)}, bf16[3,256,128]{2,1,0:T(8,128)(2,1)S(1)}, u32[]{:S(2)}, u32[]{:S(2)}) %collective-permute-start.32) | collective-permute-done | bytes 196640 | tf_op jit(solution)/shard_map/ppermute | solution.py:398
  198.6 0.7 copy.6
  (49 shorter events, 0.8 us)
Async XLA Ops:
  6.5 47.1 %copy-start = (bf16[1,128,4096]{2,1,0:T(8,128)(2,1)S(1)}, bf16[1,128,4096]{2,1,0:T(8,128)(2,1)}, u32[]{:S(2)}) copy-start(bf16[1,128,4096]{2,1,0:T(8,128)(2,1)} %param.4) | copy-start | bytes 3145732
  6.5 98.1 %all-gather.2.cloned.1.call-start = ((), (), s32[]{:S(2)}) async-start(), calls=%async_computation.2 | async-start | bytes 3538944 | tf_op jit(solution)/shard_map/all_gather | solution.py:366
  6.5 32.6 %collective-permute-start.2 = (bf16[128,4096]{1,0:T(8,128)(2,1)}, bf16[128,4096]{1,0:T(8,128)(2,1)}, u32[]{:S(2)}, u32[]{:S(2)}) collective-permute-start(bf16[128,4096]{1,0:T(8,128)(2,1)} %bitcast.58), channel_id=1, source_target_pairs={{0,32},{32,64},{64,96},{96,0},{1,33},{33,65},{65,97},{97,1},{2,34}... | collective-permute-start | bytes 3145736 | tf_op jit(solution)/shard_map/ppermute | solution.py:73
  7.8 31.4 %collective-permute-start.3 = (bf16[128,4096]{1,0:T(8,128)(2,1)}, bf16[128,4096]{1,0:T(8,128)(2,1)S(1)}, u32[]{:S(2)}, u32[]{:S(2)}) collective-permute-start(bf16[128,4096]{1,0:T(8,128)(2,1)} %bitcast.59), channel_id=1, source_target_pairs={{0,96},{32,0},{64,32},{96,64},{1,97},{33,1},{65,33},{97,65},{2,98}... | collective-permute-start | bytes 3145736 | tf_op jit(solution)/shard_map/ppermute | solution.py:73
  8.0 31.2 %collective-permute-start.4 = (bf16[128,4096]{1,0:T(8,128)(2,1)}, bf16[128,4096]{1,0:T(8,128)(2,1)}, u32[]{:S(2)}, u32[]{:S(2)}) collective-permute-start(bf16[128,4096]{1,0:T(8,128)(2,1)} %bitcast.60), channel_id=1, source_target_pairs={{0,128},{128,0},{1,129},{129,1},{2,130},{130,2},{3,131},{131,3},{4... | collective-permute-start | bytes 3145736 | tf_op jit(solution)/shard_map/ppermute | solution.py:73
  13.0 25.4 %collective-permute-start = (bf16[512,384]{1,0:T(8,128)(2,1)}, bf16[512,384]{1,0:T(8,128)(2,1)S(1)}, u32[]{:S(2)}, u32[]{:S(2)}) collective-permute-start(bf16[512,384]{1,0:T(8,128)(2,1)} %shard_map.46), channel_id=1, source_target_pairs={{0,0},{128,1},{32,2},{160,3},{64,4},{192,5},{96,6},{224,7},{16,8},... | collective-permute-start | bytes 1179656 | tf_op jit(solution)/shard_map/ppermute | solution.py:365
  38.4 0.7 copy-start.4
  39.2 36.1 %copy-start.3 = (bf16[128,4096]{1,0:T(8,128)(2,1)}, bf16[128,4096]{1,0:T(8,128)(2,1)S(1)}, u32[]{:S(2)}) copy-start(bf16[128,4096]{1,0:T(8,128)(2,1)S(1)} %collective-permute-done.3) | copy-start | bytes 3145732
  39.2 28.0 %collective-permute-start.10 = (bf16[128,4096]{1,0:T(8,128)(2,1)S(1)}, bf16[128,4096]{1,0:T(8,128)(2,1)}, u32[]{:S(2)}, u32[]{:S(2)}) collective-permute-start(bf16[128,4096]{1,0:T(8,128)(2,1)S(1)} %collective-permute-done.3), channel_id=1, source_target_pairs={{0,128},{128,0},{1,129},{129,1},{2,130},{130,2},{3,131},{131,3},{4... | collective-permute-start | bytes 3145736 | tf_op jit(solution)/shard_map/ppermute | solution.py:73
  39.3 27.9 %collective-permute-start.9 = (bf16[128,4096]{1,0:T(8,128)(2,1)S(1)}, bf16[128,4096]{1,0:T(8,128)(2,1)}, u32[]{:S(2)}, u32[]{:S(2)}) collective-permute-start(bf16[128,4096]{1,0:T(8,128)(2,1)S(1)} %collective-permute-done.3), channel_id=1, source_target_pairs={{0,96},{32,0},{64,32},{96,64},{1,97},{33,1},{65,33},{97,65},{2,98}... | collective-permute-start | bytes 3145736 | tf_op jit(solution)/shard_map/ppermute | solution.py:73
  42.2 30.8 %collective-permute-start.8 = (bf16[128,4096]{1,0:T(8,128)(2,1)}, bf16[128,4096]{1,0:T(8,128)(2,1)}, u32[]{:S(2)}, u32[]{:S(2)}) collective-permute-start(bf16[128,4096]{1,0:T(8,128)(2,1)} %collective-permute-done.4), channel_id=1, source_target_pairs={{0,32},{32,64},{64,96},{96,0},{1,33},{33,65},{65,97},{97,1},{2,34}... | collective-permute-start | bytes 3145736 | tf_op jit(solution)/shard_map/ppermute | solution.py:73
  42.2 30.8 %all-to-all-start = ((bf16[16,128,128]{2,1,0:T(8,128)(2,1)}), bf16[16,128,128]{2,1,0:T(8,128)(2,1)}, u32[]{:S(2)}, u32[]{:S(2)}) async-start(bf16[16,128,128]{2,1,0:T(8,128)(2,1)} %bitcast.5), calls=%async_computation | async-start | bytes 1048576 | tf_op jit(solution)/shard_map/all_to_all | solution.py:367
  53.7 22.4 %collective-permute-start.1 = (bf16[128,4096]{1,0:T(8,128)(2,1)S(1)}, bf16[128,4096]{1,0:T(8,128)(2,1)}, u32[]{:S(2)}, u32[]{:S(2)}) collective-permute-start(bf16[128,4096]{1,0:T(8,128)(2,1)S(1)} %bitcast.62), channel_id=1, source_target_pairs={{0,16},{16,0},{1,17},{17,1},{2,18},{18,2},{3,19},{19,3},{4,20},{20... | collective-permute-start | bytes 3145736 | tf_op jit(solution)/shard_map/ppermute | solution.py:73
  56.6 22.4 %collective-permute-start.6 = (bf16[128,4096]{1,0:T(8,128)(2,1)S(1)}, bf16[128,4096]{1,0:T(8,128)(2,1)}, u32[]{:S(2)}, u32[]{:S(2)}) collective-permute-start(bf16[128,4096]{1,0:T(8,128)(2,1)S(1)} %collective-permute-done.3), channel_id=1, source_target_pairs={{0,16},{16,0},{1,17},{17,1},{2,18},{18,2},{3,19},{19,3},{4,20},{20... | collective-permute-start | bytes 3145736 | tf_op jit(solution)/shard_map/ppermute | solution.py:73
  67.2 33.2 %collective-permute-start.7 = (bf16[128,4096]{1,0:T(8,128)(2,1)}, bf16[128,4096]{1,0:T(8,128)(2,1)}, u32[]{:S(2)}, u32[]{:S(2)}) collective-permute-start(bf16[128,4096]{1,0:T(8,128)(2,1)} %collective-permute-done.4), channel_id=1, source_target_pairs={{0,16},{16,0},{1,17},{17,1},{2,18},{18,2},{3,19},{19,3},{4,20},{20... | collective-permute-start | bytes 3145736 | tf_op jit(solution)/shard_map/ppermute | solution.py:73
  67.2 34.8 %collective-permute-start.5 = (bf16[128,4096]{1,0:T(8,128)(2,1)}, bf16[128,4096]{1,0:T(8,128)(2,1)}, u32[]{:S(2)}, u32[]{:S(2)}) collective-permute-start(bf16[128,4096]{1,0:T(8,128)(2,1)} %collective-permute-done.2), channel_id=1, source_target_pairs={{0,16},{16,0},{1,17},{17,1},{2,18},{18,2},{3,19},{19,3},{4,20},{20... | collective-permute-start | bytes 3145736 | tf_op jit(solution)/shard_map/ppermute | solution.py:73
  75.2 16.3 %collective-permute-start.14 = (bf16[48,4096]{1,0:T(8,128)(2,1)}, bf16[48,4096]{1,0:T(8,128)(2,1)S(1)}, u32[]{:S(2)}, u32[]{:S(2)}) collective-permute-start(bf16[48,4096]{1,0:T(8,128)(2,1)} %get-tuple-element.47), channel_id=1, source_target_pairs={{0,32},{32,64},{64,96},{96,0},{1,33},{33,65},{65,97},{97,1},{2,34}... | collective-permute-start | bytes 1179656 | tf_op jit(solution)/shard_map/ppermute | solution.py:73
  76.1 15.7 %collective-permute-start.15 = (bf16[48,4096]{1,0:T(8,128)(2,1)}, bf16[48,4096]{1,0:T(8,128)(2,1)S(1)}, u32[]{:S(2)}, u32[]{:S(2)}) collective-permute-start(bf16[48,4096]{1,0:T(8,128)(2,1)} %get-tuple-element.48), channel_id=1, source_target_pairs={{0,96},{32,0},{64,32},{96,64},{1,97},{33,1},{65,33},{97,65},{2,98}... | collective-permute-start | bytes 1179656 | tf_op jit(solution)/shard_map/ppermute | solution.py:73
  79.0 12.1 %collective-permute-start.16 = (bf16[32,4096]{1,0:T(8,128)(2,1)}, bf16[32,4096]{1,0:T(8,128)(2,1)S(1)}, u32[]{:S(2)}, u32[]{:S(2)}) collective-permute-start(bf16[32,4096]{1,0:T(8,128)(2,1)} %get-tuple-element.49), channel_id=1, source_target_pairs={{0,128},{128,0},{1,129},{129,1},{2,130},{130,2},{3,131},{131,3},{4... | collective-permute-start | bytes 786440 | tf_op jit(solution)/shard_map/ppermute | solution.py:73
  81.5 18.0 %all-to-all-start.1 = ((bf16[16,128,128]{2,1,0:T(8,128)(2,1)}), bf16[16,128,128]{2,1,0:T(8,128)(2,1)S(1)}, u32[]{:S(2)}, u32[]{:S(2)}) async-start(bf16[16,128,128]{2,1,0:T(8,128)(2,1)} %all-to-all-done), calls=%async_computation.1 | async-start | bytes 1048576 | tf_op jit(solution)/shard_map/all_to_all | solution.py:367
  91.1 13.5 %collective-permute-start.11 = (bf16[128,4096]{1,0:T(8,128)(2,1)}, bf16[128,4096]{1,0:T(8,128)(2,1)}, u32[]{:S(2)}, u32[]{:S(2)}) collective-permute-start(bf16[128,4096]{1,0:T(8,128)(2,1)} %collective-permute-done.8.refs_0_), channel_id=1, source_target_pairs={{0,16},{16,0},{1,17},{17,1},{2,18},{18,2},{3,19},{19,3},{4,20},{20... | collective-permute-start | bytes 3145736 | tf_op jit(solution)/shard_map/ppermute | solution.py:73
  91.6 13.0 %collective-permute-start.12 = (bf16[128,4096]{1,0:T(8,128)(2,1)}, bf16[128,4096]{1,0:T(8,128)(2,1)}, u32[]{:S(2)}, u32[]{:S(2)}) collective-permute-start(bf16[128,4096]{1,0:T(8,128)(2,1)} %collective-permute-done.9.refs_2_), channel_id=1, source_target_pairs={{0,16},{16,0},{1,17},{17,1},{2,18},{18,2},{3,19},{19,3},{4,20},{20... | collective-permute-start | bytes 3145736 | tf_op jit(solution)/shard_map/ppermute | solution.py:73
  91.7 12.9 %collective-permute-start.13 = (bf16[128,4096]{1,0:T(8,128)(2,1)}, bf16[128,4096]{1,0:T(8,128)(2,1)}, u32[]{:S(2)}, u32[]{:S(2)}) collective-permute-start(bf16[128,4096]{1,0:T(8,128)(2,1)} %collective-permute-done.10.refs_1_), channel_id=1, source_target_pairs={{0,16},{16,0},{1,17},{17,1},{2,18},{18,2},{3,19},{19,3},{4,20},{20... | collective-permute-start | bytes 3145736 | tf_op jit(solution)/shard_map/ppermute | solution.py:73
  99.6 0.8 copy-start.1
  100.4 2.5 %collective-permute-start.19 = (bf16[32,4096]{1,0:T(8,128)(2,1)S(1)}, bf16[32,4096]{1,0:T(8,128)(2,1)S(1)}, u32[]{:S(2)}, u32[]{:S(2)}) collective-permute-start(bf16[32,4096]{1,0:T(8,128)(2,1)S(1)} %collective-permute-done.16), channel_id=1, source_target_pairs={{0,16},{16,0},{1,17},{17,1},{2,18},{18,2},{3,19},{19,3},{4,20},{20... | collective-permute-start | bytes 786440 | tf_op jit(solution)/shard_map/ppermute | solution.py:73
  102.0 1.8 collective-permute-start.17
  102.9 1.7 collective-permute-start.18
  104.6 1.0 copy-start.2
  125.9 7.7 %collective-permute-start.20 = (bf16[3,256,128]{2,1,0:T(8,128)(2,1)S(1)}, bf16[3,256,128]{2,1,0:T(8,128)(2,1)S(1)}, u32[]{:S(2)}, u32[]{:S(2)}) collective-permute-start(bf16[3,256,128]{2,1,0:T(8,128)(2,1)S(1)} %get-tuple-element.80), channel_id=1, source_target_pairs={{0,1},{1,2},{2,3},{3,4},{4,5},{5,6},{6,7},{7,0},{8,9},{9,10},{10,1... | collective-permute-start | bytes 589832 | tf_op jit(solution)/shard_map/ppermute | solution.py:73
  126.0 7.7 %collective-permute-start.21 = (bf16[3,256,128]{2,1,0:T(8,128)(2,1)S(1)}, bf16[3,256,128]{2,1,0:T(8,128)(2,1)S(1)}, u32[]{:S(2)}, u32[]{:S(2)}) collective-permute-start(bf16[3,256,128]{2,1,0:T(8,128)(2,1)S(1)} %get-tuple-element.79), channel_id=1, source_target_pairs={{0,7},{1,0},{2,1},{3,2},{4,3},{5,4},{6,5},{7,6},{8,15},{9,8},{10,9... | collective-permute-start | bytes 589832 | tf_op jit(solution)/shard_map/ppermute | solution.py:73
  133.8 9.8 %collective-permute-start.23 = (bf16[2,3,256,128]{3,2,1,0:T(8,128)(2,1)S(1)}, bf16[2,3,256,128]{3,2,1,0:T(8,128)(2,1)S(1)}, u32[]{:S(2)}, u32[]{:S(2)}) collective-permute-start(bf16[2,3,256,128]{3,2,1,0:T(8,128)(2,1)S(1)} %pad_maximum_fusion.1), channel_id=1, source_target_pairs={{0,7},{1,0},{2,1},{3,2},{4,3},{5,4},{6,5},{7,6},{8,15},{9,8},{10,9... | collective-permute-start | bytes 1179656 | tf_op jit(solution)/shard_map/ppermute | solution.py:73
  136.0 10.1 %collective-permute-start.22 = (bf16[2,3,256,128]{3,2,1,0:T(8,128)(2,1)S(1)}, bf16[2,3,256,128]{3,2,1,0:T(8,128)(2,1)S(1)}, u32[]{:S(2)}, u32[]{:S(2)}) collective-permute-start(bf16[2,3,256,128]{3,2,1,0:T(8,128)(2,1)S(1)} %pad_maximum_fusion), channel_id=1, source_target_pairs={{0,1},{1,2},{2,3},{3,4},{4,5},{5,6},{6,7},{7,0},{8,9},{9,10},{10,1... | collective-permute-start | bytes 1179656 | tf_op jit(solution)/shard_map/ppermute | solution.py:73
  147.0 8.8 %collective-permute-start.25 = (bf16[2,3,256,128]{3,2,1,0:T(8,128)(2,1)}, bf16[2,3,256,128]{3,2,1,0:T(8,128)(2,1)S(1)}, u32[]{:S(2)}, u32[]{:S(2)}) collective-permute-start(bf16[2,3,256,128]{3,2,1,0:T(8,128)(2,1)} %add_convert_fusion.2), channel_id=1, source_target_pairs={{0,7},{1,0},{2,1},{3,2},{4,3},{5,4},{6,5},{7,6},{8,15},{9,8},{10,9... | collective-permute-start | bytes 1179656 | tf_op jit(solution)/shard_map/ppermute | solution.py:73
  147.9 9.3 %collective-permute-start.24 = (bf16[2,3,256,128]{3,2,1,0:T(8,128)(2,1)}, bf16[2,3,256,128]{3,2,1,0:T(8,128)(2,1)S(1)}, u32[]{:S(2)}, u32[]{:S(2)}) collective-permute-start(bf16[2,3,256,128]{3,2,1,0:T(8,128)(2,1)} %add_convert_fusion.3), channel_id=1, source_target_pairs={{0,1},{1,2},{2,3},{3,4},{4,5},{5,6},{6,7},{7,0},{8,9},{9,10},{10,1... | collective-permute-start | bytes 1179656 | tf_op jit(solution)/shard_map/ppermute | solution.py:73
  157.5 7.1 %collective-permute-start.27 = (bf16[3,256,128]{2,1,0:T(8,128)(2,1)S(1)}, bf16[3,256,128]{2,1,0:T(8,128)(2,1)S(1)}, u32[]{:S(2)}, u32[]{:S(2)}) collective-permute-start(bf16[3,256,128]{2,1,0:T(8,128)(2,1)S(1)} %get-tuple-element.75), channel_id=1, source_target_pairs={{0,1},{1,2},{2,3},{3,4},{4,5},{5,6},{6,7},{7,0},{8,9},{9,10},{10,1... | collective-permute-start | bytes 589832 | tf_op jit(solution)/shard_map/ppermute | solution.py:73
  157.6 9.2 %collective-permute-start.29 = (bf16[3,256,128]{2,1,0:T(8,128)(2,1)S(1)}, bf16[3,256,128]{2,1,0:T(8,128)(2,1)S(1)}, u32[]{:S(2)}, u32[]{:S(2)}) collective-permute-start(bf16[3,256,128]{2,1,0:T(8,128)(2,1)S(1)} %get-tuple-element.76), channel_id=1, source_target_pairs={{0,9},{1,10},{2,11},{3,12},{4,13},{5,14},{6,15},{7,8},{8,1},{9,2},... | collective-permute-start | bytes 589832 | tf_op jit(solution)/shard_map/ppermute | solution.py:394
  157.7 9.1 %collective-permute-start.28 = (bf16[3,256,128]{2,1,0:T(8,128)(2,1)S(1)}, bf16[3,256,128]{2,1,0:T(8,128)(2,1)S(1)}, u32[]{:S(2)}, u32[]{:S(2)}) collective-permute-start(bf16[3,256,128]{2,1,0:T(8,128)(2,1)S(1)} %get-tuple-element.77), channel_id=1, source_target_pairs={{0,7},{1,0},{2,1},{3,2},{4,3},{5,4},{6,5},{7,6},{8,15},{9,8},{10,9... | collective-permute-start | bytes 589832 | tf_op jit(solution)/shard_map/ppermute | solution.py:73
  160.4 7.6 %collective-permute-start.30 = (bf16[3,256,128]{2,1,0:T(8,128)(2,1)S(1)}, bf16[3,256,128]{2,1,0:T(8,128)(2,1)S(1)}, u32[]{:S(2)}, u32[]{:S(2)}) collective-permute-start(bf16[3,256,128]{2,1,0:T(8,128)(2,1)S(1)} %get-tuple-element.78), channel_id=1, source_target_pairs={{0,15},{1,8},{2,9},{3,10},{4,11},{5,12},{6,13},{7,14},{8,7},{9,0},... | collective-permute-start | bytes 589832 | tf_op jit(solution)/shard_map/ppermute | solution.py:395
  164.2 11.6 %collective-permute-start.26 = (bf16[3,256,128]{2,1,0:T(8,128)(2,1)S(1)}, bf16[3,256,128]{2,1,0:T(8,128)(2,1)S(1)}, u32[]{:S(2)}, u32[]{:S(2)}) collective-permute-start(bf16[3,256,128]{2,1,0:T(8,128)(2,1)S(1)} %dynamic-slice_bitcast_fusion.4), channel_id=1, source_target_pairs={{0,8},{8,0},{1,9},{9,1},{2,10},{10,2},{3,11},{11,3},{4,12},{12,4},... | collective-permute-start | bytes 589832 | tf_op jit(solution)/shard_map/ppermute | solution.py:73
  176.0 8.7 %collective-permute-start.31 = (bf16[3,256,128]{2,1,0:T(8,128)(2,1)S(1)}, bf16[3,256,128]{2,1,0:T(8,128)(2,1)S(1)}, u32[]{:S(2)}, u32[]{:S(2)}) collective-permute-start(bf16[3,256,128]{2,1,0:T(8,128)(2,1)S(1)} %fusion.4), channel_id=1, source_target_pairs={{0,0},{1,129},{2,34},{3,163},{4,68},{5,197},{6,102},{7,231},{8,16}... | collective-permute-start | bytes 589832 | tf_op jit(solution)/shard_map/ppermute | solution.py:397
  184.7 13.9 %collective-permute-start.32 = (bf16[3,256,128]{2,1,0:T(8,128)(2,1)S(1)}, bf16[3,256,128]{2,1,0:T(8,128)(2,1)S(1)}, u32[]{:S(2)}, u32[]{:S(2)}) collective-permute-start(bf16[3,256,128]{2,1,0:T(8,128)(2,1)S(1)} %collective-permute-done.31), channel_id=1, source_target_pairs={{0,0},{1,1},{2,6},{3,7},{4,4},{5,5},{6,2},{7,3},{8,8},{9,9},{10,14... | collective-permute-start | bytes 589832 | tf_op jit(solution)/shard_map/ppermute | solution.py:398
Sparse Core Ops, SparseCore 0:
  39.3 59.0 all-gather.1

commit v10 on v8

--- a/solution.py
+++ b/solution.py
@@ -28,6 +28,7 @@
 GROUP = 16
 CHUNK = WIDTH // 8
 SHARE = jax.ShapeDtypeStruct((2, 3, CHUNK // 2, HEAD_DIM), jnp.bfloat16)
+HALF_SHARE = jax.ShapeDtypeStruct((3, CHUNK // 2, HEAD_DIM), jnp.bfloat16)
 
 SAME_CORE = ((0, 0), (0, 1), (0, -1), (1, 0), (0, 2), (1, 1), (1, -1), (1, 2))
 SLOTS = [(dy, dx, dc) for dy, dx in SAME_CORE for dc in (0, 1)]
@@ -219,8 +220,8 @@
 
 
 def share_kernel(count, order, mask, w_ref, g_ref, *refs):
-    buffers, turned_out, out = refs[:count], refs[count], refs[count + 1 : count + 1 + len(FAR)]
-    tokens, proj, grads, turned, w, w_sem, x_sem, g_sem = refs[count + 1 + len(FAR) :]
+    buffers, turned_out, out = refs[:count], refs[count], refs[count + 1 : count + 3]
+    tokens, proj, grads, turned, w, w_sem, x_sem, g_sem = refs[count + 3 :]
     arrivals = [[] for _ in range(FRAMES)]
     for index, (buffer, at, slot, first, groups) in enumerate(PARTS):
         arrivals[slot].append(
@@ -259,20 +260,23 @@
     attend(proj, grads, mask, turned)
     store = pltpu.make_async_copy(turned, turned_out, w_sem.at[1])
     store.start()
-    for index, ahead in enumerate(FAR):
+    for ahead in FAR:
         columns = pl.ds(pl.multiple_of(order[16 + ahead] * CHUNK, CHUNK), CHUNK)
         rows = tokens[:, :, :, columns].reshape(ROWS, CHUNK)
-        weigh(turned, rows, out[index])
+        weigh(turned, rows, *out)
     store.wait()
 
 
-def weigh(turned, rows, out):
+def weigh(turned, rows, *out):
     value = jnp.dot(turned[...], rows, preferred_element_type=jnp.float32)
     for half in range(2):
         rows = slice(half * CHUNK // 2, (half + 1) * CHUNK // 2)
         for j in range(3):
             part = value[j * HEAD_DIM : (j + 1) * HEAD_DIM, rows]
-            out[half, j] = part.T.astype(jnp.bfloat16)
+            if len(out) == 2:
+                out[half][j] = part.T.astype(jnp.bfloat16)
+            else:
+                out[0][half, j] = part.T.astype(jnp.bfloat16)
 
 
 def near_kernel(count, near, order, turned_ref, *refs):
@@ -331,9 +335,9 @@
     groups = PATCHES // GROUP
     return pl.pallas_call(
         functools.partial(share_kernel, count),
-        out_shape=[jax.ShapeDtypeStruct((COLS, ROWS), jnp.bfloat16)] + [SHARE] * len(FAR),
+        out_shape=[jax.ShapeDtypeStruct((COLS, ROWS), jnp.bfloat16)] + [HALF_SHARE] * 2,
         in_specs=[SMEM, VMEM] + [HBM] * (2 + count),
-        out_specs=[HBM] + [VMEM] * len(FAR),
+        out_specs=[HBM] + [VMEM] * 2,
         scratch_shapes=[
             pltpu.VMEM((groups, FRAMES, GROUP, WIDTH), jnp.bfloat16),
             pltpu.VMEM((groups, FRAMES, GROUP, COLS), jnp.bfloat16),
@@ -371,7 +375,7 @@
         [buffer.reshape(-1, GROUP, WIDTH) for buffer in buffers] for buffers in steps
     )
     order, buffers = table[:24], first + second + third
-    turned, far = far_shares(order, visible(table[24:40]), w, g, buffers)
+    turned, *far = far_shares(order, visible(table[24:40]), w, g, buffers)
     beside = lax.optimization_barrier
     shares = lambda near: near_shares(order, turned, buffers, near)
     up, down, near = beside((shift(far[0], "z", 1), shift(far[1], "z", -1), shares(NEAR[0])))

time: 201 us -> 200 us (level)
  no operation moved by 1% of the time
where the time goes in v10:
time: 200 us; the launch traced here: 197 us
  starting transfers between devices  72.4 us (36%)
  waiting for transfers between devices  64.7 us (32%)
  Pallas kernels  39.9 us (20%)
  between operations  13.7 us (7%)
  local copies, waits for them, and re-layouts  4.52 us (2%)
    ppermute x27, starting transfers between devices, shift(): lax.ppermute(value, axis, [(i, (i + by) % count) for i in range(count)])  28.3 us
    ppermute x27, waiting for transfers between devices, shift(): lax.ppermute(value, axis, [(i, (i + by) % count) for i in range(count)])  23.3 us
    all_to_all x2, starting transfers between devices, local(): lax.all_to_all(value, axes, split_axis=0, concat_axis=0, tiled=True)  21.1 us
    pallas_call x1, Pallas kernels, far_shares(): pl.pallas_call(functools.partial(share_kernel, count), out_shape=[jax.Sha...  19 us
    pallas_call x3, Pallas kernels, near_shares(): pl.pallas_call(functools.partial(near_kernel, count, near), out_shape=[SH...  16.2 us
    ppermute x1, waiting for transfers between devices, local(): rows_w = lax.ppermute(rows_w, AXES, worker_moves())  15.5 us
    all_to_all x2, waiting for transfers between devices, local(): lax.all_to_all(value, axes, split_axis=0, concat_axis=0, tiled=True)  12.4 us
    ppermute x1, starting transfers between devices, local(): rows_w = lax.ppermute(rows_w, AXES, worker_moves())  9.82 us
  transfers between devices with their start and end apart: 34, of which 13 were waited for; matrix products, arithmetic and copies ran while one was open for 1% of the time, Pallas kernels for 11%

profile of v10, /device:TPU:3, one launch (start us, length us, event | category | flops | bytes accessed | tf_op | source)
XLA Modules:
  0.0 197.1 jit_solution(4870386730553889381)
XLA Ops:
  6.5 1.2 collective-permute-start.2
  7.8 0.3 collective-permute-start.3
  8.0 1.3 collective-permute-start.4
  9.3 0.7 constant_dynamic-slice_fusion
  10.0 0.6 slice.34
  10.6 2.4 %shard_map.46 = bf16[512,384]{1,0:T(8,128)(2,1)} custom-call(s32[1]{0:T(128)} %bitcast.2.start, bf16[3,4096,128]{2,1,0:T(8,128)(2,1)} %bitcast.73), custom_call_target="tpu_custom_call" | custom-call | tf_op jit(solution)/shard_map/pallas_call | solution.py:183
  13.0 9.8 %collective-permute-start = (bf16[512,384]{1,0:T(8,128)(2,1)}, bf16[512,384]{1,0:T(8,128)(2,1)S(1)}, u32[]{:S(2)}, u32[]{:S(2)}) collective-permute-start(bf16[512,384]{1,0:T(8,128)(2,1)} %shard_map.46), channel_id=1, source_target_pairs={{0,0},{128,1},{32,2},{160,3},{64,4},{192,5},{96,6},{224,7},{16,8},... | collective-permute-start | bytes 1179656 | tf_op jit(solution)/shard_map/ppermute | solution.py:365
  22.8 15.5 %collective-permute-done = bf16[512,384]{1,0:T(8,128)(2,1)S(1)} collective-permute-done((bf16[512,384]{1,0:T(8,128)(2,1)}, bf16[512,384]{1,0:T(8,128)(2,1)S(1)}, u32[]{:S(2)}, u32[]{:S(2)}) %collective-permute-start) | collective-permute-done | bytes 393248 | tf_op jit(solution)/shard_map/ppermute | solution.py:365
  38.4 0.8 copy-done.4
  39.2 0.1 collective-permute-start.10
  39.3 2.9 %collective-permute-start.9 = (bf16[128,4096]{1,0:T(8,128)(2,1)}, bf16[128,4096]{1,0:T(8,128)(2,1)}, u32[]{:S(2)}, u32[]{:S(2)}) collective-permute-start(bf16[128,4096]{1,0:T(8,128)(2,1)} %collective-permute-done.3), channel_id=1, source_target_pairs={{0,96},{32,0},{64,32},{96,64},{1,97},{33,1},{65,33},{97,65},{2,98}... | collective-permute-start | bytes 3145736 | tf_op jit(solution)/shard_map/ppermute | solution.py:70
  42.2 11.4 %all-to-all-start = ((bf16[16,128,128]{2,1,0:T(8,128)(2,1)}), bf16[16,128,128]{2,1,0:T(8,128)(2,1)}, u32[]{:S(2)}, u32[]{:S(2)}) async-start(bf16[16,128,128]{2,1,0:T(8,128)(2,1)} %bitcast.5), calls=%async_computation | async-start | bytes 1048576 | tf_op jit(solution)/shard_map/all_to_all | solution.py:367
  53.7 3.1 %collective-permute-start.1 = (bf16[128,4096]{1,0:T(8,128)(2,1)S(1)}, bf16[128,4096]{1,0:T(8,128)(2,1)S(1)}, u32[]{:S(2)}, u32[]{:S(2)}) collective-permute-start(bf16[128,4096]{1,0:T(8,128)(2,1)S(1)} %bitcast.48), channel_id=1, source_target_pairs={{0,16},{16,0},{1,17},{17,1},{2,18},{18,2},{3,19},{19,3},{4,20},{20... | collective-permute-start | bytes 3145736 | tf_op jit(solution)/shard_map/ppermute | solution.py:70
  56.7 0.1 collective-permute-start.6
  56.8 10.6 %collective-permute-done.10.refs_1_ = bf16[128,4096]{1,0:T(8,128)(2,1)} collective-permute-done((bf16[128,4096]{1,0:T(8,128)(2,1)}, bf16[128,4096]{1,0:T(8,128)(2,1)}, u32[]{:S(2)}, u32[]{:S(2)}) %collective-permute-start.10) | collective-permute-done | bytes 1048608 | tf_op jit(solution)/shard_map/ppermute | solution.py:70
  67.5 0.5 collective-permute-start.5
  68.0 4.9 %all-to-all-done = bf16[16,128,128]{2,1,0:T(8,128)(2,1)} async-done(((bf16[16,128,128]{2,1,0:T(8,128)(2,1)}), bf16[16,128,128]{2,1,0:T(8,128)(2,1)}, u32[]{:S(2)}, u32[]{:S(2)}) %all-to-all-start) | async-done | bytes 524320 | tf_op jit(solution)/shard_map/all_to_all | solution.py:367
  72.9 2.2 %shard_map.47 = (bf16[48,4096]{1,0:T(8,128)(2,1)}, bf16[48,4096]{1,0:T(8,128)(2,1)}, bf16[32,4096]{1,0:T(8,128)(2,1)}) custom-call(bf16[128,4096]{1,0:T(8,128)(2,1)} %collective-permute-done.8.refs_0_, bf16[128,4096]{1,0:T(8,128)(2,1)} %collective-permute-done.10.refs_1_, bf16[128,4096]{1,0:T(8,128)(2,1)} %collective-permute-done.9.refs_2_), custom_call_target="tpu_custom_call" | custom-call | flops 30000001024 | tf_op jit(solution)/shard_map/pallas_call | solution.py:92
  75.2 0.8 collective-permute-start.14
  76.0 3.2 %collective-permute-start.15 = (bf16[48,4096]{1,0:T(8,128)(2,1)}, bf16[48,4096]{1,0:T(8,128)(2,1)}, u32[]{:S(2)}, u32[]{:S(2)}) collective-permute-start(bf16[48,4096]{1,0:T(8,128)(2,1)} %get-tuple-element.49), channel_id=1, source_target_pairs={{0,96},{32,0},{64,32},{96,64},{1,97},{33,1},{65,33},{97,65},{2,98}... | collective-permute-start | bytes 1179656 | tf_op jit(solution)/shard_map/ppermute | solution.py:70
  79.2 2.3 %collective-permute-start.16 = (bf16[32,4096]{1,0:T(8,128)(2,1)}, bf16[32,4096]{1,0:T(8,128)(2,1)}, u32[]{:S(2)}, u32[]{:S(2)}) collective-permute-start(bf16[32,4096]{1,0:T(8,128)(2,1)} %get-tuple-element.50), channel_id=1, source_target_pairs={{0,128},{128,0},{1,129},{129,1},{2,130},{130,2},{3,131},{131,3},{4... | collective-permute-start | bytes 786440 | tf_op jit(solution)/shard_map/ppermute | solution.py:70
  81.5 9.7 %all-to-all-start.1 = ((bf16[16,128,128]{2,1,0:T(8,128)(2,1)}), bf16[16,128,128]{2,1,0:T(8,128)(2,1)}, u32[]{:S(2)}, u32[]{:S(2)}) async-start(bf16[16,128,128]{2,1,0:T(8,128)(2,1)} %all-to-all-done), calls=%async_computation.1 | async-start | bytes 1048576 | tf_op jit(solution)/shard_map/all_to_all | solution.py:367
  91.2 0.4 collective-permute-start.11
  91.7 0.1 collective-permute-start.12
  91.8 0.4 collective-permute-start.13
  92.3 7.5 %all-to-all-done.1 = bf16[16,128,128]{2,1,0:T(8,128)(2,1)} async-done(((bf16[16,128,128]{2,1,0:T(8,128)(2,1)}), bf16[16,128,128]{2,1,0:T(8,128)(2,1)}, u32[]{:S(2)}, u32[]{:S(2)}) %all-to-all-start.1) | async-done | bytes 524320 | tf_op jit(solution)/shard_map/all_to_all | solution.py:367
  99.8 1.3 collective-permute-start.19
  101.3 0.1 le.15
  101.4 0.1 eq.18
  101.4 0.3 collective-permute-start.17
  101.7 0.9 collective-permute-done.19
  102.6 0.4 collective-permute-start.18
  103.0 0.7 slice_bitcast_fusion.1.order
  103.7 0.1 and_convert_fusion.mask
  103.8 0.8 collective-permute-done.18
  104.6 19.0 %shard_map.48 = (bf16[384,2048]{1,0:T(8,128)(2,1)}, bf16[3,256,128]{2,1,0:T(8,128)(2,1)S(1)}, bf16[3,256,128]{2,1,0:T(8,128)(2,1)S(1)}) custom-call(s32[24]{0:T(128)S(1)} %slice_bitcast_fusion.1.order, f32[256,256]{1,0:T(8,128)S(1)} %and_convert_fusion.mask, bf16[4096,384]{1,0:T(8,128)(2,1)} %all-gather.2.cloned.1.call-done.w_ref, ...), custom_call_target="tpu_custom_call" | custom-call | flops 6442450944 | bytes 16777216 | tf_op jit(solution)/shard_map/pallas_call | solution.py:336
  123.7 0.1 collective-permute-start.20
  123.8 2.7 %collective-permute-start.21 = (bf16[3,256,128]{2,1,0:T(8,128)(2,1)S(1)}, bf16[3,256,128]{2,1,0:T(8,128)(2,1)S(1)}, u32[]{:S(2)}, u32[]{:S(2)}) collective-permute-start(bf16[3,256,128]{2,1,0:T(8,128)(2,1)S(1)} %get-tuple-element.55), channel_id=1, source_target_pairs={{0,7},{1,0},{2,1},{3,2},{4,3},{5,4},{6,5},{7,6},{8,15},{9,8},{10,9... | collective-permute-start | bytes 589832 | tf_op jit(solution)/shard_map/ppermute | solution.py:70
  126.4 4.9 %shard_map.49 = (bf16[2,3,256,128]{3,2,1,0:T(8,128)(2,1)S(1)}, bf16[2,3,256,128]{3,2,1,0:T(8,128)(2,1)S(1)}) custom-call(s32[24]{0:T(128)S(1)} %slice_bitcast_fusion.1.order, bf16[384,2048]{1,0:T(8,128)(2,1)} %get-tuple-element.56.turned_ref, bf16[8,16,4096]{2,1,0:T(8,128)(2,1)S(1)} %bitcast.50, bf16[8,16,4096]{2,1,0:T(8,128)(2,1)S(1)} %bitcast.58, ...), custom_call_target="tpu_custom_call" | custom-call | flops 1610612736 | bytes 4194304 | tf_op jit(solution)/shard_map/pallas_call | solution.py:313
  131.5 2.1 %collective-permute-start.23 = (bf16[2,3,256,128]{3,2,1,0:T(8,128)(2,1)S(1)}, bf16[2,3,256,128]{3,2,1,0:T(8,128)(2,1)S(1)}, u32[]{:S(2)}, u32[]{:S(2)}) collective-permute-start(bf16[2,3,256,128]{3,2,1,0:T(8,128)(2,1)S(1)} %pad_maximum_fusion.1), channel_id=1, source_target_pairs={{0,7},{1,0},{2,1},{3,2},{4,3},{5,4},{6,5},{7,6},{8,15},{9,8},{10,9... | collective-permute-start | bytes 1179656 | tf_op jit(solution)/shard_map/ppermute | solution.py:70
  133.8 0.1 collective-permute-start.22
  133.8 4.9 %shard_map.50 = (bf16[2,3,256,128]{3,2,1,0:T(8,128)(2,1)S(1)}, bf16[2,3,256,128]{3,2,1,0:T(8,128)(2,1)S(1)}) custom-call(s32[24]{0:T(128)S(1)} %slice_bitcast_fusion.1.order, bf16[384,2048]{1,0:T(8,128)(2,1)} %get-tuple-element.56.turned_ref, bf16[8,16,4096]{2,1,0:T(8,128)(2,1)S(1)} %bitcast.51, bf16[8,16,4096]{2,1,0:T(8,128)(2,1)S(1)} %bitcast.59, ...), custom_call_target="tpu_custom_call" | custom-call | flops 1610612736 | bytes 4194304 | tf_op jit(solution)/shard_map/pallas_call | solution.py:313
  138.8 2.5 %collective-permute-done.23 = bf16[2,3,256,128]{3,2,1,0:T(8,128)(2,1)S(1)} collective-permute-done((bf16[2,3,256,128]{3,2,1,0:T(8,128)(2,1)S(1)}, bf16[2,3,256,128]{3,2,1,0:T(8,128)(2,1)S(1)}, u32[]{:S(2)}, u32[]{:S(2)}) %collective-permute-start.23) | collective-permute-done | bytes 393248 | tf_op jit(solution)/shard_map/ppermute | solution.py:70
  141.3 2.6 %collective-permute-done.22 = bf16[2,3,256,128]{3,2,1,0:T(8,128)(2,1)S(1)} collective-permute-done((bf16[2,3,256,128]{3,2,1,0:T(8,128)(2,1)S(1)}, bf16[2,3,256,128]{3,2,1,0:T(8,128)(2,1)S(1)}, u32[]{:S(2)}, u32[]{:S(2)}) %collective-permute-start.22) | collective-permute-done | bytes 393248 | tf_op jit(solution)/shard_map/ppermute | solution.py:70
  143.9 0.1 add_convert_fusion.3
  144.0 0.2 collective-permute-start.25
  144.1 0.1 add_convert_fusion.4
  144.2 1.5 collective-permute-start.24
  145.7 6.4 %shard_map.51 = (bf16[2,3,256,128]{3,2,1,0:T(8,128)(2,1)S(1)}, bf16[2,3,256,128]{3,2,1,0:T(8,128)(2,1)S(1)}, bf16[2,3,256,128]{3,2,1,0:T(8,128)(2,1)S(1)}) custom-call(s32[24]{0:T(128)S(1)} %slice_bitcast_fusion.1.order, bf16[384,2048]{1,0:T(8,128)(2,1)} %get-tuple-element.56.turned_ref, bf16[8,16,4096]{2,1,0:T(8,128)(2,1)S(1)} %bitcast.52, ...), custom_call_target="tpu_custom_call" | custom-call | flops 2415919104 | bytes 6291456 | tf_op jit(solution)/shard_map/pallas_call | solution.py:313
  152.1 0.7 copy-done.3
  152.8 0.6 collective-permute-done.24
  153.4 0.1 add_convert_fusion.2
  153.5 0.1 collective-permute-start.26
  153.6 0.1 add_convert_fusion.1
  153.7 2.7 %collective-permute-start.27 = (bf16[2,3,256,128]{3,2,1,0:T(8,128)(2,1)S(1)}, bf16[2,3,256,128]{3,2,1,0:T(8,128)(2,1)S(1)}, u32[]{:S(2)}, u32[]{:S(2)}) collective-permute-start(bf16[2,3,256,128]{3,2,1,0:T(8,128)(2,1)S(1)} %add_convert_fusion.1), channel_id=1, source_target_pairs={{0,7},{1,0},{2,1},{3,2},{4,3},{5,4},{6,5},{7,6},{8,15},{9,8},{10,9... | collective-permute-start | bytes 1179656 | tf_op jit(solution)/shard_map/ppermute | solution.py:70
  156.5 5.3 %collective-permute-done.26 = bf16[2,3,256,128]{3,2,1,0:T(8,128)(2,1)S(1)} collective-permute-done((bf16[2,3,256,128]{3,2,1,0:T(8,128)(2,1)S(1)}, bf16[2,3,256,128]{3,2,1,0:T(8,128)(2,1)S(1)}, u32[]{:S(2)}, u32[]{:S(2)}) %collective-permute-start.26) | collective-permute-done | bytes 393248 | tf_op jit(solution)/shard_map/ppermute | solution.py:70
  161.8 1.2 add_convert_fusion
  163.0 6.6 %collective-permute-start.28 = (bf16[3,256,128]{2,1,0:T(8,128)(2,1)S(1)}, bf16[3,256,128]{2,1,0:T(8,128)(2,1)S(1)}, u32[]{:S(2)}, u32[]{:S(2)}) collective-permute-start(bf16[3,256,128]{2,1,0:T(8,128)(2,1)S(1)} %get-tuple-element.77), channel_id=1, source_target_pairs={{0,0},{1,129},{2,34},{3,163},{4,68},{5,197},{6,102},{7,231},{8,16}... | collective-permute-start | bytes 589832 | tf_op jit(solution)/shard_map/ppermute | solution.py:392
  169.6 0.1 collective-permute-start.29
  169.7 3.2 %collective-permute-done.28 = bf16[3,256,128]{2,1,0:T(8,128)(2,1)S(1)} collective-permute-done((bf16[3,256,128]{2,1,0:T(8,128)(2,1)S(1)}, bf16[3,256,128]{2,1,0:T(8,128)(2,1)S(1)}, u32[]{:S(2)}, u32[]{:S(2)}) %collective-permute-start.28) | collective-permute-done | bytes 196640 | tf_op jit(solution)/shard_map/ppermute | solution.py:392
  172.9 1.4 collective-permute-done.29
  174.3 6.5 %collective-permute-start.30 = (bf16[3,256,128]{2,1,0:T(8,128)(2,1)S(1)}, bf16[3,256,128]{2,1,0:T(8,128)(2,1)S(1)}, u32[]{:S(2)}, u32[]{:S(2)}) collective-permute-start(bf16[3,256,128]{2,1,0:T(8,128)(2,1)S(1)} %add_convert_fusion.5), channel_id=1, source_target_pairs={{0,0},{1,1},{2,6},{3,7},{4,4},{5,5},{6,2},{7,3},{8,8},{9,9},{10,14... | collective-permute-start | bytes 589832 | tf_op jit(solution)/shard_map/ppermute | solution.py:394
  180.9 8.7 %collective-permute-done.30 = bf16[3,256,128]{2,1,0:T(8,128)(2,1)S(1)} collective-permute-done((bf16[3,256,128]{2,1,0:T(8,128)(2,1)S(1)}, bf16[3,256,128]{2,1,0:T(8,128)(2,1)S(1)}, u32[]{:S(2)}, u32[]{:S(2)}) %collective-permute-start.30) | collective-permute-done | bytes 196640 | tf_op jit(solution)/shard_map/ppermute | solution.py:394
  189.6 0.7 copy.6
  (46 shorter events, 0.6 us)
Async XLA Ops:
  6.5 47.1 %copy-start = (bf16[1,128,4096]{2,1,0:T(8,128)(2,1)S(1)}, bf16[1,128,4096]{2,1,0:T(8,128)(2,1)}, u32[]{:S(2)}) copy-start(bf16[1,128,4096]{2,1,0:T(8,128)(2,1)} %param.4) | copy-start | bytes 3145732
  6.5 98.1 %all-gather.2.cloned.1.call-start = ((), (), s32[]{:S(2)}) async-start(), calls=%async_computation.2 | async-start | bytes 3538944 | tf_op jit(solution)/shard_map/all_gather | solution.py:366
  6.5 32.6 %collective-permute-start.2 = (bf16[128,4096]{1,0:T(8,128)(2,1)}, bf16[128,4096]{1,0:T(8,128)(2,1)S(1)}, u32[]{:S(2)}, u32[]{:S(2)}) collective-permute-start(bf16[128,4096]{1,0:T(8,128)(2,1)} %bitcast.45), channel_id=1, source_target_pairs={{0,32},{32,64},{64,96},{96,0},{1,33},{33,65},{65,97},{97,1},{2,34}... | collective-permute-start | bytes 3145736 | tf_op jit(solution)/shard_map/ppermute | solution.py:70
  7.8 31.4 %collective-permute-start.3 = (bf16[128,4096]{1,0:T(8,128)(2,1)}, bf16[128,4096]{1,0:T(8,128)(2,1)}, u32[]{:S(2)}, u32[]{:S(2)}) collective-permute-start(bf16[128,4096]{1,0:T(8,128)(2,1)} %bitcast.46), channel_id=1, source_target_pairs={{0,96},{32,0},{64,32},{96,64},{1,97},{33,1},{65,33},{97,65},{2,98}... | collective-permute-start | bytes 3145736 | tf_op jit(solution)/shard_map/ppermute | solution.py:70
  8.0 31.2 %collective-permute-start.4 = (bf16[128,4096]{1,0:T(8,128)(2,1)}, bf16[128,4096]{1,0:T(8,128)(2,1)}, u32[]{:S(2)}, u32[]{:S(2)}) collective-permute-start(bf16[128,4096]{1,0:T(8,128)(2,1)} %bitcast.47), channel_id=1, source_target_pairs={{0,128},{128,0},{1,129},{129,1},{2,130},{130,2},{3,131},{131,3},{4... | collective-permute-start | bytes 3145736 | tf_op jit(solution)/shard_map/ppermute | solution.py:70
  10.0 91.1 %copy-start.5 = (s32[1,48]{1,0:T(1,128)}, s32[1,48]{1,0:T(1,128)S(1)}, u32[]{:S(2)}) copy-start(s32[1,48]{1,0:T(1,128)S(1)} %constant_dynamic-slice_fusion) | copy-start | bytes 580
  13.0 25.4 %collective-permute-start = (bf16[512,384]{1,0:T(8,128)(2,1)}, bf16[512,384]{1,0:T(8,128)(2,1)S(1)}, u32[]{:S(2)}, u32[]{:S(2)}) collective-permute-start(bf16[512,384]{1,0:T(8,128)(2,1)} %shard_map.46), channel_id=1, source_target_pairs={{0,0},{128,1},{32,2},{160,3},{64,4},{192,5},{96,6},{224,7},{16,8},... | collective-permute-start | bytes 1179656 | tf_op jit(solution)/shard_map/ppermute | solution.py:365
  38.4 0.8 copy-start.4
  39.2 36.0 %copy-start.1 = (bf16[128,4096]{1,0:T(8,128)(2,1)}, bf16[128,4096]{1,0:T(8,128)(2,1)S(1)}, u32[]{:S(2)}) copy-start(bf16[128,4096]{1,0:T(8,128)(2,1)S(1)} %collective-permute-done.2) | copy-start | bytes 3145732
  39.2 28.3 %collective-permute-start.10 = (bf16[128,4096]{1,0:T(8,128)(2,1)}, bf16[128,4096]{1,0:T(8,128)(2,1)}, u32[]{:S(2)}, u32[]{:S(2)}) collective-permute-start(bf16[128,4096]{1,0:T(8,128)(2,1)} %collective-permute-done.3), channel_id=1, source_target_pairs={{0,128},{128,0},{1,129},{129,1},{2,130},{130,2},{3,131},{131,3},{4... | collective-permute-start | bytes 3145736 | tf_op jit(solution)/shard_map/ppermute | solution.py:70
  39.3 28.2 %collective-permute-start.9 = (bf16[128,4096]{1,0:T(8,128)(2,1)}, bf16[128,4096]{1,0:T(8,128)(2,1)}, u32[]{:S(2)}, u32[]{:S(2)}) collective-permute-start(bf16[128,4096]{1,0:T(8,128)(2,1)} %collective-permute-done.3), channel_id=1, source_target_pairs={{0,96},{32,0},{64,32},{96,64},{1,97},{33,1},{65,33},{97,65},{2,98}... | collective-permute-start | bytes 3145736 | tf_op jit(solution)/shard_map/ppermute | solution.py:70
  42.2 30.7 %collective-permute-start.8 = (bf16[128,4096]{1,0:T(8,128)(2,1)}, bf16[128,4096]{1,0:T(8,128)(2,1)}, u32[]{:S(2)}, u32[]{:S(2)}) collective-permute-start(bf16[128,4096]{1,0:T(8,128)(2,1)} %collective-permute-done.4), channel_id=1, source_target_pairs={{0,32},{32,64},{64,96},{96,0},{1,33},{33,65},{65,97},{97,1},{2,34}... | collective-permute-start | bytes 3145736 | tf_op jit(solution)/shard_map/ppermute | solution.py:70
  42.2 30.7 %all-to-all-start = ((bf16[16,128,128]{2,1,0:T(8,128)(2,1)}), bf16[16,128,128]{2,1,0:T(8,128)(2,1)}, u32[]{:S(2)}, u32[]{:S(2)}) async-start(bf16[16,128,128]{2,1,0:T(8,128)(2,1)} %bitcast.5), calls=%async_computation | async-start | bytes 1048576 | tf_op jit(solution)/shard_map/all_to_all | solution.py:367
  53.7 22.3 %collective-permute-start.1 = (bf16[128,4096]{1,0:T(8,128)(2,1)S(1)}, bf16[128,4096]{1,0:T(8,128)(2,1)S(1)}, u32[]{:S(2)}, u32[]{:S(2)}) collective-permute-start(bf16[128,4096]{1,0:T(8,128)(2,1)S(1)} %bitcast.48), channel_id=1, source_target_pairs={{0,16},{16,0},{1,17},{17,1},{2,18},{18,2},{3,19},{19,3},{4,20},{20... | collective-permute-start | bytes 3145736 | tf_op jit(solution)/shard_map/ppermute | solution.py:70
  56.7 22.5 %collective-permute-start.6 = (bf16[128,4096]{1,0:T(8,128)(2,1)}, bf16[128,4096]{1,0:T(8,128)(2,1)}, u32[]{:S(2)}, u32[]{:S(2)}) collective-permute-start(bf16[128,4096]{1,0:T(8,128)(2,1)} %collective-permute-done.3), channel_id=1, source_target_pairs={{0,16},{16,0},{1,17},{17,1},{2,18},{18,2},{3,19},{19,3},{4,20},{20... | collective-permute-start | bytes 3145736 | tf_op jit(solution)/shard_map/ppermute | solution.py:70
  67.5 32.3 %collective-permute-start.7 = (bf16[128,4096]{1,0:T(8,128)(2,1)}, bf16[128,4096]{1,0:T(8,128)(2,1)}, u32[]{:S(2)}, u32[]{:S(2)}) collective-permute-start(bf16[128,4096]{1,0:T(8,128)(2,1)} %collective-permute-done.4), channel_id=1, source_target_pairs={{0,16},{16,0},{1,17},{17,1},{2,18},{18,2},{3,19},{19,3},{4,20},{20... | collective-permute-start | bytes 3145736 | tf_op jit(solution)/shard_map/ppermute | solution.py:70
  67.5 33.9 %collective-permute-start.5 = (bf16[128,4096]{1,0:T(8,128)(2,1)S(1)}, bf16[128,4096]{1,0:T(8,128)(2,1)}, u32[]{:S(2)}, u32[]{:S(2)}) collective-permute-start(bf16[128,4096]{1,0:T(8,128)(2,1)S(1)} %collective-permute-done.2), channel_id=1, source_target_pairs={{0,16},{16,0},{1,17},{17,1},{2,18},{18,2},{3,19},{19,3},{4,20},{20... | collective-permute-start | bytes 3145736 | tf_op jit(solution)/shard_map/ppermute | solution.py:70
  75.2 16.5 %collective-permute-start.14 = (bf16[48,4096]{1,0:T(8,128)(2,1)}, bf16[48,4096]{1,0:T(8,128)(2,1)S(1)}, u32[]{:S(2)}, u32[]{:S(2)}) collective-permute-start(bf16[48,4096]{1,0:T(8,128)(2,1)} %get-tuple-element.48), channel_id=1, source_target_pairs={{0,32},{32,64},{64,96},{96,0},{1,33},{33,65},{65,97},{97,1},{2,34}... | collective-permute-start | bytes 1179656 | tf_op jit(solution)/shard_map/ppermute | solution.py:70
  76.0 15.8 %collective-permute-start.15 = (bf16[48,4096]{1,0:T(8,128)(2,1)}, bf16[48,4096]{1,0:T(8,128)(2,1)}, u32[]{:S(2)}, u32[]{:S(2)}) collective-permute-start(bf16[48,4096]{1,0:T(8,128)(2,1)} %get-tuple-element.49), channel_id=1, source_target_pairs={{0,96},{32,0},{64,32},{96,64},{1,97},{33,1},{65,33},{97,65},{2,98}... | collective-permute-start | bytes 1179656 | tf_op jit(solution)/shard_map/ppermute | solution.py:70
  79.2 12.0 %collective-permute-start.16 = (bf16[32,4096]{1,0:T(8,128)(2,1)}, bf16[32,4096]{1,0:T(8,128)(2,1)}, u32[]{:S(2)}, u32[]{:S(2)}) collective-permute-start(bf16[32,4096]{1,0:T(8,128)(2,1)} %get-tuple-element.50), channel_id=1, source_target_pairs={{0,128},{128,0},{1,129},{129,1},{2,130},{130,2},{3,131},{131,3},{4... | collective-permute-start | bytes 786440 | tf_op jit(solution)/shard_map/ppermute | solution.py:70
  81.5 18.3 %all-to-all-start.1 = ((bf16[16,128,128]{2,1,0:T(8,128)(2,1)}), bf16[16,128,128]{2,1,0:T(8,128)(2,1)}, u32[]{:S(2)}, u32[]{:S(2)}) async-start(bf16[16,128,128]{2,1,0:T(8,128)(2,1)} %all-to-all-done), calls=%async_computation.1 | async-start | bytes 1048576 | tf_op jit(solution)/shard_map/all_to_all | solution.py:367
  91.2 13.3 %collective-permute-start.11 = (bf16[128,4096]{1,0:T(8,128)(2,1)}, bf16[128,4096]{1,0:T(8,128)(2,1)}, u32[]{:S(2)}, u32[]{:S(2)}) collective-permute-start(bf16[128,4096]{1,0:T(8,128)(2,1)} %collective-permute-done.8.refs_0_), channel_id=1, source_target_pairs={{0,16},{16,0},{1,17},{17,1},{2,18},{18,2},{3,19},{19,3},{4,20},{20... | collective-permute-start | bytes 3145736 | tf_op jit(solution)/shard_map/ppermute | solution.py:70
  91.7 12.9 %collective-permute-start.12 = (bf16[128,4096]{1,0:T(8,128)(2,1)}, bf16[128,4096]{1,0:T(8,128)(2,1)}, u32[]{:S(2)}, u32[]{:S(2)}) collective-permute-start(bf16[128,4096]{1,0:T(8,128)(2,1)} %collective-permute-done.9.refs_2_), channel_id=1, source_target_pairs={{0,16},{16,0},{1,17},{17,1},{2,18},{18,2},{3,19},{19,3},{4,20},{20... | collective-permute-start | bytes 3145736 | tf_op jit(solution)/shard_map/ppermute | solution.py:70
  91.8 12.7 %collective-permute-start.13 = (bf16[128,4096]{1,0:T(8,128)(2,1)}, bf16[128,4096]{1,0:T(8,128)(2,1)}, u32[]{:S(2)}, u32[]{:S(2)}) collective-permute-start(bf16[128,4096]{1,0:T(8,128)(2,1)} %collective-permute-done.10.refs_1_), channel_id=1, source_target_pairs={{0,16},{16,0},{1,17},{17,1},{2,18},{18,2},{3,19},{19,3},{4,20},{20... | collective-permute-start | bytes 3145736 | tf_op jit(solution)/shard_map/ppermute | solution.py:70
  99.8 2.8 %collective-permute-start.19 = (bf16[32,4096]{1,0:T(8,128)(2,1)}, bf16[32,4096]{1,0:T(8,128)(2,1)}, u32[]{:S(2)}, u32[]{:S(2)}) collective-permute-start(bf16[32,4096]{1,0:T(8,128)(2,1)} %collective-permute-done.16), channel_id=1, source_target_pairs={{0,16},{16,0},{1,17},{17,1},{2,18},{18,2},{3,19},{19,3},{4,20},{20... | collective-permute-start | bytes 786440 | tf_op jit(solution)/shard_map/ppermute | solution.py:70
  101.4 2.4 %collective-permute-start.17 = (bf16[48,4096]{1,0:T(8,128)(2,1)S(1)}, bf16[48,4096]{1,0:T(8,128)(2,1)S(1)}, u32[]{:S(2)}, u32[]{:S(2)}) collective-permute-start(bf16[48,4096]{1,0:T(8,128)(2,1)S(1)} %collective-permute-done.14), channel_id=1, source_target_pairs={{0,16},{16,0},{1,17},{17,1},{2,18},{18,2},{3,19},{19,3},{4,20},{20... | collective-permute-start | bytes 1179656 | tf_op jit(solution)/shard_map/ppermute | solution.py:70
  102.6 1.9 collective-permute-start.18
  104.6 21.8 %copy-start.2 = (bf16[128,4096]{1,0:T(8,128)(2,1)S(1)}, bf16[128,4096]{1,0:T(8,128)(2,1)}, u32[]{:S(2)}) copy-start(bf16[128,4096]{1,0:T(8,128)(2,1)} %copy-done.1) | copy-start | bytes 3145732
  123.7 7.7 %collective-permute-start.20 = (bf16[3,256,128]{2,1,0:T(8,128)(2,1)S(1)}, bf16[3,256,128]{2,1,0:T(8,128)(2,1)S(1)}, u32[]{:S(2)}, u32[]{:S(2)}) collective-permute-start(bf16[3,256,128]{2,1,0:T(8,128)(2,1)S(1)} %get-tuple-element.54), channel_id=1, source_target_pairs={{0,1},{1,2},{2,3},{3,4},{4,5},{5,6},{6,7},{7,0},{8,9},{9,10},{10,1... | collective-permute-start | bytes 589832 | tf_op jit(solution)/shard_map/ppermute | solution.py:70
  123.8 7.6 %collective-permute-start.21 = (bf16[3,256,128]{2,1,0:T(8,128)(2,1)S(1)}, bf16[3,256,128]{2,1,0:T(8,128)(2,1)S(1)}, u32[]{:S(2)}, u32[]{:S(2)}) collective-permute-start(bf16[3,256,128]{2,1,0:T(8,128)(2,1)S(1)} %get-tuple-element.55), channel_id=1, source_target_pairs={{0,7},{1,0},{2,1},{3,2},{4,3},{5,4},{6,5},{7,6},{8,15},{9,8},{10,9... | collective-permute-start | bytes 589832 | tf_op jit(solution)/shard_map/ppermute | solution.py:70
  131.5 9.8 %collective-permute-start.23 = (bf16[2,3,256,128]{3,2,1,0:T(8,128)(2,1)S(1)}, bf16[2,3,256,128]{3,2,1,0:T(8,128)(2,1)S(1)}, u32[]{:S(2)}, u32[]{:S(2)}) collective-permute-start(bf16[2,3,256,128]{3,2,1,0:T(8,128)(2,1)S(1)} %pad_maximum_fusion.1), channel_id=1, source_target_pairs={{0,7},{1,0},{2,1},{3,2},{4,3},{5,4},{6,5},{7,6},{8,15},{9,8},{10,9... | collective-permute-start | bytes 1179656 | tf_op jit(solution)/shard_map/ppermute | solution.py:70
  133.8 10.1 %collective-permute-start.22 = (bf16[2,3,256,128]{3,2,1,0:T(8,128)(2,1)S(1)}, bf16[2,3,256,128]{3,2,1,0:T(8,128)(2,1)S(1)}, u32[]{:S(2)}, u32[]{:S(2)}) collective-permute-start(bf16[2,3,256,128]{3,2,1,0:T(8,128)(2,1)S(1)} %pad_maximum_fusion), channel_id=1, source_target_pairs={{0,1},{1,2},{2,3},{3,4},{4,5},{5,6},{6,7},{7,0},{8,9},{9,10},{10,1... | collective-permute-start | bytes 1179656 | tf_op jit(solution)/shard_map/ppermute | solution.py:70
  144.0 8.8 %collective-permute-start.25 = (bf16[2,3,256,128]{3,2,1,0:T(8,128)(2,1)S(1)}, bf16[2,3,256,128]{3,2,1,0:T(8,128)(2,1)S(1)}, u32[]{:S(2)}, u32[]{:S(2)}) collective-permute-start(bf16[2,3,256,128]{3,2,1,0:T(8,128)(2,1)S(1)} %add_convert_fusion.3), channel_id=1, source_target_pairs={{0,7},{1,0},{2,1},{3,2},{4,3},{5,4},{6,5},{7,6},{8,15},{9,8},{10,9... | collective-permute-start | bytes 1179656 | tf_op jit(solution)/shard_map/ppermute | solution.py:70
  144.2 9.2 %collective-permute-start.24 = (bf16[2,3,256,128]{3,2,1,0:T(8,128)(2,1)S(1)}, bf16[2,3,256,128]{3,2,1,0:T(8,128)(2,1)S(1)}, u32[]{:S(2)}, u32[]{:S(2)}) collective-permute-start(bf16[2,3,256,128]{3,2,1,0:T(8,128)(2,1)S(1)} %add_convert_fusion.4), channel_id=1, source_target_pairs={{0,1},{1,2},{2,3},{3,4},{4,5},{5,6},{6,7},{7,0},{8,9},{9,10},{10,1... | collective-permute-start | bytes 1179656 | tf_op jit(solution)/shard_map/ppermute | solution.py:70
  152.1 0.7 copy-start.3
  153.5 8.3 %collective-permute-start.26 = (bf16[2,3,256,128]{3,2,1,0:T(8,128)(2,1)S(1)}, bf16[2,3,256,128]{3,2,1,0:T(8,128)(2,1)S(1)}, u32[]{:S(2)}, u32[]{:S(2)}) collective-permute-start(bf16[2,3,256,128]{3,2,1,0:T(8,128)(2,1)S(1)} %add_convert_fusion.2), channel_id=1, source_target_pairs={{0,1},{1,2},{2,3},{3,4},{4,5},{5,6},{6,7},{7,0},{8,9},{9,10},{10,1... | collective-permute-start | bytes 1179656 | tf_op jit(solution)/shard_map/ppermute | solution.py:70
  153.7 8.1 %collective-permute-start.27 = (bf16[2,3,256,128]{3,2,1,0:T(8,128)(2,1)S(1)}, bf16[2,3,256,128]{3,2,1,0:T(8,128)(2,1)S(1)}, u32[]{:S(2)}, u32[]{:S(2)}) collective-permute-start(bf16[2,3,256,128]{3,2,1,0:T(8,128)(2,1)S(1)} %add_convert_fusion.1), channel_id=1, source_target_pairs={{0,7},{1,0},{2,1},{3,2},{4,3},{5,4},{6,5},{7,6},{8,15},{9,8},{10,9... | collective-permute-start | bytes 1179656 | tf_op jit(solution)/shard_map/ppermute | solution.py:70
  163.0 9.9 %collective-permute-start.28 = (bf16[3,256,128]{2,1,0:T(8,128)(2,1)S(1)}, bf16[3,256,128]{2,1,0:T(8,128)(2,1)S(1)}, u32[]{:S(2)}, u32[]{:S(2)}) collective-permute-start(bf16[3,256,128]{2,1,0:T(8,128)(2,1)S(1)} %get-tuple-element.77), channel_id=1, source_target_pairs={{0,0},{1,129},{2,34},{3,163},{4,68},{5,197},{6,102},{7,231},{8,16}... | collective-permute-start | bytes 589832 | tf_op jit(solution)/shard_map/ppermute | solution.py:392
  169.6 4.7 %collective-permute-start.29 = (bf16[3,256,128]{2,1,0:T(8,128)(2,1)S(1)}, bf16[3,256,128]{2,1,0:T(8,128)(2,1)S(1)}, u32[]{:S(2)}, u32[]{:S(2)}) collective-permute-start(bf16[3,256,128]{2,1,0:T(8,128)(2,1)S(1)} %get-tuple-element.78), channel_id=1, source_target_pairs={{0,16},{1,145},{2,50},{3,179},{4,84},{5,213},{6,118},{7,247},{8,0}... | collective-permute-start | bytes 589832 | tf_op jit(solution)/shard_map/ppermute | solution.py:392
  174.3 15.3 %collective-permute-start.30 = (bf16[3,256,128]{2,1,0:T(8,128)(2,1)S(1)}, bf16[3,256,128]{2,1,0:T(8,128)(2,1)S(1)}, u32[]{:S(2)}, u32[]{:S(2)}) collective-permute-start(bf16[3,256,128]{2,1,0:T(8,128)(2,1)S(1)} %add_convert_fusion.5), channel_id=1, source_target_pairs={{0,0},{1,1},{2,6},{3,7},{4,4},{5,5},{6,2},{7,3},{8,8},{9,9},{10,14... | collective-permute-start | bytes 589832 | tf_op jit(solution)/shard_map/ppermute | solution.py:394
Sparse Core Ops, SparseCore 0:
  39.3 59.0 all-gather.1

commit v11 on v10

--- a/solution.py
+++ b/solution.py
@@ -384,11 +384,12 @@
     for step in NEAR[1:]:
         up, down, near = beside((shift(up, "z", 1), shift(down, "z", -1), shares(step)))
         up, down = add(up, near[0]), add(down, near[1])
-    mine = add(shift(up, "z", 1), shift(down, "z", -1), near[2])
+    up, down = shift(up, "z", 1), shift(down, "z", -1)
     yh = lax.axis_index("yh")
     total = None
     for flip in range(2):
-        part = lax.dynamic_index_in_dim(mine, (yh + flip) % 2, 0, keepdims=False)
+        half = lambda value: lax.dynamic_index_in_dim(value, (yh + flip) % 2, 0, keepdims=False)
+        part = beside(add(half(up), half(down), half(near[2])))
         part = lax.ppermute(part, AXES, plane_moves(flip)).astype(jnp.float32)
         total = part if total is None else total + part
     return lax.ppermute(total.astype(jnp.bfloat16), AXES, line_moves()).transpose(1, 0, 2)

time: 200 us -> 200 us (level)
  no operation moved by 1% of the time
where the time goes in v11:
time: 200 us; the launch traced here: 197 us
  starting transfers between devices  72.4 us (36%)
  waiting for transfers between devices  64.7 us (32%)
  Pallas kernels  39.9 us (20%)
  between operations  13.7 us (7%)
  local copies, waits for them, and re-layouts  4.48 us (2%)
    ppermute x27, starting transfers between devices, shift(): lax.ppermute(value, axis, [(i, (i + by) % count) for i in range(count)])  28.3 us
    ppermute x27, waiting for transfers between devices, shift(): lax.ppermute(value, axis, [(i, (i + by) % count) for i in range(count)])  23.3 us
    all_to_all x2, starting transfers between devices, local(): lax.all_to_all(value, axes, split_axis=0, concat_axis=0, tiled=True)  21.1 us
    pallas_call x1, Pallas kernels, far_shares(): pl.pallas_call(functools.partial(share_kernel, count), out_shape=[jax.Sha...  19 us
    pallas_call x3, Pallas kernels, near_shares(): pl.pallas_call(functools.partial(near_kernel, count, near), out_shape=[SH...  16.2 us
    ppermute x1, waiting for transfers between devices, local(): rows_w = lax.ppermute(rows_w, AXES, worker_moves())  15.5 us
    all_to_all x2, waiting for transfers between devices, local(): lax.all_to_all(value, axes, split_axis=0, concat_axis=0, tiled=True)  12.4 us
    ppermute x1, starting transfers between devices, local(): rows_w = lax.ppermute(rows_w, AXES, worker_moves())  9.82 us
  transfers between devices with their start and end apart: 34, of which 13 were waited for; matrix products, arithmetic and copies ran while one was open for 1% of the time, Pallas kernels for 11%

profile of v11, /device:TPU:3, one launch (start us, length us, event | category | flops | bytes accessed | tf_op | source)
XLA Modules:
  0.0 197.1 jit_solution(5395723139322413977)
XLA Ops:
  6.5 1.2 collective-permute-start.2
  7.8 0.3 collective-permute-start.3
  8.0 1.3 collective-permute-start.4
  9.3 0.7 constant_dynamic-slice_fusion
  10.0 0.6 slice.34
  10.6 2.4 %shard_map.46 = bf16[512,384]{1,0:T(8,128)(2,1)} custom-call(s32[1]{0:T(128)} %bitcast.2.start, bf16[3,4096,128]{2,1,0:T(8,128)(2,1)} %bitcast.73), custom_call_target="tpu_custom_call" | custom-call | tf_op jit(solution)/shard_map/pallas_call | solution.py:183
  13.0 9.8 %collective-permute-start = (bf16[512,384]{1,0:T(8,128)(2,1)}, bf16[512,384]{1,0:T(8,128)(2,1)S(1)}, u32[]{:S(2)}, u32[]{:S(2)}) collective-permute-start(bf16[512,384]{1,0:T(8,128)(2,1)} %shard_map.46), channel_id=1, source_target_pairs={{0,0},{128,1},{32,2},{160,3},{64,4},{192,5},{96,6},{224,7},{16,8},... | collective-permute-start | bytes 1179656 | tf_op jit(solution)/shard_map/ppermute | solution.py:365
  22.8 15.5 %collective-permute-done = bf16[512,384]{1,0:T(8,128)(2,1)S(1)} collective-permute-done((bf16[512,384]{1,0:T(8,128)(2,1)}, bf16[512,384]{1,0:T(8,128)(2,1)S(1)}, u32[]{:S(2)}, u32[]{:S(2)}) %collective-permute-start) | collective-permute-done | bytes 393248 | tf_op jit(solution)/shard_map/ppermute | solution.py:365
  38.4 0.8 copy-done.4
  39.2 0.1 collective-permute-start.10
  39.3 2.9 %collective-permute-start.9 = (bf16[128,4096]{1,0:T(8,128)(2,1)}, bf16[128,4096]{1,0:T(8,128)(2,1)}, u32[]{:S(2)}, u32[]{:S(2)}) collective-permute-start(bf16[128,4096]{1,0:T(8,128)(2,1)} %collective-permute-done.3), channel_id=1, source_target_pairs={{0,96},{32,0},{64,32},{96,64},{1,97},{33,1},{65,33},{97,65},{2,98}... | collective-permute-start | bytes 3145736 | tf_op jit(solution)/shard_map/ppermute | solution.py:70
  42.2 11.4 %all-to-all-start = ((bf16[16,128,128]{2,1,0:T(8,128)(2,1)}), bf16[16,128,128]{2,1,0:T(8,128)(2,1)}, u32[]{:S(2)}, u32[]{:S(2)}) async-start(bf16[16,128,128]{2,1,0:T(8,128)(2,1)} %bitcast.5), calls=%async_computation | async-start | bytes 1048576 | tf_op jit(solution)/shard_map/all_to_all | solution.py:367
  53.7 3.1 %collective-permute-start.1 = (bf16[128,4096]{1,0:T(8,128)(2,1)S(1)}, bf16[128,4096]{1,0:T(8,128)(2,1)S(1)}, u32[]{:S(2)}, u32[]{:S(2)}) collective-permute-start(bf16[128,4096]{1,0:T(8,128)(2,1)S(1)} %bitcast.48), channel_id=1, source_target_pairs={{0,16},{16,0},{1,17},{17,1},{2,18},{18,2},{3,19},{19,3},{4,20},{20... | collective-permute-start | bytes 3145736 | tf_op jit(solution)/shard_map/ppermute | solution.py:70
  56.7 0.1 collective-permute-start.6
  56.8 10.6 %collective-permute-done.10.refs_1_ = bf16[128,4096]{1,0:T(8,128)(2,1)} collective-permute-done((bf16[128,4096]{1,0:T(8,128)(2,1)}, bf16[128,4096]{1,0:T(8,128)(2,1)}, u32[]{:S(2)}, u32[]{:S(2)}) %collective-permute-start.10) | collective-permute-done | bytes 1048608 | tf_op jit(solution)/shard_map/ppermute | solution.py:70
  67.5 0.5 collective-permute-start.5
  68.0 4.9 %all-to-all-done = bf16[16,128,128]{2,1,0:T(8,128)(2,1)} async-done(((bf16[16,128,128]{2,1,0:T(8,128)(2,1)}), bf16[16,128,128]{2,1,0:T(8,128)(2,1)}, u32[]{:S(2)}, u32[]{:S(2)}) %all-to-all-start) | async-done | bytes 524320 | tf_op jit(solution)/shard_map/all_to_all | solution.py:367
  72.9 2.2 %shard_map.47 = (bf16[48,4096]{1,0:T(8,128)(2,1)}, bf16[48,4096]{1,0:T(8,128)(2,1)}, bf16[32,4096]{1,0:T(8,128)(2,1)}) custom-call(bf16[128,4096]{1,0:T(8,128)(2,1)} %collective-permute-done.8.refs_0_, bf16[128,4096]{1,0:T(8,128)(2,1)} %collective-permute-done.10.refs_1_, bf16[128,4096]{1,0:T(8,128)(2,1)} %collective-permute-done.9.refs_2_), custom_call_target="tpu_custom_call" | custom-call | flops 30000001024 | tf_op jit(solution)/shard_map/pallas_call | solution.py:92
  75.2 0.8 collective-permute-start.14
  76.0 3.2 %collective-permute-start.15 = (bf16[48,4096]{1,0:T(8,128)(2,1)}, bf16[48,4096]{1,0:T(8,128)(2,1)}, u32[]{:S(2)}, u32[]{:S(2)}) collective-permute-start(bf16[48,4096]{1,0:T(8,128)(2,1)} %get-tuple-element.49), channel_id=1, source_target_pairs={{0,96},{32,0},{64,32},{96,64},{1,97},{33,1},{65,33},{97,65},{2,98}... | collective-permute-start | bytes 1179656 | tf_op jit(solution)/shard_map/ppermute | solution.py:70
  79.2 2.3 %collective-permute-start.16 = (bf16[32,4096]{1,0:T(8,128)(2,1)}, bf16[32,4096]{1,0:T(8,128)(2,1)}, u32[]{:S(2)}, u32[]{:S(2)}) collective-permute-start(bf16[32,4096]{1,0:T(8,128)(2,1)} %get-tuple-element.50), channel_id=1, source_target_pairs={{0,128},{128,0},{1,129},{129,1},{2,130},{130,2},{3,131},{131,3},{4... | collective-permute-start | bytes 786440 | tf_op jit(solution)/shard_map/ppermute | solution.py:70
  81.5 9.7 %all-to-all-start.1 = ((bf16[16,128,128]{2,1,0:T(8,128)(2,1)}), bf16[16,128,128]{2,1,0:T(8,128)(2,1)}, u32[]{:S(2)}, u32[]{:S(2)}) async-start(bf16[16,128,128]{2,1,0:T(8,128)(2,1)} %all-to-all-done), calls=%async_computation.1 | async-start | bytes 1048576 | tf_op jit(solution)/shard_map/all_to_all | solution.py:367
  91.2 0.4 collective-permute-start.11
  91.7 0.1 collective-permute-start.12
  91.8 0.4 collective-permute-start.13
  92.3 7.5 %all-to-all-done.1 = bf16[16,128,128]{2,1,0:T(8,128)(2,1)} async-done(((bf16[16,128,128]{2,1,0:T(8,128)(2,1)}), bf16[16,128,128]{2,1,0:T(8,128)(2,1)}, u32[]{:S(2)}, u32[]{:S(2)}) %all-to-all-start.1) | async-done | bytes 524320 | tf_op jit(solution)/shard_map/all_to_all | solution.py:367
  99.8 1.3 collective-permute-start.19
  101.3 0.1 le.15
  101.4 0.1 eq.22
  101.4 0.3 collective-permute-start.17
  101.7 0.9 collective-permute-done.19
  102.6 0.4 collective-permute-start.18
  103.0 0.7 slice_bitcast_fusion.1.order
  103.7 0.1 and_convert_fusion.mask
  103.8 0.8 collective-permute-done.18
  104.6 19.0 %shard_map.48 = (bf16[384,2048]{1,0:T(8,128)(2,1)}, bf16[3,256,128]{2,1,0:T(8,128)(2,1)S(1)}, bf16[3,256,128]{2,1,0:T(8,128)(2,1)S(1)}) custom-call(s32[24]{0:T(128)S(1)} %slice_bitcast_fusion.1.order, f32[256,256]{1,0:T(8,128)S(1)} %and_convert_fusion.mask, bf16[4096,384]{1,0:T(8,128)(2,1)} %all-gather.2.cloned.1.call-done.w_ref, ...), custom_call_target="tpu_custom_call" | custom-call | flops 6442450944 | bytes 16777216 | tf_op jit(solution)/shard_map/pallas_call | solution.py:336
  123.7 0.1 collective-permute-start.20
  123.8 2.7 %collective-permute-start.21 = (bf16[3,256,128]{2,1,0:T(8,128)(2,1)S(1)}, bf16[3,256,128]{2,1,0:T(8,128)(2,1)S(1)}, u32[]{:S(2)}, u32[]{:S(2)}) collective-permute-start(bf16[3,256,128]{2,1,0:T(8,128)(2,1)S(1)} %get-tuple-element.55), channel_id=1, source_target_pairs={{0,7},{1,0},{2,1},{3,2},{4,3},{5,4},{6,5},{7,6},{8,15},{9,8},{10,9... | collective-permute-start | bytes 589832 | tf_op jit(solution)/shard_map/ppermute | solution.py:70
  126.4 4.9 %shard_map.49 = (bf16[2,3,256,128]{3,2,1,0:T(8,128)(2,1)S(1)}, bf16[2,3,256,128]{3,2,1,0:T(8,128)(2,1)S(1)}) custom-call(s32[24]{0:T(128)S(1)} %slice_bitcast_fusion.1.order, bf16[384,2048]{1,0:T(8,128)(2,1)} %get-tuple-element.56.turned_ref, bf16[8,16,4096]{2,1,0:T(8,128)(2,1)S(1)} %bitcast.50, bf16[8,16,4096]{2,1,0:T(8,128)(2,1)S(1)} %bitcast.58, ...), custom_call_target="tpu_custom_call" | custom-call | flops 1610612736 | bytes 4194304 | tf_op jit(solution)/shard_map/pallas_call | solution.py:313
  131.5 2.1 %collective-permute-start.23 = (bf16[2,3,256,128]{3,2,1,0:T(8,128)(2,1)S(1)}, bf16[2,3,256,128]{3,2,1,0:T(8,128)(2,1)S(1)}, u32[]{:S(2)}, u32[]{:S(2)}) collective-permute-start(bf16[2,3,256,128]{3,2,1,0:T(8,128)(2,1)S(1)} %pad_maximum_fusion.1), channel_id=1, source_target_pairs={{0,7},{1,0},{2,1},{3,2},{4,3},{5,4},{6,5},{7,6},{8,15},{9,8},{10,9... | collective-permute-start | bytes 1179656 | tf_op jit(solution)/shard_map/ppermute | solution.py:70
  133.8 0.1 collective-permute-start.22
  133.8 4.9 %shard_map.50 = (bf16[2,3,256,128]{3,2,1,0:T(8,128)(2,1)S(1)}, bf16[2,3,256,128]{3,2,1,0:T(8,128)(2,1)S(1)}) custom-call(s32[24]{0:T(128)S(1)} %slice_bitcast_fusion.1.order, bf16[384,2048]{1,0:T(8,128)(2,1)} %get-tuple-element.56.turned_ref, bf16[8,16,4096]{2,1,0:T(8,128)(2,1)S(1)} %bitcast.51, bf16[8,16,4096]{2,1,0:T(8,128)(2,1)S(1)} %bitcast.59, ...), custom_call_target="tpu_custom_call" | custom-call | flops 1610612736 | bytes 4194304 | tf_op jit(solution)/shard_map/pallas_call | solution.py:313
  138.8 2.5 %collective-permute-done.23 = bf16[2,3,256,128]{3,2,1,0:T(8,128)(2,1)S(1)} collective-permute-done((bf16[2,3,256,128]{3,2,1,0:T(8,128)(2,1)S(1)}, bf16[2,3,256,128]{3,2,1,0:T(8,128)(2,1)S(1)}, u32[]{:S(2)}, u32[]{:S(2)}) %collective-permute-start.23) | collective-permute-done | bytes 393248 | tf_op jit(solution)/shard_map/ppermute | solution.py:70
  141.3 2.6 %collective-permute-done.22 = bf16[2,3,256,128]{3,2,1,0:T(8,128)(2,1)S(1)} collective-permute-done((bf16[2,3,256,128]{3,2,1,0:T(8,128)(2,1)S(1)}, bf16[2,3,256,128]{3,2,1,0:T(8,128)(2,1)S(1)}, u32[]{:S(2)}, u32[]{:S(2)}) %collective-permute-start.22) | collective-permute-done | bytes 393248 | tf_op jit(solution)/shard_map/ppermute | solution.py:70
  143.9 0.1 add_convert_fusion.2
  144.0 0.2 collective-permute-start.25
  144.1 0.1 add_convert_fusion.3
  144.2 1.5 collective-permute-start.24
  145.7 6.4 %shard_map.51 = (bf16[2,3,256,128]{3,2,1,0:T(8,128)(2,1)S(1)}, bf16[2,3,256,128]{3,2,1,0:T(8,128)(2,1)S(1)}, bf16[2,3,256,128]{3,2,1,0:T(8,128)(2,1)S(1)}) custom-call(s32[24]{0:T(128)S(1)} %slice_bitcast_fusion.1.order, bf16[384,2048]{1,0:T(8,128)(2,1)} %get-tuple-element.56.turned_ref, bf16[8,16,4096]{2,1,0:T(8,128)(2,1)S(1)} %bitcast.52, ...), custom_call_target="tpu_custom_call" | custom-call | flops 2415919104 | bytes 6291456 | tf_op jit(solution)/shard_map/pallas_call | solution.py:313
  152.1 0.7 copy-done.3
  152.8 0.6 collective-permute-done.24
  153.4 0.1 add_convert_fusion.1
  153.5 0.1 collective-permute-start.26
  153.6 0.1 add_convert_fusion
  153.7 2.7 %collective-permute-start.27 = (bf16[2,3,256,128]{3,2,1,0:T(8,128)(2,1)S(1)}, bf16[2,3,256,128]{3,2,1,0:T(8,128)(2,1)S(1)}, u32[]{:S(2)}, u32[]{:S(2)}) collective-permute-start(bf16[2,3,256,128]{3,2,1,0:T(8,128)(2,1)S(1)} %add_convert_fusion), channel_id=1, source_target_pairs={{0,7},{1,0},{2,1},{3,2},{4,3},{5,4},{6,5},{7,6},{8,15},{9,8},{10,9... | collective-permute-start | bytes 1179656 | tf_op jit(solution)/shard_map/ppermute | solution.py:70
  156.5 5.3 %collective-permute-done.26 = bf16[2,3,256,128]{3,2,1,0:T(8,128)(2,1)S(1)} collective-permute-done((bf16[2,3,256,128]{3,2,1,0:T(8,128)(2,1)S(1)}, bf16[2,3,256,128]{3,2,1,0:T(8,128)(2,1)S(1)}, u32[]{:S(2)}, u32[]{:S(2)}) %collective-permute-start.26) | collective-permute-done | bytes 393248 | tf_op jit(solution)/shard_map/ppermute | solution.py:70
  161.8 1.2 fusion.2
  163.0 6.6 %collective-permute-start.28 = (bf16[3,256,128]{2,1,0:T(8,128)(2,1)S(1)}, bf16[3,256,128]{2,1,0:T(8,128)(2,1)S(1)}, u32[]{:S(2)}, u32[]{:S(2)}) collective-permute-start(bf16[3,256,128]{2,1,0:T(8,128)(2,1)S(1)} %get-tuple-element.77), channel_id=1, source_target_pairs={{0,0},{1,129},{2,34},{3,163},{4,68},{5,197},{6,102},{7,231},{8,16}... | collective-permute-start | bytes 589832 | tf_op jit(solution)/shard_map/ppermute | solution.py:393
  169.5 0.1 collective-permute-start.29
  169.6 3.2 %collective-permute-done.28 = bf16[3,256,128]{2,1,0:T(8,128)(2,1)S(1)} collective-permute-done((bf16[3,256,128]{2,1,0:T(8,128)(2,1)S(1)}, bf16[3,256,128]{2,1,0:T(8,128)(2,1)S(1)}, u32[]{:S(2)}, u32[]{:S(2)}) %collective-permute-start.28) | collective-permute-done | bytes 196640 | tf_op jit(solution)/shard_map/ppermute | solution.py:393
  172.9 1.4 collective-permute-done.29
  174.3 6.5 %collective-permute-start.30 = (bf16[3,256,128]{2,1,0:T(8,128)(2,1)S(1)}, bf16[3,256,128]{2,1,0:T(8,128)(2,1)S(1)}, u32[]{:S(2)}, u32[]{:S(2)}) collective-permute-start(bf16[3,256,128]{2,1,0:T(8,128)(2,1)S(1)} %add_convert_fusion.4), channel_id=1, source_target_pairs={{0,0},{1,1},{2,6},{3,7},{4,4},{5,5},{6,2},{7,3},{8,8},{9,9},{10,14... | collective-permute-start | bytes 589832 | tf_op jit(solution)/shard_map/ppermute | solution.py:395
  180.8 8.7 %collective-permute-done.30 = bf16[3,256,128]{2,1,0:T(8,128)(2,1)S(1)} collective-permute-done((bf16[3,256,128]{2,1,0:T(8,128)(2,1)S(1)}, bf16[3,256,128]{2,1,0:T(8,128)(2,1)S(1)}, u32[]{:S(2)}, u32[]{:S(2)}) %collective-permute-start.30) | collective-permute-done | bytes 196640 | tf_op jit(solution)/shard_map/ppermute | solution.py:395
  189.6 0.7 copy.6
  (45 shorter events, 0.5 us)
Async XLA Ops:
  6.5 47.1 %copy-start = (bf16[1,128,4096]{2,1,0:T(8,128)(2,1)S(1)}, bf16[1,128,4096]{2,1,0:T(8,128)(2,1)}, u32[]{:S(2)}) copy-start(bf16[1,128,4096]{2,1,0:T(8,128)(2,1)} %param.4) | copy-start | bytes 3145732
  6.5 98.1 %all-gather.2.cloned.1.call-start = ((), (), s32[]{:S(2)}) async-start(), calls=%async_computation.2 | async-start | bytes 3538944 | tf_op jit(solution)/shard_map/all_gather | solution.py:366
  6.5 32.6 %collective-permute-start.2 = (bf16[128,4096]{1,0:T(8,128)(2,1)}, bf16[128,4096]{1,0:T(8,128)(2,1)S(1)}, u32[]{:S(2)}, u32[]{:S(2)}) collective-permute-start(bf16[128,4096]{1,0:T(8,128)(2,1)} %bitcast.45), channel_id=1, source_target_pairs={{0,32},{32,64},{64,96},{96,0},{1,33},{33,65},{65,97},{97,1},{2,34}... | collective-permute-start | bytes 3145736 | tf_op jit(solution)/shard_map/ppermute | solution.py:70
  7.8 31.4 %collective-permute-start.3 = (bf16[128,4096]{1,0:T(8,128)(2,1)}, bf16[128,4096]{1,0:T(8,128)(2,1)}, u32[]{:S(2)}, u32[]{:S(2)}) collective-permute-start(bf16[128,4096]{1,0:T(8,128)(2,1)} %bitcast.46), channel_id=1, source_target_pairs={{0,96},{32,0},{64,32},{96,64},{1,97},{33,1},{65,33},{97,65},{2,98}... | collective-permute-start | bytes 3145736 | tf_op jit(solution)/shard_map/ppermute | solution.py:70
  8.0 31.2 %collective-permute-start.4 = (bf16[128,4096]{1,0:T(8,128)(2,1)}, bf16[128,4096]{1,0:T(8,128)(2,1)}, u32[]{:S(2)}, u32[]{:S(2)}) collective-permute-start(bf16[128,4096]{1,0:T(8,128)(2,1)} %bitcast.47), channel_id=1, source_target_pairs={{0,128},{128,0},{1,129},{129,1},{2,130},{130,2},{3,131},{131,3},{4... | collective-permute-start | bytes 3145736 | tf_op jit(solution)/shard_map/ppermute | solution.py:70
  10.0 91.1 %copy-start.5 = (s32[1,48]{1,0:T(1,128)}, s32[1,48]{1,0:T(1,128)S(1)}, u32[]{:S(2)}) copy-start(s32[1,48]{1,0:T(1,128)S(1)} %constant_dynamic-slice_fusion) | copy-start | bytes 580
  13.0 25.4 %collective-permute-start = (bf16[512,384]{1,0:T(8,128)(2,1)}, bf16[512,384]{1,0:T(8,128)(2,1)S(1)}, u32[]{:S(2)}, u32[]{:S(2)}) collective-permute-start(bf16[512,384]{1,0:T(8,128)(2,1)} %shard_map.46), channel_id=1, source_target_pairs={{0,0},{128,1},{32,2},{160,3},{64,4},{192,5},{96,6},{224,7},{16,8},... | collective-permute-start | bytes 1179656 | tf_op jit(solution)/shard_map/ppermute | solution.py:365
  38.4 0.8 copy-start.4
  39.2 36.0 %copy-start.1 = (bf16[128,4096]{1,0:T(8,128)(2,1)}, bf16[128,4096]{1,0:T(8,128)(2,1)S(1)}, u32[]{:S(2)}) copy-start(bf16[128,4096]{1,0:T(8,128)(2,1)S(1)} %collective-permute-done.2) | copy-start | bytes 3145732
  39.2 28.3 %collective-permute-start.10 = (bf16[128,4096]{1,0:T(8,128)(2,1)}, bf16[128,4096]{1,0:T(8,128)(2,1)}, u32[]{:S(2)}, u32[]{:S(2)}) collective-permute-start(bf16[128,4096]{1,0:T(8,128)(2,1)} %collective-permute-done.3), channel_id=1, source_target_pairs={{0,128},{128,0},{1,129},{129,1},{2,130},{130,2},{3,131},{131,3},{4... | collective-permute-start | bytes 3145736 | tf_op jit(solution)/shard_map/ppermute | solution.py:70
  39.3 28.2 %collective-permute-start.9 = (bf16[128,4096]{1,0:T(8,128)(2,1)}, bf16[128,4096]{1,0:T(8,128)(2,1)}, u32[]{:S(2)}, u32[]{:S(2)}) collective-permute-start(bf16[128,4096]{1,0:T(8,128)(2,1)} %collective-permute-done.3), channel_id=1, source_target_pairs={{0,96},{32,0},{64,32},{96,64},{1,97},{33,1},{65,33},{97,65},{2,98}... | collective-permute-start | bytes 3145736 | tf_op jit(solution)/shard_map/ppermute | solution.py:70
  42.2 30.7 %collective-permute-start.8 = (bf16[128,4096]{1,0:T(8,128)(2,1)}, bf16[128,4096]{1,0:T(8,128)(2,1)}, u32[]{:S(2)}, u32[]{:S(2)}) collective-permute-start(bf16[128,4096]{1,0:T(8,128)(2,1)} %collective-permute-done.4), channel_id=1, source_target_pairs={{0,32},{32,64},{64,96},{96,0},{1,33},{33,65},{65,97},{97,1},{2,34}... | collective-permute-start | bytes 3145736 | tf_op jit(solution)/shard_map/ppermute | solution.py:70
  42.2 30.7 %all-to-all-start = ((bf16[16,128,128]{2,1,0:T(8,128)(2,1)}), bf16[16,128,128]{2,1,0:T(8,128)(2,1)}, u32[]{:S(2)}, u32[]{:S(2)}) async-start(bf16[16,128,128]{2,1,0:T(8,128)(2,1)} %bitcast.5), calls=%async_computation | async-start | bytes 1048576 | tf_op jit(solution)/shard_map/all_to_all | solution.py:367
  53.7 22.3 %collective-permute-start.1 = (bf16[128,4096]{1,0:T(8,128)(2,1)S(1)}, bf16[128,4096]{1,0:T(8,128)(2,1)S(1)}, u32[]{:S(2)}, u32[]{:S(2)}) collective-permute-start(bf16[128,4096]{1,0:T(8,128)(2,1)S(1)} %bitcast.48), channel_id=1, source_target_pairs={{0,16},{16,0},{1,17},{17,1},{2,18},{18,2},{3,19},{19,3},{4,20},{20... | collective-permute-start | bytes 3145736 | tf_op jit(solution)/shard_map/ppermute | solution.py:70
  56.7 22.5 %collective-permute-start.6 = (bf16[128,4096]{1,0:T(8,128)(2,1)}, bf16[128,4096]{1,0:T(8,128)(2,1)}, u32[]{:S(2)}, u32[]{:S(2)}) collective-permute-start(bf16[128,4096]{1,0:T(8,128)(2,1)} %collective-permute-done.3), channel_id=1, source_target_pairs={{0,16},{16,0},{1,17},{17,1},{2,18},{18,2},{3,19},{19,3},{4,20},{20... | collective-permute-start | bytes 3145736 | tf_op jit(solution)/shard_map/ppermute | solution.py:70
  67.5 32.3 %collective-permute-start.7 = (bf16[128,4096]{1,0:T(8,128)(2,1)}, bf16[128,4096]{1,0:T(8,128)(2,1)}, u32[]{:S(2)}, u32[]{:S(2)}) collective-permute-start(bf16[128,4096]{1,0:T(8,128)(2,1)} %collective-permute-done.4), channel_id=1, source_target_pairs={{0,16},{16,0},{1,17},{17,1},{2,18},{18,2},{3,19},{19,3},{4,20},{20... | collective-permute-start | bytes 3145736 | tf_op jit(solution)/shard_map/ppermute | solution.py:70
  67.5 33.9 %collective-permute-start.5 = (bf16[128,4096]{1,0:T(8,128)(2,1)S(1)}, bf16[128,4096]{1,0:T(8,128)(2,1)}, u32[]{:S(2)}, u32[]{:S(2)}) collective-permute-start(bf16[128,4096]{1,0:T(8,128)(2,1)S(1)} %collective-permute-done.2), channel_id=1, source_target_pairs={{0,16},{16,0},{1,17},{17,1},{2,18},{18,2},{3,19},{19,3},{4,20},{20... | collective-permute-start | bytes 3145736 | tf_op jit(solution)/shard_map/ppermute | solution.py:70
  75.2 16.5 %collective-permute-start.14 = (bf16[48,4096]{1,0:T(8,128)(2,1)}, bf16[48,4096]{1,0:T(8,128)(2,1)S(1)}, u32[]{:S(2)}, u32[]{:S(2)}) collective-permute-start(bf16[48,4096]{1,0:T(8,128)(2,1)} %get-tuple-element.48), channel_id=1, source_target_pairs={{0,32},{32,64},{64,96},{96,0},{1,33},{33,65},{65,97},{97,1},{2,34}... | collective-permute-start | bytes 1179656 | tf_op jit(solution)/shard_map/ppermute | solution.py:70
  76.0 15.8 %collective-permute-start.15 = (bf16[48,4096]{1,0:T(8,128)(2,1)}, bf16[48,4096]{1,0:T(8,128)(2,1)}, u32[]{:S(2)}, u32[]{:S(2)}) collective-permute-start(bf16[48,4096]{1,0:T(8,128)(2,1)} %get-tuple-element.49), channel_id=1, source_target_pairs={{0,96},{32,0},{64,32},{96,64},{1,97},{33,1},{65,33},{97,65},{2,98}... | collective-permute-start | bytes 1179656 | tf_op jit(solution)/shard_map/ppermute | solution.py:70
  79.2 12.0 %collective-permute-start.16 = (bf16[32,4096]{1,0:T(8,128)(2,1)}, bf16[32,4096]{1,0:T(8,128)(2,1)}, u32[]{:S(2)}, u32[]{:S(2)}) collective-permute-start(bf16[32,4096]{1,0:T(8,128)(2,1)} %get-tuple-element.50), channel_id=1, source_target_pairs={{0,128},{128,0},{1,129},{129,1},{2,130},{130,2},{3,131},{131,3},{4... | collective-permute-start | bytes 786440 | tf_op jit(solution)/shard_map/ppermute | solution.py:70
  81.5 18.3 %all-to-all-start.1 = ((bf16[16,128,128]{2,1,0:T(8,128)(2,1)}), bf16[16,128,128]{2,1,0:T(8,128)(2,1)}, u32[]{:S(2)}, u32[]{:S(2)}) async-start(bf16[16,128,128]{2,1,0:T(8,128)(2,1)} %all-to-all-done), calls=%async_computation.1 | async-start | bytes 1048576 | tf_op jit(solution)/shard_map/all_to_all | solution.py:367
  91.2 13.3 %collective-permute-start.11 = (bf16[128,4096]{1,0:T(8,128)(2,1)}, bf16[128,4096]{1,0:T(8,128)(2,1)}, u32[]{:S(2)}, u32[]{:S(2)}) collective-permute-start(bf16[128,4096]{1,0:T(8,128)(2,1)} %collective-permute-done.8.refs_0_), channel_id=1, source_target_pairs={{0,16},{16,0},{1,17},{17,1},{2,18},{18,2},{3,19},{19,3},{4,20},{20... | collective-permute-start | bytes 3145736 | tf_op jit(solution)/shard_map/ppermute | solution.py:70
  91.7 12.9 %collective-permute-start.12 = (bf16[128,4096]{1,0:T(8,128)(2,1)}, bf16[128,4096]{1,0:T(8,128)(2,1)}, u32[]{:S(2)}, u32[]{:S(2)}) collective-permute-start(bf16[128,4096]{1,0:T(8,128)(2,1)} %collective-permute-done.9.refs_2_), channel_id=1, source_target_pairs={{0,16},{16,0},{1,17},{17,1},{2,18},{18,2},{3,19},{19,3},{4,20},{20... | collective-permute-start | bytes 3145736 | tf_op jit(solution)/shard_map/ppermute | solution.py:70
  91.8 12.7 %collective-permute-start.13 = (bf16[128,4096]{1,0:T(8,128)(2,1)}, bf16[128,4096]{1,0:T(8,128)(2,1)}, u32[]{:S(2)}, u32[]{:S(2)}) collective-permute-start(bf16[128,4096]{1,0:T(8,128)(2,1)} %collective-permute-done.10.refs_1_), channel_id=1, source_target_pairs={{0,16},{16,0},{1,17},{17,1},{2,18},{18,2},{3,19},{19,3},{4,20},{20... | collective-permute-start | bytes 3145736 | tf_op jit(solution)/shard_map/ppermute | solution.py:70
  99.8 2.8 %collective-permute-start.19 = (bf16[32,4096]{1,0:T(8,128)(2,1)}, bf16[32,4096]{1,0:T(8,128)(2,1)}, u32[]{:S(2)}, u32[]{:S(2)}) collective-permute-start(bf16[32,4096]{1,0:T(8,128)(2,1)} %collective-permute-done.16), channel_id=1, source_target_pairs={{0,16},{16,0},{1,17},{17,1},{2,18},{18,2},{3,19},{19,3},{4,20},{20... | collective-permute-start | bytes 786440 | tf_op jit(solution)/shard_map/ppermute | solution.py:70
  101.4 2.4 %collective-permute-start.17 = (bf16[48,4096]{1,0:T(8,128)(2,1)S(1)}, bf16[48,4096]{1,0:T(8,128)(2,1)S(1)}, u32[]{:S(2)}, u32[]{:S(2)}) collective-permute-start(bf16[48,4096]{1,0:T(8,128)(2,1)S(1)} %collective-permute-done.14), channel_id=1, source_target_pairs={{0,16},{16,0},{1,17},{17,1},{2,18},{18,2},{3,19},{19,3},{4,20},{20... | collective-permute-start | bytes 1179656 | tf_op jit(solution)/shard_map/ppermute | solution.py:70
  102.6 1.9 collective-permute-start.18
  104.6 21.8 %copy-start.2 = (bf16[128,4096]{1,0:T(8,128)(2,1)S(1)}, bf16[128,4096]{1,0:T(8,128)(2,1)}, u32[]{:S(2)}) copy-start(bf16[128,4096]{1,0:T(8,128)(2,1)} %copy-done.1) | copy-start | bytes 3145732
  123.7 7.7 %collective-permute-start.20 = (bf16[3,256,128]{2,1,0:T(8,128)(2,1)S(1)}, bf16[3,256,128]{2,1,0:T(8,128)(2,1)S(1)}, u32[]{:S(2)}, u32[]{:S(2)}) collective-permute-start(bf16[3,256,128]{2,1,0:T(8,128)(2,1)S(1)} %get-tuple-element.54), channel_id=1, source_target_pairs={{0,1},{1,2},{2,3},{3,4},{4,5},{5,6},{6,7},{7,0},{8,9},{9,10},{10,1... | collective-permute-start | bytes 589832 | tf_op jit(solution)/shard_map/ppermute | solution.py:70
  123.8 7.6 %collective-permute-start.21 = (bf16[3,256,128]{2,1,0:T(8,128)(2,1)S(1)}, bf16[3,256,128]{2,1,0:T(8,128)(2,1)S(1)}, u32[]{:S(2)}, u32[]{:S(2)}) collective-permute-start(bf16[3,256,128]{2,1,0:T(8,128)(2,1)S(1)} %get-tuple-element.55), channel_id=1, source_target_pairs={{0,7},{1,0},{2,1},{3,2},{4,3},{5,4},{6,5},{7,6},{8,15},{9,8},{10,9... | collective-permute-start | bytes 589832 | tf_op jit(solution)/shard_map/ppermute | solution.py:70
  131.5 9.8 %collective-permute-start.23 = (bf16[2,3,256,128]{3,2,1,0:T(8,128)(2,1)S(1)}, bf16[2,3,256,128]{3,2,1,0:T(8,128)(2,1)S(1)}, u32[]{:S(2)}, u32[]{:S(2)}) collective-permute-start(bf16[2,3,256,128]{3,2,1,0:T(8,128)(2,1)S(1)} %pad_maximum_fusion.1), channel_id=1, source_target_pairs={{0,7},{1,0},{2,1},{3,2},{4,3},{5,4},{6,5},{7,6},{8,15},{9,8},{10,9... | collective-permute-start | bytes 1179656 | tf_op jit(solution)/shard_map/ppermute | solution.py:70
  133.8 10.1 %collective-permute-start.22 = (bf16[2,3,256,128]{3,2,1,0:T(8,128)(2,1)S(1)}, bf16[2,3,256,128]{3,2,1,0:T(8,128)(2,1)S(1)}, u32[]{:S(2)}, u32[]{:S(2)}) collective-permute-start(bf16[2,3,256,128]{3,2,1,0:T(8,128)(2,1)S(1)} %pad_maximum_fusion), channel_id=1, source_target_pairs={{0,1},{1,2},{2,3},{3,4},{4,5},{5,6},{6,7},{7,0},{8,9},{9,10},{10,1... | collective-permute-start | bytes 1179656 | tf_op jit(solution)/shard_map/ppermute | solution.py:70
  144.0 8.8 %collective-permute-start.25 = (bf16[2,3,256,128]{3,2,1,0:T(8,128)(2,1)S(1)}, bf16[2,3,256,128]{3,2,1,0:T(8,128)(2,1)S(1)}, u32[]{:S(2)}, u32[]{:S(2)}) collective-permute-start(bf16[2,3,256,128]{3,2,1,0:T(8,128)(2,1)S(1)} %add_convert_fusion.2), channel_id=1, source_target_pairs={{0,7},{1,0},{2,1},{3,2},{4,3},{5,4},{6,5},{7,6},{8,15},{9,8},{10,9... | collective-permute-start | bytes 1179656 | tf_op jit(solution)/shard_map/ppermute | solution.py:70
  144.2 9.2 %collective-permute-start.24 = (bf16[2,3,256,128]{3,2,1,0:T(8,128)(2,1)S(1)}, bf16[2,3,256,128]{3,2,1,0:T(8,128)(2,1)S(1)}, u32[]{:S(2)}, u32[]{:S(2)}) collective-permute-start(bf16[2,3,256,128]{3,2,1,0:T(8,128)(2,1)S(1)} %add_convert_fusion.3), channel_id=1, source_target_pairs={{0,1},{1,2},{2,3},{3,4},{4,5},{5,6},{6,7},{7,0},{8,9},{9,10},{10,1... | collective-permute-start | bytes 1179656 | tf_op jit(solution)/shard_map/ppermute | solution.py:70
  152.1 0.7 copy-start.3
  153.5 8.3 %collective-permute-start.26 = (bf16[2,3,256,128]{3,2,1,0:T(8,128)(2,1)S(1)}, bf16[2,3,256,128]{3,2,1,0:T(8,128)(2,1)S(1)}, u32[]{:S(2)}, u32[]{:S(2)}) collective-permute-start(bf16[2,3,256,128]{3,2,1,0:T(8,128)(2,1)S(1)} %add_convert_fusion.1), channel_id=1, source_target_pairs={{0,1},{1,2},{2,3},{3,4},{4,5},{5,6},{6,7},{7,0},{8,9},{9,10},{10,1... | collective-permute-start | bytes 1179656 | tf_op jit(solution)/shard_map/ppermute | solution.py:70
  153.7 8.1 %collective-permute-start.27 = (bf16[2,3,256,128]{3,2,1,0:T(8,128)(2,1)S(1)}, bf16[2,3,256,128]{3,2,1,0:T(8,128)(2,1)S(1)}, u32[]{:S(2)}, u32[]{:S(2)}) collective-permute-start(bf16[2,3,256,128]{3,2,1,0:T(8,128)(2,1)S(1)} %add_convert_fusion), channel_id=1, source_target_pairs={{0,7},{1,0},{2,1},{3,2},{4,3},{5,4},{6,5},{7,6},{8,15},{9,8},{10,9... | collective-permute-start | bytes 1179656 | tf_op jit(solution)/shard_map/ppermute | solution.py:70
  163.0 9.9 %collective-permute-start.28 = (bf16[3,256,128]{2,1,0:T(8,128)(2,1)S(1)}, bf16[3,256,128]{2,1,0:T(8,128)(2,1)S(1)}, u32[]{:S(2)}, u32[]{:S(2)}) collective-permute-start(bf16[3,256,128]{2,1,0:T(8,128)(2,1)S(1)} %get-tuple-element.77), channel_id=1, source_target_pairs={{0,0},{1,129},{2,34},{3,163},{4,68},{5,197},{6,102},{7,231},{8,16}... | collective-permute-start | bytes 589832 | tf_op jit(solution)/shard_map/ppermute | solution.py:393
  169.5 4.7 %collective-permute-start.29 = (bf16[3,256,128]{2,1,0:T(8,128)(2,1)S(1)}, bf16[3,256,128]{2,1,0:T(8,128)(2,1)S(1)}, u32[]{:S(2)}, u32[]{:S(2)}) collective-permute-start(bf16[3,256,128]{2,1,0:T(8,128)(2,1)S(1)} %get-tuple-element.78), channel_id=1, source_target_pairs={{0,16},{1,145},{2,50},{3,179},{4,84},{5,213},{6,118},{7,247},{8,0}... | collective-permute-start | bytes 589832 | tf_op jit(solution)/shard_map/ppermute | solution.py:393
  174.3 15.3 %collective-permute-start.30 = (bf16[3,256,128]{2,1,0:T(8,128)(2,1)S(1)}, bf16[3,256,128]{2,1,0:T(8,128)(2,1)S(1)}, u32[]{:S(2)}, u32[]{:S(2)}) collective-permute-start(bf16[3,256,128]{2,1,0:T(8,128)(2,1)S(1)} %add_convert_fusion.4), channel_id=1, source_target_pairs={{0,0},{1,1},{2,6},{3,7},{4,4},{5,5},{6,2},{7,3},{8,8},{9,9},{10,14... | collective-permute-start | bytes 589832 | tf_op jit(solution)/shard_map/ppermute | solution.py:395
Sparse Core Ops, SparseCore 0:
  39.3 59.0 all-gather.1
